TPU v7x, 256 devices: a whole 4x4x8 slice. The times are simulated.
256 devices in a mesh: section: 2 (over z_hi), ctx: 16 (over x, y), heads: 8 (over z_lo, core).
Axes of the slice: x: 4, y: 4, z: 8 (z_hi: 2, z_lo: 4; z = z_hi * 4 + z_lo), core: 2. Of those that a mesh axis runs over, the one named last changes fastest.
Arguments:
- grad_out: bfloat16 [4096, 4096], P('ctx'), may hold values from -6 to 6
- w_out: bfloat16 [2, 8192, 4096], P('section', 'heads', 'ctx'), may hold values from -0.09375 to 0.09375
- w_in: bfloat16 [2, 4096, 8192], P('section', 'ctx', 'heads'), may hold values from -0.09375 to 0.09375
- w_bc: bfloat16 [2, 4096, 2048], P('section', 'ctx', 'heads'), may hold values from -0.09375 to 0.09375
- x_act: bfloat16 [2, 4096, 8192], P('section', 'ctx', 'heads'), may hold values from -3 to 3
- bc_act: bfloat16 [2, 4096, 2048], P('section', 'ctx', 'heads'), may hold values from -0.29882812 to 0.29882812
- decay: float32 [2, 128, 4096], P('section', 'heads', 'ctx'), may hold values from -1.5 to 0, as said below
- skip_gain: float32 [2, 128], P('section', 'heads'), may hold values from 0.5 to 1.5
- state_in: float32 [2, 16, 128, 64, 128], P('section', 'ctx', 'heads'), may hold values from -0.6 to 0.6
Outputs:
- input_grad: bfloat16 [2, 4096, 4096], P('section', 'ctx', 'heads')
Inputs may be any that keep to these rules, and one draw needn't show every extreme that they name: Log decay factors, all negative.
All inputs are finite; a program needn't handle non-finite values.
Results may differ from a plain program's by a relative error of at most 0.039.
Values may be sent and summed in bfloat16 or wider, within the bound.
No kernel may reach another device: no remote copies, remote signals or barrier semaphores. Data moves between devices by JAX's collectives and lax.ppermute only.
A program may use at most 128 MiB of HBM per device.

v0:
```python
import jax
import jax.numpy as jnp
from jax import lax
from jax.sharding import PartitionSpec as P


def carried_in(shard, axis, combine, identity):
    count, index = (lax.axis_size(axis), lax.axis_index(axis))
    everything = jax.tree.map(
        lambda part, kind: lax.all_gather(part.astype(kind), axis),
        shard,
        (jnp.bfloat16, jnp.bfloat16),
    )
    start = jax.tree.map(
        lambda part, zero: jnp.broadcast_to(jnp.asarray(zero, part.dtype), part.shape),
        shard,
        identity,
    )

    def lap(k, before):
        at = count - 1 - k
        reached = at > index
        new = combine(
            before, jax.tree.map(lambda part, own: part[at].astype(own.dtype), everything, shard)
        )
        return jax.tree.map(lambda a, b: jnp.where(reached, a, b), new, before)

    return lax.fori_loop(0, count, lap, start)


def from_behind(value, axis, steps):
    count = lax.axis_size(axis)
    initial, last = (max(0, -steps), min(count, count - steps))
    return lax.ppermute(value, axis, [(source, source + steps) for source in range(initial, last)])


def decay_table(decay_rates):
    cumulative = jnp.cumsum(decay_rates, axis=1)
    spread = cumulative[:, :, None] - cumulative[:, None, :]
    length = decay_rates.shape[1]
    lower_mask = jnp.arange(length)[:, None] >= jnp.arange(length)[None, :]
    mixer_function = jnp.where(lower_mask[None], jnp.exp(jnp.minimum(spread, 0.0)), 0.0)
    return (cumulative, mixer_function)


def block_summary(output_gradient_rows, output_projection_values, cumulative):
    length, groups, per_group, head_size = output_gradient_rows.shape
    leading = jnp.exp(cumulative).reshape(groups, per_group, length)
    entering = jnp.einsum(
        "ght,tghp,tgn->ghpn", leading, output_gradient_rows, output_projection_values
    )
    totals = jnp.exp(cumulative[:, -1])
    return (
        totals,
        entering.reshape(groups * per_group, head_size, output_projection_values.shape[2]),
    )


def block_grads(
    output_gradient_rows,
    x_vals,
    input_projection_values,
    output_projection_values,
    cumulative,
    mixer_function,
    entry_state,
    exit_grad,
    skip,
):
    length, groups, per_group, head_size = output_gradient_rows.shape
    state_size = input_projection_values.shape[2]
    leading = jnp.exp(cumulative).reshape(groups, per_group, length)
    trailing = jnp.exp(cumulative[:, -1:] - cumulative).reshape(groups, per_group, length)
    mixer_function = mixer_function.reshape(groups, per_group, length, length)
    entry = entry_state.reshape(groups, per_group, head_size, state_size)
    leaving = exit_grad.reshape(groups, per_group, head_size, state_size)
    skip = skip.reshape(groups, per_group)
    products = jnp.einsum("tghp,sghp->ghts", output_gradient_rows, x_vals)
    weighted = mixer_function * products
    grad_c = jnp.einsum("ghts,sgn->tgn", weighted, input_projection_values) + jnp.einsum(
        "ght,tghp,ghpn->tgn", leading, output_gradient_rows, entry
    )
    common_region = jnp.einsum("lxp,fxp->xlf", output_projection_values, input_projection_values)
    input_gradient_rows = jnp.einsum(
        "eaol,eol,oeav->leav", mixer_function, common_region, output_gradient_rows
    )
    input_gradient_rows = (
        input_gradient_rows
        + jnp.einsum("ght,tgn,ghpn->tghp", trailing, input_projection_values, leaving)
        + skip[None, :, :, None] * output_gradient_rows
    )
    grad_b = jnp.einsum("ghrt,rgn->tgn", weighted, output_projection_values) + jnp.einsum(
        "ght,tghp,ghpn->tgn", trailing, x_vals, leaving
    )
    grad_bc = jnp.stack([grad_b, grad_c], axis=2).reshape(length, groups * 2 * state_size)
    return (input_gradient_rows.reshape(length, groups * per_group * head_size), grad_bc)


def contract_rows(left, right):
    return lax.dot_general(
        left, right, (((1,), (1,)), ((), ())), preferred_element_type=jnp.float32
    )


def rounded_term(partials):
    return lax.optimization_barrier(partials.astype(jnp.bfloat16)).astype(jnp.float32)


def local(grad_out, w_out, w_in, w_bc, x_act, bc_act, decay, skip_gain, state_in):
    decay_rates = decay[0]
    head_count, length = decay_rates.shape
    entry_state = state_in[0, 0]
    head_size = entry_state.shape[1]
    state_size = entry_state.shape[2]
    groups = bc_act.shape[2] // (2 * state_size)
    per_group = head_count // groups
    cumulative, mixer_function = decay_table(decay_rates)
    x_vals = x_act[0].astype(jnp.float32).reshape(length, groups, per_group, head_size)
    bc_vals = bc_act[0].astype(jnp.float32).reshape(length, groups, 2, state_size)
    input_projection_values = bc_vals[:, :, 0]
    output_projection_values = bc_vals[:, :, 1]
    skip = skip_gain[0]
    width = grad_out.shape[1]

    def combine(earlier, nearer):
        return (earlier[0] * nearer[0], nearer[1] + nearer[0][:, None, None] * earlier[1])

    def ssd_grads(grad_ssd):
        output_gradient_rows = grad_ssd.astype(jnp.float32).reshape(
            length, groups, per_group, head_size
        )
        totals, entering = block_summary(output_gradient_rows, output_projection_values, cumulative)
        identity = (jnp.ones_like(totals), jnp.zeros_like(entering))
        carried_total, exit_grad = carried_in((totals, entering), "ctx", combine, identity)
        input_gradient_rows, grad_bc = block_grads(
            output_gradient_rows,
            x_vals,
            input_projection_values,
            output_projection_values,
            cumulative,
            mixer_function,
            entry_state,
            exit_grad,
            skip,
        )
        return (input_gradient_rows.astype(jnp.bfloat16), grad_bc.astype(jnp.bfloat16))

    def full_pass(upstream, out_full, in_full, bc_full):
        grad_ssd = contract_rows(upstream, out_full).astype(jnp.bfloat16)
        input_gradient_rows, grad_bc = ssd_grads(grad_ssd)
        return contract_rows(input_gradient_rows, in_full) + contract_rows(grad_bc, bc_full)

    out_all, in_all, bc_all = (
        lax.all_gather(w_out, "ctx", axis=2, tiled=True),
        lax.all_gather(w_in, "ctx", axis=1, tiled=True),
        lax.all_gather(w_bc, "ctx", axis=1, tiled=True),
    )
    out_full = out_all[0]
    in_full = in_all[0]
    bc_full = bc_all[0]
    first = full_pass(grad_out, out_full, in_full, bc_full)
    section_idx = lax.axis_index("section")
    head_idx = lax.axis_index("heads")
    share_cols = width // lax.axis_size("heads")

    def head_total(partials):
        return lax.psum(rounded_term(partials).astype(jnp.bfloat16), "heads").astype(jnp.float32)

    middle = (grad_out.astype(jnp.float32) + head_total(first)).astype(jnp.bfloat16)
    arrived = from_behind(middle, "section", -1)
    second = full_pass(arrived, out_full, in_full, bc_full)
    result = (arrived.astype(jnp.float32) + head_total(second)).astype(jnp.bfloat16)
    chosen = jnp.where(section_idx == 1, middle, result)
    output = lax.dynamic_slice_in_dim(chosen, head_idx * share_cols, share_cols, 1)
    return output[None]


def solution(mesh):
    placed = (
        P("ctx", None),
        P("section", "heads", "ctx"),
        P("section", "ctx", "heads"),
        P("section", "ctx", "heads"),
        P("section", "ctx", "heads"),
        P("section", "ctx", "heads"),
        P("section", "heads", "ctx"),
        P("section", "heads"),
        P("section", "ctx", "heads", None, None),
    )
    return jax.shard_map(
        local, mesh=mesh, in_specs=placed, out_specs=P("section", "ctx", "heads"), check_vma=False
    )
```

profile of v0, /device:TPU:32, one launch (start us, length us, event | category | flops | bytes accessed | tf_op | source)
XLA Modules:
  0.0 669.4 jit_solution(10770871379139882900)
XLA Ops:
  10.2 85.5 %all-gather.9.cloned.1.call-done = bf16[1,1024,4096]{2,1,0:T(8,128)(2,1)} async-done(((bf16[1,1024,256]{2,1,0:T(8,128)(2,1)}), bf16[1,1024,4096]{2,1,0:T(8,128)(2,1)}) %all-gather.9.cloned.1.call-update) | async-done | bytes 8388624 | tf_op jit(solution)/shard_map/all_gather | solution.py:154
  95.8 6.4 fusion.53
  107.5 38.5 %all-reduce = bf16[256]{0:T(256)(128)(2,1)S(1)} all-reduce(bf16[256]{0:T(256)(128)(2,1)S(1)} %dynamic-update-slice), channel_id=3, replica_groups=mesh['section'=2,'ctx'=16,'heads'=8] {'ctx'}, use_global_device_ids=true, to_apply=%add | all-reduce | flops 256 | bytes 1024
  146.2 1.6 multiply_reduce_fusion.1
  148.2 1.2 copy.50
  149.7 10.0 %all-gather.15.cloned.1.call-done = bf16[256,64,128]{2,1,0:T(8,128)(2,1)} async-done(((bf16[16,64,128]{2,1,0:T(8,128)(2,1)}), bf16[256,64,128]{2,1,0:T(8,128)(2,1)}) %all-gather.15.cloned.1.call-update) | async-done | bytes 4194320 | tf_op jit(solution)/shard_map/all_gather | solution.py:10
  159.7 18.4 %while.32 = (s32[]{:T(128)}, f32[16,64,128]{2,1,0:T(8,128)S(1)}, s32[]{:T(128)}, bf16[16,16,64,128]{3,2,1,0:T(8,128)(2,1)}, bf16[16,16]{1,0:T(8,128)(2,1)S(1)}, ...) while((s32[]{:T(128)}, f32[16,64,128]{2,1,0:T(8,128)S(1)}, s32[]{:T(128)}, ...), condition=%wide.region_3.4_spmd.clone, body=%wide.region_2.3_spmd.clone.sunk | while | flops 655384 | bytes 1311047 | solution.py:28
  178.8 2.4 fusion.59
  181.2 56.6 %all-gather.11.cloned.1.call-done = bf16[1,4096,1024]{2,1,0:T(8,128)(2,1)} async-done(((bf16[1,256,1024]{2,1,0:T(8,128)(2,1)}), bf16[1,4096,1024]{2,1,0:T(8,128)(2,1)}) %all-gather.11.cloned.1.call-update) | async-done | bytes 8388624 | tf_op jit(solution)/shard_map/all_gather | solution.py:155
  237.8 7.7 %fusion.4 = f32[256,4096]{1,0:T(8,128)} fusion(bf16[256,1024]{0,1:T(8,128)(2,1)S(1)} %bitcast.303, bf16[1,4096,1024]{2,1,0:T(8,128)(2,1)} %all-gather.11.cloned.1.call-done), kind=kOutput, calls=%fused_computation.8 | convolution fusion | flops 2147483648 | bytes 13107200 | tf_op jit(solution)/shard_map/dot_general | solution.py:100
  245.5 44.3 %all-gather.13.cloned.1.call-done = bf16[1,4096,256]{2,1,0:T(8,128)(2,1)} async-done(((bf16[1,256,256]{2,1,0:T(8,128)(2,1)}), bf16[1,4096,256]{2,1,0:T(8,128)(2,1)}) %all-gather.13.cloned.1.call-update) | async-done | bytes 2097168 | tf_op jit(solution)/shard_map/all_gather | solution.py:156
  289.8 5.1 fusion.10
  295.0 76.6 %all-reduce.4.cloned.1.call-done = bf16[256,4096]{1,0:T(8,128)(2,1)} async-done(((bf16[256,4096]{1,0:T(8,128)(2,1)}), bf16[256,4096]{1,0:T(8,128)(2,1)}) %all-reduce.4.cloned.1.call-update) | async-done | bytes 2097168 | tf_op jit(solution)/shard_map/psum | solution.py:167
  371.6 2.4 add_convert_fusion
  374.0 1.3 copy-done.2
  375.3 1.6 collective-permute-start
  376.9 94.9 %collective-permute-done = bf16[256,4096]{1,0:T(8,128)(2,1)S(1)} collective-permute-done((bf16[256,4096]{1,0:T(8,128)(2,1)S(1)}, bf16[256,4096]{1,0:T(8,128)(2,1)S(1)}, u32[]{:S(2)}, u32[]{:S(2)}) %collective-permute-start) | collective-permute-done | bytes 2097184 | tf_op jit(solution)/shard_map/ppermute | solution.py:34
  471.8 1.3 copy-done.11
  473.2 5.7 fusion.56
  480.2 1.3 copy.53
  481.5 1.6 multiply_reduce_fusion
  483.8 51.5 %all-gather.17.cloned.1.call-done = bf16[256,64,128]{2,1,0:T(8,128)(2,1)} async-done(((bf16[16,64,128]{2,1,0:T(8,128)(2,1)}), bf16[256,64,128]{2,1,0:T(8,128)(2,1)}) %all-gather.17.cloned.1.call-update) | async-done | bytes 4194320 | tf_op jit(solution)/shard_map/all_gather | solution.py:10
  535.3 37.1 %while.33 = (s32[]{:T(128)}, f32[16,64,128]{2,1,0:T(8,128)S(1)}, s32[]{:T(128)}, bf16[16,16,64,128]{3,2,1,0:T(8,128)(2,1)}, bf16[16,16]{1,0:T(8,128)(2,1)}, /*index=5*/s32[]{:T(128)}, s32[]{:T(128)}, s32[]{:T(128)}, s32[]{:T(128)}) while((s32[]{:T(128)}, f32[16,64,128]{2,1,0:T(8,128)S(1)}, s32[]{:T(128)}, ...), condition=%wide.region_7.8_spmd.clone, body=%wide.region_6.7_spmd.clone.sunk | while | flops 655384 | bytes 1311047 | solution.py:28
  535.3 1.3 bitcast_convert_fusion.5
  537.7 1.2 bitcast_convert_fusion.5
  542.4 1.2 bitcast_convert_fusion.5
  544.7 1.2 bitcast_convert_fusion.5
  573.0 2.5 fusion.62
  575.6 5.9 fusion.2
  581.5 2.1 fusion.11
  583.6 77.0 %all-reduce.6.cloned.1.call-done = bf16[256,4096]{1,0:T(8,128)(2,1)} async-done(((bf16[256,4096]{1,0:T(8,128)(2,1)}), bf16[256,4096]{1,0:T(8,128)(2,1)}) %all-reduce.6.cloned.1.call-update) | async-done | bytes 2097168 | tf_op jit(solution)/shard_map/psum | solution.py:167
  660.6 1.9 fusion.86
  (138 shorter events, 62.0 us)
Async XLA Ops:
  6.5 142.9 %copy-start = (f32[1,1,16,64,128]{4,3,2,1,0:T(8,128)S(1)}, f32[1,1,16,64,128]{4,3,2,1,0:T(8,128)}, u32[]{:S(2)}) copy-start(f32[1,1,16,64,128]{4,3,2,1,0:T(8,128)} %param.21) | copy-start | bytes 1572868
  6.5 89.2 %all-gather.9.cloned.1.call-start = ((), (), s32[]{:S(2)}) async-start(), calls=%async_computation | async-start | bytes 8912896 | tf_op jit(solution)/shard_map/all_gather | solution.py:154
  7.3 152.4 %all-gather.15.cloned.1.call-start = ((), (), s32[]{:S(2)}) async-start(), calls=%async_computation.5 | async-start | bytes 4456448 | tf_op jit(solution)/shard_map/all_gather | solution.py:10
  9.9 471.6 %copy-start.10 = (f32[16,256]{1,0:T(8,128)}, f32[16,256]{1,0:T(8,128)S(1)}, u32[]{:S(2)}) copy-start(f32[16,256]{1,0:T(8,128)S(1)} %copy_bitcast_fusion) | copy-start | bytes 49156
  10.2 95.8 %copy-start.14 = (u32[256]{0:T(256)S(1)}, u32[256]{0:T(256)}, u32[]{:S(2)}) copy-start(u32[256]{0:T(256)} %constant.123) | copy-start | bytes 3076
  10.2 135.8 %copy-start.6 = (bf16[1,256,1024]{2,1,0:T(8,128)(2,1)S(1)}, bf16[1,256,1024]{2,1,0:T(8,128)(2,1)}, u32[]{:S(2)}) copy-start(bf16[1,256,1024]{2,1,0:T(8,128)(2,1)} %param.17) | copy-start | bytes 1572868
  103.4 134.4 %all-gather.11.cloned.1.call-start = ((), (), s32[]{:S(2)}) async-start(), calls=%async_computation.1 | async-start | bytes 8912896 | tf_op jit(solution)/shard_map/all_gather | solution.py:155
  104.1 185.7 %all-gather.13.cloned.1.call-start = ((), (), s32[]{:S(2)}) async-start(), calls=%async_computation.2 | async-start | bytes 2228224 | tf_op jit(solution)/shard_map/all_gather | solution.py:156
  104.7 266.9 %all-reduce.4.cloned.1.call-start = ((), (), s32[]{:S(2)}) async-start(), calls=%async_computation.3 | async-start | bytes 4194304 | tf_op jit(solution)/shard_map/psum | solution.py:167
  105.0 42.9 %copy-start.7 = (pred[256,256]{1,0:T(8,128)(4,1)}, pred[256,256]{1,0:T(8,128)(4,1)S(1)}, u32[]{:S(2)}) copy-start(pred[256,256]{1,0:T(8,128)(4,1)S(1)} %iota_compare_fusion) | copy-start | bytes 196612
  159.7 19.0 %copy-start.5 = (f32[256,1024]{0,1:T(8,128)S(1)}, f32[256,1024]{0,1:T(8,128)}, u32[]{:S(2)}) copy-start(f32[256,1024]{0,1:T(8,128)} %copy.50) | copy-start | bytes 3145732
  159.7 19.1 %copy-start.13 = (f32[1,16]{1,0:T(1,128)S(1)}, f32[1,16]{1,0:T(1,128)}, u32[]{:S(2)}) copy-start(f32[1,16]{1,0:T(1,128)} %param.20) | copy-start | bytes 196
  178.1 3.1 copy-start.12
  289.8 81.8 %copy-start.3 = (bf16[256,4096]{1,0:T(8,128)(2,1)S(1)}, bf16[256,4096]{1,0:T(8,128)(2,1)}, u32[]{:S(2)}) copy-start(bf16[256,4096]{1,0:T(8,128)(2,1)} %param.13) | copy-start | bytes 6291460
  294.9 240.4 %all-gather.17.cloned.1.call-start = ((), (), s32[]{:S(2)}) async-start(), calls=%async_computation.6 | async-start | bytes 4456448 | tf_op jit(solution)/shard_map/all_gather | solution.py:10
  374.0 1.3 copy-start.2
  375.3 106.2 %copy-start.8 = (pred[256,256]{1,0:T(8,128)(4,1)S(1)}, pred[256,256]{1,0:T(8,128)(4,1)}, u32[]{:S(2)}) copy-start(pred[256,256]{1,0:T(8,128)(4,1)} %copy-done.7) | copy-start | bytes 196612
  375.3 96.5 %collective-permute-start = (bf16[256,4096]{1,0:T(8,128)(2,1)S(1)}, bf16[256,4096]{1,0:T(8,128)(2,1)S(1)}, u32[]{:S(2)}, u32[]{:S(2)}) collective-permute-start(bf16[256,4096]{1,0:T(8,128)(2,1)S(1)} %add_convert_fusion), channel_id=1, source_target_pairs={{128,0},{129,1},{130,2},{131,3},{132,4},{133,5},{134,6},{135,7},{1... | collective-permute-start | bytes 6291464 | tf_op jit(solution)/shard_map/ppermute | solution.py:34
  471.8 1.3 copy-start.11
  480.2 180.5 %all-reduce.6.cloned.1.call-start = ((), (), s32[]{:S(2)}) async-start(), calls=%async_computation.4 | async-start | bytes 4194304 | tf_op jit(solution)/shard_map/psum | solution.py:167
  535.3 37.7 %copy-start.4 = (f32[256,1024]{0,1:T(8,128)S(1)}, f32[256,1024]{0,1:T(8,128)}, u32[]{:S(2)}) copy-start(f32[256,1024]{0,1:T(8,128)} %copy.53) | copy-start | bytes 3145732
  535.3 37.7 %copy-start.9 = (pred[256,256]{1,0:T(8,128)(4,1)S(1)}, pred[256,256]{1,0:T(8,128)(4,1)}, u32[]{:S(2)}) copy-start(pred[256,256]{1,0:T(8,128)(4,1)} %copy-done.7) | copy-start | bytes 196612
  575.6 5.9 copy-start.1
Sparse Core Ops, SparseCore 0:
  9.8 85.9 all-gather.8
  103.5 56.1 all-gather.14
  162.1 75.6 all-gather.10
  240.1 49.6 all-gather.12
  295.0 76.5 all-reduce.3
  480.3 54.9 all-gather.16
  583.7 76.8 all-reduce.5
where the time goes:
time: 674 us; the launch traced here: 669 us
  waiting for transfers between devices  498 us (74%)
  other arithmetic  59.8 us (9%)
  matrix products  46.5 us (7%)
  blocking collectives  38.5 us (6%)
  between operations  14.5 us (2%)
  local copies, waits for them, and re-layouts  8.81 us (1%)
    psum x2, waiting for transfers between devices, head_total(): lax.psum(rounded_term(partials).astype(jnp.bfloat16), 'heads')  154 us
    ppermute x1, waiting for transfers between devices, from_behind(): lax.ppermute(value, axis, [(source, source + steps) for source in range(i...  94.9 us
    all_gather x1, waiting for transfers between devices, local(): lax.all_gather(w_out, 'ctx', axis=2, tiled=True)  85.5 us
    all_gather x2, waiting for transfers between devices, carried_in(): lax.all_gather(part.astype(kind), axis)  61.5 us
    all_gather x1, waiting for transfers between devices, local(): lax.all_gather(w_in, 'ctx', axis=1, tiled=True)  56.6 us
    all_gather x1, waiting for transfers between devices, local(): lax.all_gather(w_bc, 'ctx', axis=1, tiled=True)  44.3 us
    unnamed x1, blocking collectives  38.5 us
    select_n x32, other arithmetic, lap(): return jax.tree.map(lambda a, b: jnp.where(reached, a, b), new, before)  35.3 us
  transfers between devices with their start and end apart: 8, of which 8 were waited for; matrix products, arithmetic and copies ran while one was open for 6% of the time, Pallas kernels for 0%

commit v1 on v0

v1 whole, which is shorter than its diff:
```python
import jax
import jax.numpy as jnp
from jax import lax
from jax.sharding import PartitionSpec as P

SIDE = 4
CORES = 2
BOTH = (0, 1)
AXES = ("section", "ctx", "heads")


def place(section, x, y, z, core):
    return (((section * SIDE + x) * SIDE + y) * SIDE + z) * CORES + core


def routed(value, move, sections):
    pairs = []
    for section in sections:
        for x in range(SIDE):
            for y in range(SIDE):
                for z in range(SIDE):
                    for core in range(CORES):
                        here = (section, x, y, z, core)
                        pairs.append((place(*here), place(*move(*here))))
    return lax.ppermute(value, AXES, pairs)


def along_x(k):
    return lambda s, x, y, z, c: (s, (x + k) % SIDE, y, z, c)


def along_y(k):
    return lambda s, x, y, z, c: (s, x, (y + k) % SIDE, z, c)


def across_z(k):
    return lambda s, x, y, z, c: (s, x, y, z ^ k, c)


def other_core(s, x, y, z, c):
    return (s, x, y, z, 1 - c)


def dot(left, right, left_dim, right_dim):
    return lax.dot_general(
        left, right, (((left_dim,), (right_dim,)), ((), ())), preferred_element_type=jnp.float32
    )


def column_block(value, index, width):
    return lax.dynamic_slice_in_dim(value, index * width, width, 1)


def decay_tables(decay_rates):
    cumulative = jnp.cumsum(decay_rates, axis=1)
    spread = cumulative[:, :, None] - cumulative[:, None, :]
    length = decay_rates.shape[1]
    lower = jnp.arange(length)[:, None] >= jnp.arange(length)[None, :]
    kernel = jnp.where(lower[None], jnp.exp(jnp.minimum(spread, 0.0)), 0.0)
    return cumulative, kernel


def local(grad_out, w_out, w_in, w_bc, x_act, bc_act, decay, skip_gain, state_in):
    bf16, f32 = jnp.bfloat16, jnp.float32
    section = lax.axis_index("section")
    ctx = lax.axis_index("ctx")
    heads_at = lax.axis_index("heads")
    x, y = ctx // SIDE, ctx % SIDE
    z, core = heads_at // CORES, heads_at % CORES
    rows, width = grad_out.shape
    block = width // SIDE
    share = block // CORES
    fine = w_out.shape[2]
    half = rows // CORES
    head_count, head_size, state_size = state_in.shape[2:]
    inner = head_count * head_size

    def first_step(k):
        return lambda s, x, y, z, c: (
            (s, x, (y + k) % SIDE, z, c) if s == 1 else (s, (x + k) % SIDE, y, z, c)
        )

    out_at = jnp.where(section == 1, y, x)
    out_block = jnp.zeros((inner, block), bf16)
    out_parts = [w_out[0]] + [routed(w_out[0], first_step(k), BOTH) for k in (1, 2, 3)]

    pieces = []
    for k in (1, 2, 3):
        piece = lax.dynamic_slice(grad_out, (half * core, block * ((x + k) % SIDE)), (half, block))
        pieces.append(routed(piece, along_x(k), (1,)))
    mine = jnp.stack(pieces)
    theirs = routed(mine, other_core, (1,))
    others = jnp.where(
        core == 0, jnp.concatenate([mine, theirs], 1), jnp.concatenate([theirs, mine], 1)
    )
    upstream = jnp.concatenate([column_block(grad_out, x, block)[None], others], 0)

    for k, part in enumerate(out_parts):
        out_block = lax.dynamic_update_slice(out_block, part, (0, fine * ((out_at - k) % SIDE)))

    back = jnp.concatenate([w_in[0], w_bc[0]], axis=1)
    back_block = jnp.zeros((SIDE, fine, back.shape[1]), bf16)
    for k in range(SIDE):
        part = back if k == 0 else routed(back, along_y(k), BOTH)
        back_block = lax.dynamic_update_slice(back_block, part[None], ((y - k) % SIDE, 0, 0))
    back_block = back_block.reshape(block, back.shape[1])

    cumulative, kernel = decay_tables(decay[0])
    leading = jnp.repeat(jnp.exp(cumulative).T, head_size, axis=1)
    trailing = jnp.repeat(jnp.exp(cumulative[:, -1:] - cumulative).T, head_size, axis=1)
    b_rows = bc_act[0][:, :state_size]
    c_rows = bc_act[0][:, state_size:]
    common = dot(c_rows, b_rows, 1, 1)
    mixed = (kernel * common[None]).astype(bf16)
    x_rows = x_act[0]
    x_heads = x_rows.reshape(rows, head_count, head_size)
    x_trailing = (x_rows.astype(f32) * trailing).astype(bf16)
    entry = state_in[0, 0].reshape(inner, state_size).astype(bf16)
    skip = jnp.repeat(skip_gain[0], head_size)[None]
    totals = lax.all_to_all(
        jnp.broadcast_to(cumulative[:, -1][:, None], (head_count, 128)), "ctx", 0, 0
    )[:, 0]
    run = jnp.cumsum(totals)
    at = jnp.arange(head_count)
    later = at[None, :] > at[:, None]
    carry = jnp.where(later, jnp.exp(jnp.minimum((run - totals)[None, :] - run[:, None], 0.0)), 0.0)

    def mixer(grad_ssd):
        grad_f32 = grad_ssd.astype(f32)
        grad_leading = (grad_f32 * leading).astype(bf16)
        entering = dot(grad_leading, c_rows, 0, 0).astype(bf16)
        arrived = lax.all_to_all(
            entering.reshape(head_count, head_size, state_size), "ctx", 0, 0
        ).reshape(head_count, head_size * state_size)
        exits = lax.dot_general(
            carry, arrived.astype(f32), (((1,), (0,)), ((), ())), precision=lax.Precision.HIGHEST
        )
        leaving = lax.all_to_all(
            exits.astype(bf16).reshape(head_count, head_size, state_size), "ctx", 0, 0
        ).reshape(inner, state_size)
        grad_heads = grad_ssd.reshape(rows, head_count, head_size)
        products = jnp.einsum(
            "thp,shp->hts", grad_heads, x_heads, preferred_element_type=f32
        )
        weighted = jnp.sum(kernel * products, axis=0).astype(bf16)
        grad_c = dot(weighted, b_rows, 1, 0) + dot(grad_leading, entry, 1, 0)
        grad_b = dot(weighted, c_rows, 0, 0) + dot(x_trailing, leaving, 1, 0)
        within = jnp.einsum(
            "hts,thp->shp", mixed, grad_heads, preferred_element_type=f32
        ).reshape(rows, inner)
        grad_x = within + trailing * dot(b_rows, leaving, 1, 1) + skip * grad_f32
        return jnp.concatenate([grad_x, grad_b, grad_c], axis=1).astype(bf16)

    def over_heads(terms, of_z, sections):
        keep = lax.dynamic_slice_in_dim(terms, share * core, share, 2)
        give = lax.dynamic_slice_in_dim(terms, share * (1 - core), share, 2)
        got = routed(give.astype(bf16), other_core, sections)
        pair = keep.astype(f32) + got.astype(f32)
        total = lax.dynamic_index_in_dim(pair, of_z(z), 0, False)
        pair = pair.astype(bf16)
        for k in (1, 2, 3):
            sent = lax.dynamic_index_in_dim(pair, of_z(z ^ k), 0, False)
            total = total + routed(sent, across_z(k), sections).astype(f32)
        return total

    partial = dot(upstream.reshape(SIDE * rows, block), out_block, 1, 1)
    partial = partial.reshape(SIDE, rows, inner)
    grad_ssd = partial[0]
    partial = partial.astype(bf16)
    for k in (1, 2, 3):
        grad_ssd = grad_ssd + routed(partial[k], along_x(-k), (1,)).astype(f32)
    grads = mixer(grad_ssd.astype(bf16))
    grads_all = jnp.stack([grads] + [routed(grads, along_x(k), (1,)) for k in (1, 2, 3)])
    terms = dot(grads_all.reshape(SIDE * rows, -1), back_block, 1, 1)
    total = over_heads(terms.reshape(SIDE, rows, block), lambda z: z, (1,))
    own = lax.dynamic_index_in_dim(upstream, z, 0, False)
    middle = (lax.dynamic_slice_in_dim(own, share * core, share, 1).astype(f32) + total).astype(bf16)

    arrived = routed(middle, lambda s, x, y, z, c: (0, (x - z) % SIDE, y, x, c), (1,))
    settled = routed(middle, lambda s, x, y, z, c: (s, (x - z) % SIDE, y, x, c), (1,))

    out_whole = [out_block] + [routed(out_block, along_y(k), (0,)) for k in (1, 2, 3)]
    back_whole = [back_block] + [routed(back_block, along_x(k), (0,)) for k in (1, 2, 3)]

    line = jnp.zeros((rows, SIDE, share), bf16)
    for k in range(SIDE):
        part = arrived if k == 0 else routed(arrived, across_z(k), (0,))
        line = lax.dynamic_update_slice(line, part[:, None], (0, z ^ k, 0))
    other = routed(line, other_core, (0,))
    lower = jnp.where(core == 0, jnp.stack([line, other], 2), jnp.stack([other, line], 2))
    lower = lower.reshape(rows, SIDE, SIDE, fine)
    grad_ssd = jnp.zeros((rows, inner), f32)
    for k in range(SIDE):
        columns = lax.dynamic_index_in_dim(lower, (y - k) % SIDE, 2, False).reshape(rows, block)
        grad_ssd = grad_ssd + dot(columns, out_whole[k], 1, 1)
    grads = mixer(grad_ssd.astype(bf16))
    terms = jnp.stack([dot(grads, back_whole[k], 1, 1) for k in range(SIDE)])
    total = over_heads(terms, lambda z: (x - z) % SIDE, (0,))
    result = (arrived.astype(f32) + total).astype(bf16)
    return jnp.where(section == 1, settled, result)[None]


def solution(mesh):
    placed = (
        P("ctx", None),
        P("section", "heads", "ctx"),
        P("section", "ctx", "heads"),
        P("section", "ctx", "heads"),
        P("section", "ctx", "heads"),
        P("section", "ctx", "heads"),
        P("section", "heads", "ctx"),
        P("section", "heads"),
        P("section", "ctx", "heads", None, None),
    )
    return jax.shard_map(
        local, mesh=mesh, in_specs=placed, out_specs=P("section", "ctx", "heads"), check_vma=False
    )
```

time: 674 us -> 463 us (0.69)
  waiting for transfers between devices: 498 us -> 239 us
  starting transfers between devices: 1.83 us -> 109 us
  blocking collectives: 38.5 us -> 0 us
  other arithmetic: 59.8 us -> 23.7 us
  local copies, waits for them, and re-layouts: 8.81 us -> 36.5 us
  between operations: 14.5 us -> 1.07 us
    all_gather x5 -> x0, waiting for transfers between devices: 248 us -> none  [the longest x1 85.5 us: local(): lax.all_gather(w_out, 'ctx', axis=2, tiled=True)]
    psum x2 -> x0, waiting for transfers between devices: 154 us -> none  [head_total(): lax.psum(rounded_term(partials).astype(jnp.bfloat16), 'heads')]
    ppermute x1 -> x36, waiting for transfers between devices: 94.9 us -> 183 us  [routed(): return lax.ppermute(value, AXES, pairs)]
    ppermute x1 -> x36, starting transfers between devices: 1.59 us -> 76.7 us  [routed(): return lax.ppermute(value, AXES, pairs)]
    all_to_all x0 -> x5, waiting for transfers between devices: none -> 55.8 us  [the longest x2 40.8 us: mixer(): lax.all_to_all(entering.reshape(head_count, head_size, state_size), 'ctx'...]
    unnamed x1 -> x0, blocking collectives: 38.5 us -> none
    select_n x32 -> x2, other arithmetic: 35.3 us -> 2.09 us  [the longest x1 1.8 us: local(): jnp.where(core == 0, jnp.concatenate([mine, theirs], 1), jnp.concatenate(...]
    all_to_all x0 -> x5, starting transfers between devices: none -> 32 us  [the longest x2 16.2 us: mixer(): lax.all_to_all(entering.reshape(head_count, head_size, state_size), 'ctx'...]
  transfers between devices with their start and end apart: 8 -> 41, of which waited for: 8 -> 13; matrix products, arithmetic and copies ran while one was open for 6% -> 19% of each run, Pallas kernels for 0% -> 0%
where the time goes in v1:
time: 463 us; the launch traced here: 461 us
  waiting for transfers between devices  239 us (52%)
  starting transfers between devices  109 us (24%)
  matrix products  52.3 us (11%)
  local copies, waits for them, and re-layouts  36.5 us (8%)
  other arithmetic  23.7 us (5%)
    ppermute x36, waiting for transfers between devices, routed(): return lax.ppermute(value, AXES, pairs)  183 us
    ppermute x36, starting transfers between devices, routed(): return lax.ppermute(value, AXES, pairs)  76.7 us
    dot_general x23, matrix products, dot(): lax.dot_general(left, right, (((left_dim,), (right_dim,)), ((), ())), pre...  42.6 us
    all_to_all x2, waiting for transfers between devices, mixer(): lax.all_to_all(entering.reshape(head_count, head_size, state_size), 'ctx'...  40.8 us
    all_to_all x2, starting transfers between devices, mixer(): lax.all_to_all(entering.reshape(head_count, head_size, state_size), 'ctx'...  16.2 us
    all_to_all x2, waiting for transfers between devices, mixer(): lax.all_to_all(exits.astype(bf16).reshape(head_count, head_size, state_si...  15 us
    all_to_all x2, starting transfers between devices, mixer(): lax.all_to_all(exits.astype(bf16).reshape(head_count, head_size, state_si...  10.3 us
  transfers between devices with their start and end apart: 41, of which 13 were waited for; matrix products, arithmetic and copies ran while one was open for 19% of the time, Pallas kernels for 0%

profile of v1, /device:TPU:32, one launch (start us, length us, event | category | flops | bytes accessed | tf_op | source)
XLA Modules:
  0.0 460.8 jit_solution(291927482996690016)
XLA Ops:
  1.5 2.7 collective-permute-start.5
  10.0 5.5 %all-to-all-start = ((f32[16,1,128]{2,1,0:T(1,128)}), f32[16,1,128]{2,1,0:T(1,128)}, u32[]{:S(2)}, u32[]{:S(2)}) async-start(f32[16,1,128]{2,1,0:T(1,128)} %broadcast_in_dim.79), calls=%async_computation | async-start | bytes 16384 | tf_op jit(solution)/shard_map/all_to_all | solution.py:120
  22.4 3.1 collective-permute-start.6
  47.3 6.0 %fusion.81 = (bf16[1024,1024]{0,1:T(8,128)(2,1)S(1)}, f32[1024,1024]{0,1:T(8,128)}) fusion(bf16[1024,1024]{1,0:T(8,128)(2,1)S(1)} %bitcast.213, bf16[1024,1024]{1,0:T(8,128)(2,1)} %constant_dynamic-update-slice_fusion.4), kind=kOutput, calls=%fused_computation.159 | convolution fusion | flops 2148532224 | bytes 10485760 | tf_op jit(solution)/shard_map/dot_general | solution.py:45
  70.7 4.4 all-to-all-start.1
  75.1 2.8 multiply_reduce_fusion.1
  85.6 4.7 %all-to-all-start.2 = ((bf16[16,64,128]{2,1,0:T(8,128)(2,1)}), bf16[16,64,128]{2,1,0:T(8,128)(2,1)}, u32[]{:S(2)}, u32[]{:S(2)}) async-start(bf16[16,64,128]{2,1,0:T(8,128)(2,1)} %bitcast.223), calls=%async_computation.2 | async-start | bytes 524288 | tf_op jit(solution)/shard_map/all_to_all | solution.py:138
  92.1 6.7 %all-to-all-done.2 = bf16[16,64,128]{2,1,0:T(8,128)(2,1)} async-done(((bf16[16,64,128]{2,1,0:T(8,128)(2,1)}), bf16[16,64,128]{2,1,0:T(8,128)(2,1)}, u32[]{:S(2)}, u32[]{:S(2)}) %all-to-all-start.2) | async-done | bytes 262176 | tf_op jit(solution)/shard_map/all_to_all | solution.py:138
  108.2 4.7 %fusion = f32[4,256,1024]{2,1,0:T(8,128)S(1)} fusion(bf16[1024,1280,1]{1,0,2:T(8,128)(2,1)} %bitcast.36, bf16[1,256,1280]{1,2,0:T(8,128)(2,1)S(1)} %bitcast.248, bf16[1,256,1280]{1,2,0:T(8,128)(2,1)S(1)} %bitcast.247, bf16[1,256,1280]{1,2,0:T(8,128)(2,1)S(1)} %bitcast.246, bf16[1,256,128]{1,2,0:T(8,128)(2,1)S(1)} %bitcast.244, ...), kind=kOutput, calls=%fused_computation.9 | convolution fusion | flops 2700083200 | bytes 9437184 | tf_op jit(solution)/shard_map/dot_general | solution.py:45
  117.7 3.7 fusion.77
  130.7 101.4 %collective-permute-done.21 = bf16[256,512]{1,0:T(8,128)(2,1)S(1)} collective-permute-done((bf16[256,512]{1,0:T(8,128)(2,1)}, bf16[256,512]{1,0:T(8,128)(2,1)S(1)}, u32[]{:S(2)}, u32[]{:S(2)}) %collective-permute-start.21) | collective-permute-done | bytes 262176 | tf_op jit(solution)/shard_map/ppermute | solution.py:25
  236.0 5.4 %collective-permute-start.24 = (bf16[256,512]{1,0:T(8,128)(2,1)S(1)}, bf16[256,512]{1,0:T(8,128)(2,1)S(1)}, u32[]{:S(2)}, u32[]{:S(2)}) collective-permute-start(bf16[256,512]{1,0:T(8,128)(2,1)S(1)} %collective-permute-done.21), channel_id=1, source_target_pairs={{0,6},{1,7},{2,4},{3,5},{4,2},{5,3},{6,0},{7,1},{8,14},{9,15},{10,... | collective-permute-start | bytes 786440 | tf_op jit(solution)/shard_map/ppermute | solution.py:25
  241.4 3.5 collective-permute-start.27
  245.1 3.4 collective-permute-start.28
  248.6 3.7 collective-permute-done.23
  252.5 6.4 %collective-permute-done.24 = bf16[256,512]{1,0:T(8,128)(2,1)S(1)} collective-permute-done((bf16[256,512]{1,0:T(8,128)(2,1)S(1)}, bf16[256,512]{1,0:T(8,128)(2,1)S(1)}, u32[]{:S(2)}, u32[]{:S(2)}) %collective-permute-start.24) | collective-permute-done | bytes 262176 | tf_op jit(solution)/shard_map/ppermute | solution.py:25
  261.1 9.4 %collective-permute-start.29 = (bf16[1024,1280]{1,0:T(8,128)(2,1)}, bf16[1024,1280]{1,0:T(8,128)(2,1)}, u32[]{:S(2)}, u32[]{:S(2)}) collective-permute-start(bf16[1024,1280]{1,0:T(8,128)(2,1)} %bitcast.35), channel_id=1, source_target_pairs={{0,32},{1,33},{2,34},{3,35},{4,36},{5,37},{6,38},{7,39},{8,40},{9,... | collective-permute-start | bytes 7864328 | tf_op jit(solution)/shard_map/ppermute | solution.py:25
  270.4 4.0 collective-permute-start.30
  274.9 3.4 collective-permute-start.31
  280.7 7.9 %collective-permute-done.27 = bf16[1024,1024]{1,0:T(8,128)(2,1)} collective-permute-done((bf16[1024,1024]{1,0:T(8,128)(2,1)}, bf16[1024,1024]{1,0:T(8,128)(2,1)}, u32[]{:S(2)}, u32[]{:S(2)}) %collective-permute-start.27) | collective-permute-done | bytes 2097184 | tf_op jit(solution)/shard_map/ppermute | solution.py:25
  290.9 41.0 %collective-permute-done.28 = bf16[1024,1024]{1,0:T(8,128)(2,1)} collective-permute-done((bf16[1024,1024]{1,0:T(8,128)(2,1)}, bf16[1024,1024]{1,0:T(8,128)(2,1)}, u32[]{:S(2)}, u32[]{:S(2)}) %collective-permute-start.28) | collective-permute-done | bytes 2097184 | tf_op jit(solution)/shard_map/ppermute | solution.py:25
  337.7 11.8 %all-to-all-start.3 = ((bf16[16,64,128]{2,1,0:T(8,128)(2,1)}), bf16[16,64,128]{2,1,0:T(8,128)(2,1)S(1)}, u32[]{:S(2)}, u32[]{:S(2)}) async-start(bf16[16,64,128]{2,1,0:T(8,128)(2,1)} %bitcast.55), calls=%async_computation.3 | async-start | bytes 524288 | tf_op jit(solution)/shard_map/all_to_all | solution.py:132
  352.6 38.5 %all-to-all-done.3 = bf16[16,64,128]{2,1,0:T(8,128)(2,1)S(1)} async-done(((bf16[16,64,128]{2,1,0:T(8,128)(2,1)}), bf16[16,64,128]{2,1,0:T(8,128)(2,1)S(1)}, u32[]{:S(2)}, u32[]{:S(2)}) %all-to-all-start.3) | async-done | bytes 262176 | tf_op jit(solution)/shard_map/all_to_all | solution.py:132
  392.3 5.6 %all-to-all-start.4 = ((bf16[16,64,128]{2,1,0:T(8,128)(2,1)}), bf16[16,64,128]{2,1,0:T(8,128)(2,1)S(1)}, u32[]{:S(2)}, u32[]{:S(2)}) async-start(bf16[16,64,128]{2,1,0:T(8,128)(2,1)} %bitcast.81), calls=%async_computation.4 | async-start | bytes 524288 | tf_op jit(solution)/shard_map/all_to_all | solution.py:138
  398.3 8.3 %all-to-all-done.4 = bf16[16,64,128]{2,1,0:T(8,128)(2,1)S(1)} async-done(((bf16[16,64,128]{2,1,0:T(8,128)(2,1)}), bf16[16,64,128]{2,1,0:T(8,128)(2,1)S(1)}, u32[]{:S(2)}, u32[]{:S(2)}) %all-to-all-start.4) | async-done | bytes 262176 | tf_op jit(solution)/shard_map/all_to_all | solution.py:138
  408.5 2.6 convolution_bitcast_fusion.3
  411.2 2.6 convolution_bitcast_fusion.2
  413.8 2.6 convolution_bitcast_fusion.1
  416.5 2.6 convolution_bitcast_fusion
  430.5 4.9 %collective-permute-start.34 = (bf16[256,512]{1,0:T(8,128)(2,1)S(1)}, bf16[256,512]{1,0:T(8,128)(2,1)}, u32[]{:S(2)}, u32[]{:S(2)}) collective-permute-start(bf16[256,512]{1,0:T(8,128)(2,1)S(1)} %get-tuple-element.23), channel_id=1, source_target_pairs={{0,4},{1,5},{2,6},{3,7},{4,0},{5,1},{6,2},{7,3},{8,12},{9,13},{10,... | collective-permute-start | bytes 786440 | tf_op jit(solution)/shard_map/ppermute | solution.py:25
  440.1 13.1 %collective-permute-done.34 = bf16[256,512]{1,0:T(8,128)(2,1)} collective-permute-done((bf16[256,512]{1,0:T(8,128)(2,1)S(1)}, bf16[256,512]{1,0:T(8,128)(2,1)}, u32[]{:S(2)}, u32[]{:S(2)}) %collective-permute-start.34) | collective-permute-done | bytes 262176 | tf_op jit(solution)/shard_map/ppermute | solution.py:25
  453.3 5.6 %collective-permute-done.35 = bf16[256,512]{1,0:T(8,128)(2,1)} collective-permute-done((bf16[256,512]{1,0:T(8,128)(2,1)S(1)}, bf16[256,512]{1,0:T(8,128)(2,1)}, u32[]{:S(2)}, u32[]{:S(2)}) %collective-permute-start.35) | collective-permute-done | bytes 262176 | tf_op jit(solution)/shard_map/ppermute | solution.py:25
  (185 shorter events, 127.8 us)
Async XLA Ops:
  0.0 37.0 %collective-permute-start.4 = (bf16[1024,256]{1,0:T(8,128)(2,1)}, bf16[1024,256]{1,0:T(8,128)(2,1)}, u32[]{:S(2)}, u32[]{:S(2)}) collective-permute-start(bf16[1024,256]{1,0:T(8,128)(2,1)} %bitcast.6), channel_id=1, source_target_pairs={{0,32},{1,33},{2,34},{3,35},{4,36},{5,37},{6,38},{7,39},{8,40},{9,... | collective-permute-start | bytes 1572872 | tf_op jit(solution)/shard_map/ppermute | solution.py:25
  1.5 40.0 %collective-permute-start.5 = (bf16[1024,256]{1,0:T(8,128)(2,1)}, bf16[1024,256]{1,0:T(8,128)(2,1)}, u32[]{:S(2)}, u32[]{:S(2)}) collective-permute-start(bf16[1024,256]{1,0:T(8,128)(2,1)} %bitcast.6), channel_id=1, source_target_pairs={{0,64},{1,65},{2,66},{3,67},{4,68},{5,69},{6,70},{7,71},{8,72},{9,... | collective-permute-start | bytes 1572872 | tf_op jit(solution)/shard_map/ppermute | solution.py:25
  5.5 17.0 %collective-permute-start = (bf16[128,1024]{1,0:T(8,128)(2,1)S(1)}, bf16[128,1024]{1,0:T(8,128)(2,1)S(1)}, u32[]{:S(2)}, u32[]{:S(2)}) collective-permute-start(bf16[128,1024]{1,0:T(8,128)(2,1)S(1)} %get-tuple-element.18), channel_id=1, source_target_pairs={{128,160},{129,161},{130,162},{131,163},{132,164},{133,165},{134,1... | collective-permute-start | bytes 786440 | tf_op jit(solution)/shard_map/ppermute | solution.py:25
  6.1 19.3 %collective-permute-start.1 = (bf16[128,1024]{1,0:T(8,128)(2,1)S(1)}, bf16[128,1024]{1,0:T(8,128)(2,1)S(1)}, u32[]{:S(2)}, u32[]{:S(2)}) collective-permute-start(bf16[128,1024]{1,0:T(8,128)(2,1)S(1)} %get-tuple-element.20), channel_id=1, source_target_pairs={{128,192},{129,193},{130,194},{131,195},{132,196},{133,197},{134,1... | collective-permute-start | bytes 786440 | tf_op jit(solution)/shard_map/ppermute | solution.py:25
  6.8 20.1 %collective-permute-start.2 = (bf16[128,1024]{1,0:T(8,128)(2,1)S(1)}, bf16[128,1024]{1,0:T(8,128)(2,1)S(1)}, u32[]{:S(2)}, u32[]{:S(2)}) collective-permute-start(bf16[128,1024]{1,0:T(8,128)(2,1)S(1)} %get-tuple-element.19), channel_id=1, source_target_pairs={{128,224},{129,225},{130,226},{131,227},{132,228},{133,229},{134,2... | collective-permute-start | bytes 786440 | tf_op jit(solution)/shard_map/ppermute | solution.py:25
  10.0 47.5 %all-to-all-start = ((f32[16,1,128]{2,1,0:T(1,128)}), f32[16,1,128]{2,1,0:T(1,128)}, u32[]{:S(2)}, u32[]{:S(2)}) async-start(f32[16,1,128]{2,1,0:T(1,128)} %broadcast_in_dim.79), calls=%async_computation | async-start | bytes 16384 | tf_op jit(solution)/shard_map/all_to_all | solution.py:120
  22.4 21.0 %collective-permute-start.6 = (bf16[1024,256]{1,0:T(8,128)(2,1)}, bf16[1024,256]{1,0:T(8,128)(2,1)}, u32[]{:S(2)}, u32[]{:S(2)}) collective-permute-start(bf16[1024,256]{1,0:T(8,128)(2,1)} %bitcast.6), channel_id=1, source_target_pairs={{0,96},{1,97},{2,98},{3,99},{4,100},{5,101},{6,102},{7,103},{8,104... | collective-permute-start | bytes 1572872 | tf_op jit(solution)/shard_map/ppermute | solution.py:25
  25.5 37.7 %collective-permute-start.13 = (bf16[256,1280]{1,0:T(8,128)(2,1)}, bf16[256,1280]{1,0:T(8,128)(2,1)}, u32[]{:S(2)}, u32[]{:S(2)}) collective-permute-start(bf16[256,1280]{1,0:T(8,128)(2,1)} %pad_maximum_fusion.4), channel_id=1, source_target_pairs={{0,8},{1,9},{2,10},{3,11},{4,12},{5,13},{6,14},{7,15},{8,16},{9,17... | collective-permute-start | bytes 1966088 | tf_op jit(solution)/shard_map/ppermute | solution.py:25
  27.1 18.3 %collective-permute-start.3 = (bf16[3,128,1024]{2,1,0:T(8,128)(2,1)S(1)}, bf16[3,128,1024]{2,1,0:T(8,128)(2,1)}, u32[]{:S(2)}, u32[]{:S(2)}) collective-permute-start(bf16[3,128,1024]{2,1,0:T(8,128)(2,1)S(1)} %pad_maximum_fusion.2), channel_id=1, source_target_pairs={{128,129},{129,128},{130,131},{131,130},{132,133},{133,132},{134,1... | collective-permute-start | bytes 2359304 | tf_op jit(solution)/shard_map/ppermute | solution.py:25
  37.0 67.3 %collective-permute-start.14 = (bf16[256,1280]{1,0:T(8,128)(2,1)}, bf16[256,1280]{1,0:T(8,128)(2,1)}, u32[]{:S(2)}, u32[]{:S(2)}) collective-permute-start(bf16[256,1280]{1,0:T(8,128)(2,1)} %pad_maximum_fusion.4), channel_id=1, source_target_pairs={{0,16},{1,17},{2,18},{3,19},{4,20},{5,21},{6,22},{7,23},{8,24},{9,... | collective-permute-start | bytes 1966088 | tf_op jit(solution)/shard_map/ppermute | solution.py:25
  54.5 12.2 %collective-permute-start.7 = (bf16[256,1024]{0,1:T(8,128)(2,1)}, bf16[256,1024]{0,1:T(8,128)(2,1)S(1)}, u32[]{:S(2)}, u32[]{:S(2)}) collective-permute-start(bf16[256,1024]{0,1:T(8,128)(2,1)} %get-tuple-element.15), channel_id=1, source_target_pairs={{128,224},{129,225},{130,226},{131,227},{132,228},{133,229},{134,2... | collective-permute-start | bytes 1572872 | tf_op jit(solution)/shard_map/ppermute | solution.py:25
  55.3 11.4 %collective-permute-start.8 = (bf16[256,1024]{0,1:T(8,128)(2,1)}, bf16[256,1024]{0,1:T(8,128)(2,1)S(1)}, u32[]{:S(2)}, u32[]{:S(2)}) collective-permute-start(bf16[256,1024]{0,1:T(8,128)(2,1)} %get-tuple-element.17), channel_id=1, source_target_pairs={{128,192},{129,193},{130,194},{131,195},{132,196},{133,197},{134,1... | collective-permute-start | bytes 1572872 | tf_op jit(solution)/shard_map/ppermute | solution.py:25
  63.2 43.0 %collective-permute-start.15 = (bf16[256,1280]{1,0:T(8,128)(2,1)}, bf16[256,1280]{1,0:T(8,128)(2,1)}, u32[]{:S(2)}, u32[]{:S(2)}) collective-permute-start(bf16[256,1280]{1,0:T(8,128)(2,1)} %pad_maximum_fusion.4), channel_id=1, source_target_pairs={{0,24},{1,25},{2,26},{3,27},{4,28},{5,29},{6,30},{7,31},{8,0},{9,1... | collective-permute-start | bytes 1966088 | tf_op jit(solution)/shard_map/ppermute | solution.py:25
  70.7 12.7 %all-to-all-start.1 = ((bf16[16,64,128]{2,1,0:T(8,128)(2,1)}), bf16[16,64,128]{2,1,0:T(8,128)(2,1)}, u32[]{:S(2)}, u32[]{:S(2)}) async-start(bf16[16,64,128]{2,1,0:T(8,128)(2,1)} %bitcast.222), calls=%async_computation.1 | async-start | bytes 524288 | tf_op jit(solution)/shard_map/all_to_all | solution.py:132
  85.6 13.2 %all-to-all-start.2 = ((bf16[16,64,128]{2,1,0:T(8,128)(2,1)}), bf16[16,64,128]{2,1,0:T(8,128)(2,1)}, u32[]{:S(2)}, u32[]{:S(2)}) async-start(bf16[16,64,128]{2,1,0:T(8,128)(2,1)} %bitcast.223), calls=%async_computation.2 | async-start | bytes 524288 | tf_op jit(solution)/shard_map/all_to_all | solution.py:138
  127.1 105.1 %collective-permute-start.21 = (bf16[256,512]{1,0:T(8,128)(2,1)}, bf16[256,512]{1,0:T(8,128)(2,1)S(1)}, u32[]{:S(2)}, u32[]{:S(2)}) collective-permute-start(bf16[256,512]{1,0:T(8,128)(2,1)} %fusion.34), channel_id=1, source_target_pairs={{128,0},{129,1},{130,96},{131,97},{132,64},{133,65},{134,32},{135,... | collective-permute-start | bytes 786440 | tf_op jit(solution)/shard_map/ppermute | solution.py:25
  128.4 146.5 %collective-permute-start.26 = (bf16[1024,1024]{1,0:T(8,128)(2,1)}, bf16[1024,1024]{1,0:T(8,128)(2,1)}, u32[]{:S(2)}, u32[]{:S(2)}) collective-permute-start(bf16[1024,1024]{1,0:T(8,128)(2,1)} %constant_dynamic-update-slice_fusion.4), channel_id=1, source_target_pairs={{0,8},{1,9},{2,10},{3,11},{4,12},{5,13},{6,14},{7,15},{8,16},{9,17... | collective-permute-start | bytes 6291464 | tf_op jit(solution)/shard_map/ppermute | solution.py:25
  232.1 13.0 %collective-permute-start.22 = (bf16[256,512]{1,0:T(8,128)(2,1)S(1)}, bf16[256,512]{1,0:T(8,128)(2,1)S(1)}, u32[]{:S(2)}, u32[]{:S(2)}) collective-permute-start(bf16[256,512]{1,0:T(8,128)(2,1)S(1)} %collective-permute-done.21), channel_id=1, source_target_pairs={{0,2},{1,3},{2,0},{3,1},{4,6},{5,7},{6,4},{7,5},{8,10},{9,11},{10,... | collective-permute-start | bytes 786440 | tf_op jit(solution)/shard_map/ppermute | solution.py:25
  234.1 18.3 %collective-permute-start.23 = (bf16[256,512]{1,0:T(8,128)(2,1)S(1)}, bf16[256,512]{1,0:T(8,128)(2,1)S(1)}, u32[]{:S(2)}, u32[]{:S(2)}) collective-permute-start(bf16[256,512]{1,0:T(8,128)(2,1)S(1)} %collective-permute-done.21), channel_id=1, source_target_pairs={{0,4},{1,5},{2,6},{3,7},{4,0},{5,1},{6,2},{7,3},{8,12},{9,13},{10,... | collective-permute-start | bytes 786440 | tf_op jit(solution)/shard_map/ppermute | solution.py:25
  236.0 22.9 %collective-permute-start.24 = (bf16[256,512]{1,0:T(8,128)(2,1)S(1)}, bf16[256,512]{1,0:T(8,128)(2,1)S(1)}, u32[]{:S(2)}, u32[]{:S(2)}) collective-permute-start(bf16[256,512]{1,0:T(8,128)(2,1)S(1)} %collective-permute-done.21), channel_id=1, source_target_pairs={{0,6},{1,7},{2,4},{3,5},{4,2},{5,3},{6,0},{7,1},{8,14},{9,15},{10,... | collective-permute-start | bytes 786440 | tf_op jit(solution)/shard_map/ppermute | solution.py:25
  241.4 47.2 %collective-permute-start.27 = (bf16[1024,1024]{1,0:T(8,128)(2,1)}, bf16[1024,1024]{1,0:T(8,128)(2,1)}, u32[]{:S(2)}, u32[]{:S(2)}) collective-permute-start(bf16[1024,1024]{1,0:T(8,128)(2,1)} %constant_dynamic-update-slice_fusion.4), channel_id=1, source_target_pairs={{0,16},{1,17},{2,18},{3,19},{4,20},{5,21},{6,22},{7,23},{8,24},{9,... | collective-permute-start | bytes 6291464 | tf_op jit(solution)/shard_map/ppermute | solution.py:25
  245.1 86.8 %collective-permute-start.28 = (bf16[1024,1024]{1,0:T(8,128)(2,1)}, bf16[1024,1024]{1,0:T(8,128)(2,1)}, u32[]{:S(2)}, u32[]{:S(2)}) collective-permute-start(bf16[1024,1024]{1,0:T(8,128)(2,1)} %constant_dynamic-update-slice_fusion.4), channel_id=1, source_target_pairs={{0,24},{1,25},{2,26},{3,27},{4,28},{5,29},{6,30},{7,31},{8,0},{9,1... | collective-permute-start | bytes 6291464 | tf_op jit(solution)/shard_map/ppermute | solution.py:25
  259.1 11.3 %collective-permute-start.25 = (bf16[256,4,512]{0,2,1:T(8,128)(2,1)S(1)}, bf16[256,4,512]{0,2,1:T(8,128)(2,1)S(1)}, u32[]{:S(2)}, u32[]{:S(2)}) collective-permute-start(bf16[256,4,512]{0,2,1:T(8,128)(2,1)S(1)} %constant_dynamic-update-slice_fusion), channel_id=1, source_target_pairs={{0,1},{1,0},{2,3},{3,2},{4,5},{5,4},{6,7},{7,6},{8,9},{9,8},{10,11... | collective-permute-start | bytes 3145736 | tf_op jit(solution)/shard_map/ppermute | solution.py:25
  261.1 150.1 %collective-permute-start.29 = (bf16[1024,1280]{1,0:T(8,128)(2,1)}, bf16[1024,1280]{1,0:T(8,128)(2,1)}, u32[]{:S(2)}, u32[]{:S(2)}) collective-permute-start(bf16[1024,1280]{1,0:T(8,128)(2,1)} %bitcast.35), channel_id=1, source_target_pairs={{0,32},{1,33},{2,34},{3,35},{4,36},{5,37},{6,38},{7,39},{8,40},{9,... | collective-permute-start | bytes 7864328 | tf_op jit(solution)/shard_map/ppermute | solution.py:25
  270.4 143.4 %collective-permute-start.30 = (bf16[1024,1280]{1,0:T(8,128)(2,1)}, bf16[1024,1280]{1,0:T(8,128)(2,1)}, u32[]{:S(2)}, u32[]{:S(2)}) collective-permute-start(bf16[1024,1280]{1,0:T(8,128)(2,1)} %bitcast.35), channel_id=1, source_target_pairs={{0,64},{1,65},{2,66},{3,67},{4,68},{5,69},{6,70},{7,71},{8,72},{9,... | collective-permute-start | bytes 7864328 | tf_op jit(solution)/shard_map/ppermute | solution.py:25
  274.9 141.6 %collective-permute-start.31 = (bf16[1024,1280]{1,0:T(8,128)(2,1)}, bf16[1024,1280]{1,0:T(8,128)(2,1)}, u32[]{:S(2)}, u32[]{:S(2)}) collective-permute-start(bf16[1024,1280]{1,0:T(8,128)(2,1)} %bitcast.35), channel_id=1, source_target_pairs={{0,96},{1,97},{2,98},{3,99},{4,100},{5,101},{6,102},{7,103},{8,104... | collective-permute-start | bytes 7864328 | tf_op jit(solution)/shard_map/ppermute | solution.py:25
  337.7 53.4 %all-to-all-start.3 = ((bf16[16,64,128]{2,1,0:T(8,128)(2,1)}), bf16[16,64,128]{2,1,0:T(8,128)(2,1)S(1)}, u32[]{:S(2)}, u32[]{:S(2)}) async-start(bf16[16,64,128]{2,1,0:T(8,128)(2,1)} %bitcast.55), calls=%async_computation.3 | async-start | bytes 524288 | tf_op jit(solution)/shard_map/all_to_all | solution.py:132
  392.3 14.3 %all-to-all-start.4 = ((bf16[16,64,128]{2,1,0:T(8,128)(2,1)}), bf16[16,64,128]{2,1,0:T(8,128)(2,1)S(1)}, u32[]{:S(2)}, u32[]{:S(2)}) async-start(bf16[16,64,128]{2,1,0:T(8,128)(2,1)} %bitcast.81), calls=%async_computation.4 | async-start | bytes 524288 | tf_op jit(solution)/shard_map/all_to_all | solution.py:138
  423.9 13.9 %collective-permute-start.20 = (bf16[256,512]{1,0:T(8,128)(2,1)}, bf16[256,512]{1,0:T(8,128)(2,1)}, u32[]{:S(2)}, u32[]{:S(2)}) collective-permute-start(bf16[256,512]{1,0:T(8,128)(2,1)} %fusion.34), channel_id=1, source_target_pairs={{128,128},{129,129},{130,224},{131,225},{132,192},{133,193},{134,1... | collective-permute-start | bytes 786440 | tf_op jit(solution)/shard_map/ppermute | solution.py:25
  428.5 11.6 %collective-permute-start.33 = (bf16[256,512]{1,0:T(8,128)(2,1)S(1)}, bf16[256,512]{1,0:T(8,128)(2,1)S(1)}, u32[]{:S(2)}, u32[]{:S(2)}) collective-permute-start(bf16[256,512]{1,0:T(8,128)(2,1)S(1)} %get-tuple-element.21), channel_id=1, source_target_pairs={{0,2},{1,3},{2,0},{3,1},{4,6},{5,7},{6,4},{7,5},{8,10},{9,11},{10,... | collective-permute-start | bytes 786440 | tf_op jit(solution)/shard_map/ppermute | solution.py:25
  430.5 22.8 %collective-permute-start.34 = (bf16[256,512]{1,0:T(8,128)(2,1)S(1)}, bf16[256,512]{1,0:T(8,128)(2,1)}, u32[]{:S(2)}, u32[]{:S(2)}) collective-permute-start(bf16[256,512]{1,0:T(8,128)(2,1)S(1)} %get-tuple-element.23), channel_id=1, source_target_pairs={{0,4},{1,5},{2,6},{3,7},{4,0},{5,1},{6,2},{7,3},{8,12},{9,13},{10,... | collective-permute-start | bytes 786440 | tf_op jit(solution)/shard_map/ppermute | solution.py:25
  435.3 23.5 %collective-permute-start.35 = (bf16[256,512]{1,0:T(8,128)(2,1)S(1)}, bf16[256,512]{1,0:T(8,128)(2,1)}, u32[]{:S(2)}, u32[]{:S(2)}) collective-permute-start(bf16[256,512]{1,0:T(8,128)(2,1)S(1)} %get-tuple-element.22), channel_id=1, source_target_pairs={{0,6},{1,7},{2,4},{3,5},{4,2},{5,3},{6,0},{7,1},{8,14},{9,15},{10,... | collective-permute-start | bytes 786440 | tf_op jit(solution)/shard_map/ppermute | solution.py:25
  (32 other events, 338.6 us)

commit v2 on v1

v2 whole, which is shorter than its diff:
```python
import jax
import jax.numpy as jnp
from jax import lax
from jax.experimental import pallas as pl
from jax.experimental.pallas import tpu as pltpu
from jax.sharding import PartitionSpec as P

SIDE = 4
CORES = 2
BOTH = (0, 1)
AXES = ("section", "ctx", "heads")
VMEM = 40 * 1024 * 1024
bf16, f32 = jnp.bfloat16, jnp.float32


def place(section, x, y, z, core):
    return (((section * SIDE + x) * SIDE + y) * SIDE + z) * CORES + core


def routed(value, move, sections):
    pairs = []
    for section in sections:
        for x in range(SIDE):
            for y in range(SIDE):
                for z in range(SIDE):
                    for core in range(CORES):
                        here = (section, x, y, z, core)
                        pairs.append((place(*here), place(*move(*here))))
    return lax.ppermute(value, AXES, pairs)


def along_x(k):
    return lambda s, x, y, z, c: (s, (x + k) % SIDE, y, z, c)


def along_y(k):
    return lambda s, x, y, z, c: (s, x, (y + k) % SIDE, z, c)


def across_z(k):
    return lambda s, x, y, z, c: (s, x, y, z ^ k, c)


def other_core(s, x, y, z, c):
    return (s, x, y, z, 1 - c)


def hop(to_section):
    return lambda s, x, y, z, c: (s if to_section is None else to_section, (x - z) % SIDE, y, x, c)


def first_step(k):
    return lambda s, x, y, z, c: (along_y if s == 1 else along_x)(k)(s, x, y, z, c)


def dot(left, right, left_dim, right_dim):
    return lax.dot_general(
        left, right, (((left_dim,), (right_dim,)), ((), ())), preferred_element_type=f32
    )


def call(body, outs, args, at, grid=None, ins=None, out_specs=None, scratch=(), flops=0):
    whole = lambda a: pl.BlockSpec(a.shape, lambda *_, n=len(a.shape): (0,) * n)
    grid = grid or (1,)
    ins = [s or whole(a) for s, a in zip(ins or [None] * len(args), args)]
    out_specs = [s or whole(o) for s, o in zip(out_specs or [None] * len(outs), outs)]
    moved = sum(a.size * a.dtype.itemsize for a in (*args, *outs))
    return pl.pallas_call(
        body,
        grid_spec=pltpu.PrefetchScalarGridSpec(
            num_scalar_prefetch=1, grid=grid, in_specs=ins, out_specs=out_specs, scratch_shapes=list(scratch)
        ),
        out_shape=list(outs),
        compiler_params=pltpu.CompilerParams(vmem_limit_bytes=VMEM),
        cost_estimate=pl.CostEstimate(flops=flops, bytes_accessed=moved, transcendentals=0),
    )(at, *args)


def struct(shape, dtype=bf16):
    return jax.ShapeDtypeStruct(shape, dtype)


def behind(index, k):
    return lax.rem(index + SIDE - k, SIDE)


def span(index, size):
    return pl.ds(pl.multiple_of(index * size, size), size)


def rows_body(at, own, mine, theirs, w0, w1, w2, w3, out, piece, u):
    k = pl.program_id(0)
    y, z, core = at[1], at[2], at[3]
    half = mine.shape[1]
    fine = w0.shape[1]

    @pl.when(k == 0)
    def _():
        u[...] = own[...]

    @pl.when(k > 0)
    def _():
        u[span(core, half), :] = mine[0]
        u[span(1 - core, half), :] = theirs[0]

    @pl.when(k == z)
    def _():
        piece[...] = u[:, span(core, piece.shape[1])]

    total = None
    for j, w in enumerate((w0, w1, w2, w3)):
        term = dot(u[:, span(behind(y, j), fine)], w[...], 1, 1)
        total = term if total is None else total + term
    out[0] = total.astype(bf16)


def entering(grad, leading, c_rows, totals, states):
    size = totals.shape[0]
    scaled = (grad.astype(f32) * leading).astype(bf16)
    summed = dot(scaled, c_rows, 0, 0).astype(bf16)
    states[:, : states.shape[1] - totals.shape[1], :] = summed.reshape(
        size, summed.shape[0] // size, summed.shape[1]
    )
    states[:, states.shape[1] - totals.shape[1] :, :] = totals


def sum_body(at, own, r1, r2, r3, leading, c_rows, totals, grad, states):
    total = own[0].astype(f32)
    for r in (r1, r2, r3):
        total = total + r[...].astype(f32)
    rounded = total.astype(bf16)
    grad[...] = rounded
    entering(rounded, leading[...], c_rows[...], totals[...], states)


def lower_body(at, p0, p1, p2, p3, other, w0, w1, w2, w3, leading, c_rows, totals, grad, states, u):
    x, y, z, core = at[0], at[1], at[2], at[3]
    share = p0.shape[1]
    block = share * CORES
    fine = block // SIDE

    @pl.when(pl.program_id(0) == 0)
    def _():
        for q, part in enumerate((p0, p1, p2, p3)):
            base = (z ^ q) * CORES
            u[:, span(base + core, share)] = part[...]
            u[:, span(base + 1 - core, share)] = other[q]

    total = None
    for k, w in enumerate((w0, w1, w2, w3)):
        for j in range(SIDE):
            columns = u[:, span(behind(x, j) * SIDE + behind(y, k), fine)]
            term = dot(columns, w[j], 1, 1)
            total = term if total is None else total + term
    rounded = total.astype(bf16)
    grad[...] = rounded
    entering(rounded, leading[...], c_rows[...], totals[...], states)


def scan_body(at, states, exits):
    count, size, _ = exits.shape
    held = jnp.zeros(exits.shape[1:], f32)
    for k in range(count - 1, -1, -1):
        exits[k] = held.astype(bf16)
        total = states[k, size : size + 16, :].astype(f32)
        held = (total[0:1] + total[1:2]) * held + states[k, :size, :].astype(f32)


def within_body(at, grad, x_rows, kernel, mixed, leading, entry, b_rows, c_rows, skip, out, bc, weights):
    step = pl.program_id(0)
    pair = grad[...]
    x_pair = x_rows[...]
    low = lax.broadcasted_iota(jnp.int32, pair.shape, 1) < pair.shape[1] // 2
    none = jnp.zeros_like(pair)
    first = jnp.where(low, pair, none)
    second = jnp.where(low, none, pair)
    weighted = kernel[0].astype(f32) * dot(first, x_pair, 1, 1)
    weighted = weighted + kernel[1].astype(f32) * dot(second, x_pair, 1, 1)
    wide = pair.astype(f32)
    inside = jnp.where(low, dot(mixed[0], pair, 0, 0), dot(mixed[1], pair, 0, 0))
    out[...] = inside + skip[...] * wide
    from_entry = dot((wide * leading[...]).astype(bf16), entry[...], 1, 0)
    size = b_rows.shape[1]

    @pl.when(step == 0)
    def _():
        weights[...] = weighted
        bc[:, size:] = from_entry

    @pl.when(step > 0)
    def _():
        weights[...] += weighted
        bc[:, size:] += from_entry

    @pl.when(step == pl.num_programs(0) - 1)
    def _():
        rounded = weights[...].astype(bf16)
        bc[:, :size] = dot(rounded, c_rows[...], 0, 0)
        bc[:, size:] += dot(rounded, b_rows[...], 1, 0)


def finish_body(at, inside, bc, trailing, x_trailing, b_rows, leaving, out):
    inner = inside.shape[1]
    size = b_rows.shape[1]
    width = 256
    grad_b = bc[:, :size]
    for t in range(inner // width):
        columns = slice(t * width, (t + 1) * width)
        state = leaving[columns, :]
        gained = trailing[:, columns] * dot(b_rows[...], state, 1, 1)
        out[:, columns] = (inside[:, columns] + gained).astype(bf16)
        grad_b = grad_b + dot(x_trailing[:, columns], state, 1, 0)
    out[:, inner : inner + size] = grad_b.astype(bf16)
    out[:, inner + size :] = bc[:, size:].astype(bf16)


def back_body(at, g0, g1, g2, g3, weights, keep, give, u, g):
    k = pl.program_id(0)
    y, core = at[1], at[3]
    fine = weights.shape[1]
    share = keep.shape[2]
    for i, part in enumerate((g0, g1, g2, g3)):

        @pl.when(k == i)
        def _():
            g[...] = part[...]

    for j in range(SIDE):
        u[:, span(behind(y, j), fine)] = dot(g[...], weights[j], 1, 1).astype(bf16)
    keep[0] = u[:, span(core, share)]
    give[0] = u[:, span(1 - core, share)]


def whole_body(at, g, w0, w1, w2, w3, keep, give):
    x, y, z, core = at[0], at[1], at[2], at[3]
    fine = w0.shape[1]
    column = behind(y, pl.program_id(0))
    for k, w in enumerate((w0, w1, w2, w3)):
        q = z ^ behind(x, k)
        term = dot(g[...], w[0], 1, 1).astype(bf16)
        columns = span(lax.rem(column, CORES), fine)

        @pl.when(column // CORES == core)
        def _():
            keep[q, :, columns] = term

        @pl.when(column // CORES != core)
        def _():
            give[q, :, columns] = term


def pair_body(at, keep, got, s1, s2, s3):
    for q, out in ((1, s1), (2, s2), (3, s3)):
        out[...] = (keep[q].astype(f32) + got[q].astype(f32)).astype(bf16)


def total_body(at, keep, got, r1, r2, r3, upstream, out):
    total = keep[0].astype(f32) + got[0].astype(f32)
    for r in (r1, r2, r3):
        total = total + r[...].astype(f32)
    out[...] = (total + upstream[...].astype(f32)).astype(bf16)


def decay_tables(decay_rates):
    cumulative = jnp.cumsum(decay_rates, axis=1)
    spread = cumulative[:, :, None] - cumulative[:, None, :]
    length = decay_rates.shape[1]
    lower = jnp.arange(length)[:, None] >= jnp.arange(length)[None, :]
    kernel = jnp.where(lower[None], jnp.exp(jnp.minimum(spread, 0.0)), 0.0)
    return cumulative, kernel


def local(grad_out, w_out, w_in, w_bc, x_act, bc_act, decay, skip_gain, state_in):
    section = lax.axis_index("section")
    ctx = lax.axis_index("ctx")
    heads_at = lax.axis_index("heads")
    x, y = ctx // SIDE, ctx % SIDE
    z, core = heads_at // CORES, heads_at % CORES
    at = jnp.stack([x, y, z, core]).astype(jnp.int32)
    rows, width = grad_out.shape
    block = width // SIDE
    share = block // CORES
    fine = w_out.shape[2]
    half = rows // CORES
    head_count, head_size, state_size = state_in.shape[2:]
    inner = head_count * head_size
    outer = inner + 2 * state_size
    tiles = inner // 256
    tile_heads = head_count // tiles
    pad = 16

    out_parts = [w_out[0]] + [routed(w_out[0], first_step(k), BOTH) for k in (1, 2, 3)]

    pieces = []
    for k in (1, 2, 3):
        piece = lax.dynamic_slice(grad_out, (half * core, block * ((x + k) % SIDE)), (half, block))
        pieces.append(routed(piece, along_x(k), (1,)))
    mine = jnp.stack(pieces)
    theirs = routed(mine, other_core, (1,))

    back = jnp.concatenate([w_in[0], w_bc[0]], axis=1)
    back, out_parts = lax.optimization_barrier((back, out_parts))
    back_set = jnp.stack([back] + [routed(back, along_y(k), BOTH) for k in (1, 2, 3)])
    out_set = jnp.stack(out_parts)

    cumulative, kernel = decay_tables(decay[0])
    leading = jnp.repeat(jnp.exp(cumulative).T, head_size, axis=1)
    trailing = jnp.repeat(jnp.exp(cumulative[:, -1:] - cumulative).T, head_size, axis=1)
    b_rows = bc_act[0][:, :state_size]
    c_rows = bc_act[0][:, state_size:]
    common = dot(c_rows, b_rows, 1, 1)
    mixed = (kernel * common[None]).astype(bf16)
    kernel = kernel.astype(bf16)
    x_rows = x_act[0]
    x_trailing = (x_rows.astype(f32) * trailing).astype(bf16)
    entry = state_in[0, 0].reshape(inner, state_size).astype(bf16)
    skip = jnp.repeat(skip_gain[0], head_size)[None]
    total = jnp.exp(cumulative[:, -1])
    high = total.astype(bf16)
    low = (total - high.astype(f32)).astype(bf16)
    totals = jnp.concatenate(
        [high[:, None], low[:, None], jnp.zeros((head_count, pad - 2), bf16)], axis=1
    )
    totals = jnp.broadcast_to(totals[:, :, None], (head_count, pad, state_size))

    per_tile = pl.BlockSpec((rows, 256), lambda t, p: (0, t))
    tile_totals = pl.BlockSpec((tile_heads, pad, state_size), lambda t, p: (t, 0, 0))
    tile_states = pl.BlockSpec((tile_heads, head_size + pad, state_size), lambda t, p: (t, 0, 0))
    state_shape = struct((head_count, head_size + pad, state_size))

    def mixer(grad_ssd, states):
        arrived = lax.all_to_all(states, "ctx", 0, 0)
        (exits,) = call(scan_body, [struct((head_count, head_size, state_size))], [arrived], at)
        leaving = lax.all_to_all(exits, "ctx", 0, 0).reshape(inner, state_size)
        pair = pl.BlockSpec((rows, 128), lambda t, p: (0, t))
        table = pl.BlockSpec((2, rows, rows), lambda t, p: (t, 0, 0))
        inside, bc = call(
            within_body,
            [struct((rows, inner), f32), struct((rows, 2 * state_size), f32)],
            [grad_ssd, x_rows, kernel, mixed, leading, entry, b_rows, c_rows, skip],
            at,
            grid=(inner // 128,),
            ins=[
                pair, pair, table, table, pair,
                pl.BlockSpec((128, state_size), lambda t, p: (t, 0)),
                None, None,
                pl.BlockSpec((1, 128), lambda t, p: (0, t)),
            ],
            out_specs=[pair, None],
            scratch=[pltpu.VMEM((rows, rows), f32)],
            flops=4 * rows * rows * inner,
        )
        (grads,) = call(
            finish_body,
            [struct((rows, outer))],
            [inside, bc, trailing, x_trailing, b_rows, leaving],
            at,
            flops=4 * rows * inner * state_size,
        )
        return grads

    def over_heads(keep, give, upstream, sections):
        got = routed(give, other_core, sections)
        chunk = struct((rows, share))
        sent = call(pair_body, [chunk] * 3, [keep, got], at)
        received = [routed(s, across_z(k), sections) for k, s in zip((1, 2, 3), sent)]
        one = pl.BlockSpec((1, rows, share), lambda t, p: (0, 0, 0))
        (total,) = call(
            total_body, [chunk], [keep, got, *received, upstream], at, ins=[one, one] + [None] * 4
        )
        return total

    third = pl.BlockSpec((1, half, block), lambda k, p: (jnp.maximum(k - 1, 0), 0, 0))
    partial, own = call(
        rows_body,
        [struct((SIDE, rows, inner)), struct((rows, share))],
        [grad_out, mine, theirs, *out_parts],
        at,
        grid=(SIDE,),
        ins=[pl.BlockSpec((rows, block), lambda k, p: (0, p[0])), third, third] + [None] * 4,
        out_specs=[pl.BlockSpec((1, rows, inner), lambda k, p: (k, 0, 0)), None],
        scratch=[pltpu.VMEM((rows, block), bf16)],
        flops=2 * SIDE * rows * block * inner,
    )
    received = [routed(partial[k], along_x(-k), (1,)) for k in (1, 2, 3)]
    grad_ssd, states = call(
        sum_body,
        [struct((rows, inner)), state_shape],
        [partial, *received, leading, c_rows, totals],
        at,
        grid=(tiles,),
        ins=[pl.BlockSpec((1, rows, 256), lambda t, p: (0, 0, t))] + [per_tile] * 4 + [None, tile_totals],
        out_specs=[per_tile, tile_states],
        flops=2 * rows * inner * state_size,
    )
    grads = mixer(grad_ssd, states)

    out_whole = [routed(out_set, along_y(k), (0,)) for k in (1, 2, 3)]
    back_whole = [routed(back_set, along_x(k), (0,)) for k in (1, 2, 3)]

    grads_all = [grads] + [routed(grads, along_x(k), (1,)) for k in (1, 2, 3)]
    grads_all, out_whole, back_whole = lax.optimization_barrier((grads_all, out_whole, back_whole))
    chunks = struct((SIDE, rows, share))
    by_z = pl.BlockSpec((1, rows, share), lambda k, p: (p[2] ^ k, 0, 0))
    keep, give = call(
        back_body,
        [chunks, chunks],
        [*grads_all, back_set],
        at,
        grid=(SIDE,),
        out_specs=[by_z, by_z],
        scratch=[pltpu.VMEM((rows, block), bf16), pltpu.VMEM((rows, outer), bf16)],
        flops=2 * SIDE * rows * block * outer,
    )
    middle = over_heads(keep, give, own, (1,))

    arrived = routed(middle, hop(0), (1,))
    settled = routed(middle, hop(None), (1,))

    parts = [arrived] + [routed(arrived, across_z(k), (0,)) for k in (1, 2, 3)]
    other = routed(jnp.stack(parts), other_core, (0,))
    weights = pl.BlockSpec((SIDE, 256, fine), lambda t, p: (0, t, 0))
    grad_ssd, states = call(
        lower_body,
        [struct((rows, inner)), state_shape],
        [*parts, other, out_set, *out_whole, leading, c_rows, totals],
        at,
        grid=(tiles,),
        ins=[None] * 5 + [weights] * 4 + [per_tile, None, tile_totals],
        out_specs=[per_tile, tile_states],
        scratch=[pltpu.VMEM((rows, width), bf16)],
        flops=2 * rows * width * inner,
    )
    grads = mixer(grad_ssd, states)
    weights = pl.BlockSpec((1, fine, outer), lambda t, p: (t, 0, 0))
    keep, give = call(
        whole_body,
        [chunks, chunks],
        [grads, back_set, *back_whole],
        at,
        grid=(SIDE,),
        ins=[None] + [weights] * 4,
        flops=2 * rows * width * outer,
    )
    result = over_heads(keep, give, arrived, (0,))
    return jnp.where(section == 1, settled, result)[None]


def solution(mesh):
    placed = (
        P("ctx", None),
        P("section", "heads", "ctx"),
        P("section", "ctx", "heads"),
        P("section", "ctx", "heads"),
        P("section", "ctx", "heads"),
        P("section", "ctx", "heads"),
        P("section", "heads", "ctx"),
        P("section", "heads"),
        P("section", "ctx", "heads", None, None),
    )
    return jax.shard_map(
        local, mesh=mesh, in_specs=placed, out_specs=P("section", "ctx", "heads"), check_vma=False
    )
```

time: 463 us -> 488 us (1.054)
  matrix products: 52.3 us -> 0.89 us
  Pallas kernels: 0 us -> 49.8 us
  waiting for transfers between devices: 239 us -> 275 us
  starting transfers between devices: 109 us -> 82.9 us
  blocking collectives: 0 us -> 24.3 us
  other arithmetic: 23.7 us -> 15.2 us
    pallas_call x0 -> x15, Pallas kernels: none -> 49.8 us  [call(): pl.pallas_call(body, grid_spec=pltpu.PrefetchScalarGridSpec(num_scalar_pr...]
    all_to_all x5 -> x3, waiting for transfers between devices: 55.8 us -> 100 us  [the longest x1 100 us: mixer(): arrived = lax.all_to_all(states, 'ctx', 0, 0)]
    dot_general x23 -> x1, matrix products: 42.6 us -> 0.89 us  [dot(): lax.dot_general(left, right, (((left_dim,), (right_dim,)), ((), ())), pre...]
    all_to_all x0 -> x1, blocking collectives: none -> 24.3 us  [mixer(): arrived = lax.all_to_all(states, 'ctx', 0, 0)]
    unnamed x49 -> x104, local copies, waits for them, and re-layouts: 8.58 us -> 29.3 us
    all_to_all x5 -> x3, starting transfers between devices: 32 us -> 18.2 us  [the longest x1 9.84 us: mixer(): arrived = lax.all_to_all(states, 'ctx', 0, 0)]
    dynamic_update_slice x11 -> x0, local copies, waits for them, and re-layouts: 13.7 us -> none  [the longest x4 7.68 us: local(): lax.dynamic_update_slice(out_block, part, (0, fine * ((out_at - k) % SIDE)))]
    ppermute x36, starting transfers between devices: 76.7 us -> 64.7 us  [routed(): return lax.ppermute(value, AXES, pairs)]
  transfers between devices with their start and end apart: 41 -> 39, of which waited for: 13 -> 12; matrix products, arithmetic and copies ran while one was open for 19% -> 4% of each run, Pallas kernels for 0% -> 4%
where the time goes in v2:
time: 488 us; the launch traced here: 485 us
  waiting for transfers between devices  275 us (56%)
  starting transfers between devices  82.9 us (17%)
  Pallas kernels  49.8 us (10%)
  local copies, waits for them, and re-layouts  36.2 us (7%)
  blocking collectives  24.3 us (5%)
  other arithmetic  15.2 us (3%)
    ppermute x36, waiting for transfers between devices, routed(): return lax.ppermute(value, AXES, pairs)  175 us
    all_to_all x1, waiting for transfers between devices, mixer(): arrived = lax.all_to_all(states, 'ctx', 0, 0)  100 us
    ppermute x36, starting transfers between devices, routed(): return lax.ppermute(value, AXES, pairs)  64.7 us
    pallas_call x15, Pallas kernels, call(): pl.pallas_call(body, grid_spec=pltpu.PrefetchScalarGridSpec(num_scalar_pr...  49.8 us
    unnamed x104, local copies, waits for them, and re-layouts  29.3 us
    all_to_all x1, blocking collectives, mixer(): arrived = lax.all_to_all(states, 'ctx', 0, 0)  24.3 us
    all_to_all x1, starting transfers between devices, mixer(): arrived = lax.all_to_all(states, 'ctx', 0, 0)  9.84 us
  transfers between devices with their start and end apart: 39, of which 12 were waited for; matrix products, arithmetic and copies ran while one was open for 4% of the time, Pallas kernels for 4%

profile of v2, /device:TPU:32, one launch (start us, length us, event | category | flops | bytes accessed | tf_op | source)
XLA Modules:
  0.0 485.3 jit_solution(3000640767847654124)
XLA Ops:
  1.9 2.8 collective-permute-start.6
  10.4 17.1 %collective-permute-done.6.w3 = bf16[1024,256]{1,0:T(8,128)(2,1)S(1)} collective-permute-done((bf16[1024,256]{1,0:T(8,128)(2,1)}, bf16[1024,256]{1,0:T(8,128)(2,1)S(1)}, u32[]{:S(2)}, u32[]{:S(2)}) %collective-permute-start.6) | collective-permute-done | bytes 524320 | tf_op jit(solution)/shard_map/ppermute | solution.py:29
  27.6 3.6 collective-permute-done.4.w1
  32.8 4.9 %collective-permute-start.15 = (bf16[4,1024,256]{2,1,0:T(8,128)(2,1)}, bf16[4,1024,256]{2,1,0:T(8,128)(2,1)}, u32[]{:S(2)}, u32[]{:S(2)}) collective-permute-start(bf16[4,1024,256]{2,1,0:T(8,128)(2,1)} %pad_maximum_fusion.1.w0), channel_id=1, source_target_pairs={{0,24},{1,25},{2,26},{3,27},{4,28},{5,29},{6,30},{7,31},{8,0},{9,1... | collective-permute-start | bytes 6291464 | tf_op jit(solution)/shard_map/ppermute | solution.py:29
  41.8 5.9 %collective-permute-start.14 = (bf16[4,1024,256]{2,1,0:T(8,128)(2,1)}, bf16[4,1024,256]{2,1,0:T(8,128)(2,1)}, u32[]{:S(2)}, u32[]{:S(2)}) collective-permute-start(bf16[4,1024,256]{2,1,0:T(8,128)(2,1)} %pad_maximum_fusion.1.w0), channel_id=1, source_target_pairs={{0,16},{1,17},{2,18},{3,19},{4,20},{5,21},{6,22},{7,23},{8,24},{9,... | collective-permute-start | bytes 6291464 | tf_op jit(solution)/shard_map/ppermute | solution.py:29
  53.6 3.8 shard_map.91
  59.3 96.8 %collective-permute-done.18 = bf16[256,1280]{1,0:T(8,128)(2,1)S(1)} collective-permute-done((bf16[256,1280]{1,0:T(8,128)(2,1)}, bf16[256,1280]{1,0:T(8,128)(2,1)S(1)}, u32[]{:S(2)}, u32[]{:S(2)}) %collective-permute-start.18) | collective-permute-done | bytes 655392 | tf_op jit(solution)/shard_map/ppermute | solution.py:29
  167.7 3.5 pad_maximum_fusion.weights.w0
  173.2 2.7 collective-permute-start.20
  175.9 3.3 collective-permute-start.19
  180.3 3.7 shard_map.92
  185.6 9.8 %all-to-all-start = ((bf16[16,80,128]{2,1,0:T(8,128)(2,1)}), bf16[16,80,128]{2,1,0:T(8,128)(2,1)}, u32[]{:S(2)}, u32[]{:S(2)}) async-start(bf16[16,80,128]{2,1,0:T(8,128)(2,1)} %copy-done.29), calls=%async_computation | async-start | bytes 655360 | tf_op jit(solution)/shard_map/all_to_all | solution.py:332
  195.4 3.1 multiply_convert_fusion
  198.5 100.2 %all-to-all-done.states = bf16[16,80,128]{2,1,0:T(8,128)(2,1)} async-done(((bf16[16,80,128]{2,1,0:T(8,128)(2,1)}), bf16[16,80,128]{2,1,0:T(8,128)(2,1)}, u32[]{:S(2)}, u32[]{:S(2)}) %all-to-all-start) | async-done | bytes 327712 | tf_op jit(solution)/shard_map/all_to_all | solution.py:332
  301.0 4.2 all-to-all-start.1
  309.8 4.3 shard_map.93
  324.5 6.2 %shard_map.96 = (bf16[4,256,512]{2,1,0:T(8,128)(2,1)S(1)}, bf16[4,256,512]{2,1,0:T(8,128)(2,1)S(1)}) custom-call(s32[4]{0:T(128)S(1)} %pad_add_fusion.at, bf16[256,1280]{1,0:T(8,128)(2,1)S(1)} %shard_map.95.g0, bf16[256,1280]{1,0:T(8,128)(2,1)S(1)} %collective-permute-done.10.g1, bf16[256,1280]{1,0:T(8,128)(2,1)S(1)} %collective-permute-done.11.g2, ...), custom_call_target="tpu_custom_call" | custom-call | flops 2684354560 | bytes 7340032 | tf_op jit(solution)/shard_map/pallas_call | solution.py:68
  336.5 18.5 %collective-permute-done.27.p0.upstream = bf16[256,512]{1,0:T(8,128)(2,1)S(1)} collective-permute-done((bf16[256,512]{1,0:T(8,128)(2,1)S(1)}, bf16[256,512]{1,0:T(8,128)(2,1)S(1)}, u32[]{:S(2)}, u32[]{:S(2)}) %collective-permute-start.27) | collective-permute-done | bytes 262176 | tf_op jit(solution)/shard_map/ppermute | solution.py:29
  358.9 5.4 %collective-permute-start.28 = (bf16[256,512]{1,0:T(8,128)(2,1)S(1)}, bf16[256,512]{1,0:T(8,128)(2,1)S(1)}, u32[]{:S(2)}, u32[]{:S(2)}) collective-permute-start(bf16[256,512]{1,0:T(8,128)(2,1)S(1)} %collective-permute-done.27.p0.upstream), channel_id=1, source_target_pairs={{0,2},{1,3},{2,0},{3,1},{4,6},{5,7},{6,4},{7,5},{8,10},{9,11},{10,... | collective-permute-start | bytes 786440 | tf_op jit(solution)/shard_map/ppermute | solution.py:29
  364.2 9.6 %collective-permute-done.30.p3 = bf16[256,512]{1,0:T(8,128)(2,1)S(1)} collective-permute-done((bf16[256,512]{1,0:T(8,128)(2,1)S(1)}, bf16[256,512]{1,0:T(8,128)(2,1)S(1)}, u32[]{:S(2)}, u32[]{:S(2)}) %collective-permute-start.30) | collective-permute-done | bytes 262176 | tf_op jit(solution)/shard_map/ppermute | solution.py:29
  373.8 4.1 collective-permute-done.29.p2
  382.6 7.0 %shard_map.99 = (bf16[256,1024]{1,0:T(8,128)(2,1)S(1)}, bf16[16,80,128]{2,1,0:T(8,128)(2,1)S(1)}) custom-call(s32[4]{0:T(128)S(1)} %pad_add_fusion.at, bf16[256,512]{1,0:T(8,128)(2,1)S(1)} %collective-permute-done.27.p0.upstream, bf16[256,512]{1,0:T(8,128)(2,1)S(1)} %collective-permute-done.28.p1, bf16[256,512]{1,0:T(8,128)(2,1)S(1)} %collective-permute-done.29.p2, ...), custom_call_target="tpu_custom_call" | custom-call | flops 2147483648 | bytes 12517376 | tf_op jit(solution)/shard_map/pallas_call | solution.py:68
  390.4 24.3 %all_to_all.20.states = bf16[16,80,128]{2,1,0:T(8,128)(2,1)S(1)} all-to-all(bf16[16,80,128]{2,1,0:T(8,128)(2,1)S(1)} %get-tuple-element.66), channel_id=1, replica_groups=mesh['section'=2,'ctx'=16,'heads'=8] {'ctx'}, dimensions={0} | all-to-all | bytes 655360 | tf_op jit(solution)/shard_map/all_to_all | solution.py:332
  416.0 4.2 all-to-all-start.3
  423.9 4.3 shard_map.100
  436.3 10.8 %shard_map.103 = (bf16[4,256,512]{2,1,0:T(8,128)(2,1)S(1)}, bf16[4,256,512]{2,1,0:T(8,128)(2,1)S(1)}) custom-call(s32[4]{0:T(128)S(1)} %pad_add_fusion.at, bf16[256,1280]{1,0:T(8,128)(2,1)S(1)} %shard_map.102.g, bf16[4,256,1280]{2,1,0:T(8,128)(2,1)} %pad_maximum_fusion.weights.w0, bf16[4,256,1280]{2,1,0:T(8,128)(2,1)} %collective-permute-done.19.w1, ...), custom_call_target="tpu_custom_call" | custom-call | flops 2684354560 | bytes 13238272 | tf_op jit(solution)/shard_map/pallas_call | solution.py:68
  449.2 2.6 collective-permute-done.32.got
  453.3 2.9 collective-permute-start.33
  456.2 3.5 collective-permute-start.34
  459.8 2.8 collective-permute-start.35
  465.8 12.2 %collective-permute-done.34.r2 = bf16[256,512]{1,0:T(8,128)(2,1)S(1)} collective-permute-done((bf16[256,512]{1,0:T(8,128)(2,1)}, bf16[256,512]{1,0:T(8,128)(2,1)S(1)}, u32[]{:S(2)}, u32[]{:S(2)}) %collective-permute-start.34) | collective-permute-done | bytes 262176 | tf_op jit(solution)/shard_map/ppermute | solution.py:29
  478.0 5.7 %collective-permute-done.35.r3 = bf16[256,512]{1,0:T(8,128)(2,1)S(1)} collective-permute-done((bf16[256,512]{1,0:T(8,128)(2,1)}, bf16[256,512]{1,0:T(8,128)(2,1)S(1)}, u32[]{:S(2)}, u32[]{:S(2)}) %collective-permute-start.35) | collective-permute-done | bytes 262176 | tf_op jit(solution)/shard_map/ppermute | solution.py:29
  (200 shorter events, 90.6 us)
Async XLA Ops:
  1.3 5.9 %collective-permute-start = (bf16[128,1024]{1,0:T(8,128)(2,1)S(1)}, bf16[128,1024]{1,0:T(8,128)(2,1)S(1)}, u32[]{:S(2)}, u32[]{:S(2)}) collective-permute-start(bf16[128,1024]{1,0:T(8,128)(2,1)S(1)} %get-tuple-element.80), channel_id=1, source_target_pairs={{128,160},{129,161},{130,162},{131,163},{132,164},{133,165},{134,1... | collective-permute-start | bytes 786440 | tf_op jit(solution)/shard_map/ppermute | solution.py:29
  1.9 25.6 %collective-permute-start.6 = (bf16[1024,256]{1,0:T(8,128)(2,1)}, bf16[1024,256]{1,0:T(8,128)(2,1)S(1)}, u32[]{:S(2)}, u32[]{:S(2)}) collective-permute-start(bf16[1024,256]{1,0:T(8,128)(2,1)} %bitcast.61), channel_id=1, source_target_pairs={{0,96},{1,97},{2,98},{3,99},{4,100},{5,101},{6,102},{7,103},{8,104... | collective-permute-start | bytes 1572872 | tf_op jit(solution)/shard_map/ppermute | solution.py:29
  4.8 22.8 %collective-permute-start.5 = (bf16[1024,256]{1,0:T(8,128)(2,1)}, bf16[1024,256]{1,0:T(8,128)(2,1)S(1)}, u32[]{:S(2)}, u32[]{:S(2)}) collective-permute-start(bf16[1024,256]{1,0:T(8,128)(2,1)} %bitcast.62), channel_id=1, source_target_pairs={{0,64},{1,65},{2,66},{3,67},{4,68},{5,69},{6,70},{7,71},{8,72},{9,... | collective-permute-start | bytes 1572872 | tf_op jit(solution)/shard_map/ppermute | solution.py:29
  5.6 25.5 %collective-permute-start.4 = (bf16[1024,256]{1,0:T(8,128)(2,1)}, bf16[1024,256]{1,0:T(8,128)(2,1)S(1)}, u32[]{:S(2)}, u32[]{:S(2)}) collective-permute-start(bf16[1024,256]{1,0:T(8,128)(2,1)} %bitcast.63), channel_id=1, source_target_pairs={{0,32},{1,33},{2,34},{3,35},{4,36},{5,37},{6,38},{7,39},{8,40},{9,... | collective-permute-start | bytes 1572872 | tf_op jit(solution)/shard_map/ppermute | solution.py:29
  6.5 3.2 collective-permute-start.1
  7.1 2.5 collective-permute-start.2
  9.7 31.1 %collective-permute-start.3 = (bf16[3,128,1024]{2,1,0:T(8,128)(2,1)S(1)}, bf16[3,128,1024]{2,1,0:T(8,128)(2,1)S(1)}, u32[]{:S(2)}, u32[]{:S(2)}) collective-permute-start(bf16[3,128,1024]{2,1,0:T(8,128)(2,1)S(1)} %pad_maximum_fusion.3.mine), channel_id=1, source_target_pairs={{128,129},{129,128},{130,131},{131,130},{132,133},{133,132},{134,1... | collective-permute-start | bytes 2359304 | tf_op jit(solution)/shard_map/ppermute | solution.py:29
  32.8 143.1 %collective-permute-start.15 = (bf16[4,1024,256]{2,1,0:T(8,128)(2,1)}, bf16[4,1024,256]{2,1,0:T(8,128)(2,1)}, u32[]{:S(2)}, u32[]{:S(2)}) collective-permute-start(bf16[4,1024,256]{2,1,0:T(8,128)(2,1)} %pad_maximum_fusion.1.w0), channel_id=1, source_target_pairs={{0,24},{1,25},{2,26},{3,27},{4,28},{5,29},{6,30},{7,31},{8,0},{9,1... | collective-permute-start | bytes 6291464 | tf_op jit(solution)/shard_map/ppermute | solution.py:29
  38.6 117.5 %collective-permute-start.18 = (bf16[256,1280]{1,0:T(8,128)(2,1)}, bf16[256,1280]{1,0:T(8,128)(2,1)S(1)}, u32[]{:S(2)}, u32[]{:S(2)}) collective-permute-start(bf16[256,1280]{1,0:T(8,128)(2,1)} %pad_maximum_fusion.4), channel_id=1, source_target_pairs={{0,24},{1,25},{2,26},{3,27},{4,28},{5,29},{6,30},{7,31},{8,0},{9,1... | collective-permute-start | bytes 1966088 | tf_op jit(solution)/shard_map/ppermute | solution.py:29
  39.5 118.3 %collective-permute-start.17 = (bf16[256,1280]{1,0:T(8,128)(2,1)}, bf16[256,1280]{1,0:T(8,128)(2,1)S(1)}, u32[]{:S(2)}, u32[]{:S(2)}) collective-permute-start(bf16[256,1280]{1,0:T(8,128)(2,1)} %pad_maximum_fusion.4), channel_id=1, source_target_pairs={{0,16},{1,17},{2,18},{3,19},{4,20},{5,21},{6,22},{7,23},{8,24},{9,... | collective-permute-start | bytes 1966088 | tf_op jit(solution)/shard_map/ppermute | solution.py:29
  39.8 119.4 %collective-permute-start.16 = (bf16[256,1280]{1,0:T(8,128)(2,1)}, bf16[256,1280]{1,0:T(8,128)(2,1)S(1)}, u32[]{:S(2)}, u32[]{:S(2)}) collective-permute-start(bf16[256,1280]{1,0:T(8,128)(2,1)} %pad_maximum_fusion.4), channel_id=1, source_target_pairs={{0,8},{1,9},{2,10},{3,11},{4,12},{5,13},{6,14},{7,15},{8,16},{9,17... | collective-permute-start | bytes 1966088 | tf_op jit(solution)/shard_map/ppermute | solution.py:29
  41.8 280.4 %collective-permute-start.14 = (bf16[4,1024,256]{2,1,0:T(8,128)(2,1)}, bf16[4,1024,256]{2,1,0:T(8,128)(2,1)}, u32[]{:S(2)}, u32[]{:S(2)}) collective-permute-start(bf16[4,1024,256]{2,1,0:T(8,128)(2,1)} %pad_maximum_fusion.1.w0), channel_id=1, source_target_pairs={{0,16},{1,17},{2,18},{3,19},{4,20},{5,21},{6,22},{7,23},{8,24},{9,... | collective-permute-start | bytes 6291464 | tf_op jit(solution)/shard_map/ppermute | solution.py:29
  156.1 9.7 %collective-permute-start.9 = (bf16[256,1024]{1,0:T(8,128)(2,1)}, bf16[256,1024]{1,0:T(8,128)(2,1)}, u32[]{:S(2)}, u32[]{:S(2)}) collective-permute-start(bf16[256,1024]{1,0:T(8,128)(2,1)} %get-tuple-element.77), channel_id=1, source_target_pairs={{128,160},{129,161},{130,162},{131,163},{132,164},{133,165},{134,1... | collective-permute-start | bytes 1572872 | tf_op jit(solution)/shard_map/ppermute | solution.py:29
  157.8 13.5 %collective-permute-start.8 = (bf16[256,1024]{1,0:T(8,128)(2,1)}, bf16[256,1024]{1,0:T(8,128)(2,1)}, u32[]{:S(2)}, u32[]{:S(2)}) collective-permute-start(bf16[256,1024]{1,0:T(8,128)(2,1)} %get-tuple-element.78), channel_id=1, source_target_pairs={{128,192},{129,193},{130,194},{131,195},{132,196},{133,197},{134,1... | collective-permute-start | bytes 1572872 | tf_op jit(solution)/shard_map/ppermute | solution.py:29
  159.2 13.9 %collective-permute-start.7 = (bf16[256,1024]{1,0:T(8,128)(2,1)}, bf16[256,1024]{1,0:T(8,128)(2,1)}, u32[]{:S(2)}, u32[]{:S(2)}) collective-permute-start(bf16[256,1024]{1,0:T(8,128)(2,1)} %get-tuple-element.79), channel_id=1, source_target_pairs={{128,224},{129,225},{130,226},{131,227},{132,228},{133,229},{134,2... | collective-permute-start | bytes 1572872 | tf_op jit(solution)/shard_map/ppermute | solution.py:29
  165.8 157.0 %collective-permute-start.13 = (bf16[4,1024,256]{2,1,0:T(8,128)(2,1)}, bf16[4,1024,256]{2,1,0:T(8,128)(2,1)}, u32[]{:S(2)}, u32[]{:S(2)}) collective-permute-start(bf16[4,1024,256]{2,1,0:T(8,128)(2,1)} %pad_maximum_fusion.1.w0), channel_id=1, source_target_pairs={{0,8},{1,9},{2,10},{3,11},{4,12},{5,13},{6,14},{7,15},{8,16},{9,17... | collective-permute-start | bytes 6291464 | tf_op jit(solution)/shard_map/ppermute | solution.py:29
  171.2 153.2 %collective-permute-start.21 = (bf16[4,256,1280]{2,1,0:T(8,128)(2,1)}, bf16[4,256,1280]{2,1,0:T(8,128)(2,1)}, u32[]{:S(2)}, u32[]{:S(2)}) collective-permute-start(bf16[4,256,1280]{2,1,0:T(8,128)(2,1)} %pad_maximum_fusion.weights.w0), channel_id=1, source_target_pairs={{0,96},{1,97},{2,98},{3,99},{4,100},{5,101},{6,102},{7,103},{8,104... | collective-permute-start | bytes 7864328 | tf_op jit(solution)/shard_map/ppermute | solution.py:29
  173.2 151.3 %collective-permute-start.20 = (bf16[4,256,1280]{2,1,0:T(8,128)(2,1)}, bf16[4,256,1280]{2,1,0:T(8,128)(2,1)}, u32[]{:S(2)}, u32[]{:S(2)}) collective-permute-start(bf16[4,256,1280]{2,1,0:T(8,128)(2,1)} %pad_maximum_fusion.weights.w0), channel_id=1, source_target_pairs={{0,64},{1,65},{2,66},{3,67},{4,68},{5,69},{6,70},{7,71},{8,72},{9,... | collective-permute-start | bytes 7864328 | tf_op jit(solution)/shard_map/ppermute | solution.py:29
  175.9 148.6 %collective-permute-start.19 = (bf16[4,256,1280]{2,1,0:T(8,128)(2,1)}, bf16[4,256,1280]{2,1,0:T(8,128)(2,1)}, u32[]{:S(2)}, u32[]{:S(2)}) collective-permute-start(bf16[4,256,1280]{2,1,0:T(8,128)(2,1)} %pad_maximum_fusion.weights.w0), channel_id=1, source_target_pairs={{0,32},{1,33},{2,34},{3,35},{4,36},{5,37},{6,38},{7,39},{8,40},{9,... | collective-permute-start | bytes 7864328 | tf_op jit(solution)/shard_map/ppermute | solution.py:29
  185.6 113.2 %all-to-all-start = ((bf16[16,80,128]{2,1,0:T(8,128)(2,1)}), bf16[16,80,128]{2,1,0:T(8,128)(2,1)}, u32[]{:S(2)}, u32[]{:S(2)}) async-start(bf16[16,80,128]{2,1,0:T(8,128)(2,1)} %copy-done.29), calls=%async_computation | async-start | bytes 655360 | tf_op jit(solution)/shard_map/all_to_all | solution.py:332
  301.0 14.7 %all-to-all-start.1 = ((bf16[16,64,128]{2,1,0:T(8,128)(2,1)}), bf16[16,64,128]{2,1,0:T(8,128)(2,1)}, u32[]{:S(2)}, u32[]{:S(2)}) async-start(bf16[16,64,128]{2,1,0:T(8,128)(2,1)} %copy-done.11), calls=%async_computation.1 | async-start | bytes 524288 | tf_op jit(solution)/shard_map/all_to_all | solution.py:334
  335.2 19.8 %collective-permute-start.27 = (bf16[256,512]{1,0:T(8,128)(2,1)S(1)}, bf16[256,512]{1,0:T(8,128)(2,1)S(1)}, u32[]{:S(2)}, u32[]{:S(2)}) collective-permute-start(bf16[256,512]{1,0:T(8,128)(2,1)S(1)} %shard_map.98), channel_id=1, source_target_pairs={{128,0},{129,1},{130,96},{131,97},{132,64},{133,65},{134,32},{135,... | collective-permute-start | bytes 786440 | tf_op jit(solution)/shard_map/ppermute | solution.py:29
  355.0 18.8 %collective-permute-start.30 = (bf16[256,512]{1,0:T(8,128)(2,1)S(1)}, bf16[256,512]{1,0:T(8,128)(2,1)S(1)}, u32[]{:S(2)}, u32[]{:S(2)}) collective-permute-start(bf16[256,512]{1,0:T(8,128)(2,1)S(1)} %collective-permute-done.27.p0.upstream), channel_id=1, source_target_pairs={{0,6},{1,7},{2,4},{3,5},{4,2},{5,3},{6,0},{7,1},{8,14},{9,15},{10,... | collective-permute-start | bytes 786440 | tf_op jit(solution)/shard_map/ppermute | solution.py:29
  356.9 21.0 %collective-permute-start.29 = (bf16[256,512]{1,0:T(8,128)(2,1)S(1)}, bf16[256,512]{1,0:T(8,128)(2,1)S(1)}, u32[]{:S(2)}, u32[]{:S(2)}) collective-permute-start(bf16[256,512]{1,0:T(8,128)(2,1)S(1)} %collective-permute-done.27.p0.upstream), channel_id=1, source_target_pairs={{0,4},{1,5},{2,6},{3,7},{4,0},{5,1},{6,2},{7,3},{8,12},{9,13},{10,... | collective-permute-start | bytes 786440 | tf_op jit(solution)/shard_map/ppermute | solution.py:29
  358.9 19.0 %collective-permute-start.28 = (bf16[256,512]{1,0:T(8,128)(2,1)S(1)}, bf16[256,512]{1,0:T(8,128)(2,1)S(1)}, u32[]{:S(2)}, u32[]{:S(2)}) collective-permute-start(bf16[256,512]{1,0:T(8,128)(2,1)S(1)} %collective-permute-done.27.p0.upstream), channel_id=1, source_target_pairs={{0,2},{1,3},{2,0},{3,1},{4,6},{5,7},{6,4},{7,5},{8,10},{9,11},{10,... | collective-permute-start | bytes 786440 | tf_op jit(solution)/shard_map/ppermute | solution.py:29
  378.0 4.6 collective-permute-start.31
  416.0 13.9 %all-to-all-start.3 = ((bf16[16,64,128]{2,1,0:T(8,128)(2,1)}), bf16[16,64,128]{2,1,0:T(8,128)(2,1)}, u32[]{:S(2)}, u32[]{:S(2)}) async-start(bf16[16,64,128]{2,1,0:T(8,128)(2,1)} %copy-done.10), calls=%async_computation.3 | async-start | bytes 524288 | tf_op jit(solution)/shard_map/all_to_all | solution.py:334
  447.1 4.7 collective-permute-start.32
  453.3 12.5 %collective-permute-start.33 = (bf16[256,512]{1,0:T(8,128)(2,1)}, bf16[256,512]{1,0:T(8,128)(2,1)S(1)}, u32[]{:S(2)}, u32[]{:S(2)}) collective-permute-start(bf16[256,512]{1,0:T(8,128)(2,1)} %get-tuple-element.72), channel_id=1, source_target_pairs={{0,2},{1,3},{2,0},{3,1},{4,6},{5,7},{6,4},{7,5},{8,10},{9,11},{10,... | collective-permute-start | bytes 786440 | tf_op jit(solution)/shard_map/ppermute | solution.py:29
  456.2 21.8 %collective-permute-start.34 = (bf16[256,512]{1,0:T(8,128)(2,1)}, bf16[256,512]{1,0:T(8,128)(2,1)S(1)}, u32[]{:S(2)}, u32[]{:S(2)}) collective-permute-start(bf16[256,512]{1,0:T(8,128)(2,1)} %get-tuple-element.73), channel_id=1, source_target_pairs={{0,4},{1,5},{2,6},{3,7},{4,0},{5,1},{6,2},{7,3},{8,12},{9,13},{10,... | collective-permute-start | bytes 786440 | tf_op jit(solution)/shard_map/ppermute | solution.py:29
  459.8 24.0 %collective-permute-start.35 = (bf16[256,512]{1,0:T(8,128)(2,1)}, bf16[256,512]{1,0:T(8,128)(2,1)S(1)}, u32[]{:S(2)}, u32[]{:S(2)}) collective-permute-start(bf16[256,512]{1,0:T(8,128)(2,1)} %get-tuple-element.74), channel_id=1, source_target_pairs={{0,6},{1,7},{2,4},{3,5},{4,2},{5,3},{6,0},{7,1},{8,14},{9,15},{10,... | collective-permute-start | bytes 786440 | tf_op jit(solution)/shard_map/ppermute | solution.py:29
  462.6 22.0 %collective-permute-start.26 = (bf16[256,512]{1,0:T(8,128)(2,1)S(1)}, bf16[256,512]{1,0:T(8,128)(2,1)}, u32[]{:S(2)}, u32[]{:S(2)}) collective-permute-start(bf16[256,512]{1,0:T(8,128)(2,1)S(1)} %copy-done.34), channel_id=1, source_target_pairs={{128,128},{129,129},{130,224},{131,225},{132,192},{133,193},{134,1... | collective-permute-start | bytes 786440 | tf_op jit(solution)/shard_map/ppermute | solution.py:29
  (59 other events, 738.4 us)

commit v3 on v1

v3 whole, which is shorter than its diff:
```python
import jax
import jax.numpy as jnp
from jax import lax
from jax.experimental import pallas as pl
from jax.experimental.pallas import tpu as pltpu
from jax.sharding import PartitionSpec as P

SIDE = 4
CORES = 2
BOTH = (0, 1)
AXES = ("section", "ctx", "heads")
VMEM = 20 * 1024 * 1024
bf16, f32 = jnp.bfloat16, jnp.float32


def place(section, x, y, z, core):
    return (((section * SIDE + x) * SIDE + y) * SIDE + z) * CORES + core


def routed(value, move, sections):
    pairs = []
    for section in sections:
        for x in range(SIDE):
            for y in range(SIDE):
                for z in range(SIDE):
                    for core in range(CORES):
                        here = (section, x, y, z, core)
                        pairs.append((place(*here), place(*move(*here))))
    return lax.ppermute(value, AXES, pairs)


def first_half(value, axis):
    return lax.slice_in_dim(value, 0, value.shape[axis] // 2, axis=axis)


def second_half(value, axis):
    return lax.slice_in_dim(value, value.shape[axis] // 2, value.shape[axis], axis=axis)


def sides(value, along, sections):
    return [routed(value, along(k), sections) for k in (1, 3)]


def far(both, along, sections, axis):
    before, after = both
    return [
        routed(first_half(before, axis), along(1), sections),
        routed(second_half(after, axis), along(3), sections),
    ]


def along_x(k):
    return lambda s, x, y, z, c: (s, (x + k) % SIDE, y, z, c)


def along_y(k):
    return lambda s, x, y, z, c: (s, x, (y + k) % SIDE, z, c)


def across_z(k):
    return lambda s, x, y, z, c: (s, x, y, z ^ k, c)


def other_core(s, x, y, z, c):
    return (s, x, y, z, 1 - c)


def hop(to_section):
    return lambda s, x, y, z, c: (s if to_section is None else to_section, (x - z) % SIDE, y, x, c)


def first_step(k):
    return lambda s, x, y, z, c: (along_y if s == 1 else along_x)(k)(s, x, y, z, c)


def dot(left, right, left_dim, right_dim):
    return lax.dot_general(
        left, right, (((left_dim,), (right_dim,)), ((), ())), preferred_element_type=f32
    )


def call(body, outs, args, at, scratch=(), flops=0, remote=()):
    moved = sum(a.size * a.dtype.itemsize for a in (*args, *outs))
    vmem = pl.BlockSpec(memory_space=pltpu.VMEM)
    ins = [pl.BlockSpec(memory_space=pl.ANY) if i in remote else vmem for i in range(len(args))]
    return pl.pallas_call(
        body,
        in_specs=[pl.BlockSpec(memory_space=pltpu.SMEM)] + ins,
        out_specs=[vmem] * len(outs),
        out_shape=list(outs),
        scratch_shapes=list(scratch),
        compiler_params=pltpu.CompilerParams(vmem_limit_bytes=VMEM),
        cost_estimate=pl.CostEstimate(flops=flops, bytes_accessed=moved, transcendentals=0),
    )(at, *args)


def struct(shape, dtype=bf16):
    return jax.ShapeDtypeStruct(shape, dtype)


def behind(index, k):
    return lax.rem(index + SIDE - k, SIDE)


def span(index, size):
    return pl.ds(pl.multiple_of(index * size, size), size)


def tables_body(
    at, decay, bc_rows, x_rows, state,
    kernel, mixed, x_heads, x_trailing, entry, leading, trailing, totals, b_cols, c_cols, c_rows,
):
    count, length = decay.shape
    size = b_cols.shape[0]
    each = x_heads.shape[0] // count
    exact = lax.Precision.HIGHEST
    earlier = lax.broadcasted_iota(jnp.int32, (length, length), 0)
    later = lax.broadcasted_iota(jnp.int32, (length, length), 1)
    lower = earlier >= later
    inner = (((1,), (0,)), ((), ()))
    last = (((1,), (1,)), ((), ()))
    rates = decay[...]
    sums = lax.dot_general(
        rates, (earlier <= later).astype(f32), inner, precision=exact, preferred_element_type=f32
    )
    columns = lax.dot_general(
        lower.astype(f32), rates, last, precision=exact, preferred_element_type=f32
    )
    b_part, c_part = bc_rows[:, :size], bc_rows[:, size:]
    common = dot(c_part, b_part, 1, 1)
    b_cols[...] = b_part.astype(f32).T.astype(bf16)
    c_cols[...] = c_part.astype(f32).T.astype(bf16)
    c_rows[...] = c_part
    lead = jnp.exp(sums)
    trail = jnp.exp(sums[:, length - 1 :] - sums)
    leading[...] = lead
    trailing[...] = trail
    first = lax.broadcasted_iota(jnp.int32, totals.shape[1:], 0) == 0
    for head in range(count):
        spread = columns[:, head : head + 1] - sums[head : head + 1, :]
        weights = jnp.where(lower, jnp.exp(jnp.minimum(spread, 0.0)), 0.0)
        kernel[head] = weights.astype(bf16)
        mixed[head] = (weights * common).astype(bf16)
        total = jnp.broadcast_to(lead[head : head + 1, length - 1 :], totals.shape[1:])
        high = total.astype(bf16).astype(f32)
        totals[head] = jnp.where(first, high, total - high).astype(bf16)
    for pair in range(count // 2):
        both = slice(pair * 2 * each, (pair + 1) * 2 * each)
        x_pair = x_rows[:, both].astype(f32).T
        x_heads[both, :] = x_pair.astype(bf16)
        for i in range(2):
            head = 2 * pair + i
            own = slice(head * each, (head + 1) * each)
            x_trailing[own, :] = (
                x_pair[i * each : (i + 1) * each, :] * trail[head : head + 1, :]
            ).astype(bf16)
        flat = jnp.concatenate([state[2 * pair], state[2 * pair + 1]], axis=0)
        entry[:, both] = flat.T.astype(bf16)


def rows_body(at, own, mine, theirs, w0, w1, wl, wh, w3, o0, o1, o2, o3, piece, u):
    y, z, core = at[1], at[2], at[3]
    fine = w0.shape[1]
    rows = mine.shape[1]
    half = wl.shape[0]
    u[0] = own[...]
    for k in (1, 2, 3):
        u[k, span(core, rows), :] = mine[k - 1]
        u[k, span(1 - core, rows), :] = theirs[k - 1]
    piece[...] = u[z, :, span(core, piece.shape[0])].astype(f32).T.astype(bf16)
    for k, out in enumerate((o0, o1, o2, o3)):
        total = None
        for j, w in enumerate((w0, w1, None, w3)):
            columns = u[k, :, span(behind(y, j), fine)]
            if w is None:
                term = jnp.concatenate([dot(wl[...], columns, 1, 1), dot(wh[...], columns, 1, 1)], axis=0)
            else:
                term = dot(w[...], columns, 1, 1)
            total = term if total is None else total + term
        out[...] = total.astype(bf16)


def entering(grad, leading, c_rows, totals, states):
    count = totals.shape[0]
    each = grad.shape[0] // count
    wide = grad.astype(f32)
    scaled = [
        (wide[h * each : (h + 1) * each] * leading[h : h + 1, :]).astype(bf16) for h in range(count)
    ]
    summed = dot(jnp.concatenate(scaled, axis=0), c_rows[...], 1, 0).astype(bf16)
    for h in range(count):
        states[h, :each, :] = summed[h * each : (h + 1) * each]
        states[h, each:, :] = totals[h]


def sum_body(at, own, r1, r2, r3, leading, c_rows, totals, grad, states):
    total = own[...].astype(f32)
    for r in (r1, r2, r3):
        total = total + r[...].astype(f32)
    rounded = total.astype(bf16)
    grad[...] = rounded
    entering(rounded, leading, c_rows, totals, states)


def lower_body(
    at, p0, p1, p2, p3, other, w0, w1, wl, wh, w3, leading, c_rows, totals, grad, states, u
):
    x, y, z, core = at[0], at[1], at[2], at[3]
    share = p0.shape[0]
    fine = share * CORES // SIDE
    for q, part in enumerate((p0, p1, p2, p3)):
        base = (z ^ q) * CORES
        u[span(base + core, share), :] = part[...]
        u[span(base + 1 - core, share), :] = other[q]
    total = None
    for k in range(SIDE):
        for j in range(SIDE):
            w = (w0, w1, wl if j < CORES else wh, w3)[k][j % CORES if k == 2 else j]
            rows = u[span(behind(x, j) * SIDE + behind(y, k), fine), :]
            term = dot(w, rows, 1, 0)
            total = term if total is None else total + term
    rounded = total.astype(bf16)
    grad[...] = rounded
    entering(rounded, leading, c_rows, totals, states)


def scan_body(at, states, exits):
    count, size, _ = exits.shape
    held = jnp.zeros(exits.shape[1:], f32)
    for k in range(count - 1, -1, -1):
        exits[k] = held.astype(bf16)
        total = states[k, size : size + 16, :].astype(f32)
        held = (total[0:1] + total[1:2]) * held + states[k, :size, :].astype(f32)


def block_body(
    at, grad, kernel, mixed, x_heads, x_trailing, leading, trailing, gain, entry, b_cols, c_cols, leaving,
    out, own_kernel, own_mixed, own_x, own_trailing, sems,
):
    copies = [
        pltpu.make_async_copy(source, target, sems.at[i])
        for i, (source, target) in enumerate(
            ((x_heads, own_x), (kernel, own_kernel), (mixed, own_mixed), (x_trailing, own_trailing))
        )
    ]
    for copy in copies:
        copy.start()
    count = leading.shape[0]
    inner = grad.shape[0]
    each = inner // count
    size = b_cols.shape[0]
    scaled = []
    for h in range(count):
        own = slice(h * each, (h + 1) * each)
        scaled.append((grad[own, :].astype(f32) * leading[h : h + 1, :]).astype(bf16))
    grad_c = dot(entry[...], jnp.concatenate(scaled, axis=0), 1, 0)
    gained = dot(leaving[...], b_cols[...], 1, 0)
    for copy in copies:
        copy.wait()
    weighted = None
    for h in range(count):
        own = slice(h * each, (h + 1) * each)
        g = grad[own, :]
        term = own_kernel[h].astype(f32) * dot(g, own_x[own, :], 0, 0)
        weighted = term if weighted is None else weighted + term
        inside = dot(g, own_mixed[h], 1, 0) + gain[h : h + 1, :] * g.astype(f32)
        out[own, :] = (inside + trailing[h : h + 1, :] * gained[own, :]).astype(bf16)
    rounded = weighted.astype(bf16)
    grad_b = dot(c_cols[...], rounded, 1, 0) + dot(leaving[...], own_trailing[...], 0, 0)
    out[inner : inner + size, :] = grad_b.astype(bf16)
    out[inner + size :, :] = (grad_c + dot(b_cols[...], rounded, 1, 1)).astype(bf16)


def to_halves(u, q, core, keep, give):
    share = keep.shape[1]
    keep[q] = u[span(core, share), :]
    give[q] = u[span(1 - core, share), :]


def back_body(at, g0, g1, gl, gh, g3, w0, w1, wl, wh, w3, keep, give, u, g2):
    y, z, core = at[1], at[2], at[3]
    fine, half = w0.shape[0], wl.shape[0]
    g2[: gl.shape[0], :] = gl[...]
    g2[gl.shape[0] :, :] = gh[...]
    for k, g in enumerate((g0, g1, g2, g3)):
        for j, w in enumerate((w0, w1, None, w3)):
            rows = span(behind(y, j), fine)
            if w is None:
                term = jnp.concatenate([dot(wl[...], g[...], 1, 0), dot(wh[...], g[...], 1, 0)], axis=0)
            else:
                term = dot(w[...], g[...], 1, 0)
            u[k, rows, :] = term.astype(bf16)
        to_halves(u.at[k], z ^ k, core, keep, give)


def whole_body(at, g, w0, w1, wl, wh, w3, keep, give, u):
    x, y, z, core = at[0], at[1], at[2], at[3]
    fine = w0.shape[1]
    for k in range(SIDE):
        for j in range(SIDE):
            w = (w0, w1, wl if j < CORES else wh, w3)[k][j % CORES if k == 2 else j]
            u[k, span(behind(y, j), fine), :] = dot(w, g[...], 1, 0).astype(bf16)
        to_halves(u.at[k], z ^ behind(x, k), core, keep, give)


def pair_body(at, keep, got, s1, s2, s3):
    for q, out in ((1, s1), (2, s2), (3, s3)):
        out[...] = (keep[q].astype(f32) + got[q].astype(f32)).astype(bf16)


def total_of(keep, got, received, upstream):
    total = keep[0].astype(f32) + got[0].astype(f32)
    for r in received:
        total = total + r[...].astype(f32)
    return total + upstream[...].astype(f32)


def total_body(at, keep, got, r1, r2, r3, upstream, out):
    out[...] = total_of(keep, got, (r1, r2, r3), upstream).astype(bf16)


def result_body(at, keep, got, r1, r2, r3, upstream, settled, out):
    total = total_of(keep, got, (r1, r2, r3), upstream).astype(bf16).astype(f32)
    chosen = jnp.where(at[4] == 1, settled[...].astype(f32), total)
    out[0] = chosen.T.astype(bf16)


def local(grad_out, w_out, w_in, w_bc, x_act, bc_act, decay, skip_gain, state_in):
    tie = lax.optimization_barrier
    section = lax.axis_index("section")
    ctx = lax.axis_index("ctx")
    heads_at = lax.axis_index("heads")
    x, y = ctx // SIDE, ctx % SIDE
    z, core = heads_at // CORES, heads_at % CORES
    at = jnp.stack([x, y, z, core, section]).astype(jnp.int32)
    rows, width = grad_out.shape
    block = width // SIDE
    share = block // CORES
    half = rows // CORES
    head_count, head_size, state_size = state_in.shape[2:]
    inner = head_count * head_size
    outer = inner + 2 * state_size
    pad = 16
    steps = (1, 2, 3)

    upstream = lax.dynamic_slice_in_dim(grad_out, block * x, block, 1)
    mine = []
    for k in steps:
        piece = lax.dynamic_slice(grad_out, (half * core, block * ((x + k) % SIDE)), (half, block))
        mine.append(routed(piece, along_x(k), (1,)))
    mine = jnp.stack(mine)
    theirs = routed(mine, other_core, (1,))

    out_sides = sides(w_out[0], first_step, BOTH)
    out_far = far(out_sides, first_step, BOTH, 0)
    back = jnp.concatenate([w_in[0], w_bc[0]], axis=1)

    (
        kernel, mixed, x_heads, x_trailing, entry, leading, trailing, totals, b_cols, c_cols, c_rows
    ) = call(
        tables_body,
        [
            struct((head_count, rows, rows)), struct((head_count, rows, rows)),
            struct((inner, rows)), struct((inner, rows)), struct((state_size, inner)),
            struct((head_count, rows), f32), struct((head_count, rows), f32),
            struct((head_count, pad, state_size)), struct((state_size, rows)),
            struct((state_size, rows)), struct((rows, state_size)),
        ],
        [decay[0], bc_act[0], x_act[0], state_in[0, 0]],
        at,
        flops=2 * rows * rows * inner,
    )
    gain = jnp.broadcast_to(skip_gain[0][:, None], (head_count, rows))
    out_sides, out_far, back, leading, gain = tie((out_sides, out_far, back, leading, gain))

    state_shape = struct((head_count, head_size + pad, state_size))

    def exchange(states):
        return lax.all_to_all(states, "ctx", 0, 0)

    def scanned(arrived):
        (exits,) = call(scan_body, [struct((head_count, head_size, state_size))], [arrived], at)
        return exits

    def within(grad_ssd, leaving):
        (grads,) = call(
            block_body,
            [struct((outer, rows))],
            [
                grad_ssd, kernel, mixed, x_heads, x_trailing, leading, trailing, gain, entry, b_cols, c_cols,
                leaving.reshape(inner, state_size),
            ],
            at,
            scratch=[
                pltpu.VMEM(kernel.shape, bf16), pltpu.VMEM(mixed.shape, bf16),
                pltpu.VMEM(x_heads.shape, bf16), pltpu.VMEM(x_trailing.shape, bf16),
                pltpu.SemaphoreType.DMA((4,)),
            ],
            flops=4 * rows * rows * inner,
            remote=(1, 2, 3, 4),
        )
        return grads

    chunk = struct((share, rows))
    chunks = struct((SIDE, share, rows))

    def over_heads(keep, give, sections):
        got = routed(give, other_core, sections)
        sent = call(pair_body, [chunk] * 3, [keep, got], at)
        return [keep, got] + [routed(s, across_z(k), sections) for k, s in zip(steps, sent)]

    *partial, own = call(
        rows_body,
        [struct((inner, rows))] * SIDE + [chunk],
        [upstream, mine, theirs, w_out[0], out_sides[0], *out_far, out_sides[1]],
        at,
        scratch=[pltpu.VMEM((SIDE, rows, block), bf16)],
        flops=2 * SIDE * rows * block * inner,
    )
    partial, back, out_sides, out_far = tie((partial, back, out_sides, out_far))
    received = [routed(partial[k], along_x(-k), (1,)) for k in steps]
    back_sides = sides(back, along_y, BOTH)
    out_set = jnp.stack([w_out[0], out_sides[0], jnp.concatenate(out_far, 0), out_sides[1]])
    received, back_sides, out_set = tie((received, back_sides, out_set))
    grad_ssd, states = call(
        sum_body,
        [struct((inner, rows)), state_shape],
        [partial[0], *received, leading, c_rows, totals],
        at,
        flops=2 * rows * inner * state_size,
    )

    states, back_sides, out_set = tie((states, back_sides, out_set))
    arrived = exchange(states)
    back_far = far(back_sides, along_y, BOTH, 0)
    whole_sides = sides(out_set, along_y, (0,))
    arrived, back_far, whole_sides = tie((arrived, back_far, whole_sides))
    exits = scanned(arrived)
    back_set = jnp.stack([back, back_sides[0], jnp.concatenate(back_far, 0), back_sides[1]])
    exits, back_set, whole_sides = tie((exits, back_set, whole_sides))
    leaving = exchange(exits)
    whole_far = far(whole_sides, along_y, (0,), 0)
    width_sides = sides(back_set, along_x, (0,))
    leaving, whole_far, width_sides = tie((leaving, whole_far, width_sides))
    grads = within(grad_ssd, leaving)

    grads_sides = sides(grads, along_x, (1,))
    grads_far = far(grads_sides, along_x, (1,), 0)
    wide = [pltpu.VMEM((SIDE, block, rows), bf16)]
    keep, give = call(
        back_body,
        [chunks, chunks],
        [
            grads, grads_sides[0], *grads_far, grads_sides[1],
            back, back_sides[0], *back_far, back_sides[1],
        ],
        at,
        scratch=wide + [pltpu.VMEM((outer, rows), bf16)],
        flops=2 * SIDE * rows * block * outer,
    )
    sums = over_heads(keep, give, (1,))
    (middle,) = call(total_body, [chunk], [*sums, own], at)

    arrived = routed(middle, hop(0), (1,))
    settled = routed(middle, hop(None), (1,))

    arrived, width_sides = tie((arrived, width_sides))
    width_far = far(width_sides, along_x, (0,), 0)
    parts = [arrived] + [routed(arrived, across_z(k), (0,)) for k in steps]
    other = routed(jnp.stack(parts), other_core, (0,))
    grad_ssd, states = call(
        lower_body,
        [struct((inner, rows)), state_shape],
        [*parts, other, out_set, whole_sides[0], *whole_far, whole_sides[1], leading, c_rows, totals],
        at,
        scratch=[pltpu.VMEM((width, rows), bf16)],
        flops=2 * rows * width * inner,
    )
    held, width_far, settled = tie((exchange(states), width_far, settled))
    grads = within(grad_ssd, exchange(scanned(held)))
    keep, give = call(
        whole_body,
        [chunks, chunks],
        [grads, back_set, width_sides[0], *width_far, width_sides[1]],
        at,
        scratch=wide,
        flops=2 * rows * width * outer,
    )
    sums = over_heads(keep, give, (0,))
    (result,) = call(result_body, [struct((1, rows, share))], [*sums, arrived, settled], at)
    return result


def solution(mesh):
    placed = (
        P("ctx", None),
        P("section", "heads", "ctx"),
        P("section", "ctx", "heads"),
        P("section", "ctx", "heads"),
        P("section", "ctx", "heads"),
        P("section", "ctx", "heads"),
        P("section", "heads", "ctx"),
        P("section", "heads"),
        P("section", "ctx", "heads", None, None),
    )
    return jax.shard_map(
        local, mesh=mesh, in_specs=placed, out_specs=P("section", "ctx", "heads"), check_vma=False
    )
```

time: 463 us -> 349 us (0.75)
  waiting for transfers between devices: 239 us -> 93 us
  blocking collectives: 0 us -> 118 us
  matrix products: 52.3 us -> 0 us
  Pallas kernels: 0 us -> 29.2 us
  starting transfers between devices: 109 us -> 87.6 us
  other arithmetic: 23.7 us -> 2.36 us
  local copies, waits for them, and re-layouts: 36.5 us -> 17.2 us
    all_to_all x0 -> x3, blocking collectives: none -> 118 us  [exchange(): return lax.all_to_all(states, 'ctx', 0, 0)]
    ppermute x36 -> x41, waiting for transfers between devices: 183 us -> 92.6 us  [routed(): return lax.ppermute(value, AXES, pairs)]
    all_to_all x5 -> x1, waiting for transfers between devices: 55.8 us -> 0.38 us  [exchange(): return lax.all_to_all(states, 'ctx', 0, 0)]
    dot_general x29 -> x0, matrix products: 52.3 us -> none  [the longest x23 42.6 us: dot(): lax.dot_general(left, right, (((left_dim,), (right_dim,)), ((), ())), pre...]
    pallas_call x0 -> x14, Pallas kernels: none -> 29.2 us  [call(): pl.pallas_call(body, in_specs=[pl.BlockSpec(memory_space=pltpu.SMEM)] + i...]
    all_to_all x5 -> x1, starting transfers between devices: 32 us -> 4.65 us  [exchange(): return lax.all_to_all(states, 'ctx', 0, 0)]
    dynamic_update_slice x11 -> x0, local copies, waits for them, and re-layouts: 13.7 us -> none  [the longest x4 7.68 us: local(): lax.dynamic_update_slice(out_block, part, (0, fine * ((out_at - k) % SIDE)))]
    convert_element_type x5 -> x0, other arithmetic: 11 us -> none  [the longest x2 5.75 us: over_heads(): pair = pair.astype(bf16)]
  transfers between devices with their start and end apart: 41 -> 42, of which waited for: 13 -> 14; matrix products, arithmetic and copies ran while one was open for 19% -> 2% of each run, Pallas kernels for 0% -> 2%
where the time goes in v3:
time: 349 us; the launch traced here: 348 us
  blocking collectives  118 us (34%)
  waiting for transfers between devices  93 us (27%)
  starting transfers between devices  87.6 us (25%)
  Pallas kernels  29.2 us (8%)
  local copies, waits for them, and re-layouts  17.2 us (5%)
    all_to_all x3, blocking collectives, exchange(): return lax.all_to_all(states, 'ctx', 0, 0)  118 us
    ppermute x41, waiting for transfers between devices, routed(): return lax.ppermute(value, AXES, pairs)  92.6 us
    ppermute x41, starting transfers between devices, routed(): return lax.ppermute(value, AXES, pairs)  83 us
    pallas_call x14, Pallas kernels, call(): pl.pallas_call(body, in_specs=[pl.BlockSpec(memory_space=pltpu.SMEM)] + i...  29.2 us
    unnamed x66, local copies, waits for them, and re-layouts  12.2 us
  transfers between devices with their start and end apart: 42, of which 14 were waited for; matrix products, arithmetic and copies ran while one was open for 2% of the time, Pallas kernels for 2%

profile of v3, /device:TPU:32, one launch (start us, length us, event | category | flops | bytes accessed | tf_op | source)
XLA Modules:
  0.0 347.9 jit_solution(16980978343181891196)
XLA Ops:
  3.4 2.8 collective-permute-start.5
  9.2 8.6 %collective-permute-done.5.w3 = bf16[1024,256]{1,0:T(8,128)(2,1)S(1)} collective-permute-done((bf16[1024,256]{1,0:T(8,128)(2,1)}, bf16[1024,256]{1,0:T(8,128)(2,1)S(1)}, u32[]{:S(2)}, u32[]{:S(2)}) %collective-permute-start.5) | collective-permute-done | bytes 524320 | tf_op jit(solution)/shard_map/ppermute | solution.py:29
  17.7 3.7 %collective-permute-start.7 = (bf16[512,256]{1,0:T(8,128)(2,1)S(1)}, bf16[512,256]{1,0:T(8,128)(2,1)S(1)}, u32[]{:S(2)}, u32[]{:S(2)}) collective-permute-start(bf16[512,256]{1,0:T(8,128)(2,1)S(1)} %slice.41), channel_id=1, source_target_pairs={{0,96},{1,97},{2,98},{3,99},{4,100},{5,101},{6,102},{7,103},{8,104... | collective-permute-start | bytes 786440 | tf_op jit(solution)/shard_map/ppermute | solution.py:29
  26.3 3.3 collective-permute-done.6.wl
  29.7 3.7 %shard_map.92 = (bf16[1024,256]{1,0:T(8,128)(2,1)S(1)}, bf16[1024,256]{1,0:T(8,128)(2,1)S(1)}, bf16[1024,256]{1,0:T(8,128)(2,1)S(1)}, bf16[1024,256]{1,0:T(8,128)(2,1)S(1)}, bf16[512,256]{1,0:T(8,128)(2,1)S(1)}) custom-call(s32[5]{0:T(128)S(1)} %stack.77.at, bf16[256,1024]{1,0:T(8,128)(2,1)S(1)} %constant_dynamic-slice_fusion.own, ...), custom_call_target="tpu_custom_call" | custom-call | flops 2147483648 | bytes 6553600 | tf_op jit(solution)/shard_map/pallas_call | solution.py:86
  33.4 3.1 collective-permute-start.12
  38.9 9.5 %collective-permute-done.12.w3 = bf16[256,1280]{1,0:T(8,128)(2,1)S(1)} collective-permute-done((bf16[256,1280]{1,0:T(8,128)(2,1)S(1)}, bf16[256,1280]{1,0:T(8,128)(2,1)S(1)}, u32[]{:S(2)}, u32[]{:S(2)}) %collective-permute-start.12) | collective-permute-done | bytes 655392 | tf_op jit(solution)/shard_map/ppermute | solution.py:29
  48.4 3.4 collective-permute-done.11.w1
  55.0 3.7 %collective-permute-start.15 = (bf16[4,1024,256]{2,1,0:T(8,128)(2,1)S(1)}, bf16[4,1024,256]{2,1,0:T(8,128)(2,1)S(1)}, u32[]{:S(2)}, u32[]{:S(2)}) collective-permute-start(bf16[4,1024,256]{2,1,0:T(8,128)(2,1)S(1)} %pad_maximum_fusion.1.w0), channel_id=1, source_target_pairs={{0,8},{1,9},{2,10},{3,11},{4,12},{5,13},{6,14},{7,15},{8,16},{9,17... | collective-permute-start | bytes 6291464 | tf_op jit(solution)/shard_map/ppermute | solution.py:29
  60.9 51.9 %all_to_all.20.states = bf16[16,80,128]{2,1,0:T(8,128)(2,1)S(1)} all-to-all(bf16[16,80,128]{2,1,0:T(8,128)(2,1)S(1)} %get-tuple-element.121), channel_id=1, replica_groups=mesh['section'=2,'ctx'=16,'heads'=8] {'ctx'}, dimensions={0} | all-to-all | bytes 655360 | tf_op jit(solution)/shard_map/all_to_all | solution.py:379
  113.8 3.2 collective-permute-start.20
  121.7 3.9 %collective-permute-start.17 = (bf16[2,1024,256]{2,1,0:T(8,128)(2,1)S(1)}, bf16[2,1024,256]{2,1,0:T(8,128)(2,1)S(1)}, u32[]{:S(2)}, u32[]{:S(2)}) collective-permute-start(bf16[2,1024,256]{2,1,0:T(8,128)(2,1)S(1)} %slice.34), channel_id=1, source_target_pairs={{0,8},{1,9},{2,10},{3,11},{4,12},{5,13},{6,14},{7,15},{8,16},{9,17... | collective-permute-start | bytes 3145736 | tf_op jit(solution)/shard_map/ppermute | solution.py:29
  125.7 52.6 %all_to_all.21 = bf16[16,64,128]{2,1,0:T(8,128)(2,1)S(1)} all-to-all(bf16[16,64,128]{2,1,0:T(8,128)(2,1)S(1)} %shard_map.94), channel_id=1, replica_groups=mesh['section'=2,'ctx'=16,'heads'=8] {'ctx'}, dimensions={0} | all-to-all | bytes 524288 | tf_op jit(solution)/shard_map/all_to_all | solution.py:379
  178.3 2.8 shard_map.95.g0
  184.0 3.5 %shard_map.96 = (bf16[4,512,256]{2,1,0:T(8,128)(2,1)S(1)}, bf16[4,512,256]{2,1,0:T(8,128)(2,1)S(1)}) custom-call(s32[5]{0:T(128)S(1)} %stack.77.at, bf16[1280,256]{1,0:T(8,128)(2,1)S(1)} %shard_map.95.g0, bf16[1280,256]{1,0:T(8,128)(2,1)S(1)} %collective-permute-done.21.g1, bf16[640,256]{1,0:T(8,128)(2,1)S(1)} %collective-permute-done.22.gl, ...), custom_call_target="tpu_custom_call" | custom-call | flops 2684354560 | bytes 7340032 | tf_op jit(solution)/shard_map/pallas_call | solution.py:86
  193.2 11.8 %collective-permute-done.29.p0.upstream = bf16[512,256]{1,0:T(8,128)(2,1)S(1)} collective-permute-done((bf16[512,256]{1,0:T(8,128)(2,1)S(1)}, bf16[512,256]{1,0:T(8,128)(2,1)S(1)}, u32[]{:S(2)}, u32[]{:S(2)}) %collective-permute-start.29) | collective-permute-done | bytes 262176 | tf_op jit(solution)/shard_map/ppermute | solution.py:29
  205.1 5.4 %collective-permute-start.32 = (bf16[512,256]{1,0:T(8,128)(2,1)S(1)}, bf16[512,256]{1,0:T(8,128)(2,1)S(1)}, u32[]{:S(2)}, u32[]{:S(2)}) collective-permute-start(bf16[512,256]{1,0:T(8,128)(2,1)S(1)} %collective-permute-done.29.p0.upstream), channel_id=1, source_target_pairs={{0,6},{1,7},{2,4},{3,5},{4,2},{5,3},{6,0},{7,1},{8,14},{9,15},{10,... | collective-permute-start | bytes 786440 | tf_op jit(solution)/shard_map/ppermute | solution.py:29
  210.4 3.1 collective-permute-start.31
  213.5 3.4 collective-permute-start.30
  216.9 6.3 %collective-permute-done.32.p3 = bf16[512,256]{1,0:T(8,128)(2,1)S(1)} collective-permute-done((bf16[512,256]{1,0:T(8,128)(2,1)S(1)}, bf16[512,256]{1,0:T(8,128)(2,1)S(1)}, u32[]{:S(2)}, u32[]{:S(2)}) %collective-permute-start.32) | collective-permute-done | bytes 262176 | tf_op jit(solution)/shard_map/ppermute | solution.py:29
  229.7 13.4 %collective-permute-start.35 = (bf16[2,256,1280]{2,1,0:T(8,128)(2,1)}, bf16[2,256,1280]{2,1,0:T(8,128)(2,1)}, u32[]{:S(2)}, u32[]{:S(2)}) collective-permute-start(bf16[2,256,1280]{2,1,0:T(8,128)(2,1)} %slice.39), channel_id=1, source_target_pairs={{0,96},{1,97},{2,98},{3,99},{4,100},{5,101},{6,102},{7,103},{8,104... | collective-permute-start | bytes 3932168 | tf_op jit(solution)/shard_map/ppermute | solution.py:29
  245.1 3.3 shard_map.99
  249.9 4.6 %all-to-all-start.2 = ((bf16[16,80,128]{2,1,0:T(8,128)(2,1)}), bf16[16,80,128]{2,1,0:T(8,128)(2,1)}, u32[]{:S(2)}, u32[]{:S(2)}) async-start(bf16[16,80,128]{2,1,0:T(8,128)(2,1)} %copy-done.17), calls=%async_computation.2 | async-start | bytes 655360 | tf_op jit(solution)/shard_map/all_to_all | solution.py:379
  256.0 18.3 %collective-permute-done.35.wh = bf16[2,256,1280]{2,1,0:T(8,128)(2,1)} collective-permute-done((bf16[2,256,1280]{2,1,0:T(8,128)(2,1)}, bf16[2,256,1280]{2,1,0:T(8,128)(2,1)}, u32[]{:S(2)}, u32[]{:S(2)}) %collective-permute-start.35) | collective-permute-done | bytes 1310752 | tf_op jit(solution)/shard_map/ppermute | solution.py:29
  274.3 5.6 %collective-permute-done.34.wl = bf16[2,256,1280]{2,1,0:T(8,128)(2,1)} collective-permute-done((bf16[2,256,1280]{2,1,0:T(8,128)(2,1)}, bf16[2,256,1280]{2,1,0:T(8,128)(2,1)}, u32[]{:S(2)}, u32[]{:S(2)}) %collective-permute-start.34) | collective-permute-done | bytes 1310752 | tf_op jit(solution)/shard_map/ppermute | solution.py:29
  281.9 13.0 %all_to_all.22 = bf16[16,64,128]{2,1,0:T(8,128)(2,1)S(1)} all-to-all(bf16[16,64,128]{2,1,0:T(8,128)(2,1)S(1)} %shard_map.100), channel_id=1, replica_groups=mesh['section'=2,'ctx'=16,'heads'=8] {'ctx'}, dimensions={0} | all-to-all | bytes 524288 | tf_op jit(solution)/shard_map/all_to_all | solution.py:379
  303.2 2.7 shard_map.101.g
  306.0 4.7 %shard_map.102 = (bf16[4,512,256]{2,1,0:T(8,128)(2,1)S(1)}, bf16[4,512,256]{2,1,0:T(8,128)(2,1)S(1)}) custom-call(s32[5]{0:T(128)S(1)} %copy-done.27, bf16[1280,256]{1,0:T(8,128)(2,1)S(1)} %shard_map.101.g, bf16[4,256,1280]{2,1,0:T(8,128)(2,1)S(1)} %pad_maximum_fusion.w0, bf16[4,256,1280]{2,1,0:T(8,128)(2,1)S(1)} %copy-done.7, ...), custom_call_target="tpu_custom_call" | custom-call | flops 2684354560 | bytes 13238272 | tf_op jit(solution)/shard_map/pallas_call | solution.py:86
  318.7 3.6 %collective-permute-start.39 = (bf16[512,256]{1,0:T(8,128)(2,1)S(1)}, bf16[512,256]{1,0:T(8,128)(2,1)S(1)}, u32[]{:S(2)}, u32[]{:S(2)}) collective-permute-start(bf16[512,256]{1,0:T(8,128)(2,1)S(1)} %get-tuple-element.156), channel_id=1, source_target_pairs={{0,4},{1,5},{2,6},{3,7},{4,0},{5,1},{6,2},{7,3},{8,12},{9,13},{10,... | collective-permute-start | bytes 786440 | tf_op jit(solution)/shard_map/ppermute | solution.py:29
  322.3 3.0 collective-permute-start.40
  327.8 12.5 %collective-permute-done.39.r2 = bf16[512,256]{1,0:T(8,128)(2,1)S(1)} collective-permute-done((bf16[512,256]{1,0:T(8,128)(2,1)S(1)}, bf16[512,256]{1,0:T(8,128)(2,1)S(1)}, u32[]{:S(2)}, u32[]{:S(2)}) %collective-permute-start.39) | collective-permute-done | bytes 262176 | tf_op jit(solution)/shard_map/ppermute | solution.py:29
  340.2 6.1 %collective-permute-done.40.r3 = bf16[512,256]{1,0:T(8,128)(2,1)S(1)} collective-permute-done((bf16[512,256]{1,0:T(8,128)(2,1)S(1)}, bf16[512,256]{1,0:T(8,128)(2,1)S(1)}, u32[]{:S(2)}, u32[]{:S(2)}) %collective-permute-start.40) | collective-permute-done | bytes 262176 | tf_op jit(solution)/shard_map/ppermute | solution.py:29
  (156 shorter events, 66.5 us)
Async XLA Ops:
  1.2 5.0 %collective-permute-start = (bf16[128,1024]{1,0:T(8,128)(2,1)S(1)}, bf16[128,1024]{1,0:T(8,128)(2,1)S(1)}, u32[]{:S(2)}, u32[]{:S(2)}) collective-permute-start(bf16[128,1024]{1,0:T(8,128)(2,1)S(1)} %get-tuple-element.159), channel_id=1, source_target_pairs={{128,160},{129,161},{130,162},{131,163},{132,164},{133,165},{134,1... | collective-permute-start | bytes 786440 | tf_op jit(solution)/shard_map/ppermute | solution.py:29
  2.0 4.2 %collective-permute-start.2 = (bf16[128,1024]{1,0:T(8,128)(2,1)S(1)}, bf16[128,1024]{1,0:T(8,128)(2,1)S(1)}, u32[]{:S(2)}, u32[]{:S(2)}) collective-permute-start(bf16[128,1024]{1,0:T(8,128)(2,1)S(1)} %get-tuple-element.160), channel_id=1, source_target_pairs={{128,224},{129,225},{130,226},{131,227},{132,228},{133,229},{134,2... | collective-permute-start | bytes 786440 | tf_op jit(solution)/shard_map/ppermute | solution.py:29
  2.7 3.5 %collective-permute-start.1 = (bf16[128,1024]{1,0:T(8,128)(2,1)S(1)}, bf16[128,1024]{1,0:T(8,128)(2,1)S(1)}, u32[]{:S(2)}, u32[]{:S(2)}) collective-permute-start(bf16[128,1024]{1,0:T(8,128)(2,1)S(1)} %get-tuple-element.161), channel_id=1, source_target_pairs={{128,192},{129,193},{130,194},{131,195},{132,196},{133,197},{134,1... | collective-permute-start | bytes 786440 | tf_op jit(solution)/shard_map/ppermute | solution.py:29
  3.4 14.3 %collective-permute-start.5 = (bf16[1024,256]{1,0:T(8,128)(2,1)}, bf16[1024,256]{1,0:T(8,128)(2,1)S(1)}, u32[]{:S(2)}, u32[]{:S(2)}) collective-permute-start(bf16[1024,256]{1,0:T(8,128)(2,1)} %bitcast.44), channel_id=1, source_target_pairs={{0,96},{1,97},{2,98},{3,99},{4,100},{5,101},{6,102},{7,103},{8,104... | collective-permute-start | bytes 1572872 | tf_op jit(solution)/shard_map/ppermute | solution.py:29
  6.2 15.2 %collective-permute-start.4 = (bf16[1024,256]{1,0:T(8,128)(2,1)}, bf16[1024,256]{1,0:T(8,128)(2,1)S(1)}, u32[]{:S(2)}, u32[]{:S(2)}) collective-permute-start(bf16[1024,256]{1,0:T(8,128)(2,1)} %bitcast.45), channel_id=1, source_target_pairs={{0,32},{1,33},{2,34},{3,35},{4,36},{5,37},{6,38},{7,39},{8,40},{9,... | collective-permute-start | bytes 1572872 | tf_op jit(solution)/shard_map/ppermute | solution.py:29
  6.4 23.3 %collective-permute-start.3 = (bf16[3,128,1024]{2,1,0:T(8,128)(2,1)S(1)}, bf16[3,128,1024]{2,1,0:T(8,128)(2,1)}, u32[]{:S(2)}, u32[]{:S(2)}) collective-permute-start(bf16[3,128,1024]{2,1,0:T(8,128)(2,1)S(1)} %pad_maximum_fusion.3.mine), channel_id=1, source_target_pairs={{128,129},{129,128},{130,131},{131,130},{132,133},{133,132},{134,1... | collective-permute-start | bytes 2359304 | tf_op jit(solution)/shard_map/ppermute | solution.py:29
  17.7 8.5 %collective-permute-start.7 = (bf16[512,256]{1,0:T(8,128)(2,1)S(1)}, bf16[512,256]{1,0:T(8,128)(2,1)S(1)}, u32[]{:S(2)}, u32[]{:S(2)}) collective-permute-start(bf16[512,256]{1,0:T(8,128)(2,1)S(1)} %slice.41), channel_id=1, source_target_pairs={{0,96},{1,97},{2,98},{3,99},{4,100},{5,101},{6,102},{7,103},{8,104... | collective-permute-start | bytes 786440 | tf_op jit(solution)/shard_map/ppermute | solution.py:29
  21.4 8.2 %collective-permute-start.6 = (bf16[512,256]{1,0:T(8,128)(2,1)S(1)}, bf16[512,256]{1,0:T(8,128)(2,1)S(1)}, u32[]{:S(2)}, u32[]{:S(2)}) collective-permute-start(bf16[512,256]{1,0:T(8,128)(2,1)S(1)} %slice.40), channel_id=1, source_target_pairs={{0,32},{1,33},{2,34},{3,35},{4,36},{5,37},{6,38},{7,39},{8,40},{9,... | collective-permute-start | bytes 786440 | tf_op jit(solution)/shard_map/ppermute | solution.py:29
  33.4 15.0 %collective-permute-start.12 = (bf16[256,1280]{1,0:T(8,128)(2,1)S(1)}, bf16[256,1280]{1,0:T(8,128)(2,1)S(1)}, u32[]{:S(2)}, u32[]{:S(2)}) collective-permute-start(bf16[256,1280]{1,0:T(8,128)(2,1)S(1)} %pad_maximum_fusion.4.w0), channel_id=1, source_target_pairs={{0,24},{1,25},{2,26},{3,27},{4,28},{5,29},{6,30},{7,31},{8,0},{9,1... | collective-permute-start | bytes 1966088 | tf_op jit(solution)/shard_map/ppermute | solution.py:29
  36.5 15.3 %collective-permute-start.11 = (bf16[256,1280]{1,0:T(8,128)(2,1)S(1)}, bf16[256,1280]{1,0:T(8,128)(2,1)S(1)}, u32[]{:S(2)}, u32[]{:S(2)}) collective-permute-start(bf16[256,1280]{1,0:T(8,128)(2,1)S(1)} %pad_maximum_fusion.4.w0), channel_id=1, source_target_pairs={{0,8},{1,9},{2,10},{3,11},{4,12},{5,13},{6,14},{7,15},{8,16},{9,17... | collective-permute-start | bytes 1966088 | tf_op jit(solution)/shard_map/ppermute | solution.py:29
  36.5 2.4 collective-permute-start.8
  52.8 59.9 %collective-permute-start.16 = (bf16[4,1024,256]{2,1,0:T(8,128)(2,1)S(1)}, bf16[4,1024,256]{2,1,0:T(8,128)(2,1)S(1)}, u32[]{:S(2)}, u32[]{:S(2)}) collective-permute-start(bf16[4,1024,256]{2,1,0:T(8,128)(2,1)S(1)} %pad_maximum_fusion.1.w0), channel_id=1, source_target_pairs={{0,24},{1,25},{2,26},{3,27},{4,28},{5,29},{6,30},{7,31},{8,0},{9,1... | collective-permute-start | bytes 6291464 | tf_op jit(solution)/shard_map/ppermute | solution.py:29
  55.0 57.8 %collective-permute-start.15 = (bf16[4,1024,256]{2,1,0:T(8,128)(2,1)S(1)}, bf16[4,1024,256]{2,1,0:T(8,128)(2,1)S(1)}, u32[]{:S(2)}, u32[]{:S(2)}) collective-permute-start(bf16[4,1024,256]{2,1,0:T(8,128)(2,1)S(1)} %pad_maximum_fusion.1.w0), channel_id=1, source_target_pairs={{0,8},{1,9},{2,10},{3,11},{4,12},{5,13},{6,14},{7,15},{8,16},{9,17... | collective-permute-start | bytes 6291464 | tf_op jit(solution)/shard_map/ppermute | solution.py:29
  58.7 54.0 %collective-permute-start.14 = (bf16[128,1280]{1,0:T(8,128)(2,1)S(1)}, bf16[128,1280]{1,0:T(8,128)(2,1)S(1)}, u32[]{:S(2)}, u32[]{:S(2)}) collective-permute-start(bf16[128,1280]{1,0:T(8,128)(2,1)S(1)} %slice.33), channel_id=1, source_target_pairs={{0,24},{1,25},{2,26},{3,27},{4,28},{5,29},{6,30},{7,31},{8,0},{9,1... | collective-permute-start | bytes 983048 | tf_op jit(solution)/shard_map/ppermute | solution.py:29
  60.3 52.5 %collective-permute-start.13 = (bf16[128,1280]{1,0:T(8,128)(2,1)S(1)}, bf16[128,1280]{1,0:T(8,128)(2,1)S(1)}, u32[]{:S(2)}, u32[]{:S(2)}) collective-permute-start(bf16[128,1280]{1,0:T(8,128)(2,1)S(1)} %slice.32), channel_id=1, source_target_pairs={{0,8},{1,9},{2,10},{3,11},{4,12},{5,13},{6,14},{7,15},{8,16},{9,17... | collective-permute-start | bytes 983048 | tf_op jit(solution)/shard_map/ppermute | solution.py:29
  113.8 64.5 %collective-permute-start.20 = (bf16[4,256,1280]{2,1,0:T(8,128)(2,1)S(1)}, bf16[4,256,1280]{2,1,0:T(8,128)(2,1)S(1)}, u32[]{:S(2)}, u32[]{:S(2)}) collective-permute-start(bf16[4,256,1280]{2,1,0:T(8,128)(2,1)S(1)} %pad_maximum_fusion.w0), channel_id=1, source_target_pairs={{0,96},{1,97},{2,98},{3,99},{4,100},{5,101},{6,102},{7,103},{8,104... | collective-permute-start | bytes 7864328 | tf_op jit(solution)/shard_map/ppermute | solution.py:29
  117.0 61.3 %collective-permute-start.19 = (bf16[4,256,1280]{2,1,0:T(8,128)(2,1)S(1)}, bf16[4,256,1280]{2,1,0:T(8,128)(2,1)S(1)}, u32[]{:S(2)}, u32[]{:S(2)}) collective-permute-start(bf16[4,256,1280]{2,1,0:T(8,128)(2,1)S(1)} %pad_maximum_fusion.w0), channel_id=1, source_target_pairs={{0,32},{1,33},{2,34},{3,35},{4,36},{5,37},{6,38},{7,39},{8,40},{9,... | collective-permute-start | bytes 7864328 | tf_op jit(solution)/shard_map/ppermute | solution.py:29
  119.8 58.4 %collective-permute-start.18 = (bf16[2,1024,256]{2,1,0:T(8,128)(2,1)S(1)}, bf16[2,1024,256]{2,1,0:T(8,128)(2,1)S(1)}, u32[]{:S(2)}, u32[]{:S(2)}) collective-permute-start(bf16[2,1024,256]{2,1,0:T(8,128)(2,1)S(1)} %slice.35), channel_id=1, source_target_pairs={{0,24},{1,25},{2,26},{3,27},{4,28},{5,29},{6,30},{7,31},{8,0},{9,1... | collective-permute-start | bytes 3145736 | tf_op jit(solution)/shard_map/ppermute | solution.py:29
  121.7 56.5 %collective-permute-start.17 = (bf16[2,1024,256]{2,1,0:T(8,128)(2,1)S(1)}, bf16[2,1024,256]{2,1,0:T(8,128)(2,1)S(1)}, u32[]{:S(2)}, u32[]{:S(2)}) collective-permute-start(bf16[2,1024,256]{2,1,0:T(8,128)(2,1)S(1)} %slice.34), channel_id=1, source_target_pairs={{0,8},{1,9},{2,10},{3,11},{4,12},{5,13},{6,14},{7,15},{8,16},{9,17... | collective-permute-start | bytes 3145736 | tf_op jit(solution)/shard_map/ppermute | solution.py:29
  189.1 2.1 collective-permute-start.26
  191.9 13.1 %collective-permute-start.29 = (bf16[512,256]{1,0:T(8,128)(2,1)S(1)}, bf16[512,256]{1,0:T(8,128)(2,1)S(1)}, u32[]{:S(2)}, u32[]{:S(2)}) collective-permute-start(bf16[512,256]{1,0:T(8,128)(2,1)S(1)} %shard_map.98), channel_id=1, source_target_pairs={{128,0},{129,1},{130,96},{131,97},{132,64},{133,65},{134,32},{135,... | collective-permute-start | bytes 786440 | tf_op jit(solution)/shard_map/ppermute | solution.py:29
  205.1 18.2 %collective-permute-start.32 = (bf16[512,256]{1,0:T(8,128)(2,1)S(1)}, bf16[512,256]{1,0:T(8,128)(2,1)S(1)}, u32[]{:S(2)}, u32[]{:S(2)}) collective-permute-start(bf16[512,256]{1,0:T(8,128)(2,1)S(1)} %collective-permute-done.29.p0.upstream), channel_id=1, source_target_pairs={{0,6},{1,7},{2,4},{3,5},{4,2},{5,3},{6,0},{7,1},{8,14},{9,15},{10,... | collective-permute-start | bytes 786440 | tf_op jit(solution)/shard_map/ppermute | solution.py:29
  210.4 14.8 %collective-permute-start.31 = (bf16[512,256]{1,0:T(8,128)(2,1)S(1)}, bf16[512,256]{1,0:T(8,128)(2,1)S(1)}, u32[]{:S(2)}, u32[]{:S(2)}) collective-permute-start(bf16[512,256]{1,0:T(8,128)(2,1)S(1)} %collective-permute-done.29.p0.upstream), channel_id=1, source_target_pairs={{0,4},{1,5},{2,6},{3,7},{4,0},{5,1},{6,2},{7,3},{8,12},{9,13},{10,... | collective-permute-start | bytes 786440 | tf_op jit(solution)/shard_map/ppermute | solution.py:29
  213.5 11.7 %collective-permute-start.30 = (bf16[512,256]{1,0:T(8,128)(2,1)S(1)}, bf16[512,256]{1,0:T(8,128)(2,1)S(1)}, u32[]{:S(2)}, u32[]{:S(2)}) collective-permute-start(bf16[512,256]{1,0:T(8,128)(2,1)S(1)} %collective-permute-done.29.p0.upstream), channel_id=1, source_target_pairs={{0,2},{1,3},{2,0},{3,1},{4,6},{5,7},{6,4},{7,5},{8,10},{9,11},{10,... | collective-permute-start | bytes 786440 | tf_op jit(solution)/shard_map/ppermute | solution.py:29
  225.4 19.6 %collective-permute-start.33 = (bf16[4,512,256]{2,1,0:T(8,128)(2,1)S(1)}, bf16[4,512,256]{2,1,0:T(8,128)(2,1)S(1)}, u32[]{:S(2)}, u32[]{:S(2)}) collective-permute-start(bf16[4,512,256]{2,1,0:T(8,128)(2,1)S(1)} %pad_maximum_fusion.2), channel_id=1, source_target_pairs={{0,1},{1,0},{2,3},{3,2},{4,5},{5,4},{6,7},{7,6},{8,9},{9,8},{10,11... | collective-permute-start | bytes 3145736 | tf_op jit(solution)/shard_map/ppermute | solution.py:29
  229.7 44.6 %collective-permute-start.35 = (bf16[2,256,1280]{2,1,0:T(8,128)(2,1)}, bf16[2,256,1280]{2,1,0:T(8,128)(2,1)}, u32[]{:S(2)}, u32[]{:S(2)}) collective-permute-start(bf16[2,256,1280]{2,1,0:T(8,128)(2,1)} %slice.39), channel_id=1, source_target_pairs={{0,96},{1,97},{2,98},{3,99},{4,100},{5,101},{6,102},{7,103},{8,104... | collective-permute-start | bytes 3932168 | tf_op jit(solution)/shard_map/ppermute | solution.py:29
  243.1 36.8 %collective-permute-start.34 = (bf16[2,256,1280]{2,1,0:T(8,128)(2,1)}, bf16[2,256,1280]{2,1,0:T(8,128)(2,1)}, u32[]{:S(2)}, u32[]{:S(2)}) collective-permute-start(bf16[2,256,1280]{2,1,0:T(8,128)(2,1)} %slice.38), channel_id=1, source_target_pairs={{0,32},{1,33},{2,34},{3,35},{4,36},{5,37},{6,38},{7,39},{8,40},{9,... | collective-permute-start | bytes 3932168 | tf_op jit(solution)/shard_map/ppermute | solution.py:29
  249.9 30.4 %all-to-all-start.2 = ((bf16[16,80,128]{2,1,0:T(8,128)(2,1)}), bf16[16,80,128]{2,1,0:T(8,128)(2,1)}, u32[]{:S(2)}, u32[]{:S(2)}) async-start(bf16[16,80,128]{2,1,0:T(8,128)(2,1)} %copy-done.17), calls=%async_computation.2 | async-start | bytes 655360 | tf_op jit(solution)/shard_map/all_to_all | solution.py:379
  310.7 4.7 %collective-permute-start.37 = (bf16[4,512,256]{2,1,0:T(8,128)(2,1)S(1)}, bf16[4,512,256]{2,1,0:T(8,128)(2,1)S(1)}, u32[]{:S(2)}, u32[]{:S(2)}) collective-permute-start(bf16[4,512,256]{2,1,0:T(8,128)(2,1)S(1)} %get-tuple-element.154), channel_id=1, source_target_pairs={{0,1},{1,0},{2,3},{3,2},{4,5},{5,4},{6,7},{7,6},{8,9},{9,8},{10,11... | collective-permute-start | bytes 3145736 | tf_op jit(solution)/shard_map/ppermute | solution.py:29
  316.1 11.7 %collective-permute-start.38 = (bf16[512,256]{1,0:T(8,128)(2,1)S(1)}, bf16[512,256]{1,0:T(8,128)(2,1)S(1)}, u32[]{:S(2)}, u32[]{:S(2)}) collective-permute-start(bf16[512,256]{1,0:T(8,128)(2,1)S(1)} %get-tuple-element.155), channel_id=1, source_target_pairs={{0,2},{1,3},{2,0},{3,1},{4,6},{5,7},{6,4},{7,5},{8,10},{9,11},{10,... | collective-permute-start | bytes 786440 | tf_op jit(solution)/shard_map/ppermute | solution.py:29
  318.7 21.5 %collective-permute-start.39 = (bf16[512,256]{1,0:T(8,128)(2,1)S(1)}, bf16[512,256]{1,0:T(8,128)(2,1)S(1)}, u32[]{:S(2)}, u32[]{:S(2)}) collective-permute-start(bf16[512,256]{1,0:T(8,128)(2,1)S(1)} %get-tuple-element.156), channel_id=1, source_target_pairs={{0,4},{1,5},{2,6},{3,7},{4,0},{5,1},{6,2},{7,3},{8,12},{9,13},{10,... | collective-permute-start | bytes 786440 | tf_op jit(solution)/shard_map/ppermute | solution.py:29
  322.3 24.0 %collective-permute-start.40 = (bf16[512,256]{1,0:T(8,128)(2,1)S(1)}, bf16[512,256]{1,0:T(8,128)(2,1)S(1)}, u32[]{:S(2)}, u32[]{:S(2)}) collective-permute-start(bf16[512,256]{1,0:T(8,128)(2,1)S(1)} %get-tuple-element.157), channel_id=1, source_target_pairs={{0,6},{1,7},{2,4},{3,5},{4,2},{5,3},{6,0},{7,1},{8,14},{9,15},{10,... | collective-permute-start | bytes 786440 | tf_op jit(solution)/shard_map/ppermute | solution.py:29
  (43 other events, 1424.5 us)

commit v4 on v3

--- a/solution.py
+++ b/solution.py
@@ -10,6 +10,7 @@
 BOTH = (0, 1)
 AXES = ("section", "ctx", "heads")
 VMEM = 20 * 1024 * 1024
+MOST = 54 * 1024 * 1024
 bf16, f32 = jnp.bfloat16, jnp.float32
 
 
@@ -66,7 +67,7 @@
 
 
 def hop(to_section):
-    return lambda s, x, y, z, c: (s if to_section is None else to_section, (x - z) % SIDE, y, x, c)
+    return lambda s, x, y, z, c: (s if to_section is None else to_section, x ^ z, y, x, c)
 
 
 def first_step(k):
@@ -79,19 +80,62 @@
     )
 
 
-def call(body, outs, args, at, scratch=(), flops=0, remote=()):
+class Late:
+    def __init__(self, source, held, sem):
+        self.held, self.copy, self.waited = held, pltpu.make_async_copy(source, held, sem), False
+        self.shape = held.shape
+
+    def __getitem__(self, index):
+        if not self.waited:
+            self.copy.wait()
+            self.waited = True
+        return self.held[index]
+
+
+def call(body, outs, args, at=None, scratch=(), flops=0, remote=(), away=(), vmem_limit=VMEM):
     moved = sum(a.size * a.dtype.itemsize for a in (*args, *outs))
-    vmem = pl.BlockSpec(memory_space=pltpu.VMEM)
-    ins = [pl.BlockSpec(memory_space=pl.ANY) if i in remote else vmem for i in range(len(args))]
+    vmem, hbm = pl.BlockSpec(memory_space=pltpu.VMEM), pl.BlockSpec(memory_space=pltpu.HBM)
+    own = [pltpu.VMEM(args[i].shape, args[i].dtype) for i in remote]
+    own += [pltpu.VMEM(outs[i].shape, outs[i].dtype) for i in away]
+
+    def kernel(*refs):
+        refs = list(refs)
+        first = refs[:1] if at is not None else []
+        refs = refs[len(first) :]
+        ins, results = refs[: len(args)], refs[len(args) : len(args) + len(outs)]
+        held = refs[len(args) + len(outs) :]
+        sems = held.pop() if own else None
+        held, extra = held[: len(own)], held[len(own) :]
+        late = []
+        for n, i in enumerate(remote):
+            late.append(Late(ins[i], held[n], sems.at[n]))
+            late[-1].copy.start()
+            ins[i] = late[-1]
+        targets = list(results)
+        for n, i in enumerate(away):
+            results[i] = held[len(remote) + n]
+        body(*first, *ins, *results, *extra)
+        for operand in late:
+            operand[...] if not operand.waited else None
+        copies = [
+            pltpu.make_async_copy(results[i], targets[i], sems.at[len(remote) + n])
+            for n, i in enumerate(away)
+        ]
+        for copy in copies:
+            copy.start()
+        for copy in copies:
+            copy.wait()
+
     return pl.pallas_call(
-        body,
-        in_specs=[pl.BlockSpec(memory_space=pltpu.SMEM)] + ins,
-        out_specs=[vmem] * len(outs),
+        kernel,
+        in_specs=[pl.BlockSpec(memory_space=pltpu.SMEM)] * (at is not None)
+        + [hbm if i in remote else vmem for i in range(len(args))],
+        out_specs=[hbm if i in away else vmem for i in range(len(outs))],
         out_shape=list(outs),
-        scratch_shapes=list(scratch),
-        compiler_params=pltpu.CompilerParams(vmem_limit_bytes=VMEM),
+        scratch_shapes=own + list(scratch) + ([pltpu.SemaphoreType.DMA((len(own),))] if own else []),
+        compiler_params=pltpu.CompilerParams(vmem_limit_bytes=vmem_limit),
         cost_estimate=pl.CostEstimate(flops=flops, bytes_accessed=moved, transcendentals=0),
-    )(at, *args)
+    )(*([at] if at is not None else []), *args)
 
 
 def struct(shape, dtype=bf16):
@@ -107,7 +151,7 @@
 
 
 def tables_body(
-    at, decay, bc_rows, x_rows, state,
+    decay, bc_rows, x_rows, state,
     kernel, mixed, x_heads, x_trailing, entry, leading, trailing, totals, b_cols, c_cols, c_rows,
 ):
     count, length = decay.shape
@@ -158,16 +202,15 @@
         entry[:, both] = flat.T.astype(bf16)
 
 
-def rows_body(at, own, mine, theirs, w0, w1, wl, wh, w3, o0, o1, o2, o3, piece, u):
-    y, z, core = at[1], at[2], at[3]
-    fine = w0.shape[1]
-    rows = mine.shape[1]
-    half = wl.shape[0]
-    u[0] = own[...]
-    for k in (1, 2, 3):
-        u[k, span(core, rows), :] = mine[k - 1]
-        u[k, span(1 - core, rows), :] = theirs[k - 1]
-    piece[...] = u[z, :, span(core, piece.shape[0])].astype(f32).T.astype(bf16)
+def rows_body(at, u1, u2, u3, v1, v2, v3, w1, wl, wh, w3, w0, whole, o0, o1, o2, o3, piece, u):
+    x, y, z, core = at[0], at[1], at[2], at[3]
+    fine = w1.shape[1]
+    rows = u1.shape[0]
+    for k, mine, theirs in ((1, u1, v1), (2, u2, v2), (3, u3, v3)):
+        u[k, span(core, rows), :] = mine[...]
+        u[k, span(1 - core, rows), :] = theirs[...]
+    u[0] = whole[:, span(x, u.shape[2])]
+    piece[...] = u[behind(x, x ^ z), :, span(core, piece.shape[0])].astype(f32).T.astype(bf16)
     for k, out in enumerate((o0, o1, o2, o3)):
         total = None
         for j, w in enumerate((w0, w1, None, w3)):
@@ -193,7 +236,7 @@
         states[h, each:, :] = totals[h]
 
 
-def sum_body(at, own, r1, r2, r3, leading, c_rows, totals, grad, states):
+def sum_body(own, r1, r2, r3, leading, c_rows, totals, grad, states):
     total = own[...].astype(f32)
     for r in (r1, r2, r3):
         total = total + r[...].astype(f32)
@@ -224,7 +267,7 @@
     entering(rounded, leading, c_rows, totals, states)
 
 
-def scan_body(at, states, exits):
+def scan_body(states, exits):
     count, size, _ = exits.shape
     held = jnp.zeros(exits.shape[1:], f32)
     for k in range(count - 1, -1, -1):
@@ -234,17 +277,8 @@
 
 
 def block_body(
-    at, grad, kernel, mixed, x_heads, x_trailing, leading, trailing, gain, entry, b_cols, c_cols, leaving,
-    out, own_kernel, own_mixed, own_x, own_trailing, sems,
+    grad, leading, entry, leaving, b_cols, x_heads, kernel, mixed, gain, trailing, x_trailing, c_cols, out
 ):
-    copies = [
-        pltpu.make_async_copy(source, target, sems.at[i])
-        for i, (source, target) in enumerate(
-            ((x_heads, own_x), (kernel, own_kernel), (mixed, own_mixed), (x_trailing, own_trailing))
-        )
-    ]
-    for copy in copies:
-        copy.start()
     count = leading.shape[0]
     inner = grad.shape[0]
     each = inner // count
@@ -255,18 +289,16 @@
         scaled.append((grad[own, :].astype(f32) * leading[h : h + 1, :]).astype(bf16))
     grad_c = dot(entry[...], jnp.concatenate(scaled, axis=0), 1, 0)
     gained = dot(leaving[...], b_cols[...], 1, 0)
-    for copy in copies:
-        copy.wait()
     weighted = None
     for h in range(count):
         own = slice(h * each, (h + 1) * each)
         g = grad[own, :]
-        term = own_kernel[h].astype(f32) * dot(g, own_x[own, :], 0, 0)
+        term = kernel[h].astype(f32) * dot(g, x_heads[own, :], 0, 0)
         weighted = term if weighted is None else weighted + term
-        inside = dot(g, own_mixed[h], 1, 0) + gain[h : h + 1, :] * g.astype(f32)
+        inside = dot(g, mixed[h], 1, 0) + gain[h : h + 1, :] * g.astype(f32)
         out[own, :] = (inside + trailing[h : h + 1, :] * gained[own, :]).astype(bf16)
     rounded = weighted.astype(bf16)
-    grad_b = dot(c_cols[...], rounded, 1, 0) + dot(leaving[...], own_trailing[...], 0, 0)
+    grad_b = dot(c_cols[...], rounded, 1, 0) + dot(leaving[...], x_trailing[...], 0, 0)
     out[inner : inner + size, :] = grad_b.astype(bf16)
     out[inner + size :, :] = (grad_c + dot(b_cols[...], rounded, 1, 1)).astype(bf16)
 
@@ -278,8 +310,8 @@
 
 
 def back_body(at, g0, g1, gl, gh, g3, w0, w1, wl, wh, w3, keep, give, u, g2):
-    y, z, core = at[1], at[2], at[3]
-    fine, half = w0.shape[0], wl.shape[0]
+    x, y, z, core = at[0], at[1], at[2], at[3]
+    fine = w0.shape[0]
     g2[: gl.shape[0], :] = gl[...]
     g2[gl.shape[0] :, :] = gh[...]
     for k, g in enumerate((g0, g1, g2, g3)):
@@ -290,7 +322,7 @@
             else:
                 term = dot(w[...], g[...], 1, 0)
             u[k, rows, :] = term.astype(bf16)
-        to_halves(u.at[k], z ^ k, core, keep, give)
+        to_halves(u.at[k], z ^ x ^ behind(x, k), core, keep, give)
 
 
 def whole_body(at, g, w0, w1, wl, wh, w3, keep, give, u):
@@ -303,7 +335,7 @@
         to_halves(u.at[k], z ^ behind(x, k), core, keep, give)
 
 
-def pair_body(at, keep, got, s1, s2, s3):
+def pair_body(keep, got, s1, s2, s3):
     for q, out in ((1, s1), (2, s2), (3, s3)):
         out[...] = (keep[q].astype(f32) + got[q].astype(f32)).astype(bf16)
 
@@ -315,7 +347,7 @@
     return total + upstream[...].astype(f32)
 
 
-def total_body(at, keep, got, r1, r2, r3, upstream, out):
+def total_body(keep, got, r1, r2, r3, upstream, out):
     out[...] = total_of(keep, got, (r1, r2, r3), upstream).astype(bf16)
 
 
@@ -343,17 +375,17 @@
     pad = 16
     steps = (1, 2, 3)
 
-    upstream = lax.dynamic_slice_in_dim(grad_out, block * x, block, 1)
+    out_sides = sides(w_out[0], first_step, BOTH)
+    out_far = far(out_sides, first_step, BOTH, 0)
     mine = []
     for k in steps:
         piece = lax.dynamic_slice(grad_out, (half * core, block * ((x + k) % SIDE)), (half, block))
         mine.append(routed(piece, along_x(k), (1,)))
-    mine = jnp.stack(mine)
-    theirs = routed(mine, other_core, (1,))
-
-    out_sides = sides(w_out[0], first_step, BOTH)
-    out_far = far(out_sides, first_step, BOTH, 0)
+    theirs = [routed(piece, other_core, (1,)) for piece in mine]
+
     back = jnp.concatenate([w_in[0], w_bc[0]], axis=1)
+    out_far, back = tie((out_far, back))
+    back_sides = sides(back, along_y, BOTH)
 
     (
         kernel, mixed, x_heads, x_trailing, entry, leading, trailing, totals, b_cols, c_cols, c_rows
@@ -367,11 +399,11 @@
             struct((state_size, rows)), struct((rows, state_size)),
         ],
         [decay[0], bc_act[0], x_act[0], state_in[0, 0]],
-        at,
+        remote=range(4),
         flops=2 * rows * rows * inner,
     )
     gain = jnp.broadcast_to(skip_gain[0][:, None], (head_count, rows))
-    out_sides, out_far, back, leading, gain = tie((out_sides, out_far, back, leading, gain))
+    out_sides, out_far, leading, gain = tie((out_sides, out_far, leading, gain))
 
     state_shape = struct((head_count, head_size + pad, state_size))
 
@@ -379,25 +411,22 @@
         return lax.all_to_all(states, "ctx", 0, 0)
 
     def scanned(arrived):
-        (exits,) = call(scan_body, [struct((head_count, head_size, state_size))], [arrived], at)
+        (exits,) = call(
+            scan_body, [struct((head_count, head_size, state_size))], [arrived], away=(0,)
+        )
         return exits
 
-    def within(grad_ssd, leaving):
+    def within(grad_ssd, leaving, vmem_limit=VMEM):
         (grads,) = call(
             block_body,
             [struct((outer, rows))],
             [
-                grad_ssd, kernel, mixed, x_heads, x_trailing, leading, trailing, gain, entry, b_cols, c_cols,
-                leaving.reshape(inner, state_size),
-            ],
-            at,
-            scratch=[
-                pltpu.VMEM(kernel.shape, bf16), pltpu.VMEM(mixed.shape, bf16),
-                pltpu.VMEM(x_heads.shape, bf16), pltpu.VMEM(x_trailing.shape, bf16),
-                pltpu.SemaphoreType.DMA((4,)),
+                grad_ssd, leading, entry, leaving.reshape(inner, state_size), b_cols, x_heads, kernel, mixed,
+                gain, trailing, x_trailing, c_cols,
             ],
             flops=4 * rows * rows * inner,
-            remote=(1, 2, 3, 4),
+            remote=range(12),
+            vmem_limit=vmem_limit,
         )
         return grads
 
@@ -406,42 +435,44 @@
 
     def over_heads(keep, give, sections):
         got = routed(give, other_core, sections)
-        sent = call(pair_body, [chunk] * 3, [keep, got], at)
+        sent = call(pair_body, [chunk] * 3, [keep, got])
         return [keep, got] + [routed(s, across_z(k), sections) for k, s in zip(steps, sent)]
 
     *partial, own = call(
         rows_body,
         [struct((inner, rows))] * SIDE + [chunk],
-        [upstream, mine, theirs, w_out[0], out_sides[0], *out_far, out_sides[1]],
+        [*mine, *theirs, out_sides[0], *out_far, out_sides[1], w_out[0], grad_out],
         at,
+        remote=(10, 11),
         scratch=[pltpu.VMEM((SIDE, rows, block), bf16)],
         flops=2 * SIDE * rows * block * inner,
     )
-    partial, back, out_sides, out_far = tie((partial, back, out_sides, out_far))
+    partial, out_sides, out_far = tie((partial, out_sides, out_far))
     received = [routed(partial[k], along_x(-k), (1,)) for k in steps]
-    back_sides = sides(back, along_y, BOTH)
-    out_set = jnp.stack([w_out[0], out_sides[0], jnp.concatenate(out_far, 0), out_sides[1]])
-    received, back_sides, out_set = tie((received, back_sides, out_set))
+    back_far = far(back_sides, along_y, BOTH, 0)
+    out_set = jnp.concatenate([w_out[0], out_sides[0], *out_far, out_sides[1]]).reshape(SIDE, inner, -1)
+    received, back_far, out_set = tie((received, back_far, out_set))
+    back_set = jnp.concatenate([back, back_sides[0], *back_far, back_sides[1]]).reshape(SIDE, -1, outer)
     grad_ssd, states = call(
         sum_body,
         [struct((inner, rows)), state_shape],
         [partial[0], *received, leading, c_rows, totals],
-        at,
+        remote=(4, 5, 6),
+        away=(0, 1),
         flops=2 * rows * inner * state_size,
     )
 
-    states, back_sides, out_set = tie((states, back_sides, out_set))
+    states, out_set, back_set = tie((states, out_set, back_set))
     arrived = exchange(states)
-    back_far = far(back_sides, along_y, BOTH, 0)
     whole_sides = sides(out_set, along_y, (0,))
-    arrived, back_far, whole_sides = tie((arrived, back_far, whole_sides))
+    width_sides = sides(back_set, along_x, (0,))
+    arrived, whole_sides, width_sides = tie((arrived, whole_sides, width_sides))
     exits = scanned(arrived)
-    back_set = jnp.stack([back, back_sides[0], jnp.concatenate(back_far, 0), back_sides[1]])
-    exits, back_set, whole_sides = tie((exits, back_set, whole_sides))
+    exits, whole_sides, width_sides = tie((exits, whole_sides, width_sides))
     leaving = exchange(exits)
     whole_far = far(whole_sides, along_y, (0,), 0)
-    width_sides = sides(back_set, along_x, (0,))
-    leaving, whole_far, width_sides = tie((leaving, whole_far, width_sides))
+    width_far = far(width_sides, along_x, (0,), 0)
+    leaving, whole_far, width_far = tie((leaving, whole_far, width_far))
     grads = within(grad_ssd, leaving)
 
     grads_sides = sides(grads, along_x, (1,))
@@ -459,13 +490,11 @@
         flops=2 * SIDE * rows * block * outer,
     )
     sums = over_heads(keep, give, (1,))
-    (middle,) = call(total_body, [chunk], [*sums, own], at)
+    (middle,) = call(total_body, [chunk], [*sums, own])
 
     arrived = routed(middle, hop(0), (1,))
     settled = routed(middle, hop(None), (1,))
 
-    arrived, width_sides = tie((arrived, width_sides))
-    width_far = far(width_sides, along_x, (0,), 0)
     parts = [arrived] + [routed(arrived, across_z(k), (0,)) for k in steps]
     other = routed(jnp.stack(parts), other_core, (0,))
     grad_ssd, states = call(
@@ -474,10 +503,12 @@
         [*parts, other, out_set, whole_sides[0], *whole_far, whole_sides[1], leading, c_rows, totals],
         at,
         scratch=[pltpu.VMEM((width, rows), bf16)],
+        remote=range(10, 13),
+        away=(0, 1),
         flops=2 * rows * width * inner,
     )
-    held, width_far, settled = tie((exchange(states), width_far, settled))
-    grads = within(grad_ssd, exchange(scanned(held)))
+    held, settled = tie((exchange(states), settled))
+    grads = within(grad_ssd, exchange(scanned(held)), MOST)
     keep, give = call(
         whole_body,
         [chunks, chunks],

time: 349 us -> 319 us (0.914)
  blocking collectives: 118 us -> 83.3 us
  starting transfers between devices: 87.6 us -> 93.2 us
  local copies, waits for them, and re-layouts: 17.2 us -> 12.8 us
    all_to_all x3, blocking collectives: 118 us -> 83.3 us  [exchange(): return lax.all_to_all(states, 'ctx', 0, 0)]
    all_to_all x1, starting transfers between devices: 4.65 us -> 15.1 us  [exchange(): return lax.all_to_all(states, 'ctx', 0, 0)]
    all_to_all x1, waiting for transfers between devices: 0.38 us -> 8.77 us  [exchange(): return lax.all_to_all(states, 'ctx', 0, 0)]
    ppermute x41 -> x43, waiting for transfers between devices: 92.6 us -> 87.6 us  [routed(): return lax.ppermute(value, AXES, pairs)]
    ppermute x41 -> x43, starting transfers between devices: 83 us -> 78 us  [routed(): return lax.ppermute(value, AXES, pairs)]
    unnamed x66 -> x80, local copies, waits for them, and re-layouts: 12.2 us -> 10.4 us
  transfers between devices with their start and end apart: 42 -> 44, of which waited for: 14 -> 14; matrix products, arithmetic and copies ran while one was open for 2% -> 1% of each run, Pallas kernels for 2% -> 2%
where the time goes in v4:
time: 319 us; the launch traced here: 318 us
  waiting for transfers between devices  96.3 us (30%)
  starting transfers between devices  93.2 us (29%)
  blocking collectives  83.3 us (26%)
  Pallas kernels  29.8 us (9%)
  local copies, waits for them, and re-layouts  12.8 us (4%)
    ppermute x43, waiting for transfers between devices, routed(): return lax.ppermute(value, AXES, pairs)  87.6 us
    all_to_all x3, blocking collectives, exchange(): return lax.all_to_all(states, 'ctx', 0, 0)  83.3 us
    ppermute x43, starting transfers between devices, routed(): return lax.ppermute(value, AXES, pairs)  78 us
    pallas_call x14, Pallas kernels, call(): pl.pallas_call(kernel, in_specs=[pl.BlockSpec(memory_space=pltpu.SMEM)] *...  29.8 us
    all_to_all x1, starting transfers between devices, exchange(): return lax.all_to_all(states, 'ctx', 0, 0)  15.1 us
    unnamed x80, local copies, waits for them, and re-layouts  10.4 us
    all_to_all x1, waiting for transfers between devices, exchange(): return lax.all_to_all(states, 'ctx', 0, 0)  8.77 us
  transfers between devices with their start and end apart: 44, of which 14 were waited for; matrix products, arithmetic and copies ran while one was open for 1% of the time, Pallas kernels for 2%

profile of v4, /device:TPU:32, one launch (start us, length us, event | category | flops | bytes accessed | tf_op | source)
XLA Modules:
  0.0 318.2 jit_solution(7737240186043982280)
XLA Ops:
  11.0 3.3 %collective-permute-done.7.refs_10_ = bf16[1024,256]{1,0:T(8,128)(2,1)S(1)} collective-permute-done((bf16[1024,256]{1,0:T(8,128)(2,1)}, bf16[1024,256]{1,0:T(8,128)(2,1)S(1)}, u32[]{:S(2)}, u32[]{:S(2)}) %collective-permute-start.7) | collective-permute-done | bytes 524320 | tf_op jit(solution)/shard_map/ppermute | solution.py:30
  14.3 3.7 %collective-permute-start.9 = (bf16[512,256]{1,0:T(8,128)(2,1)S(1)}, bf16[512,256]{1,0:T(8,128)(2,1)S(1)}, u32[]{:S(2)}, u32[]{:S(2)}) collective-permute-start(bf16[512,256]{1,0:T(8,128)(2,1)S(1)} %slice.41), channel_id=1, source_target_pairs={{0,96},{1,97},{2,98},{3,99},{4,100},{5,101},{6,102},{7,103},{8,104... | collective-permute-start | bytes 786440 | tf_op jit(solution)/shard_map/ppermute | solution.py:30
  22.9 3.3 %collective-permute-done.8.refs_8_ = bf16[512,256]{1,0:T(8,128)(2,1)S(1)} collective-permute-done((bf16[512,256]{1,0:T(8,128)(2,1)S(1)}, bf16[512,256]{1,0:T(8,128)(2,1)S(1)}, u32[]{:S(2)}, u32[]{:S(2)}) %collective-permute-start.8) | collective-permute-done | bytes 262176 | tf_op jit(solution)/shard_map/ppermute | solution.py:30
  26.2 3.0 collective-permute-start.15
  30.9 4.0 %shard_map.92 = (bf16[1024,256]{1,0:T(8,128)(2,1)S(1)}, bf16[1024,256]{1,0:T(8,128)(2,1)S(1)}, bf16[1024,256]{1,0:T(8,128)(2,1)S(1)}, bf16[1024,256]{1,0:T(8,128)(2,1)S(1)}, bf16[512,256]{1,0:T(8,128)(2,1)S(1)}) custom-call(s32[5]{0:T(128)S(1)} %copy-done.33, bf16[128,1024]{1,0:T(8,128)(2,1)} %collective-permute-done.refs_1_, ...), custom_call_target="tpu_custom_call" | custom-call | flops 2147483648 | bytes 8126464 | tf_op jit(solution)/shard_map/pallas_call | solution.py:129
  37.2 3.9 %collective-permute-done.15.refs_10_ = bf16[256,1280]{1,0:T(8,128)(2,1)S(1)} collective-permute-done((bf16[256,1280]{1,0:T(8,128)(2,1)S(1)}, bf16[256,1280]{1,0:T(8,128)(2,1)S(1)}, u32[]{:S(2)}, u32[]{:S(2)}) %collective-permute-start.15) | collective-permute-done | bytes 655392 | tf_op jit(solution)/shard_map/ppermute | solution.py:30
  41.1 3.8 %collective-permute-start.16 = (bf16[128,1280]{1,0:T(8,128)(2,1)S(1)}, bf16[128,1280]{1,0:T(8,128)(2,1)S(1)}, u32[]{:S(2)}, u32[]{:S(2)}) collective-permute-start(bf16[128,1280]{1,0:T(8,128)(2,1)S(1)} %slice.43), channel_id=1, source_target_pairs={{0,24},{1,25},{2,26},{3,27},{4,28},{5,29},{6,30},{7,31},{8,0},{9,1... | collective-permute-start | bytes 983048 | tf_op jit(solution)/shard_map/ppermute | solution.py:30
  45.3 4.2 %collective-permute-done.16.refs_9_ = bf16[128,1280]{1,0:T(8,128)(2,1)S(1)} collective-permute-done((bf16[128,1280]{1,0:T(8,128)(2,1)S(1)}, bf16[128,1280]{1,0:T(8,128)(2,1)S(1)}, u32[]{:S(2)}, u32[]{:S(2)}) %collective-permute-start.16) | collective-permute-done | bytes 327712 | tf_op jit(solution)/shard_map/ppermute | solution.py:30
  49.5 4.0 %collective-permute-done.14.refs_8_ = bf16[128,1280]{1,0:T(8,128)(2,1)S(1)} collective-permute-done((bf16[128,1280]{1,0:T(8,128)(2,1)S(1)}, bf16[128,1280]{1,0:T(8,128)(2,1)S(1)}, u32[]{:S(2)}, u32[]{:S(2)}) %collective-permute-start.14) | collective-permute-done | bytes 327712 | tf_op jit(solution)/shard_map/ppermute | solution.py:30
  57.0 3.5 %collective-permute-start.19 = (bf16[4,256,1280]{2,1,0:T(8,128)(2,1)S(1)}, bf16[4,256,1280]{2,1,0:T(8,128)(2,1)S(1)}, u32[]{:S(2)}, u32[]{:S(2)}) collective-permute-start(bf16[4,256,1280]{2,1,0:T(8,128)(2,1)S(1)} %bitcast.23), channel_id=1, source_target_pairs={{0,32},{1,33},{2,34},{3,35},{4,36},{5,37},{6,38},{7,39},{8,40},{9,... | collective-permute-start | bytes 7864328 | tf_op jit(solution)/shard_map/ppermute | solution.py:30
  63.9 3.9 %collective-permute-start.17 = (bf16[4,1024,256]{2,1,0:T(8,128)(2,1)S(1)}, bf16[4,1024,256]{2,1,0:T(8,128)(2,1)S(1)}, u32[]{:S(2)}, u32[]{:S(2)}) collective-permute-start(bf16[4,1024,256]{2,1,0:T(8,128)(2,1)S(1)} %bitcast.26), channel_id=1, source_target_pairs={{0,8},{1,9},{2,10},{3,11},{4,12},{5,13},{6,14},{7,15},{8,16},{9,17... | collective-permute-start | bytes 6291464 | tf_op jit(solution)/shard_map/ppermute | solution.py:30
  67.8 49.3 %all_to_all.20.refs_0_ = bf16[16,80,128]{2,1,0:T(8,128)(2,1)S(1)} all-to-all(bf16[16,80,128]{2,1,0:T(8,128)(2,1)S(1)} %get-tuple-element.110), channel_id=1, replica_groups=mesh['section'=2,'ctx'=16,'heads'=8] {'ctx'}, dimensions={0} | all-to-all | bytes 655360 | tf_op jit(solution)/shard_map/all_to_all | solution.py:411
  121.7 3.7 %collective-permute-start.23 = (bf16[2,256,1280]{2,1,0:T(8,128)(2,1)S(1)}, bf16[2,256,1280]{2,1,0:T(8,128)(2,1)S(1)}, u32[]{:S(2)}, u32[]{:S(2)}) collective-permute-start(bf16[2,256,1280]{2,1,0:T(8,128)(2,1)S(1)} %slice.36), channel_id=1, source_target_pairs={{0,32},{1,33},{2,34},{3,35},{4,36},{5,37},{6,38},{7,39},{8,40},{9,... | collective-permute-start | bytes 3932168 | tf_op jit(solution)/shard_map/ppermute | solution.py:30
  125.5 5.2 %collective-permute-start.22 = (bf16[2,1024,256]{2,1,0:T(8,128)(2,1)S(1)}, bf16[2,1024,256]{2,1,0:T(8,128)(2,1)S(1)}, u32[]{:S(2)}, u32[]{:S(2)}) collective-permute-start(bf16[2,1024,256]{2,1,0:T(8,128)(2,1)S(1)} %slice.35), channel_id=1, source_target_pairs={{0,24},{1,25},{2,26},{3,27},{4,28},{5,29},{6,30},{7,31},{8,0},{9,1... | collective-permute-start | bytes 3145736 | tf_op jit(solution)/shard_map/ppermute | solution.py:30
  132.7 21.7 %all_to_all.21 = bf16[16,64,128]{2,1,0:T(8,128)(2,1)S(1)} all-to-all(bf16[16,64,128]{2,1,0:T(8,128)(2,1)S(1)} %shard_map.94), channel_id=1, replica_groups=mesh['section'=2,'ctx'=16,'heads'=8] {'ctx'}, dimensions={0} | all-to-all | bytes 524288 | tf_op jit(solution)/shard_map/all_to_all | solution.py:411
  155.6 3.1 shard_map.95.refs_1_
  161.6 3.6 %shard_map.96 = (bf16[4,512,256]{2,1,0:T(8,128)(2,1)S(1)}, bf16[4,512,256]{2,1,0:T(8,128)(2,1)S(1)}) custom-call(s32[5]{0:T(128)S(1)} %copy-done.33, bf16[1280,256]{1,0:T(8,128)(2,1)S(1)} %shard_map.95.refs_1_, bf16[1280,256]{1,0:T(8,128)(2,1)S(1)} %collective-permute-done.25.refs_2_, bf16[640,256]{1,0:T(8,128)(2,1)S(1)} %collective-permute-done.26.refs_3_, ...), custom_call_target="tpu_custom_call" | custom-call | flops 2684354560 | bytes 7340032 | tf_op jit(solution)/shard_map/pallas_call | solution.py:129
  169.7 35.0 %collective-permute-done.33.refs_1_.refs_6_ = bf16[512,256]{1,0:T(8,128)(2,1)S(1)} collective-permute-done((bf16[512,256]{1,0:T(8,128)(2,1)S(1)}, bf16[512,256]{1,0:T(8,128)(2,1)S(1)}, u32[]{:S(2)}, u32[]{:S(2)}) %collective-permute-start.33) | collective-permute-done | bytes 262176 | tf_op jit(solution)/shard_map/ppermute | solution.py:30
  204.8 2.9 collective-permute-start.36
  209.6 4.4 %collective-permute-start.34 = (bf16[512,256]{1,0:T(8,128)(2,1)S(1)}, bf16[512,256]{1,0:T(8,128)(2,1)S(1)}, u32[]{:S(2)}, u32[]{:S(2)}) collective-permute-start(bf16[512,256]{1,0:T(8,128)(2,1)S(1)} %collective-permute-done.33.refs_1_.refs_6_), channel_id=1, source_target_pairs={{0,2},{1,3},{2,0},{3,1},{4,6},{5,7},{6,4},{7,5},{8,10},{9,11},{10,... | collective-permute-start | bytes 786440 | tf_op jit(solution)/shard_map/ppermute | solution.py:30
  214.0 6.1 %collective-permute-done.36.refs_4_ = bf16[512,256]{1,0:T(8,128)(2,1)S(1)} collective-permute-done((bf16[512,256]{1,0:T(8,128)(2,1)S(1)}, bf16[512,256]{1,0:T(8,128)(2,1)S(1)}, u32[]{:S(2)}, u32[]{:S(2)}) %collective-permute-start.36) | collective-permute-done | bytes 262176 | tf_op jit(solution)/shard_map/ppermute | solution.py:30
  226.2 4.7 %shard_map.99 = (bf16[1024,256]{1,0:T(8,128)(2,1)S(1)}, bf16[16,80,128]{2,1,0:T(8,128)(2,1)}) custom-call(s32[5]{0:T(128)S(1)} %copy-done.33, bf16[512,256]{1,0:T(8,128)(2,1)S(1)} %collective-permute-done.33.refs_1_.refs_6_, bf16[512,256]{1,0:T(8,128)(2,1)S(1)} %collective-permute-done.34.refs_2_, bf16[512,256]{1,0:T(8,128)(2,1)S(1)} %collective-permute-done.35.refs_3_, ...), custom_call_target="tpu_custom_call" | custom-call | flops 2147483648 | bytes 11485184 | tf_op jit(solution)/shard_map/pallas_call | solution.py:129
  231.7 15.1 %all-to-all-start.2 = ((bf16[16,80,128]{2,1,0:T(8,128)(2,1)}), bf16[16,80,128]{2,1,0:T(8,128)(2,1)S(1)}, u32[]{:S(2)}, u32[]{:S(2)}) async-start(bf16[16,80,128]{2,1,0:T(8,128)(2,1)} %get-tuple-element.141), calls=%async_computation.2 | async-start | bytes 655360 | tf_op jit(solution)/shard_map/all_to_all | solution.py:411
  247.5 8.8 %all-to-all-done.2.refs_0_ = bf16[16,80,128]{2,1,0:T(8,128)(2,1)S(1)} async-done(((bf16[16,80,128]{2,1,0:T(8,128)(2,1)}), bf16[16,80,128]{2,1,0:T(8,128)(2,1)S(1)}, u32[]{:S(2)}, u32[]{:S(2)}) %all-to-all-start.2) | async-done | bytes 327712 | tf_op jit(solution)/shard_map/all_to_all | solution.py:411
  256.4 12.2 %all_to_all.22 = bf16[16,64,128]{2,1,0:T(8,128)(2,1)} all-to-all(bf16[16,64,128]{2,1,0:T(8,128)(2,1)S(1)} %shard_map.100), channel_id=1, replica_groups=mesh['section'=2,'ctx'=16,'heads'=8] {'ctx'}, dimensions={0} | all-to-all | bytes 524288 | tf_op jit(solution)/shard_map/all_to_all | solution.py:411
  268.6 5.3 %shard_map.101.refs_1_ = bf16[1280,256]{1,0:T(8,128)(2,1)} custom-call(bf16[1024,256]{1,0:T(8,128)(2,1)} %copy-done.20, f32[16,256]{1,0:T(8,128)} %copy-done.28, bf16[128,1024]{1,0:T(8,128)(2,1)} %copy-done.19, bf16[1024,128]{1,0:T(8,128)(2,1)} %bitcast.40, bf16[128,256]{1,0:T(8,128)(2,1)} %copy-done.26, bf16[1024,256]{1,0:T(8,128)(2,1)} %copy-done.9, ...), custom_call_target="tpu_custom_call" | custom-call | flops 268435456 | bytes 7127040 | tf_op jit(solution)/shard_map/pallas_call | solution.py:129
  276.4 3.5 %shard_map.102 = (bf16[4,512,256]{2,1,0:T(8,128)(2,1)S(1)}, bf16[4,512,256]{2,1,0:T(8,128)(2,1)S(1)}) custom-call(s32[5]{0:T(128)S(1)} %copy-done.34, bf16[1280,256]{1,0:T(8,128)(2,1)S(1)} %copy-done.8, bf16[4,256,1280]{2,1,0:T(8,128)(2,1)S(1)} %bitcast.24, bf16[4,256,1280]{2,1,0:T(8,128)(2,1)S(1)} %copy-done.5, bf16[2,256,1280]{2,1,0:T(8,128)(2,1)S(1)} %copy-done.14, ...), custom_call_target="tpu_custom_call" | custom-call | flops 2684354560 | bytes 13238272 | tf_op jit(solution)/shard_map/pallas_call | solution.py:129
  284.7 5.4 %collective-permute-start.40 = (bf16[512,256]{1,0:T(8,128)(2,1)S(1)}, bf16[512,256]{1,0:T(8,128)(2,1)S(1)}, u32[]{:S(2)}, u32[]{:S(2)}) collective-permute-start(bf16[512,256]{1,0:T(8,128)(2,1)S(1)} %get-tuple-element.147), channel_id=1, source_target_pairs={{0,2},{1,3},{2,0},{3,1},{4,6},{5,7},{6,4},{7,5},{8,10},{9,11},{10,... | collective-permute-start | bytes 786440 | tf_op jit(solution)/shard_map/ppermute | solution.py:30
  292.6 2.8 collective-permute-start.42
  295.4 3.4 %collective-permute-done.40.refs_3_ = bf16[512,256]{1,0:T(8,128)(2,1)S(1)} collective-permute-done((bf16[512,256]{1,0:T(8,128)(2,1)S(1)}, bf16[512,256]{1,0:T(8,128)(2,1)S(1)}, u32[]{:S(2)}, u32[]{:S(2)}) %collective-permute-start.40) | collective-permute-done | bytes 262176 | tf_op jit(solution)/shard_map/ppermute | solution.py:30
  298.8 11.7 %collective-permute-done.41.refs_4_ = bf16[512,256]{1,0:T(8,128)(2,1)S(1)} collective-permute-done((bf16[512,256]{1,0:T(8,128)(2,1)S(1)}, bf16[512,256]{1,0:T(8,128)(2,1)S(1)}, u32[]{:S(2)}, u32[]{:S(2)}) %collective-permute-start.41) | collective-permute-done | bytes 262176 | tf_op jit(solution)/shard_map/ppermute | solution.py:30
  310.5 6.1 %collective-permute-done.42.refs_5_ = bf16[512,256]{1,0:T(8,128)(2,1)S(1)} collective-permute-done((bf16[512,256]{1,0:T(8,128)(2,1)S(1)}, bf16[512,256]{1,0:T(8,128)(2,1)S(1)}, u32[]{:S(2)}, u32[]{:S(2)}) %collective-permute-start.42) | collective-permute-done | bytes 262176 | tf_op jit(solution)/shard_map/ppermute | solution.py:30
  (170 shorter events, 62.5 us)
Async XLA Ops:
  0.0 14.3 %collective-permute-start.7 = (bf16[1024,256]{1,0:T(8,128)(2,1)}, bf16[1024,256]{1,0:T(8,128)(2,1)S(1)}, u32[]{:S(2)}, u32[]{:S(2)}) collective-permute-start(bf16[1024,256]{1,0:T(8,128)(2,1)} %bitcast.35), channel_id=1, source_target_pairs={{0,96},{1,97},{2,98},{3,99},{4,100},{5,101},{6,102},{7,103},{8,104... | collective-permute-start | bytes 1572872 | tf_op jit(solution)/shard_map/ppermute | solution.py:30
  2.8 15.2 %collective-permute-start.6 = (bf16[1024,256]{1,0:T(8,128)(2,1)}, bf16[1024,256]{1,0:T(8,128)(2,1)S(1)}, u32[]{:S(2)}, u32[]{:S(2)}) collective-permute-start(bf16[1024,256]{1,0:T(8,128)(2,1)} %bitcast.36), channel_id=1, source_target_pairs={{0,32},{1,33},{2,34},{3,35},{4,36},{5,37},{6,38},{7,39},{8,40},{9,... | collective-permute-start | bytes 1572872 | tf_op jit(solution)/shard_map/ppermute | solution.py:30
  3.9 4.9 %collective-permute-start.2 = (bf16[128,1024]{1,0:T(8,128)(2,1)S(1)}, bf16[128,1024]{1,0:T(8,128)(2,1)}, u32[]{:S(2)}, u32[]{:S(2)}) collective-permute-start(bf16[128,1024]{1,0:T(8,128)(2,1)S(1)} %get-tuple-element.151), channel_id=1, source_target_pairs={{128,224},{129,225},{130,226},{131,227},{132,228},{133,229},{134,2... | collective-permute-start | bytes 786440 | tf_op jit(solution)/shard_map/ppermute | solution.py:30
  8.8 20.5 %collective-permute-start.5 = (bf16[128,1024]{1,0:T(8,128)(2,1)}, bf16[128,1024]{1,0:T(8,128)(2,1)S(1)}, u32[]{:S(2)}, u32[]{:S(2)}) collective-permute-start(bf16[128,1024]{1,0:T(8,128)(2,1)} %collective-permute-done.2.refs_3_), channel_id=1, source_target_pairs={{128,129},{129,128},{130,131},{131,130},{132,133},{133,132},{134,1... | collective-permute-start | bytes 786440 | tf_op jit(solution)/shard_map/ppermute | solution.py:30
  9.6 19.6 %collective-permute-start.4 = (bf16[128,1024]{1,0:T(8,128)(2,1)}, bf16[128,1024]{1,0:T(8,128)(2,1)S(1)}, u32[]{:S(2)}, u32[]{:S(2)}) collective-permute-start(bf16[128,1024]{1,0:T(8,128)(2,1)} %collective-permute-done.1.refs_2_), channel_id=1, source_target_pairs={{128,129},{129,128},{130,131},{131,130},{132,133},{133,132},{134,1... | collective-permute-start | bytes 786440 | tf_op jit(solution)/shard_map/ppermute | solution.py:30
  10.3 18.9 %collective-permute-start.3 = (bf16[128,1024]{1,0:T(8,128)(2,1)}, bf16[128,1024]{1,0:T(8,128)(2,1)S(1)}, u32[]{:S(2)}, u32[]{:S(2)}) collective-permute-start(bf16[128,1024]{1,0:T(8,128)(2,1)} %collective-permute-done.refs_1_), channel_id=1, source_target_pairs={{128,129},{129,128},{130,131},{131,130},{132,133},{133,132},{134,1... | collective-permute-start | bytes 786440 | tf_op jit(solution)/shard_map/ppermute | solution.py:30
  14.3 8.6 %collective-permute-start.9 = (bf16[512,256]{1,0:T(8,128)(2,1)S(1)}, bf16[512,256]{1,0:T(8,128)(2,1)S(1)}, u32[]{:S(2)}, u32[]{:S(2)}) collective-permute-start(bf16[512,256]{1,0:T(8,128)(2,1)S(1)} %slice.41), channel_id=1, source_target_pairs={{0,96},{1,97},{2,98},{3,99},{4,100},{5,101},{6,102},{7,103},{8,104... | collective-permute-start | bytes 786440 | tf_op jit(solution)/shard_map/ppermute | solution.py:30
  18.0 8.2 %collective-permute-start.8 = (bf16[512,256]{1,0:T(8,128)(2,1)S(1)}, bf16[512,256]{1,0:T(8,128)(2,1)S(1)}, u32[]{:S(2)}, u32[]{:S(2)}) collective-permute-start(bf16[512,256]{1,0:T(8,128)(2,1)S(1)} %slice.40), channel_id=1, source_target_pairs={{0,32},{1,33},{2,34},{3,35},{4,36},{5,37},{6,38},{7,39},{8,40},{9,... | collective-permute-start | bytes 786440 | tf_op jit(solution)/shard_map/ppermute | solution.py:30
  26.2 14.9 %collective-permute-start.15 = (bf16[256,1280]{1,0:T(8,128)(2,1)S(1)}, bf16[256,1280]{1,0:T(8,128)(2,1)S(1)}, u32[]{:S(2)}, u32[]{:S(2)}) collective-permute-start(bf16[256,1280]{1,0:T(8,128)(2,1)S(1)} %pad_maximum_fusion.1.refs_6_), channel_id=1, source_target_pairs={{0,24},{1,25},{2,26},{3,27},{4,28},{5,29},{6,30},{7,31},{8,0},{9,1... | collective-permute-start | bytes 1966088 | tf_op jit(solution)/shard_map/ppermute | solution.py:30
  29.2 15.7 %collective-permute-start.13 = (bf16[256,1280]{1,0:T(8,128)(2,1)S(1)}, bf16[256,1280]{1,0:T(8,128)(2,1)S(1)}, u32[]{:S(2)}, u32[]{:S(2)}) collective-permute-start(bf16[256,1280]{1,0:T(8,128)(2,1)S(1)} %pad_maximum_fusion.1.refs_6_), channel_id=1, source_target_pairs={{0,8},{1,9},{2,10},{3,11},{4,12},{5,13},{6,14},{7,15},{8,16},{9,17... | collective-permute-start | bytes 1966088 | tf_op jit(solution)/shard_map/ppermute | solution.py:30
  34.9 10.4 %collective-permute-start.10 = (bf16[1024,256]{1,0:T(8,128)(2,1)S(1)}, bf16[1024,256]{1,0:T(8,128)(2,1)S(1)}, u32[]{:S(2)}, u32[]{:S(2)}) collective-permute-start(bf16[1024,256]{1,0:T(8,128)(2,1)S(1)} %get-tuple-element.90), channel_id=1, source_target_pairs={{128,224},{129,225},{130,226},{131,227},{132,228},{133,229},{134,2... | collective-permute-start | bytes 1572872 | tf_op jit(solution)/shard_map/ppermute | solution.py:30
  35.6 9.7 %collective-permute-start.11 = (bf16[1024,256]{1,0:T(8,128)(2,1)S(1)}, bf16[1024,256]{1,0:T(8,128)(2,1)S(1)}, u32[]{:S(2)}, u32[]{:S(2)}) collective-permute-start(bf16[1024,256]{1,0:T(8,128)(2,1)S(1)} %get-tuple-element.91), channel_id=1, source_target_pairs={{128,192},{129,193},{130,194},{131,195},{132,196},{133,197},{134,1... | collective-permute-start | bytes 1572872 | tf_op jit(solution)/shard_map/ppermute | solution.py:30
  36.3 9.0 %collective-permute-start.12 = (bf16[1024,256]{1,0:T(8,128)(2,1)S(1)}, bf16[1024,256]{1,0:T(8,128)(2,1)S(1)}, u32[]{:S(2)}, u32[]{:S(2)}) collective-permute-start(bf16[1024,256]{1,0:T(8,128)(2,1)S(1)} %get-tuple-element.92), channel_id=1, source_target_pairs={{128,160},{129,161},{130,162},{131,163},{132,164},{133,165},{134,1... | collective-permute-start | bytes 1572872 | tf_op jit(solution)/shard_map/ppermute | solution.py:30
  41.1 8.4 %collective-permute-start.16 = (bf16[128,1280]{1,0:T(8,128)(2,1)S(1)}, bf16[128,1280]{1,0:T(8,128)(2,1)S(1)}, u32[]{:S(2)}, u32[]{:S(2)}) collective-permute-start(bf16[128,1280]{1,0:T(8,128)(2,1)S(1)} %slice.43), channel_id=1, source_target_pairs={{0,24},{1,25},{2,26},{3,27},{4,28},{5,29},{6,30},{7,31},{8,0},{9,1... | collective-permute-start | bytes 983048 | tf_op jit(solution)/shard_map/ppermute | solution.py:30
  44.9 8.5 %collective-permute-start.14 = (bf16[128,1280]{1,0:T(8,128)(2,1)S(1)}, bf16[128,1280]{1,0:T(8,128)(2,1)S(1)}, u32[]{:S(2)}, u32[]{:S(2)}) collective-permute-start(bf16[128,1280]{1,0:T(8,128)(2,1)S(1)} %slice.42), channel_id=1, source_target_pairs={{0,8},{1,9},{2,10},{3,11},{4,12},{5,13},{6,14},{7,15},{8,16},{9,17... | collective-permute-start | bytes 983048 | tf_op jit(solution)/shard_map/ppermute | solution.py:30
  54.6 62.5 %collective-permute-start.20 = (bf16[4,256,1280]{2,1,0:T(8,128)(2,1)S(1)}, bf16[4,256,1280]{2,1,0:T(8,128)(2,1)S(1)}, u32[]{:S(2)}, u32[]{:S(2)}) collective-permute-start(bf16[4,256,1280]{2,1,0:T(8,128)(2,1)S(1)} %bitcast.22), channel_id=1, source_target_pairs={{0,96},{1,97},{2,98},{3,99},{4,100},{5,101},{6,102},{7,103},{8,104... | collective-permute-start | bytes 7864328 | tf_op jit(solution)/shard_map/ppermute | solution.py:30
  57.0 60.2 %collective-permute-start.19 = (bf16[4,256,1280]{2,1,0:T(8,128)(2,1)S(1)}, bf16[4,256,1280]{2,1,0:T(8,128)(2,1)S(1)}, u32[]{:S(2)}, u32[]{:S(2)}) collective-permute-start(bf16[4,256,1280]{2,1,0:T(8,128)(2,1)S(1)} %bitcast.23), channel_id=1, source_target_pairs={{0,32},{1,33},{2,34},{3,35},{4,36},{5,37},{6,38},{7,39},{8,40},{9,... | collective-permute-start | bytes 7864328 | tf_op jit(solution)/shard_map/ppermute | solution.py:30
  61.9 55.2 %collective-permute-start.18 = (bf16[4,1024,256]{2,1,0:T(8,128)(2,1)S(1)}, bf16[4,1024,256]{2,1,0:T(8,128)(2,1)S(1)}, u32[]{:S(2)}, u32[]{:S(2)}) collective-permute-start(bf16[4,1024,256]{2,1,0:T(8,128)(2,1)S(1)} %bitcast.25), channel_id=1, source_target_pairs={{0,24},{1,25},{2,26},{3,27},{4,28},{5,29},{6,30},{7,31},{8,0},{9,1... | collective-permute-start | bytes 6291464 | tf_op jit(solution)/shard_map/ppermute | solution.py:30
  63.9 53.3 %collective-permute-start.17 = (bf16[4,1024,256]{2,1,0:T(8,128)(2,1)S(1)}, bf16[4,1024,256]{2,1,0:T(8,128)(2,1)S(1)}, u32[]{:S(2)}, u32[]{:S(2)}) collective-permute-start(bf16[4,1024,256]{2,1,0:T(8,128)(2,1)S(1)} %bitcast.26), channel_id=1, source_target_pairs={{0,8},{1,9},{2,10},{3,11},{4,12},{5,13},{6,14},{7,15},{8,16},{9,17... | collective-permute-start | bytes 6291464 | tf_op jit(solution)/shard_map/ppermute | solution.py:30
  119.5 34.9 %collective-permute-start.24 = (bf16[2,256,1280]{2,1,0:T(8,128)(2,1)S(1)}, bf16[2,256,1280]{2,1,0:T(8,128)(2,1)S(1)}, u32[]{:S(2)}, u32[]{:S(2)}) collective-permute-start(bf16[2,256,1280]{2,1,0:T(8,128)(2,1)S(1)} %slice.37), channel_id=1, source_target_pairs={{0,96},{1,97},{2,98},{3,99},{4,100},{5,101},{6,102},{7,103},{8,104... | collective-permute-start | bytes 3932168 | tf_op jit(solution)/shard_map/ppermute | solution.py:30
  121.7 33.9 %collective-permute-start.23 = (bf16[2,256,1280]{2,1,0:T(8,128)(2,1)S(1)}, bf16[2,256,1280]{2,1,0:T(8,128)(2,1)S(1)}, u32[]{:S(2)}, u32[]{:S(2)}) collective-permute-start(bf16[2,256,1280]{2,1,0:T(8,128)(2,1)S(1)} %slice.36), channel_id=1, source_target_pairs={{0,32},{1,33},{2,34},{3,35},{4,36},{5,37},{6,38},{7,39},{8,40},{9,... | collective-permute-start | bytes 3932168 | tf_op jit(solution)/shard_map/ppermute | solution.py:30
  125.5 28.9 %collective-permute-start.22 = (bf16[2,1024,256]{2,1,0:T(8,128)(2,1)S(1)}, bf16[2,1024,256]{2,1,0:T(8,128)(2,1)S(1)}, u32[]{:S(2)}, u32[]{:S(2)}) collective-permute-start(bf16[2,1024,256]{2,1,0:T(8,128)(2,1)S(1)} %slice.35), channel_id=1, source_target_pairs={{0,24},{1,25},{2,26},{3,27},{4,28},{5,29},{6,30},{7,31},{8,0},{9,1... | collective-permute-start | bytes 3145736 | tf_op jit(solution)/shard_map/ppermute | solution.py:30
  130.8 23.7 %collective-permute-start.21 = (bf16[2,1024,256]{2,1,0:T(8,128)(2,1)S(1)}, bf16[2,1024,256]{2,1,0:T(8,128)(2,1)S(1)}, u32[]{:S(2)}, u32[]{:S(2)}) collective-permute-start(bf16[2,1024,256]{2,1,0:T(8,128)(2,1)S(1)} %slice.34), channel_id=1, source_target_pairs={{0,8},{1,9},{2,10},{3,11},{4,12},{5,13},{6,14},{7,15},{8,16},{9,17... | collective-permute-start | bytes 3145736 | tf_op jit(solution)/shard_map/ppermute | solution.py:30
  168.4 36.3 %collective-permute-start.33 = (bf16[512,256]{1,0:T(8,128)(2,1)S(1)}, bf16[512,256]{1,0:T(8,128)(2,1)S(1)}, u32[]{:S(2)}, u32[]{:S(2)}) collective-permute-start(bf16[512,256]{1,0:T(8,128)(2,1)S(1)} %shard_map.98), channel_id=1, source_target_pairs={{128,0},{129,1},{130,32},{131,33},{132,64},{133,65},{134,96},{135,... | collective-permute-start | bytes 786440 | tf_op jit(solution)/shard_map/ppermute | solution.py:30
  204.8 15.3 %collective-permute-start.36 = (bf16[512,256]{1,0:T(8,128)(2,1)S(1)}, bf16[512,256]{1,0:T(8,128)(2,1)S(1)}, u32[]{:S(2)}, u32[]{:S(2)}) collective-permute-start(bf16[512,256]{1,0:T(8,128)(2,1)S(1)} %collective-permute-done.33.refs_1_.refs_6_), channel_id=1, source_target_pairs={{0,6},{1,7},{2,4},{3,5},{4,2},{5,3},{6,0},{7,1},{8,14},{9,15},{10,... | collective-permute-start | bytes 786440 | tf_op jit(solution)/shard_map/ppermute | solution.py:30
  207.7 13.8 %collective-permute-start.35 = (bf16[512,256]{1,0:T(8,128)(2,1)S(1)}, bf16[512,256]{1,0:T(8,128)(2,1)S(1)}, u32[]{:S(2)}, u32[]{:S(2)}) collective-permute-start(bf16[512,256]{1,0:T(8,128)(2,1)S(1)} %collective-permute-done.33.refs_1_.refs_6_), channel_id=1, source_target_pairs={{0,4},{1,5},{2,6},{3,7},{4,0},{5,1},{6,2},{7,3},{8,12},{9,13},{10,... | collective-permute-start | bytes 786440 | tf_op jit(solution)/shard_map/ppermute | solution.py:30
  209.6 11.9 %collective-permute-start.34 = (bf16[512,256]{1,0:T(8,128)(2,1)S(1)}, bf16[512,256]{1,0:T(8,128)(2,1)S(1)}, u32[]{:S(2)}, u32[]{:S(2)}) collective-permute-start(bf16[512,256]{1,0:T(8,128)(2,1)S(1)} %collective-permute-done.33.refs_1_.refs_6_), channel_id=1, source_target_pairs={{0,2},{1,3},{2,0},{3,1},{4,6},{5,7},{6,4},{7,5},{8,10},{9,11},{10,... | collective-permute-start | bytes 786440 | tf_op jit(solution)/shard_map/ppermute | solution.py:30
  231.7 24.6 %all-to-all-start.2 = ((bf16[16,80,128]{2,1,0:T(8,128)(2,1)}), bf16[16,80,128]{2,1,0:T(8,128)(2,1)S(1)}, u32[]{:S(2)}, u32[]{:S(2)}) async-start(bf16[16,80,128]{2,1,0:T(8,128)(2,1)} %get-tuple-element.141), calls=%async_computation.2 | async-start | bytes 655360 | tf_op jit(solution)/shard_map/all_to_all | solution.py:411
  279.9 4.6 %collective-permute-start.39 = (bf16[4,512,256]{2,1,0:T(8,128)(2,1)S(1)}, bf16[4,512,256]{2,1,0:T(8,128)(2,1)S(1)}, u32[]{:S(2)}, u32[]{:S(2)}) collective-permute-start(bf16[4,512,256]{2,1,0:T(8,128)(2,1)S(1)} %get-tuple-element.146), channel_id=1, source_target_pairs={{0,1},{1,0},{2,3},{3,2},{4,5},{5,4},{6,7},{7,6},{8,9},{9,8},{10,11... | collective-permute-start | bytes 3145736 | tf_op jit(solution)/shard_map/ppermute | solution.py:30
  284.7 14.1 %collective-permute-start.40 = (bf16[512,256]{1,0:T(8,128)(2,1)S(1)}, bf16[512,256]{1,0:T(8,128)(2,1)S(1)}, u32[]{:S(2)}, u32[]{:S(2)}) collective-permute-start(bf16[512,256]{1,0:T(8,128)(2,1)S(1)} %get-tuple-element.147), channel_id=1, source_target_pairs={{0,2},{1,3},{2,0},{3,1},{4,6},{5,7},{6,4},{7,5},{8,10},{9,11},{10,... | collective-permute-start | bytes 786440 | tf_op jit(solution)/shard_map/ppermute | solution.py:30
  290.1 20.4 %collective-permute-start.41 = (bf16[512,256]{1,0:T(8,128)(2,1)S(1)}, bf16[512,256]{1,0:T(8,128)(2,1)S(1)}, u32[]{:S(2)}, u32[]{:S(2)}) collective-permute-start(bf16[512,256]{1,0:T(8,128)(2,1)S(1)} %get-tuple-element.148), channel_id=1, source_target_pairs={{0,4},{1,5},{2,6},{3,7},{4,0},{5,1},{6,2},{7,3},{8,12},{9,13},{10,... | collective-permute-start | bytes 786440 | tf_op jit(solution)/shard_map/ppermute | solution.py:30
  292.6 24.1 %collective-permute-start.42 = (bf16[512,256]{1,0:T(8,128)(2,1)S(1)}, bf16[512,256]{1,0:T(8,128)(2,1)S(1)}, u32[]{:S(2)}, u32[]{:S(2)}) collective-permute-start(bf16[512,256]{1,0:T(8,128)(2,1)S(1)} %get-tuple-element.149), channel_id=1, source_target_pairs={{0,6},{1,7},{2,4},{3,5},{4,2},{5,3},{6,0},{7,1},{8,14},{9,15},{10,... | collective-permute-start | bytes 786440 | tf_op jit(solution)/shard_map/ppermute | solution.py:30
  (48 other events, 1662.9 us)

commit v5 on v4

--- a/solution.py
+++ b/solution.py
@@ -1,3 +1,5 @@
+import functools
+
 import jax
 import jax.numpy as jnp
 from jax import lax
@@ -116,7 +118,8 @@
             results[i] = held[len(remote) + n]
         body(*first, *ins, *results, *extra)
         for operand in late:
-            operand[...] if not operand.waited else None
+            if not operand.waited:
+                operand[...]
         copies = [
             pltpu.make_async_copy(results[i], targets[i], sems.at[len(remote) + n])
             for n, i in enumerate(away)
@@ -202,14 +205,15 @@
         entry[:, both] = flat.T.astype(bf16)
 
 
-def rows_body(at, u1, u2, u3, v1, v2, v3, w1, wl, wh, w3, w0, whole, o0, o1, o2, o3, piece, u):
+def rows_body(at, own, u1, u2, v2, u3, w1, wl, wh, w3, w0, o0, o1, o2, o3, piece, u):
     x, y, z, core = at[0], at[1], at[2], at[3]
     fine = w1.shape[1]
-    rows = u1.shape[0]
-    for k, mine, theirs in ((1, u1, v1), (2, u2, v2), (3, u3, v3)):
-        u[k, span(core, rows), :] = mine[...]
-        u[k, span(1 - core, rows), :] = theirs[...]
-    u[0] = whole[:, span(x, u.shape[2])]
+    half = u2.shape[0]
+    u[0] = own[...]
+    u[1] = u1[...]
+    u[2, span(core, half), :] = u2[...]
+    u[2, span(1 - core, half), :] = v2[...]
+    u[3] = u3[...]
     piece[...] = u[behind(x, x ^ z), :, span(core, piece.shape[0])].astype(f32).T.astype(bf16)
     for k, out in enumerate((o0, o1, o2, o3)):
         total = None
@@ -246,15 +250,15 @@
 
 
 def lower_body(
-    at, p0, p1, p2, p3, other, w0, w1, wl, wh, w3, leading, c_rows, totals, grad, states, u
+    at, a0, a1, a2, a3, b0, b1, b2, b3, other_a, other_b, w0, w1, wl, wh, w3, leading, c_rows, totals, grad, states, u
 ):
     x, y, z, core = at[0], at[1], at[2], at[3]
-    share = p0.shape[0]
-    fine = share * CORES // SIDE
-    for q, part in enumerate((p0, p1, p2, p3)):
+    fine = a0.shape[0]
+    for q in range(SIDE):
         base = (z ^ q) * CORES
-        u[span(base + core, share), :] = part[...]
-        u[span(base + 1 - core, share), :] = other[q]
+        for i, (parts, other) in enumerate((((a0, a1, a2, a3), other_a), ((b0, b1, b2, b3), other_b))):
+            u[span((base + core) * 2 + i, fine), :] = parts[q][...]
+            u[span((base + 1 - core) * 2 + i, fine), :] = other[q]
     total = None
     for k in range(SIDE):
         for j in range(SIDE):
@@ -303,13 +307,15 @@
     out[inner + size :, :] = (grad_c + dot(b_cols[...], rounded, 1, 1)).astype(bf16)
 
 
-def to_halves(u, q, core, keep, give):
+def to_halves(u, q, core, keep, gives):
     share = keep.shape[1]
     keep[q] = u[span(core, share), :]
-    give[q] = u[span(1 - core, share), :]
-
-
-def back_body(at, g0, g1, gl, gh, g3, w0, w1, wl, wh, w3, keep, give, u, g2):
+    part = share // len(gives)
+    for i, give in enumerate(gives):
+        give[q] = u[span((1 - core) * len(gives) + i, part), :]
+
+
+def back_body(at, g0, g1, gl, gh, g3, w0, w1, wl, wh, w3, keep, give_a, give_b, u, g2):
     x, y, z, core = at[0], at[1], at[2], at[3]
     fine = w0.shape[0]
     g2[: gl.shape[0], :] = gl[...]
@@ -322,7 +328,7 @@
             else:
                 term = dot(w[...], g[...], 1, 0)
             u[k, rows, :] = term.astype(bf16)
-        to_halves(u.at[k], z ^ x ^ behind(x, k), core, keep, give)
+        to_halves(u.at[k], z ^ x ^ behind(x, k), core, keep, (give_a, give_b))
 
 
 def whole_body(at, g, w0, w1, wl, wh, w3, keep, give, u):
@@ -332,27 +338,35 @@
         for j in range(SIDE):
             w = (w0, w1, wl if j < CORES else wh, w3)[k][j % CORES if k == 2 else j]
             u[k, span(behind(y, j), fine), :] = dot(w, g[...], 1, 0).astype(bf16)
-        to_halves(u.at[k], z ^ behind(x, k), core, keep, give)
-
-
-def pair_body(keep, got, s1, s2, s3):
+        to_halves(u.at[k], z ^ behind(x, k), core, keep, (give,))
+
+
+def rows_of(keep, q, got, part):
+    size = got.shape[1]
+    return keep[q, part * size : (part + 1) * size, :].astype(f32) + got[q].astype(f32)
+
+
+def pair_body(part, keep, got, s1, s2, s3):
     for q, out in ((1, s1), (2, s2), (3, s3)):
-        out[...] = (keep[q].astype(f32) + got[q].astype(f32)).astype(bf16)
-
-
-def total_of(keep, got, received, upstream):
-    total = keep[0].astype(f32) + got[0].astype(f32)
+        out[...] = rows_of(keep, q, got, part).astype(bf16)
+
+
+def total_of(part, keep, got, received, upstream):
+    total = rows_of(keep, 0, got, part)
     for r in received:
         total = total + r[...].astype(f32)
-    return total + upstream[...].astype(f32)
-
-
-def total_body(keep, got, r1, r2, r3, upstream, out):
-    out[...] = total_of(keep, got, (r1, r2, r3), upstream).astype(bf16)
-
-
-def result_body(at, keep, got, r1, r2, r3, upstream, settled, out):
-    total = total_of(keep, got, (r1, r2, r3), upstream).astype(bf16).astype(f32)
+    return total + upstream.astype(f32)
+
+
+def total_body(part, keep, got, r1, r2, r3, upstream, out):
+    size = out.shape[0]
+    own = upstream[part * size : (part + 1) * size, :]
+    out[...] = total_of(part, keep, got, (r1, r2, r3), own).astype(bf16)
+
+
+def result_body(at, keep, got, r1, r2, r3, upper, lower, settled, out):
+    upstream = jnp.concatenate([upper[...], lower[...]], axis=0)
+    total = total_of(0, keep, got, (r1, r2, r3), upstream).astype(bf16).astype(f32)
     chosen = jnp.where(at[4] == 1, settled[...].astype(f32), total)
     out[0] = chosen.T.astype(bf16)
 
@@ -377,11 +391,13 @@
 
     out_sides = sides(w_out[0], first_step, BOTH)
     out_far = far(out_sides, first_step, BOTH, 0)
-    mine = []
-    for k in steps:
-        piece = lax.dynamic_slice(grad_out, (half * core, block * ((x + k) % SIDE)), (half, block))
-        mine.append(routed(piece, along_x(k), (1,)))
-    theirs = [routed(piece, other_core, (1,)) for piece in mine]
+    pieces = []
+    for k in range(SIDE):
+        low, count = (half * core, half) if k == 2 else (0, rows)
+        pieces.append(lax.dynamic_slice(grad_out, (low, block * ((x + k) % SIDE)), (count, block)))
+    own, *pieces = tie(pieces)
+    before, across, after = [routed(p, along_x(k), (1,)) for k, p in zip(steps, pieces)]
+    upstream = [own, before, across, routed(across, other_core, (1,)), after]
 
     back = jnp.concatenate([w_in[0], w_bc[0]], axis=1)
     out_far, back = tie((out_far, back))
@@ -433,17 +449,17 @@
     chunk = struct((share, rows))
     chunks = struct((SIDE, share, rows))
 
-    def over_heads(keep, give, sections):
+    def over_heads(keep, give, sections, part=0):
         got = routed(give, other_core, sections)
-        sent = call(pair_body, [chunk] * 3, [keep, got])
+        sent = call(functools.partial(pair_body, part), [struct(give.shape[1:])] * 3, [keep, got])
         return [keep, got] + [routed(s, across_z(k), sections) for k, s in zip(steps, sent)]
 
     *partial, own = call(
         rows_body,
         [struct((inner, rows))] * SIDE + [chunk],
-        [*mine, *theirs, out_sides[0], *out_far, out_sides[1], w_out[0], grad_out],
+        [*upstream, out_sides[0], *out_far, out_sides[1], w_out[0]],
         at,
-        remote=(10, 11),
+        remote=(9,),
         scratch=[pltpu.VMEM((SIDE, rows, block), bf16)],
         flops=2 * SIDE * rows * block * inner,
     )
@@ -451,7 +467,9 @@
     received = [routed(partial[k], along_x(-k), (1,)) for k in steps]
     back_far = far(back_sides, along_y, BOTH, 0)
     out_set = jnp.concatenate([w_out[0], out_sides[0], *out_far, out_sides[1]]).reshape(SIDE, inner, -1)
-    received, back_far, out_set = tie((received, back_far, out_set))
+    back_far, out_set = tie((back_far, out_set))
+    whole_sides = sides(out_set, along_y, (0,))
+    received, back_far = tie((received, back_far))
     back_set = jnp.concatenate([back, back_sides[0], *back_far, back_sides[1]]).reshape(SIDE, -1, outer)
     grad_ssd, states = call(
         sum_body,
@@ -462,9 +480,8 @@
         flops=2 * rows * inner * state_size,
     )
 
-    states, out_set, back_set = tie((states, out_set, back_set))
+    states, back_set = tie((states, back_set))
     arrived = exchange(states)
-    whole_sides = sides(out_set, along_y, (0,))
     width_sides = sides(back_set, along_x, (0,))
     arrived, whole_sides, width_sides = tie((arrived, whole_sides, width_sides))
     exits = scanned(arrived)
@@ -478,9 +495,10 @@
     grads_sides = sides(grads, along_x, (1,))
     grads_far = far(grads_sides, along_x, (1,), 0)
     wide = [pltpu.VMEM((SIDE, block, rows), bf16)]
-    keep, give = call(
+    halves = struct((SIDE, share // 2, rows))
+    keep, *gives = call(
         back_body,
-        [chunks, chunks],
+        [chunks, halves, halves],
         [
             grads, grads_sides[0], *grads_far, grads_sides[1],
             back, back_sides[0], *back_far, back_sides[1],
@@ -489,21 +507,23 @@
         scratch=wide + [pltpu.VMEM((outer, rows), bf16)],
         flops=2 * SIDE * rows * block * outer,
     )
-    sums = over_heads(keep, give, (1,))
-    (middle,) = call(total_body, [chunk], [*sums, own])
-
-    arrived = routed(middle, hop(0), (1,))
-    settled = routed(middle, hop(None), (1,))
-
-    parts = [arrived] + [routed(arrived, across_z(k), (0,)) for k in steps]
-    other = routed(jnp.stack(parts), other_core, (0,))
+    middle = []
+    for i, give in enumerate(gives):
+        sums = over_heads(keep, give, (1,), i)
+        middle += call(functools.partial(total_body, i), [struct((share // 2, rows))], [*sums, own])
+
+    arrived = [routed(m, hop(0), (1,)) for m in middle]
+    settled = routed(jnp.concatenate(middle), hop(None), (1,))
+
+    parts = [[a] + [routed(a, across_z(k), (0,)) for k in steps] for a in arrived]
+    others = [routed(jnp.stack(p), other_core, (0,)) for p in parts]
     grad_ssd, states = call(
         lower_body,
         [struct((inner, rows)), state_shape],
-        [*parts, other, out_set, whole_sides[0], *whole_far, whole_sides[1], leading, c_rows, totals],
+        [*parts[0], *parts[1], *others, out_set, whole_sides[0], *whole_far, whole_sides[1], leading, c_rows, totals],
         at,
         scratch=[pltpu.VMEM((width, rows), bf16)],
-        remote=range(10, 13),
+        remote=range(15, 18),
         away=(0, 1),
         flops=2 * rows * width * inner,
     )
@@ -518,7 +538,7 @@
         flops=2 * rows * width * outer,
     )
     sums = over_heads(keep, give, (0,))
-    (result,) = call(result_body, [struct((1, rows, share))], [*sums, arrived, settled], at)
+    (result,) = call(result_body, [struct((1, rows, share))], [*sums, *arrived, settled], at)
     return result
 
 

time: 319 us -> 306 us (0.959)
  waiting for transfers between devices: 96.3 us -> 63 us
  starting transfers between devices: 93.2 us -> 107 us
  local copies, waits for them, and re-layouts: 12.8 us -> 16.2 us
    ppermute x43 -> x50, waiting for transfers between devices: 87.6 us -> 54.3 us  [routed(): return lax.ppermute(value, AXES, pairs)]
    ppermute x43 -> x50, starting transfers between devices: 78 us -> 93.6 us  [routed(): return lax.ppermute(value, AXES, pairs)]
    pallas_call x14 -> x16, Pallas kernels: 29.8 us -> 29.8 us  [call(): pl.pallas_call(kernel, in_specs=[pl.BlockSpec(memory_space=pltpu.SMEM)] *...]
  transfers between devices with their start and end apart: 44 -> 51, of which waited for: 14 -> 14; matrix products, arithmetic and copies ran while one was open for 1% -> 2% of each run, Pallas kernels for 2% -> 2%
where the time goes in v5:
time: 306 us; the launch traced here: 304 us
  starting transfers between devices  107 us (35%)
  blocking collectives  85.3 us (28%)
  waiting for transfers between devices  63 us (21%)
  Pallas kernels  29.8 us (10%)
  local copies, waits for them, and re-layouts  16.2 us (5%)
    ppermute x50, starting transfers between devices, routed(): return lax.ppermute(value, AXES, pairs)  93.6 us
    all_to_all x3, blocking collectives, exchange(): return lax.all_to_all(states, 'ctx', 0, 0)  85.3 us
    ppermute x50, waiting for transfers between devices, routed(): return lax.ppermute(value, AXES, pairs)  54.3 us
    pallas_call x16, Pallas kernels, call(): pl.pallas_call(kernel, in_specs=[pl.BlockSpec(memory_space=pltpu.SMEM)] *...  29.8 us
    all_to_all x1, starting transfers between devices, exchange(): return lax.all_to_all(states, 'ctx', 0, 0)  13.3 us
    unnamed x80, local copies, waits for them, and re-layouts  11.4 us
    all_to_all x1, waiting for transfers between devices, exchange(): return lax.all_to_all(states, 'ctx', 0, 0)  8.74 us
  transfers between devices with their start and end apart: 51, of which 14 were waited for; matrix products, arithmetic and copies ran while one was open for 2% of the time, Pallas kernels for 2%

profile of v5, /device:TPU:32, one launch (start us, length us, event | category | flops | bytes accessed | tf_op | source)
XLA Modules:
  0.0 304.2 jit_solution(12899693583154778716)
XLA Ops:
  14.3 3.7 %collective-permute-start.7 = (bf16[512,256]{1,0:T(8,128)(2,1)S(1)}, bf16[512,256]{1,0:T(8,128)(2,1)S(1)}, u32[]{:S(2)}, u32[]{:S(2)}) collective-permute-start(bf16[512,256]{1,0:T(8,128)(2,1)S(1)} %slice.41), channel_id=1, source_target_pairs={{0,96},{1,97},{2,98},{3,99},{4,100},{5,101},{6,102},{7,103},{8,104... | collective-permute-start | bytes 786440 | tf_op jit(solution)/shard_map/ppermute | solution.py:32
  26.5 3.1 %collective-permute-start.13 = (bf16[256,1280]{1,0:T(8,128)(2,1)S(1)}, bf16[256,1280]{1,0:T(8,128)(2,1)S(1)}, u32[]{:S(2)}, u32[]{:S(2)}) collective-permute-start(bf16[256,1280]{1,0:T(8,128)(2,1)S(1)} %pad_maximum_fusion.refs_6_), channel_id=1, source_target_pairs={{0,24},{1,25},{2,26},{3,27},{4,28},{5,29},{6,30},{7,31},{8,0},{9,1... | collective-permute-start | bytes 1966088 | tf_op jit(solution)/shard_map/ppermute | solution.py:32
  29.8 4.0 %shard_map.92 = (bf16[1024,256]{1,0:T(8,128)(2,1)S(1)}, bf16[1024,256]{1,0:T(8,128)(2,1)S(1)}, bf16[1024,256]{1,0:T(8,128)(2,1)S(1)}, bf16[1024,256]{1,0:T(8,128)(2,1)S(1)}, bf16[512,256]{1,0:T(8,128)(2,1)S(1)}) custom-call(s32[5]{0:T(128)S(1)} %copy-done.33, bf16[256,1024]{1,0:T(8,128)(2,1)S(1)} %copy-done.20, ...), custom_call_target="tpu_custom_call" | custom-call | flops 2147483648 | bytes 6553600 | tf_op jit(solution)/shard_map/pallas_call | solution.py:132
  36.0 6.4 %collective-permute-done.13.refs_10_ = bf16[256,1280]{1,0:T(8,128)(2,1)S(1)} collective-permute-done((bf16[256,1280]{1,0:T(8,128)(2,1)S(1)}, bf16[256,1280]{1,0:T(8,128)(2,1)S(1)}, u32[]{:S(2)}, u32[]{:S(2)}) %collective-permute-start.13) | collective-permute-done | bytes 655392 | tf_op jit(solution)/shard_map/ppermute | solution.py:32
  42.5 3.8 %collective-permute-start.14 = (bf16[128,1280]{1,0:T(8,128)(2,1)S(1)}, bf16[128,1280]{1,0:T(8,128)(2,1)S(1)}, u32[]{:S(2)}, u32[]{:S(2)}) collective-permute-start(bf16[128,1280]{1,0:T(8,128)(2,1)S(1)} %slice.43), channel_id=1, source_target_pairs={{0,24},{1,25},{2,26},{3,27},{4,28},{5,29},{6,30},{7,31},{8,0},{9,1... | collective-permute-start | bytes 983048 | tf_op jit(solution)/shard_map/ppermute | solution.py:32
  46.7 4.5 %collective-permute-done.14.refs_9_ = bf16[128,1280]{1,0:T(8,128)(2,1)S(1)} collective-permute-done((bf16[128,1280]{1,0:T(8,128)(2,1)S(1)}, bf16[128,1280]{1,0:T(8,128)(2,1)S(1)}, u32[]{:S(2)}, u32[]{:S(2)}) %collective-permute-start.14) | collective-permute-done | bytes 327712 | tf_op jit(solution)/shard_map/ppermute | solution.py:32
  51.2 3.7 %collective-permute-done.12.refs_8_ = bf16[128,1280]{1,0:T(8,128)(2,1)S(1)} collective-permute-done((bf16[128,1280]{1,0:T(8,128)(2,1)S(1)}, bf16[128,1280]{1,0:T(8,128)(2,1)S(1)}, u32[]{:S(2)}, u32[]{:S(2)}) %collective-permute-start.12) | collective-permute-done | bytes 327712 | tf_op jit(solution)/shard_map/ppermute | solution.py:32
  56.0 4.1 %collective-permute-start.18 = (bf16[4,256,1280]{2,1,0:T(8,128)(2,1)S(1)}, bf16[4,256,1280]{2,1,0:T(8,128)(2,1)S(1)}, u32[]{:S(2)}, u32[]{:S(2)}) collective-permute-start(bf16[4,256,1280]{2,1,0:T(8,128)(2,1)S(1)} %bitcast.26), channel_id=1, source_target_pairs={{0,96},{1,97},{2,98},{3,99},{4,100},{5,101},{6,102},{7,103},{8,104... | collective-permute-start | bytes 7864328 | tf_op jit(solution)/shard_map/ppermute | solution.py:32
  65.5 3.9 %collective-permute-start.15 = (bf16[4,1024,256]{2,1,0:T(8,128)(2,1)S(1)}, bf16[4,1024,256]{2,1,0:T(8,128)(2,1)S(1)}, u32[]{:S(2)}, u32[]{:S(2)}) collective-permute-start(bf16[4,1024,256]{2,1,0:T(8,128)(2,1)S(1)} %bitcast.30), channel_id=1, source_target_pairs={{0,8},{1,9},{2,10},{3,11},{4,12},{5,13},{6,14},{7,15},{8,16},{9,17... | collective-permute-start | bytes 6291464 | tf_op jit(solution)/shard_map/ppermute | solution.py:32
  69.4 51.3 %all_to_all.20.refs_0_ = bf16[16,80,128]{2,1,0:T(8,128)(2,1)S(1)} all-to-all(bf16[16,80,128]{2,1,0:T(8,128)(2,1)S(1)} %get-tuple-element.124), channel_id=1, replica_groups=mesh['section'=2,'ctx'=16,'heads'=8] {'ctx'}, dimensions={0} | all-to-all | bytes 655360 | tf_op jit(solution)/shard_map/all_to_all | solution.py:427
  125.2 3.7 %collective-permute-start.21 = (bf16[2,256,1280]{2,1,0:T(8,128)(2,1)S(1)}, bf16[2,256,1280]{2,1,0:T(8,128)(2,1)S(1)}, u32[]{:S(2)}, u32[]{:S(2)}) collective-permute-start(bf16[2,256,1280]{2,1,0:T(8,128)(2,1)S(1)} %slice.36), channel_id=1, source_target_pairs={{0,32},{1,33},{2,34},{3,35},{4,36},{5,37},{6,38},{7,39},{8,40},{9,... | collective-permute-start | bytes 3932168 | tf_op jit(solution)/shard_map/ppermute | solution.py:32
  129.1 5.2 %collective-permute-start.20 = (bf16[2,1024,256]{2,1,0:T(8,128)(2,1)S(1)}, bf16[2,1024,256]{2,1,0:T(8,128)(2,1)S(1)}, u32[]{:S(2)}, u32[]{:S(2)}) collective-permute-start(bf16[2,1024,256]{2,1,0:T(8,128)(2,1)S(1)} %slice.35), channel_id=1, source_target_pairs={{0,24},{1,25},{2,26},{3,27},{4,28},{5,29},{6,30},{7,31},{8,0},{9,1... | collective-permute-start | bytes 3145736 | tf_op jit(solution)/shard_map/ppermute | solution.py:32
  136.2 21.9 %all_to_all.21 = bf16[16,64,128]{2,1,0:T(8,128)(2,1)S(1)} all-to-all(bf16[16,64,128]{2,1,0:T(8,128)(2,1)S(1)} %shard_map.94), channel_id=1, replica_groups=mesh['section'=2,'ctx'=16,'heads'=8] {'ctx'}, dimensions={0} | all-to-all | bytes 524288 | tf_op jit(solution)/shard_map/all_to_all | solution.py:427
  158.3 3.1 %shard_map.95.refs_1_ = bf16[1280,256]{1,0:T(8,128)(2,1)S(1)} custom-call(bf16[1024,256]{1,0:T(8,128)(2,1)S(1)} %get-tuple-element.119.refs_0_, f32[16,256]{1,0:T(8,128)S(1)} %get-tuple-element.116.refs_4_.refs_1_.refs_16_, bf16[128,1024]{1,0:T(8,128)(2,1)S(1)} %get-tuple-element.120.refs_2_, bf16[1024,128]{1,0:T(8,128)(2,1)S(1)} %bitcast.34, ...), custom_call_target="tpu_custom_call" | custom-call | flops 268435456 | bytes 7127040 | tf_op jit(solution)/shard_map/pallas_call | solution.py:132
  164.3 3.6 %shard_map.96 = (bf16[4,512,256]{2,1,0:T(8,128)(2,1)S(1)}, bf16[4,256,256]{2,1,0:T(8,128)(2,1)S(1)}, bf16[4,256,256]{2,1,0:T(8,128)(2,1)S(1)}) custom-call(s32[5]{0:T(128)S(1)} %copy-done.33, bf16[1280,256]{1,0:T(8,128)(2,1)S(1)} %shard_map.95.refs_1_, bf16[1280,256]{1,0:T(8,128)(2,1)S(1)} %collective-permute-done.23.refs_2_, ...), custom_call_target="tpu_custom_call" | custom-call | flops 2684354560 | bytes 7340032 | tf_op jit(solution)/shard_map/pallas_call | solution.py:132
  176.4 10.7 %collective-permute-done.31.refs_1_.refs_6_ = bf16[256,256]{1,0:T(8,128)(2,1)S(1)} collective-permute-done((bf16[256,256]{1,0:T(8,128)(2,1)S(1)}, bf16[256,256]{1,0:T(8,128)(2,1)S(1)}, u32[]{:S(2)}, u32[]{:S(2)}) %collective-permute-start.31) | collective-permute-done | bytes 131104 | tf_op jit(solution)/shard_map/ppermute | solution.py:32
  187.1 5.5 %collective-permute-start.34 = (bf16[256,256]{1,0:T(8,128)(2,1)S(1)}, bf16[256,256]{1,0:T(8,128)(2,1)S(1)}, u32[]{:S(2)}, u32[]{:S(2)}) collective-permute-start(bf16[256,256]{1,0:T(8,128)(2,1)S(1)} %collective-permute-done.31.refs_1_.refs_6_), channel_id=1, source_target_pairs={{0,6},{1,7},{2,4},{3,5},{4,2},{5,3},{6,0},{7,1},{8,14},{9,15},{10,... | collective-permute-start | bytes 393224 | tf_op jit(solution)/shard_map/ppermute | solution.py:32
  194.5 3.4 %collective-permute-start.32 = (bf16[256,256]{1,0:T(8,128)(2,1)S(1)}, bf16[256,256]{1,0:T(8,128)(2,1)S(1)}, u32[]{:S(2)}, u32[]{:S(2)}) collective-permute-start(bf16[256,256]{1,0:T(8,128)(2,1)S(1)} %collective-permute-done.31.refs_1_.refs_6_), channel_id=1, source_target_pairs={{0,2},{1,3},{2,0},{3,1},{4,6},{5,7},{6,4},{7,5},{8,10},{9,11},{10,... | collective-permute-start | bytes 393224 | tf_op jit(solution)/shard_map/ppermute | solution.py:32
  197.9 3.9 %collective-permute-start.42 = (bf16[256,256]{1,0:T(8,128)(2,1)S(1)}, bf16[256,256]{1,0:T(8,128)(2,1)S(1)}, u32[]{:S(2)}, u32[]{:S(2)}) collective-permute-start(bf16[256,256]{1,0:T(8,128)(2,1)S(1)} %collective-permute-done.39.refs_5_.refs_7_), channel_id=1, source_target_pairs={{0,6},{1,7},{2,4},{3,5},{4,2},{5,3},{6,0},{7,1},{8,14},{9,15},{10,... | collective-permute-start | bytes 393224 | tf_op jit(solution)/shard_map/ppermute | solution.py:32
  201.9 2.8 collective-permute-start.41
  204.7 2.9 collective-permute-start.40
  215.4 4.7 %shard_map.101 = (bf16[1024,256]{1,0:T(8,128)(2,1)S(1)}, bf16[16,80,128]{2,1,0:T(8,128)(2,1)}) custom-call(s32[5]{0:T(128)S(1)} %copy-done.33, bf16[256,256]{1,0:T(8,128)(2,1)S(1)} %collective-permute-done.31.refs_1_.refs_6_, bf16[256,256]{1,0:T(8,128)(2,1)S(1)} %collective-permute-done.32.refs_2_, bf16[256,256]{1,0:T(8,128)(2,1)S(1)} %collective-permute-done.33.refs_3_, ...), custom_call_target="tpu_custom_call" | custom-call | flops 2147483648 | bytes 11485184 | tf_op jit(solution)/shard_map/pallas_call | solution.py:132
  220.9 13.3 %all-to-all-start.2 = ((bf16[16,80,128]{2,1,0:T(8,128)(2,1)}), bf16[16,80,128]{2,1,0:T(8,128)(2,1)S(1)}, u32[]{:S(2)}, u32[]{:S(2)}) async-start(bf16[16,80,128]{2,1,0:T(8,128)(2,1)} %get-tuple-element.159), calls=%async_computation.2 | async-start | bytes 655360 | tf_op jit(solution)/shard_map/all_to_all | solution.py:427
  234.9 8.7 %all-to-all-done.2.refs_0_ = bf16[16,80,128]{2,1,0:T(8,128)(2,1)S(1)} async-done(((bf16[16,80,128]{2,1,0:T(8,128)(2,1)}), bf16[16,80,128]{2,1,0:T(8,128)(2,1)S(1)}, u32[]{:S(2)}, u32[]{:S(2)}) %all-to-all-start.2) | async-done | bytes 327712 | tf_op jit(solution)/shard_map/all_to_all | solution.py:427
  243.8 12.2 %all_to_all.22 = bf16[16,64,128]{2,1,0:T(8,128)(2,1)} all-to-all(bf16[16,64,128]{2,1,0:T(8,128)(2,1)S(1)} %shard_map.102), channel_id=1, replica_groups=mesh['section'=2,'ctx'=16,'heads'=8] {'ctx'}, dimensions={0} | all-to-all | bytes 524288 | tf_op jit(solution)/shard_map/all_to_all | solution.py:427
  256.0 5.4 %shard_map.103.refs_1_ = bf16[1280,256]{1,0:T(8,128)(2,1)} custom-call(bf16[1024,256]{1,0:T(8,128)(2,1)} %copy-done.21, f32[16,256]{1,0:T(8,128)} %copy-done.28, bf16[128,1024]{1,0:T(8,128)(2,1)} %copy-done.19, bf16[1024,128]{1,0:T(8,128)(2,1)} %bitcast.48, bf16[128,256]{1,0:T(8,128)(2,1)} %copy-done.26, bf16[1024,256]{1,0:T(8,128)(2,1)} %copy-done.9, ...), custom_call_target="tpu_custom_call" | custom-call | flops 268435456 | bytes 7127040 | tf_op jit(solution)/shard_map/pallas_call | solution.py:132
  263.8 3.5 %shard_map.104 = (bf16[4,512,256]{2,1,0:T(8,128)(2,1)S(1)}, bf16[4,512,256]{2,1,0:T(8,128)(2,1)S(1)}) custom-call(s32[5]{0:T(128)S(1)} %copy-done.34, bf16[1280,256]{1,0:T(8,128)(2,1)S(1)} %copy-done.8, bf16[4,256,1280]{2,1,0:T(8,128)(2,1)S(1)} %bitcast.28, bf16[4,256,1280]{2,1,0:T(8,128)(2,1)S(1)} %copy-done.5, bf16[2,256,1280]{2,1,0:T(8,128)(2,1)S(1)} %copy-done.14, ...), custom_call_target="tpu_custom_call" | custom-call | flops 2684354560 | bytes 13238272 | tf_op jit(solution)/shard_map/pallas_call | solution.py:132
  272.1 3.7 %collective-permute-start.47 = (bf16[512,256]{1,0:T(8,128)(2,1)S(1)}, bf16[512,256]{1,0:T(8,128)(2,1)S(1)}, u32[]{:S(2)}, u32[]{:S(2)}) collective-permute-start(bf16[512,256]{1,0:T(8,128)(2,1)S(1)} %get-tuple-element.165), channel_id=1, source_target_pairs={{0,2},{1,3},{2,0},{3,1},{4,6},{5,7},{6,4},{7,5},{8,10},{9,11},{10,... | collective-permute-start | bytes 786440 | tf_op jit(solution)/shard_map/ppermute | solution.py:32
  275.8 4.5 %collective-permute-start.48 = (bf16[512,256]{1,0:T(8,128)(2,1)S(1)}, bf16[512,256]{1,0:T(8,128)(2,1)S(1)}, u32[]{:S(2)}, u32[]{:S(2)}) collective-permute-start(bf16[512,256]{1,0:T(8,128)(2,1)S(1)} %get-tuple-element.166), channel_id=1, source_target_pairs={{0,4},{1,5},{2,6},{3,7},{4,0},{5,1},{6,2},{7,3},{8,12},{9,13},{10,... | collective-permute-start | bytes 786440 | tf_op jit(solution)/shard_map/ppermute | solution.py:32
  282.2 4.2 %collective-permute-done.47.refs_3_ = bf16[512,256]{1,0:T(8,128)(2,1)S(1)} collective-permute-done((bf16[512,256]{1,0:T(8,128)(2,1)S(1)}, bf16[512,256]{1,0:T(8,128)(2,1)S(1)}, u32[]{:S(2)}, u32[]{:S(2)}) %collective-permute-start.47) | collective-permute-done | bytes 262176 | tf_op jit(solution)/shard_map/ppermute | solution.py:32
  286.4 11.5 %collective-permute-done.48.refs_4_ = bf16[512,256]{1,0:T(8,128)(2,1)S(1)} collective-permute-done((bf16[512,256]{1,0:T(8,128)(2,1)S(1)}, bf16[512,256]{1,0:T(8,128)(2,1)S(1)}, u32[]{:S(2)}, u32[]{:S(2)}) %collective-permute-start.48) | collective-permute-done | bytes 262176 | tf_op jit(solution)/shard_map/ppermute | solution.py:32
  297.9 4.8 %collective-permute-done.49.refs_5_ = bf16[512,256]{1,0:T(8,128)(2,1)S(1)} collective-permute-done((bf16[512,256]{1,0:T(8,128)(2,1)S(1)}, bf16[512,256]{1,0:T(8,128)(2,1)S(1)}, u32[]{:S(2)}, u32[]{:S(2)}) %collective-permute-start.49) | collective-permute-done | bytes 262176 | tf_op jit(solution)/shard_map/ppermute | solution.py:32
  (189 shorter events, 71.5 us)
Async XLA Ops:
  0.0 14.3 %collective-permute-start.5 = (bf16[1024,256]{1,0:T(8,128)(2,1)}, bf16[1024,256]{1,0:T(8,128)(2,1)S(1)}, u32[]{:S(2)}, u32[]{:S(2)}) collective-permute-start(bf16[1024,256]{1,0:T(8,128)(2,1)} %bitcast.43), channel_id=1, source_target_pairs={{0,96},{1,97},{2,98},{3,99},{4,100},{5,101},{6,102},{7,103},{8,104... | collective-permute-start | bytes 1572872 | tf_op jit(solution)/shard_map/ppermute | solution.py:32
  2.8 15.2 %collective-permute-start.4 = (bf16[1024,256]{1,0:T(8,128)(2,1)}, bf16[1024,256]{1,0:T(8,128)(2,1)S(1)}, u32[]{:S(2)}, u32[]{:S(2)}) collective-permute-start(bf16[1024,256]{1,0:T(8,128)(2,1)} %bitcast.44), channel_id=1, source_target_pairs={{0,32},{1,33},{2,34},{3,35},{4,36},{5,37},{6,38},{7,39},{8,40},{9,... | collective-permute-start | bytes 1572872 | tf_op jit(solution)/shard_map/ppermute | solution.py:32
  7.6 22.1 %collective-permute-start = (bf16[256,1024]{1,0:T(8,128)(2,1)}, bf16[256,1024]{1,0:T(8,128)(2,1)}, u32[]{:S(2)}, u32[]{:S(2)}) collective-permute-start(bf16[256,1024]{1,0:T(8,128)(2,1)} %get-tuple-element.88), channel_id=1, source_target_pairs={{128,160},{129,161},{130,162},{131,163},{132,164},{133,165},{134,1... | collective-permute-start | bytes 1572872 | tf_op jit(solution)/shard_map/ppermute | solution.py:32
  9.1 20.6 %collective-permute-start.3 = (bf16[256,1024]{1,0:T(8,128)(2,1)}, bf16[256,1024]{1,0:T(8,128)(2,1)}, u32[]{:S(2)}, u32[]{:S(2)}) collective-permute-start(bf16[256,1024]{1,0:T(8,128)(2,1)} %get-tuple-element.90), channel_id=1, source_target_pairs={{128,224},{129,225},{130,226},{131,227},{132,228},{133,229},{134,2... | collective-permute-start | bytes 1572872 | tf_op jit(solution)/shard_map/ppermute | solution.py:32
  11.3 18.5 %collective-permute-start.2 = (bf16[128,1024]{1,0:T(8,128)(2,1)}, bf16[128,1024]{1,0:T(8,128)(2,1)S(1)}, u32[]{:S(2)}, u32[]{:S(2)}) collective-permute-start(bf16[128,1024]{1,0:T(8,128)(2,1)} %collective-permute-done.1.refs_3_), channel_id=1, source_target_pairs={{128,129},{129,128},{130,131},{131,130},{132,133},{133,132},{134,1... | collective-permute-start | bytes 786440 | tf_op jit(solution)/shard_map/ppermute | solution.py:32
  14.3 12.2 %collective-permute-start.7 = (bf16[512,256]{1,0:T(8,128)(2,1)S(1)}, bf16[512,256]{1,0:T(8,128)(2,1)S(1)}, u32[]{:S(2)}, u32[]{:S(2)}) collective-permute-start(bf16[512,256]{1,0:T(8,128)(2,1)S(1)} %slice.41), channel_id=1, source_target_pairs={{0,96},{1,97},{2,98},{3,99},{4,100},{5,101},{6,102},{7,103},{8,104... | collective-permute-start | bytes 786440 | tf_op jit(solution)/shard_map/ppermute | solution.py:32
  26.5 15.9 %collective-permute-start.13 = (bf16[256,1280]{1,0:T(8,128)(2,1)S(1)}, bf16[256,1280]{1,0:T(8,128)(2,1)S(1)}, u32[]{:S(2)}, u32[]{:S(2)}) collective-permute-start(bf16[256,1280]{1,0:T(8,128)(2,1)S(1)} %pad_maximum_fusion.refs_6_), channel_id=1, source_target_pairs={{0,24},{1,25},{2,26},{3,27},{4,28},{5,29},{6,30},{7,31},{8,0},{9,1... | collective-permute-start | bytes 1966088 | tf_op jit(solution)/shard_map/ppermute | solution.py:32
  29.6 16.6 %collective-permute-start.11 = (bf16[256,1280]{1,0:T(8,128)(2,1)S(1)}, bf16[256,1280]{1,0:T(8,128)(2,1)S(1)}, u32[]{:S(2)}, u32[]{:S(2)}) collective-permute-start(bf16[256,1280]{1,0:T(8,128)(2,1)S(1)} %pad_maximum_fusion.refs_6_), channel_id=1, source_target_pairs={{0,8},{1,9},{2,10},{3,11},{4,12},{5,13},{6,14},{7,15},{8,16},{9,17... | collective-permute-start | bytes 1966088 | tf_op jit(solution)/shard_map/ppermute | solution.py:32
  33.8 21.1 %collective-permute-start.8 = (bf16[1024,256]{1,0:T(8,128)(2,1)S(1)}, bf16[1024,256]{1,0:T(8,128)(2,1)S(1)}, u32[]{:S(2)}, u32[]{:S(2)}) collective-permute-start(bf16[1024,256]{1,0:T(8,128)(2,1)S(1)} %get-tuple-element.103), channel_id=1, source_target_pairs={{128,224},{129,225},{130,226},{131,227},{132,228},{133,229},{134,2... | collective-permute-start | bytes 1572872 | tf_op jit(solution)/shard_map/ppermute | solution.py:32
  34.5 20.4 %collective-permute-start.9 = (bf16[1024,256]{1,0:T(8,128)(2,1)S(1)}, bf16[1024,256]{1,0:T(8,128)(2,1)S(1)}, u32[]{:S(2)}, u32[]{:S(2)}) collective-permute-start(bf16[1024,256]{1,0:T(8,128)(2,1)S(1)} %get-tuple-element.104), channel_id=1, source_target_pairs={{128,192},{129,193},{130,194},{131,195},{132,196},{133,197},{134,1... | collective-permute-start | bytes 1572872 | tf_op jit(solution)/shard_map/ppermute | solution.py:32
  35.2 19.7 %collective-permute-start.10 = (bf16[1024,256]{1,0:T(8,128)(2,1)S(1)}, bf16[1024,256]{1,0:T(8,128)(2,1)S(1)}, u32[]{:S(2)}, u32[]{:S(2)}) collective-permute-start(bf16[1024,256]{1,0:T(8,128)(2,1)S(1)} %get-tuple-element.105), channel_id=1, source_target_pairs={{128,160},{129,161},{130,162},{131,163},{132,164},{133,165},{134,1... | collective-permute-start | bytes 1572872 | tf_op jit(solution)/shard_map/ppermute | solution.py:32
  42.5 8.7 %collective-permute-start.14 = (bf16[128,1280]{1,0:T(8,128)(2,1)S(1)}, bf16[128,1280]{1,0:T(8,128)(2,1)S(1)}, u32[]{:S(2)}, u32[]{:S(2)}) collective-permute-start(bf16[128,1280]{1,0:T(8,128)(2,1)S(1)} %slice.43), channel_id=1, source_target_pairs={{0,24},{1,25},{2,26},{3,27},{4,28},{5,29},{6,30},{7,31},{8,0},{9,1... | collective-permute-start | bytes 983048 | tf_op jit(solution)/shard_map/ppermute | solution.py:32
  46.3 8.6 %collective-permute-start.12 = (bf16[128,1280]{1,0:T(8,128)(2,1)S(1)}, bf16[128,1280]{1,0:T(8,128)(2,1)S(1)}, u32[]{:S(2)}, u32[]{:S(2)}) collective-permute-start(bf16[128,1280]{1,0:T(8,128)(2,1)S(1)} %slice.42), channel_id=1, source_target_pairs={{0,8},{1,9},{2,10},{3,11},{4,12},{5,13},{6,14},{7,15},{8,16},{9,17... | collective-permute-start | bytes 983048 | tf_op jit(solution)/shard_map/ppermute | solution.py:32
  56.0 64.7 %collective-permute-start.18 = (bf16[4,256,1280]{2,1,0:T(8,128)(2,1)S(1)}, bf16[4,256,1280]{2,1,0:T(8,128)(2,1)S(1)}, u32[]{:S(2)}, u32[]{:S(2)}) collective-permute-start(bf16[4,256,1280]{2,1,0:T(8,128)(2,1)S(1)} %bitcast.26), channel_id=1, source_target_pairs={{0,96},{1,97},{2,98},{3,99},{4,100},{5,101},{6,102},{7,103},{8,104... | collective-permute-start | bytes 7864328 | tf_op jit(solution)/shard_map/ppermute | solution.py:32
  60.2 60.5 %collective-permute-start.17 = (bf16[4,256,1280]{2,1,0:T(8,128)(2,1)S(1)}, bf16[4,256,1280]{2,1,0:T(8,128)(2,1)S(1)}, u32[]{:S(2)}, u32[]{:S(2)}) collective-permute-start(bf16[4,256,1280]{2,1,0:T(8,128)(2,1)S(1)} %bitcast.27), channel_id=1, source_target_pairs={{0,32},{1,33},{2,34},{3,35},{4,36},{5,37},{6,38},{7,39},{8,40},{9,... | collective-permute-start | bytes 7864328 | tf_op jit(solution)/shard_map/ppermute | solution.py:32
  63.6 57.1 %collective-permute-start.16 = (bf16[4,1024,256]{2,1,0:T(8,128)(2,1)S(1)}, bf16[4,1024,256]{2,1,0:T(8,128)(2,1)S(1)}, u32[]{:S(2)}, u32[]{:S(2)}) collective-permute-start(bf16[4,1024,256]{2,1,0:T(8,128)(2,1)S(1)} %bitcast.29), channel_id=1, source_target_pairs={{0,24},{1,25},{2,26},{3,27},{4,28},{5,29},{6,30},{7,31},{8,0},{9,1... | collective-permute-start | bytes 6291464 | tf_op jit(solution)/shard_map/ppermute | solution.py:32
  65.5 55.2 %collective-permute-start.15 = (bf16[4,1024,256]{2,1,0:T(8,128)(2,1)S(1)}, bf16[4,1024,256]{2,1,0:T(8,128)(2,1)S(1)}, u32[]{:S(2)}, u32[]{:S(2)}) collective-permute-start(bf16[4,1024,256]{2,1,0:T(8,128)(2,1)S(1)} %bitcast.30), channel_id=1, source_target_pairs={{0,8},{1,9},{2,10},{3,11},{4,12},{5,13},{6,14},{7,15},{8,16},{9,17... | collective-permute-start | bytes 6291464 | tf_op jit(solution)/shard_map/ppermute | solution.py:32
  123.1 35.1 %collective-permute-start.22 = (bf16[2,256,1280]{2,1,0:T(8,128)(2,1)S(1)}, bf16[2,256,1280]{2,1,0:T(8,128)(2,1)S(1)}, u32[]{:S(2)}, u32[]{:S(2)}) collective-permute-start(bf16[2,256,1280]{2,1,0:T(8,128)(2,1)S(1)} %slice.37), channel_id=1, source_target_pairs={{0,96},{1,97},{2,98},{3,99},{4,100},{5,101},{6,102},{7,103},{8,104... | collective-permute-start | bytes 3932168 | tf_op jit(solution)/shard_map/ppermute | solution.py:32
  125.2 33.0 %collective-permute-start.21 = (bf16[2,256,1280]{2,1,0:T(8,128)(2,1)S(1)}, bf16[2,256,1280]{2,1,0:T(8,128)(2,1)S(1)}, u32[]{:S(2)}, u32[]{:S(2)}) collective-permute-start(bf16[2,256,1280]{2,1,0:T(8,128)(2,1)S(1)} %slice.36), channel_id=1, source_target_pairs={{0,32},{1,33},{2,34},{3,35},{4,36},{5,37},{6,38},{7,39},{8,40},{9,... | collective-permute-start | bytes 3932168 | tf_op jit(solution)/shard_map/ppermute | solution.py:32
  129.1 29.1 %collective-permute-start.20 = (bf16[2,1024,256]{2,1,0:T(8,128)(2,1)S(1)}, bf16[2,1024,256]{2,1,0:T(8,128)(2,1)S(1)}, u32[]{:S(2)}, u32[]{:S(2)}) collective-permute-start(bf16[2,1024,256]{2,1,0:T(8,128)(2,1)S(1)} %slice.35), channel_id=1, source_target_pairs={{0,24},{1,25},{2,26},{3,27},{4,28},{5,29},{6,30},{7,31},{8,0},{9,1... | collective-permute-start | bytes 3145736 | tf_op jit(solution)/shard_map/ppermute | solution.py:32
  134.3 23.8 %collective-permute-start.19 = (bf16[2,1024,256]{2,1,0:T(8,128)(2,1)S(1)}, bf16[2,1024,256]{2,1,0:T(8,128)(2,1)S(1)}, u32[]{:S(2)}, u32[]{:S(2)}) collective-permute-start(bf16[2,1024,256]{2,1,0:T(8,128)(2,1)S(1)} %slice.34), channel_id=1, source_target_pairs={{0,8},{1,9},{2,10},{3,11},{4,12},{5,13},{6,14},{7,15},{8,16},{9,17... | collective-permute-start | bytes 3145736 | tf_op jit(solution)/shard_map/ppermute | solution.py:32
  173.7 13.4 %collective-permute-start.31 = (bf16[256,256]{1,0:T(8,128)(2,1)S(1)}, bf16[256,256]{1,0:T(8,128)(2,1)S(1)}, u32[]{:S(2)}, u32[]{:S(2)}) collective-permute-start(bf16[256,256]{1,0:T(8,128)(2,1)S(1)} %shard_map.98), channel_id=1, source_target_pairs={{128,0},{129,1},{130,32},{131,33},{132,64},{133,65},{134,96},{135,... | collective-permute-start | bytes 393224 | tf_op jit(solution)/shard_map/ppermute | solution.py:32
  175.1 22.8 %collective-permute-start.39 = (bf16[256,256]{1,0:T(8,128)(2,1)S(1)}, bf16[256,256]{1,0:T(8,128)(2,1)S(1)}, u32[]{:S(2)}, u32[]{:S(2)}) collective-permute-start(bf16[256,256]{1,0:T(8,128)(2,1)S(1)} %shard_map.100), channel_id=1, source_target_pairs={{128,0},{129,1},{130,32},{131,33},{132,64},{133,65},{134,96},{135,... | collective-permute-start | bytes 393224 | tf_op jit(solution)/shard_map/ppermute | solution.py:32
  187.1 17.6 %collective-permute-start.34 = (bf16[256,256]{1,0:T(8,128)(2,1)S(1)}, bf16[256,256]{1,0:T(8,128)(2,1)S(1)}, u32[]{:S(2)}, u32[]{:S(2)}) collective-permute-start(bf16[256,256]{1,0:T(8,128)(2,1)S(1)} %collective-permute-done.31.refs_1_.refs_6_), channel_id=1, source_target_pairs={{0,6},{1,7},{2,4},{3,5},{4,2},{5,3},{6,0},{7,1},{8,14},{9,15},{10,... | collective-permute-start | bytes 393224 | tf_op jit(solution)/shard_map/ppermute | solution.py:32
  192.6 15.0 %collective-permute-start.33 = (bf16[256,256]{1,0:T(8,128)(2,1)S(1)}, bf16[256,256]{1,0:T(8,128)(2,1)S(1)}, u32[]{:S(2)}, u32[]{:S(2)}) collective-permute-start(bf16[256,256]{1,0:T(8,128)(2,1)S(1)} %collective-permute-done.31.refs_1_.refs_6_), channel_id=1, source_target_pairs={{0,4},{1,5},{2,6},{3,7},{4,0},{5,1},{6,2},{7,3},{8,12},{9,13},{10,... | collective-permute-start | bytes 393224 | tf_op jit(solution)/shard_map/ppermute | solution.py:32
  194.5 13.0 %collective-permute-start.32 = (bf16[256,256]{1,0:T(8,128)(2,1)S(1)}, bf16[256,256]{1,0:T(8,128)(2,1)S(1)}, u32[]{:S(2)}, u32[]{:S(2)}) collective-permute-start(bf16[256,256]{1,0:T(8,128)(2,1)S(1)} %collective-permute-done.31.refs_1_.refs_6_), channel_id=1, source_target_pairs={{0,2},{1,3},{2,0},{3,1},{4,6},{5,7},{6,4},{7,5},{8,10},{9,11},{10,... | collective-permute-start | bytes 393224 | tf_op jit(solution)/shard_map/ppermute | solution.py:32
  197.9 12.0 %collective-permute-start.42 = (bf16[256,256]{1,0:T(8,128)(2,1)S(1)}, bf16[256,256]{1,0:T(8,128)(2,1)S(1)}, u32[]{:S(2)}, u32[]{:S(2)}) collective-permute-start(bf16[256,256]{1,0:T(8,128)(2,1)S(1)} %collective-permute-done.39.refs_5_.refs_7_), channel_id=1, source_target_pairs={{0,6},{1,7},{2,4},{3,5},{4,2},{5,3},{6,0},{7,1},{8,14},{9,15},{10,... | collective-permute-start | bytes 393224 | tf_op jit(solution)/shard_map/ppermute | solution.py:32
  201.9 8.8 %collective-permute-start.41 = (bf16[256,256]{1,0:T(8,128)(2,1)S(1)}, bf16[256,256]{1,0:T(8,128)(2,1)S(1)}, u32[]{:S(2)}, u32[]{:S(2)}) collective-permute-start(bf16[256,256]{1,0:T(8,128)(2,1)S(1)} %collective-permute-done.39.refs_5_.refs_7_), channel_id=1, source_target_pairs={{0,4},{1,5},{2,6},{3,7},{4,0},{5,1},{6,2},{7,3},{8,12},{9,13},{10,... | collective-permute-start | bytes 393224 | tf_op jit(solution)/shard_map/ppermute | solution.py:32
  220.9 22.8 %all-to-all-start.2 = ((bf16[16,80,128]{2,1,0:T(8,128)(2,1)}), bf16[16,80,128]{2,1,0:T(8,128)(2,1)S(1)}, u32[]{:S(2)}, u32[]{:S(2)}) async-start(bf16[16,80,128]{2,1,0:T(8,128)(2,1)} %get-tuple-element.159), calls=%async_computation.2 | async-start | bytes 655360 | tf_op jit(solution)/shard_map/all_to_all | solution.py:427
  272.1 14.3 %collective-permute-start.47 = (bf16[512,256]{1,0:T(8,128)(2,1)S(1)}, bf16[512,256]{1,0:T(8,128)(2,1)S(1)}, u32[]{:S(2)}, u32[]{:S(2)}) collective-permute-start(bf16[512,256]{1,0:T(8,128)(2,1)S(1)} %get-tuple-element.165), channel_id=1, source_target_pairs={{0,2},{1,3},{2,0},{3,1},{4,6},{5,7},{6,4},{7,5},{8,10},{9,11},{10,... | collective-permute-start | bytes 786440 | tf_op jit(solution)/shard_map/ppermute | solution.py:32
  275.8 22.1 %collective-permute-start.48 = (bf16[512,256]{1,0:T(8,128)(2,1)S(1)}, bf16[512,256]{1,0:T(8,128)(2,1)S(1)}, u32[]{:S(2)}, u32[]{:S(2)}) collective-permute-start(bf16[512,256]{1,0:T(8,128)(2,1)S(1)} %get-tuple-element.166), channel_id=1, source_target_pairs={{0,4},{1,5},{2,6},{3,7},{4,0},{5,1},{6,2},{7,3},{8,12},{9,13},{10,... | collective-permute-start | bytes 786440 | tf_op jit(solution)/shard_map/ppermute | solution.py:32
  280.3 22.4 %collective-permute-start.49 = (bf16[512,256]{1,0:T(8,128)(2,1)S(1)}, bf16[512,256]{1,0:T(8,128)(2,1)S(1)}, u32[]{:S(2)}, u32[]{:S(2)}) collective-permute-start(bf16[512,256]{1,0:T(8,128)(2,1)S(1)} %get-tuple-element.167), channel_id=1, source_target_pairs={{0,6},{1,7},{2,4},{3,5},{4,2},{5,3},{6,0},{7,1},{8,14},{9,15},{10,... | collective-permute-start | bytes 786440 | tf_op jit(solution)/shard_map/ppermute | solution.py:32
  (55 other events, 1647.3 us)

commit v6 on v5

--- a/solution.py
+++ b/solution.py
@@ -11,6 +11,7 @@
 CORES = 2
 BOTH = (0, 1)
 AXES = ("section", "ctx", "heads")
+ORDER = (2, 3, 1)
 VMEM = 20 * 1024 * 1024
 MOST = 54 * 1024 * 1024
 bf16, f32 = jnp.bfloat16, jnp.float32
@@ -94,13 +95,13 @@
         return self.held[index]
 
 
-def call(body, outs, args, at=None, scratch=(), flops=0, remote=(), away=(), vmem_limit=VMEM):
+def call(body, outs, args, at=None, scratch=(), flops=0, remote=(), away=(), aliases=(), vmem_limit=VMEM, where=None):
     moved = sum(a.size * a.dtype.itemsize for a in (*args, *outs))
     vmem, hbm = pl.BlockSpec(memory_space=pltpu.VMEM), pl.BlockSpec(memory_space=pltpu.HBM)
     own = [pltpu.VMEM(args[i].shape, args[i].dtype) for i in remote]
     own += [pltpu.VMEM(outs[i].shape, outs[i].dtype) for i in away]
 
-    def kernel(*refs):
+    def run(refs):
         refs = list(refs)
         first = refs[:1] if at is not None else []
         refs = refs[len(first) :]
@@ -129,12 +130,19 @@
         for copy in copies:
             copy.wait()
 
+    def kernel(*refs):
+        if where is None:
+            run(refs)
+        else:
+            pl.when(refs[0][refs[0].shape[0] - 1] == where)(lambda: run(refs))
+
     return pl.pallas_call(
         kernel,
         in_specs=[pl.BlockSpec(memory_space=pltpu.SMEM)] * (at is not None)
         + [hbm if i in remote else vmem for i in range(len(args))],
         out_specs=[hbm if i in away else vmem for i in range(len(outs))],
         out_shape=list(outs),
+        input_output_aliases=dict(aliases),
         scratch_shapes=own + list(scratch) + ([pltpu.SemaphoreType.DMA((len(own),))] if own else []),
         compiler_params=pltpu.CompilerParams(vmem_limit_bytes=vmem_limit),
         cost_estimate=pl.CostEstimate(flops=flops, bytes_accessed=moved, transcendentals=0),
@@ -315,20 +323,26 @@
         give[q] = u[span((1 - core) * len(gives) + i, part), :]
 
 
-def back_body(at, g0, g1, gl, gh, g3, w0, w1, wl, wh, w3, keep, give_a, give_b, u, g2):
-    x, y, z, core = at[0], at[1], at[2], at[3]
-    fine = w0.shape[0]
-    g2[: gl.shape[0], :] = gl[...]
-    g2[gl.shape[0] :, :] = gh[...]
-    for k, g in enumerate((g0, g1, g2, g3)):
-        for j, w in enumerate((w0, w1, None, w3)):
-            rows = span(behind(y, j), fine)
-            if w is None:
-                term = jnp.concatenate([dot(wl[...], g[...], 1, 0), dot(wh[...], g[...], 1, 0)], axis=0)
-            else:
-                term = dot(w[...], g[...], 1, 0)
-            u[k, rows, :] = term.astype(bf16)
+def block_terms(at, g, weights, u):
+    for j, w in enumerate(weights):
+        rows = span(behind(at[1], j), u.shape[0] // SIDE)
+        term = [dot(part[...], g[...], 1, 0) for part in w]
+        u[rows, :] = jnp.concatenate(term, axis=0).astype(bf16)
+
+
+def near_body(at, g0, g1, g3, w0, w1, wl, wh, w3, keep, give_a, give_b, u):
+    x, z, core = at[0], at[2], at[3]
+    for k, g in ((0, g0), (1, g1), (3, g3)):
+        block_terms(at, g, ((w0,), (w1,), (wl, wh), (w3,)), u.at[k])
         to_halves(u.at[k], z ^ x ^ behind(x, k), core, keep, (give_a, give_b))
+
+
+def far_body(at, gl, gh, w0, w1, wl, wh, w3, k0, k1, k2, keep, give_a, give_b, u, g):
+    x, z, core = at[0], at[2], at[3]
+    g[: gl.shape[0], :] = gl[...]
+    g[gl.shape[0] :, :] = gh[...]
+    block_terms(at, g, ((w0,), (w1,), (wl, wh), (w3,)), u)
+    to_halves(u, z ^ x ^ behind(x, 2), core, keep, (give_a, give_b))
 
 
 def whole_body(at, g, w0, w1, wl, wh, w3, keep, give, u):
@@ -347,7 +361,7 @@
 
 
 def pair_body(part, keep, got, s1, s2, s3):
-    for q, out in ((1, s1), (2, s2), (3, s3)):
+    for q, out in zip(ORDER, (s1, s2, s3)):
         out[...] = rows_of(keep, q, got, part).astype(bf16)
 
 
@@ -395,7 +409,8 @@
     for k in range(SIDE):
         low, count = (half * core, half) if k == 2 else (0, rows)
         pieces.append(lax.dynamic_slice(grad_out, (low, block * ((x + k) % SIDE)), (count, block)))
-    own, *pieces = tie(pieces)
+    own, *pieces = pieces
+    pieces = tie(pieces)
     before, across, after = [routed(p, along_x(k), (1,)) for k, p in zip(steps, pieces)]
     upstream = [own, before, across, routed(across, other_core, (1,)), after]
 
@@ -452,7 +467,7 @@
     def over_heads(keep, give, sections, part=0):
         got = routed(give, other_core, sections)
         sent = call(functools.partial(pair_body, part), [struct(give.shape[1:])] * 3, [keep, got])
-        return [keep, got] + [routed(s, across_z(k), sections) for k, s in zip(steps, sent)]
+        return [keep, got] + [routed(s, across_z(k), sections) for k, s in zip(ORDER, sent)]
 
     *partial, own = call(
         rows_body,
@@ -462,6 +477,7 @@
         remote=(9,),
         scratch=[pltpu.VMEM((SIDE, rows, block), bf16)],
         flops=2 * SIDE * rows * block * inner,
+        where=1,
     )
     partial, out_sides, out_far = tie((partial, out_sides, out_far))
     received = [routed(partial[k], along_x(-k), (1,)) for k in steps]
@@ -496,17 +512,27 @@
     grads_far = far(grads_sides, along_x, (1,), 0)
     wide = [pltpu.VMEM((SIDE, block, rows), bf16)]
     halves = struct((SIDE, share // 2, rows))
+    weights = [back, back_sides[0], *back_far, back_sides[1]]
+    first = call(
+        near_body,
+        [chunks, halves, halves],
+        [grads, *grads_sides, *weights],
+        at,
+        scratch=wide,
+        flops=6 * rows * block * outer,
+        where=1,
+    )
     keep, *gives = call(
-        back_body,
+        far_body,
         [chunks, halves, halves],
-        [
-            grads, grads_sides[0], *grads_far, grads_sides[1],
-            back, back_sides[0], *back_far, back_sides[1],
-        ],
+        [*grads_far, *weights, *first],
         at,
-        scratch=wide + [pltpu.VMEM((outer, rows), bf16)],
-        flops=2 * SIDE * rows * block * outer,
-    )
+        scratch=[pltpu.VMEM((block, rows), bf16), pltpu.VMEM((outer, rows), bf16)],
+        flops=2 * rows * block * outer,
+        aliases={8: 0, 9: 1, 10: 2},
+        where=1,
+    )
+
     middle = []
     for i, give in enumerate(gives):
         sums = over_heads(keep, give, (1,), i)

time: 306 us -> 304 us (level)
  Pallas kernels: 29.8 us -> 24.6 us
    pallas_call x16 -> x17, Pallas kernels: 29.8 us -> 24.6 us  [call(): pl.pallas_call(kernel, in_specs=[pl.BlockSpec(memory_space=pltpu.SMEM)] *...]
  transfers between devices with their start and end apart: 51 -> 51, of which waited for: 14 -> 12; matrix products, arithmetic and copies ran while one was open for 2% -> 2% of each run, Pallas kernels for 2% -> 1%
where the time goes in v6:
time: 304 us; the launch traced here: 302 us
  starting transfers between devices  108 us (36%)
  blocking collectives  85.3 us (28%)
  waiting for transfers between devices  64.6 us (21%)
  Pallas kernels  24.6 us (8%)
  local copies, waits for them, and re-layouts  16.2 us (5%)
    ppermute x50, starting transfers between devices, routed(): return lax.ppermute(value, AXES, pairs)  93.2 us
    all_to_all x3, blocking collectives, exchange(): return lax.all_to_all(states, 'ctx', 0, 0)  85.3 us
    ppermute x50, waiting for transfers between devices, routed(): return lax.ppermute(value, AXES, pairs)  55.9 us
    pallas_call x17, Pallas kernels, call(): pl.pallas_call(kernel, in_specs=[pl.BlockSpec(memory_space=pltpu.SMEM)] *...  24.6 us
    all_to_all x1, starting transfers between devices, exchange(): return lax.all_to_all(states, 'ctx', 0, 0)  14.7 us
    unnamed x80, local copies, waits for them, and re-layouts  11.5 us
    all_to_all x1, waiting for transfers between devices, exchange(): return lax.all_to_all(states, 'ctx', 0, 0)  8.74 us
  transfers between devices with their start and end apart: 51, of which 12 were waited for; matrix products, arithmetic and copies ran while one was open for 2% of the time, Pallas kernels for 1%

profile of v6, /device:TPU:32, one launch (start us, length us, event | category | flops | bytes accessed | tf_op | source)
XLA Modules:
  0.0 301.7 jit_solution(13896026716516098662)
XLA Ops:
  0.0 2.8 collective-permute-start.5
  3.7 2.6 constant_dynamic-slice_fusion
  14.3 3.7 %collective-permute-start.7 = (bf16[512,256]{1,0:T(8,128)(2,1)S(1)}, bf16[512,256]{1,0:T(8,128)(2,1)S(1)}, u32[]{:S(2)}, u32[]{:S(2)}) collective-permute-start(bf16[512,256]{1,0:T(8,128)(2,1)S(1)} %slice.41), channel_id=1, source_target_pairs={{0,96},{1,97},{2,98},{3,99},{4,100},{5,101},{6,102},{7,103},{8,104... | collective-permute-start | bytes 786440 | tf_op jit(solution)/shard_map/ppermute | solution.py:33
  26.5 3.1 %collective-permute-start.13 = (bf16[256,1280]{1,0:T(8,128)(2,1)S(1)}, bf16[256,1280]{1,0:T(8,128)(2,1)S(1)}, u32[]{:S(2)}, u32[]{:S(2)}) collective-permute-start(bf16[256,1280]{1,0:T(8,128)(2,1)S(1)} %pad_maximum_fusion.refs_4_.refs_3_), channel_id=1, source_target_pairs={{0,24},{1,25},{2,26},{3,27},{4,28},{5,29},{6,30},{7,31},{8,0},{9,1... | collective-permute-start | bytes 1966088 | tf_op jit(solution)/shard_map/ppermute | solution.py:33
  33.4 9.1 %collective-permute-done.13.refs_8_.refs_7_ = bf16[256,1280]{1,0:T(8,128)(2,1)S(1)} collective-permute-done((bf16[256,1280]{1,0:T(8,128)(2,1)S(1)}, bf16[256,1280]{1,0:T(8,128)(2,1)S(1)}, u32[]{:S(2)}, u32[]{:S(2)}) %collective-permute-start.13) | collective-permute-done | bytes 655392 | tf_op jit(solution)/shard_map/ppermute | solution.py:33
  42.5 3.8 %collective-permute-start.14 = (bf16[128,1280]{1,0:T(8,128)(2,1)S(1)}, bf16[128,1280]{1,0:T(8,128)(2,1)S(1)}, u32[]{:S(2)}, u32[]{:S(2)}) collective-permute-start(bf16[128,1280]{1,0:T(8,128)(2,1)S(1)} %slice.43), channel_id=1, source_target_pairs={{0,24},{1,25},{2,26},{3,27},{4,28},{5,29},{6,30},{7,31},{8,0},{9,1... | collective-permute-start | bytes 983048 | tf_op jit(solution)/shard_map/ppermute | solution.py:33
  46.7 4.5 %collective-permute-done.14.refs_7_.refs_6_ = bf16[128,1280]{1,0:T(8,128)(2,1)S(1)} collective-permute-done((bf16[128,1280]{1,0:T(8,128)(2,1)S(1)}, bf16[128,1280]{1,0:T(8,128)(2,1)S(1)}, u32[]{:S(2)}, u32[]{:S(2)}) %collective-permute-start.14) | collective-permute-done | bytes 327712 | tf_op jit(solution)/shard_map/ppermute | solution.py:33
  51.2 3.7 %collective-permute-done.12.refs_6_.refs_5_ = bf16[128,1280]{1,0:T(8,128)(2,1)S(1)} collective-permute-done((bf16[128,1280]{1,0:T(8,128)(2,1)S(1)}, bf16[128,1280]{1,0:T(8,128)(2,1)S(1)}, u32[]{:S(2)}, u32[]{:S(2)}) %collective-permute-start.12) | collective-permute-done | bytes 327712 | tf_op jit(solution)/shard_map/ppermute | solution.py:33
  56.0 4.1 %collective-permute-start.18 = (bf16[4,256,1280]{2,1,0:T(8,128)(2,1)S(1)}, bf16[4,256,1280]{2,1,0:T(8,128)(2,1)S(1)}, u32[]{:S(2)}, u32[]{:S(2)}) collective-permute-start(bf16[4,256,1280]{2,1,0:T(8,128)(2,1)S(1)} %bitcast.26), channel_id=1, source_target_pairs={{0,96},{1,97},{2,98},{3,99},{4,100},{5,101},{6,102},{7,103},{8,104... | collective-permute-start | bytes 7864328 | tf_op jit(solution)/shard_map/ppermute | solution.py:33
  65.5 3.9 %collective-permute-start.15 = (bf16[4,1024,256]{2,1,0:T(8,128)(2,1)S(1)}, bf16[4,1024,256]{2,1,0:T(8,128)(2,1)S(1)}, u32[]{:S(2)}, u32[]{:S(2)}) collective-permute-start(bf16[4,1024,256]{2,1,0:T(8,128)(2,1)S(1)} %bitcast.30), channel_id=1, source_target_pairs={{0,8},{1,9},{2,10},{3,11},{4,12},{5,13},{6,14},{7,15},{8,16},{9,17... | collective-permute-start | bytes 6291464 | tf_op jit(solution)/shard_map/ppermute | solution.py:33
  69.4 51.3 %all_to_all.20.refs_0_ = bf16[16,80,128]{2,1,0:T(8,128)(2,1)S(1)} all-to-all(bf16[16,80,128]{2,1,0:T(8,128)(2,1)S(1)} %get-tuple-element.125), channel_id=1, replica_groups=mesh['section'=2,'ctx'=16,'heads'=8] {'ctx'}, dimensions={0} | all-to-all | bytes 655360 | tf_op jit(solution)/shard_map/all_to_all | solution.py:442
  125.2 3.7 %collective-permute-start.21 = (bf16[2,256,1280]{2,1,0:T(8,128)(2,1)S(1)}, bf16[2,256,1280]{2,1,0:T(8,128)(2,1)S(1)}, u32[]{:S(2)}, u32[]{:S(2)}) collective-permute-start(bf16[2,256,1280]{2,1,0:T(8,128)(2,1)S(1)} %slice.36), channel_id=1, source_target_pairs={{0,32},{1,33},{2,34},{3,35},{4,36},{5,37},{6,38},{7,39},{8,40},{9,... | collective-permute-start | bytes 3932168 | tf_op jit(solution)/shard_map/ppermute | solution.py:33
  129.0 5.2 %collective-permute-start.20 = (bf16[2,1024,256]{2,1,0:T(8,128)(2,1)S(1)}, bf16[2,1024,256]{2,1,0:T(8,128)(2,1)S(1)}, u32[]{:S(2)}, u32[]{:S(2)}) collective-permute-start(bf16[2,1024,256]{2,1,0:T(8,128)(2,1)S(1)} %slice.35), channel_id=1, source_target_pairs={{0,24},{1,25},{2,26},{3,27},{4,28},{5,29},{6,30},{7,31},{8,0},{9,1... | collective-permute-start | bytes 3145736 | tf_op jit(solution)/shard_map/ppermute | solution.py:33
  136.2 21.9 %all_to_all.21 = bf16[16,64,128]{2,1,0:T(8,128)(2,1)S(1)} all-to-all(bf16[16,64,128]{2,1,0:T(8,128)(2,1)S(1)} %shard_map.94), channel_id=1, replica_groups=mesh['section'=2,'ctx'=16,'heads'=8] {'ctx'}, dimensions={0} | all-to-all | bytes 524288 | tf_op jit(solution)/shard_map/all_to_all | solution.py:442
  158.2 3.1 %shard_map.95.refs_1_ = bf16[1280,256]{1,0:T(8,128)(2,1)S(1)} custom-call(bf16[1024,256]{1,0:T(8,128)(2,1)S(1)} %get-tuple-element.120.refs_0_, f32[16,256]{1,0:T(8,128)S(1)} %get-tuple-element.117.refs_4_.refs_1_.refs_16_, bf16[128,1024]{1,0:T(8,128)(2,1)S(1)} %get-tuple-element.121.refs_2_, bf16[1024,128]{1,0:T(8,128)(2,1)S(1)} %bitcast.34, ...), custom_call_target="tpu_custom_call" | custom-call | flops 268435456 | bytes 7127040 | tf_op jit(solution)/shard_map/pallas_call | solution.py:139
  173.9 11.8 %collective-permute-done.31.refs_1_.refs_6_ = bf16[256,256]{1,0:T(8,128)(2,1)S(1)} collective-permute-done((bf16[256,256]{1,0:T(8,128)(2,1)S(1)}, bf16[256,256]{1,0:T(8,128)(2,1)S(1)}, u32[]{:S(2)}, u32[]{:S(2)}) %collective-permute-start.31) | collective-permute-done | bytes 131104 | tf_op jit(solution)/shard_map/ppermute | solution.py:33
  185.8 5.5 %collective-permute-start.34 = (bf16[256,256]{1,0:T(8,128)(2,1)S(1)}, bf16[256,256]{1,0:T(8,128)(2,1)S(1)}, u32[]{:S(2)}, u32[]{:S(2)}) collective-permute-start(bf16[256,256]{1,0:T(8,128)(2,1)S(1)} %collective-permute-done.31.refs_1_.refs_6_), channel_id=1, source_target_pairs={{0,6},{1,7},{2,4},{3,5},{4,2},{5,3},{6,0},{7,1},{8,14},{9,15},{10,... | collective-permute-start | bytes 393224 | tf_op jit(solution)/shard_map/ppermute | solution.py:33
  193.2 3.4 %collective-permute-start.32 = (bf16[256,256]{1,0:T(8,128)(2,1)S(1)}, bf16[256,256]{1,0:T(8,128)(2,1)S(1)}, u32[]{:S(2)}, u32[]{:S(2)}) collective-permute-start(bf16[256,256]{1,0:T(8,128)(2,1)S(1)} %collective-permute-done.31.refs_1_.refs_6_), channel_id=1, source_target_pairs={{0,2},{1,3},{2,0},{3,1},{4,6},{5,7},{6,4},{7,5},{8,10},{9,11},{10,... | collective-permute-start | bytes 393224 | tf_op jit(solution)/shard_map/ppermute | solution.py:33
  196.6 3.9 %collective-permute-start.42 = (bf16[256,256]{1,0:T(8,128)(2,1)S(1)}, bf16[256,256]{1,0:T(8,128)(2,1)S(1)}, u32[]{:S(2)}, u32[]{:S(2)}) collective-permute-start(bf16[256,256]{1,0:T(8,128)(2,1)S(1)} %collective-permute-done.39.refs_5_.refs_7_), channel_id=1, source_target_pairs={{0,6},{1,7},{2,4},{3,5},{4,2},{5,3},{6,0},{7,1},{8,14},{9,15},{10,... | collective-permute-start | bytes 393224 | tf_op jit(solution)/shard_map/ppermute | solution.py:33
  200.5 2.8 collective-permute-start.41
  214.1 4.6 %shard_map.102 = (bf16[1024,256]{1,0:T(8,128)(2,1)S(1)}, bf16[16,80,128]{2,1,0:T(8,128)(2,1)}) custom-call(s32[5]{0:T(128)S(1)} %copy-done.33, bf16[256,256]{1,0:T(8,128)(2,1)S(1)} %collective-permute-done.31.refs_1_.refs_6_, bf16[256,256]{1,0:T(8,128)(2,1)S(1)} %collective-permute-done.32.refs_2_, bf16[256,256]{1,0:T(8,128)(2,1)S(1)} %collective-permute-done.33.refs_3_, ...), custom_call_target="tpu_custom_call" | custom-call | flops 2147483648 | bytes 11485184 | tf_op jit(solution)/shard_map/pallas_call | solution.py:139
  219.6 14.7 %all-to-all-start.2 = ((bf16[16,80,128]{2,1,0:T(8,128)(2,1)}), bf16[16,80,128]{2,1,0:T(8,128)(2,1)S(1)}, u32[]{:S(2)}, u32[]{:S(2)}) async-start(bf16[16,80,128]{2,1,0:T(8,128)(2,1)} %get-tuple-element.163), calls=%async_computation.2 | async-start | bytes 655360 | tf_op jit(solution)/shard_map/all_to_all | solution.py:442
  235.0 8.7 %all-to-all-done.2.refs_0_ = bf16[16,80,128]{2,1,0:T(8,128)(2,1)S(1)} async-done(((bf16[16,80,128]{2,1,0:T(8,128)(2,1)}), bf16[16,80,128]{2,1,0:T(8,128)(2,1)S(1)}, u32[]{:S(2)}, u32[]{:S(2)}) %all-to-all-start.2) | async-done | bytes 327712 | tf_op jit(solution)/shard_map/all_to_all | solution.py:442
  243.8 12.2 %all_to_all.22 = bf16[16,64,128]{2,1,0:T(8,128)(2,1)} all-to-all(bf16[16,64,128]{2,1,0:T(8,128)(2,1)S(1)} %shard_map.103), channel_id=1, replica_groups=mesh['section'=2,'ctx'=16,'heads'=8] {'ctx'}, dimensions={0} | all-to-all | bytes 524288 | tf_op jit(solution)/shard_map/all_to_all | solution.py:442
  256.0 5.4 %shard_map.104.refs_1_ = bf16[1280,256]{1,0:T(8,128)(2,1)} custom-call(bf16[1024,256]{1,0:T(8,128)(2,1)} %copy-done.21, f32[16,256]{1,0:T(8,128)} %copy-done.28, bf16[128,1024]{1,0:T(8,128)(2,1)} %copy-done.19, bf16[1024,128]{1,0:T(8,128)(2,1)} %bitcast.48, bf16[128,256]{1,0:T(8,128)(2,1)} %copy-done.26, bf16[1024,256]{1,0:T(8,128)(2,1)} %copy-done.9, ...), custom_call_target="tpu_custom_call" | custom-call | flops 268435456 | bytes 7127040 | tf_op jit(solution)/shard_map/pallas_call | solution.py:139
  263.8 3.5 %shard_map.105 = (bf16[4,512,256]{2,1,0:T(8,128)(2,1)S(1)}, bf16[4,512,256]{2,1,0:T(8,128)(2,1)S(1)}) custom-call(s32[5]{0:T(128)S(1)} %copy-done.34, bf16[1280,256]{1,0:T(8,128)(2,1)S(1)} %copy-done.8, bf16[4,256,1280]{2,1,0:T(8,128)(2,1)S(1)} %bitcast.28, bf16[4,256,1280]{2,1,0:T(8,128)(2,1)S(1)} %copy-done.5, bf16[2,256,1280]{2,1,0:T(8,128)(2,1)S(1)} %copy-done.14, ...), custom_call_target="tpu_custom_call" | custom-call | flops 2684354560 | bytes 13238272 | tf_op jit(solution)/shard_map/pallas_call | solution.py:139
  269.3 2.6 collective-permute-done.46.refs_1_.refs_2_
  272.1 4.1 %collective-permute-start.47 = (bf16[512,256]{1,0:T(8,128)(2,1)S(1)}, bf16[512,256]{1,0:T(8,128)(2,1)S(1)}, u32[]{:S(2)}, u32[]{:S(2)}) collective-permute-start(bf16[512,256]{1,0:T(8,128)(2,1)S(1)} %get-tuple-element.169), channel_id=1, source_target_pairs={{0,4},{1,5},{2,6},{3,7},{4,0},{5,1},{6,2},{7,3},{8,12},{9,13},{10,... | collective-permute-start | bytes 786440 | tf_op jit(solution)/shard_map/ppermute | solution.py:33
  276.2 3.5 %collective-permute-start.48 = (bf16[512,256]{1,0:T(8,128)(2,1)S(1)}, bf16[512,256]{1,0:T(8,128)(2,1)S(1)}, u32[]{:S(2)}, u32[]{:S(2)}) collective-permute-start(bf16[512,256]{1,0:T(8,128)(2,1)S(1)} %get-tuple-element.170), channel_id=1, source_target_pairs={{0,6},{1,7},{2,4},{3,5},{4,2},{5,3},{6,0},{7,1},{8,14},{9,15},{10,... | collective-permute-start | bytes 786440 | tf_op jit(solution)/shard_map/ppermute | solution.py:33
  279.7 2.5 collective-permute-start.49
  282.2 11.0 %collective-permute-done.47.refs_3_ = bf16[512,256]{1,0:T(8,128)(2,1)S(1)} collective-permute-done((bf16[512,256]{1,0:T(8,128)(2,1)S(1)}, bf16[512,256]{1,0:T(8,128)(2,1)S(1)}, u32[]{:S(2)}, u32[]{:S(2)}) %collective-permute-start.47) | collective-permute-done | bytes 262176 | tf_op jit(solution)/shard_map/ppermute | solution.py:33
  293.3 6.9 %collective-permute-done.48.refs_4_ = bf16[512,256]{1,0:T(8,128)(2,1)S(1)} collective-permute-done((bf16[512,256]{1,0:T(8,128)(2,1)S(1)}, bf16[512,256]{1,0:T(8,128)(2,1)S(1)}, u32[]{:S(2)}, u32[]{:S(2)}) %collective-permute-start.48) | collective-permute-done | bytes 262176 | tf_op jit(solution)/shard_map/ppermute | solution.py:33
  (190 shorter events, 67.0 us)
Async XLA Ops:
  0.0 14.3 %collective-permute-start.5 = (bf16[1024,256]{1,0:T(8,128)(2,1)}, bf16[1024,256]{1,0:T(8,128)(2,1)S(1)}, u32[]{:S(2)}, u32[]{:S(2)}) collective-permute-start(bf16[1024,256]{1,0:T(8,128)(2,1)} %bitcast.43), channel_id=1, source_target_pairs={{0,96},{1,97},{2,98},{3,99},{4,100},{5,101},{6,102},{7,103},{8,104... | collective-permute-start | bytes 1572872 | tf_op jit(solution)/shard_map/ppermute | solution.py:33
  2.8 15.2 %collective-permute-start.4 = (bf16[1024,256]{1,0:T(8,128)(2,1)}, bf16[1024,256]{1,0:T(8,128)(2,1)S(1)}, u32[]{:S(2)}, u32[]{:S(2)}) collective-permute-start(bf16[1024,256]{1,0:T(8,128)(2,1)} %bitcast.44), channel_id=1, source_target_pairs={{0,32},{1,33},{2,34},{3,35},{4,36},{5,37},{6,38},{7,39},{8,40},{9,... | collective-permute-start | bytes 1572872 | tf_op jit(solution)/shard_map/ppermute | solution.py:33
  7.6 22.1 %collective-permute-start = (bf16[256,1024]{1,0:T(8,128)(2,1)}, bf16[256,1024]{1,0:T(8,128)(2,1)}, u32[]{:S(2)}, u32[]{:S(2)}) collective-permute-start(bf16[256,1024]{1,0:T(8,128)(2,1)} %get-tuple-element.89), channel_id=1, source_target_pairs={{128,160},{129,161},{130,162},{131,163},{132,164},{133,165},{134,1... | collective-permute-start | bytes 1572872 | tf_op jit(solution)/shard_map/ppermute | solution.py:33
  9.1 20.6 %collective-permute-start.3 = (bf16[256,1024]{1,0:T(8,128)(2,1)}, bf16[256,1024]{1,0:T(8,128)(2,1)}, u32[]{:S(2)}, u32[]{:S(2)}) collective-permute-start(bf16[256,1024]{1,0:T(8,128)(2,1)} %get-tuple-element.91), channel_id=1, source_target_pairs={{128,224},{129,225},{130,226},{131,227},{132,228},{133,229},{134,2... | collective-permute-start | bytes 1572872 | tf_op jit(solution)/shard_map/ppermute | solution.py:33
  11.3 18.4 %collective-permute-start.2 = (bf16[128,1024]{1,0:T(8,128)(2,1)}, bf16[128,1024]{1,0:T(8,128)(2,1)S(1)}, u32[]{:S(2)}, u32[]{:S(2)}) collective-permute-start(bf16[128,1024]{1,0:T(8,128)(2,1)} %collective-permute-done.1.refs_3_), channel_id=1, source_target_pairs={{128,129},{129,128},{130,131},{131,130},{132,133},{133,132},{134,1... | collective-permute-start | bytes 786440 | tf_op jit(solution)/shard_map/ppermute | solution.py:33
  14.3 12.2 %collective-permute-start.7 = (bf16[512,256]{1,0:T(8,128)(2,1)S(1)}, bf16[512,256]{1,0:T(8,128)(2,1)S(1)}, u32[]{:S(2)}, u32[]{:S(2)}) collective-permute-start(bf16[512,256]{1,0:T(8,128)(2,1)S(1)} %slice.41), channel_id=1, source_target_pairs={{0,96},{1,97},{2,98},{3,99},{4,100},{5,101},{6,102},{7,103},{8,104... | collective-permute-start | bytes 786440 | tf_op jit(solution)/shard_map/ppermute | solution.py:33
  18.0 8.6 %collective-permute-start.6 = (bf16[512,256]{1,0:T(8,128)(2,1)S(1)}, bf16[512,256]{1,0:T(8,128)(2,1)S(1)}, u32[]{:S(2)}, u32[]{:S(2)}) collective-permute-start(bf16[512,256]{1,0:T(8,128)(2,1)S(1)} %slice.40), channel_id=1, source_target_pairs={{0,32},{1,33},{2,34},{3,35},{4,36},{5,37},{6,38},{7,39},{8,40},{9,... | collective-permute-start | bytes 786440 | tf_op jit(solution)/shard_map/ppermute | solution.py:33
  26.5 15.9 %collective-permute-start.13 = (bf16[256,1280]{1,0:T(8,128)(2,1)S(1)}, bf16[256,1280]{1,0:T(8,128)(2,1)S(1)}, u32[]{:S(2)}, u32[]{:S(2)}) collective-permute-start(bf16[256,1280]{1,0:T(8,128)(2,1)S(1)} %pad_maximum_fusion.refs_4_.refs_3_), channel_id=1, source_target_pairs={{0,24},{1,25},{2,26},{3,27},{4,28},{5,29},{6,30},{7,31},{8,0},{9,1... | collective-permute-start | bytes 1966088 | tf_op jit(solution)/shard_map/ppermute | solution.py:33
  29.6 16.6 %collective-permute-start.11 = (bf16[256,1280]{1,0:T(8,128)(2,1)S(1)}, bf16[256,1280]{1,0:T(8,128)(2,1)S(1)}, u32[]{:S(2)}, u32[]{:S(2)}) collective-permute-start(bf16[256,1280]{1,0:T(8,128)(2,1)S(1)} %pad_maximum_fusion.refs_4_.refs_3_), channel_id=1, source_target_pairs={{0,8},{1,9},{2,10},{3,11},{4,12},{5,13},{6,14},{7,15},{8,16},{9,17... | collective-permute-start | bytes 1966088 | tf_op jit(solution)/shard_map/ppermute | solution.py:33
  31.1 23.8 %collective-permute-start.8 = (bf16[1024,256]{1,0:T(8,128)(2,1)S(1)}, bf16[1024,256]{1,0:T(8,128)(2,1)S(1)}, u32[]{:S(2)}, u32[]{:S(2)}) collective-permute-start(bf16[1024,256]{1,0:T(8,128)(2,1)S(1)} %get-tuple-element.104), channel_id=1, source_target_pairs={{128,224},{129,225},{130,226},{131,227},{132,228},{133,229},{134,2... | collective-permute-start | bytes 1572872 | tf_op jit(solution)/shard_map/ppermute | solution.py:33
  31.8 23.1 %collective-permute-start.9 = (bf16[1024,256]{1,0:T(8,128)(2,1)S(1)}, bf16[1024,256]{1,0:T(8,128)(2,1)S(1)}, u32[]{:S(2)}, u32[]{:S(2)}) collective-permute-start(bf16[1024,256]{1,0:T(8,128)(2,1)S(1)} %get-tuple-element.105), channel_id=1, source_target_pairs={{128,192},{129,193},{130,194},{131,195},{132,196},{133,197},{134,1... | collective-permute-start | bytes 1572872 | tf_op jit(solution)/shard_map/ppermute | solution.py:33
  32.5 22.4 %collective-permute-start.10 = (bf16[1024,256]{1,0:T(8,128)(2,1)S(1)}, bf16[1024,256]{1,0:T(8,128)(2,1)S(1)}, u32[]{:S(2)}, u32[]{:S(2)}) collective-permute-start(bf16[1024,256]{1,0:T(8,128)(2,1)S(1)} %get-tuple-element.106), channel_id=1, source_target_pairs={{128,160},{129,161},{130,162},{131,163},{132,164},{133,165},{134,1... | collective-permute-start | bytes 1572872 | tf_op jit(solution)/shard_map/ppermute | solution.py:33
  42.5 8.7 %collective-permute-start.14 = (bf16[128,1280]{1,0:T(8,128)(2,1)S(1)}, bf16[128,1280]{1,0:T(8,128)(2,1)S(1)}, u32[]{:S(2)}, u32[]{:S(2)}) collective-permute-start(bf16[128,1280]{1,0:T(8,128)(2,1)S(1)} %slice.43), channel_id=1, source_target_pairs={{0,24},{1,25},{2,26},{3,27},{4,28},{5,29},{6,30},{7,31},{8,0},{9,1... | collective-permute-start | bytes 983048 | tf_op jit(solution)/shard_map/ppermute | solution.py:33
  46.3 8.6 %collective-permute-start.12 = (bf16[128,1280]{1,0:T(8,128)(2,1)S(1)}, bf16[128,1280]{1,0:T(8,128)(2,1)S(1)}, u32[]{:S(2)}, u32[]{:S(2)}) collective-permute-start(bf16[128,1280]{1,0:T(8,128)(2,1)S(1)} %slice.42), channel_id=1, source_target_pairs={{0,8},{1,9},{2,10},{3,11},{4,12},{5,13},{6,14},{7,15},{8,16},{9,17... | collective-permute-start | bytes 983048 | tf_op jit(solution)/shard_map/ppermute | solution.py:33
  56.0 64.7 %collective-permute-start.18 = (bf16[4,256,1280]{2,1,0:T(8,128)(2,1)S(1)}, bf16[4,256,1280]{2,1,0:T(8,128)(2,1)S(1)}, u32[]{:S(2)}, u32[]{:S(2)}) collective-permute-start(bf16[4,256,1280]{2,1,0:T(8,128)(2,1)S(1)} %bitcast.26), channel_id=1, source_target_pairs={{0,96},{1,97},{2,98},{3,99},{4,100},{5,101},{6,102},{7,103},{8,104... | collective-permute-start | bytes 7864328 | tf_op jit(solution)/shard_map/ppermute | solution.py:33
  60.2 60.5 %collective-permute-start.17 = (bf16[4,256,1280]{2,1,0:T(8,128)(2,1)S(1)}, bf16[4,256,1280]{2,1,0:T(8,128)(2,1)S(1)}, u32[]{:S(2)}, u32[]{:S(2)}) collective-permute-start(bf16[4,256,1280]{2,1,0:T(8,128)(2,1)S(1)} %bitcast.27), channel_id=1, source_target_pairs={{0,32},{1,33},{2,34},{3,35},{4,36},{5,37},{6,38},{7,39},{8,40},{9,... | collective-permute-start | bytes 7864328 | tf_op jit(solution)/shard_map/ppermute | solution.py:33
  63.6 57.1 %collective-permute-start.16 = (bf16[4,1024,256]{2,1,0:T(8,128)(2,1)S(1)}, bf16[4,1024,256]{2,1,0:T(8,128)(2,1)S(1)}, u32[]{:S(2)}, u32[]{:S(2)}) collective-permute-start(bf16[4,1024,256]{2,1,0:T(8,128)(2,1)S(1)} %bitcast.29), channel_id=1, source_target_pairs={{0,24},{1,25},{2,26},{3,27},{4,28},{5,29},{6,30},{7,31},{8,0},{9,1... | collective-permute-start | bytes 6291464 | tf_op jit(solution)/shard_map/ppermute | solution.py:33
  65.5 55.2 %collective-permute-start.15 = (bf16[4,1024,256]{2,1,0:T(8,128)(2,1)S(1)}, bf16[4,1024,256]{2,1,0:T(8,128)(2,1)S(1)}, u32[]{:S(2)}, u32[]{:S(2)}) collective-permute-start(bf16[4,1024,256]{2,1,0:T(8,128)(2,1)S(1)} %bitcast.30), channel_id=1, source_target_pairs={{0,8},{1,9},{2,10},{3,11},{4,12},{5,13},{6,14},{7,15},{8,16},{9,17... | collective-permute-start | bytes 6291464 | tf_op jit(solution)/shard_map/ppermute | solution.py:33
  123.0 35.1 %collective-permute-start.22 = (bf16[2,256,1280]{2,1,0:T(8,128)(2,1)S(1)}, bf16[2,256,1280]{2,1,0:T(8,128)(2,1)S(1)}, u32[]{:S(2)}, u32[]{:S(2)}) collective-permute-start(bf16[2,256,1280]{2,1,0:T(8,128)(2,1)S(1)} %slice.37), channel_id=1, source_target_pairs={{0,96},{1,97},{2,98},{3,99},{4,100},{5,101},{6,102},{7,103},{8,104... | collective-permute-start | bytes 3932168 | tf_op jit(solution)/shard_map/ppermute | solution.py:33
  125.2 33.0 %collective-permute-start.21 = (bf16[2,256,1280]{2,1,0:T(8,128)(2,1)S(1)}, bf16[2,256,1280]{2,1,0:T(8,128)(2,1)S(1)}, u32[]{:S(2)}, u32[]{:S(2)}) collective-permute-start(bf16[2,256,1280]{2,1,0:T(8,128)(2,1)S(1)} %slice.36), channel_id=1, source_target_pairs={{0,32},{1,33},{2,34},{3,35},{4,36},{5,37},{6,38},{7,39},{8,40},{9,... | collective-permute-start | bytes 3932168 | tf_op jit(solution)/shard_map/ppermute | solution.py:33
  129.0 29.1 %collective-permute-start.20 = (bf16[2,1024,256]{2,1,0:T(8,128)(2,1)S(1)}, bf16[2,1024,256]{2,1,0:T(8,128)(2,1)S(1)}, u32[]{:S(2)}, u32[]{:S(2)}) collective-permute-start(bf16[2,1024,256]{2,1,0:T(8,128)(2,1)S(1)} %slice.35), channel_id=1, source_target_pairs={{0,24},{1,25},{2,26},{3,27},{4,28},{5,29},{6,30},{7,31},{8,0},{9,1... | collective-permute-start | bytes 3145736 | tf_op jit(solution)/shard_map/ppermute | solution.py:33
  134.3 23.8 %collective-permute-start.19 = (bf16[2,1024,256]{2,1,0:T(8,128)(2,1)S(1)}, bf16[2,1024,256]{2,1,0:T(8,128)(2,1)S(1)}, u32[]{:S(2)}, u32[]{:S(2)}) collective-permute-start(bf16[2,1024,256]{2,1,0:T(8,128)(2,1)S(1)} %slice.34), channel_id=1, source_target_pairs={{0,8},{1,9},{2,10},{3,11},{4,12},{5,13},{6,14},{7,15},{8,16},{9,17... | collective-permute-start | bytes 3145736 | tf_op jit(solution)/shard_map/ppermute | solution.py:33
  171.2 14.6 %collective-permute-start.31 = (bf16[256,256]{1,0:T(8,128)(2,1)S(1)}, bf16[256,256]{1,0:T(8,128)(2,1)S(1)}, u32[]{:S(2)}, u32[]{:S(2)}) collective-permute-start(bf16[256,256]{1,0:T(8,128)(2,1)S(1)} %shard_map.99), channel_id=1, source_target_pairs={{128,0},{129,1},{130,32},{131,33},{132,64},{133,65},{134,96},{135,... | collective-permute-start | bytes 393224 | tf_op jit(solution)/shard_map/ppermute | solution.py:33
  172.6 23.9 %collective-permute-start.39 = (bf16[256,256]{1,0:T(8,128)(2,1)S(1)}, bf16[256,256]{1,0:T(8,128)(2,1)S(1)}, u32[]{:S(2)}, u32[]{:S(2)}) collective-permute-start(bf16[256,256]{1,0:T(8,128)(2,1)S(1)} %shard_map.101), channel_id=1, source_target_pairs={{128,0},{129,1},{130,32},{131,33},{132,64},{133,65},{134,96},{135,... | collective-permute-start | bytes 393224 | tf_op jit(solution)/shard_map/ppermute | solution.py:33
  185.8 17.6 %collective-permute-start.34 = (bf16[256,256]{1,0:T(8,128)(2,1)S(1)}, bf16[256,256]{1,0:T(8,128)(2,1)S(1)}, u32[]{:S(2)}, u32[]{:S(2)}) collective-permute-start(bf16[256,256]{1,0:T(8,128)(2,1)S(1)} %collective-permute-done.31.refs_1_.refs_6_), channel_id=1, source_target_pairs={{0,6},{1,7},{2,4},{3,5},{4,2},{5,3},{6,0},{7,1},{8,14},{9,15},{10,... | collective-permute-start | bytes 393224 | tf_op jit(solution)/shard_map/ppermute | solution.py:33
  191.3 14.6 %collective-permute-start.33 = (bf16[256,256]{1,0:T(8,128)(2,1)S(1)}, bf16[256,256]{1,0:T(8,128)(2,1)S(1)}, u32[]{:S(2)}, u32[]{:S(2)}) collective-permute-start(bf16[256,256]{1,0:T(8,128)(2,1)S(1)} %collective-permute-done.31.refs_1_.refs_6_), channel_id=1, source_target_pairs={{0,4},{1,5},{2,6},{3,7},{4,0},{5,1},{6,2},{7,3},{8,12},{9,13},{10,... | collective-permute-start | bytes 393224 | tf_op jit(solution)/shard_map/ppermute | solution.py:33
  193.2 12.7 %collective-permute-start.32 = (bf16[256,256]{1,0:T(8,128)(2,1)S(1)}, bf16[256,256]{1,0:T(8,128)(2,1)S(1)}, u32[]{:S(2)}, u32[]{:S(2)}) collective-permute-start(bf16[256,256]{1,0:T(8,128)(2,1)S(1)} %collective-permute-done.31.refs_1_.refs_6_), channel_id=1, source_target_pairs={{0,2},{1,3},{2,0},{3,1},{4,6},{5,7},{6,4},{7,5},{8,10},{9,11},{10,... | collective-permute-start | bytes 393224 | tf_op jit(solution)/shard_map/ppermute | solution.py:33
  196.6 11.3 %collective-permute-start.42 = (bf16[256,256]{1,0:T(8,128)(2,1)S(1)}, bf16[256,256]{1,0:T(8,128)(2,1)S(1)}, u32[]{:S(2)}, u32[]{:S(2)}) collective-permute-start(bf16[256,256]{1,0:T(8,128)(2,1)S(1)} %collective-permute-done.39.refs_5_.refs_7_), channel_id=1, source_target_pairs={{0,6},{1,7},{2,4},{3,5},{4,2},{5,3},{6,0},{7,1},{8,14},{9,15},{10,... | collective-permute-start | bytes 393224 | tf_op jit(solution)/shard_map/ppermute | solution.py:33
  219.6 24.1 %all-to-all-start.2 = ((bf16[16,80,128]{2,1,0:T(8,128)(2,1)}), bf16[16,80,128]{2,1,0:T(8,128)(2,1)S(1)}, u32[]{:S(2)}, u32[]{:S(2)}) async-start(bf16[16,80,128]{2,1,0:T(8,128)(2,1)} %get-tuple-element.163), calls=%async_computation.2 | async-start | bytes 655360 | tf_op jit(solution)/shard_map/all_to_all | solution.py:442
  272.1 21.1 %collective-permute-start.47 = (bf16[512,256]{1,0:T(8,128)(2,1)S(1)}, bf16[512,256]{1,0:T(8,128)(2,1)S(1)}, u32[]{:S(2)}, u32[]{:S(2)}) collective-permute-start(bf16[512,256]{1,0:T(8,128)(2,1)S(1)} %get-tuple-element.169), channel_id=1, source_target_pairs={{0,4},{1,5},{2,6},{3,7},{4,0},{5,1},{6,2},{7,3},{8,12},{9,13},{10,... | collective-permute-start | bytes 786440 | tf_op jit(solution)/shard_map/ppermute | solution.py:33
  276.2 23.9 %collective-permute-start.48 = (bf16[512,256]{1,0:T(8,128)(2,1)S(1)}, bf16[512,256]{1,0:T(8,128)(2,1)S(1)}, u32[]{:S(2)}, u32[]{:S(2)}) collective-permute-start(bf16[512,256]{1,0:T(8,128)(2,1)S(1)} %get-tuple-element.170), channel_id=1, source_target_pairs={{0,6},{1,7},{2,4},{3,5},{4,2},{5,3},{6,0},{7,1},{8,14},{9,15},{10,... | collective-permute-start | bytes 786440 | tf_op jit(solution)/shard_map/ppermute | solution.py:33
  279.7 20.5 %collective-permute-start.49 = (bf16[512,256]{1,0:T(8,128)(2,1)S(1)}, bf16[512,256]{1,0:T(8,128)(2,1)S(1)}, u32[]{:S(2)}, u32[]{:S(2)}) collective-permute-start(bf16[512,256]{1,0:T(8,128)(2,1)S(1)} %get-tuple-element.171), channel_id=1, source_target_pairs={{0,2},{1,3},{2,0},{3,1},{4,6},{5,7},{6,4},{7,5},{8,10},{9,11},{10,... | collective-permute-start | bytes 786440 | tf_op jit(solution)/shard_map/ppermute | solution.py:33
  (55 other events, 1648.4 us)

commit v7 on v6

--- a/solution.py
+++ b/solution.py
@@ -11,7 +11,7 @@
 CORES = 2
 BOTH = (0, 1)
 AXES = ("section", "ctx", "heads")
-ORDER = (2, 3, 1)
+MIDDLE_FIRST, IN_TURN = (2, 3, 1), (1, 2, 3)
 VMEM = 20 * 1024 * 1024
 MOST = 54 * 1024 * 1024
 bf16, f32 = jnp.bfloat16, jnp.float32
@@ -360,8 +360,8 @@
     return keep[q, part * size : (part + 1) * size, :].astype(f32) + got[q].astype(f32)
 
 
-def pair_body(part, keep, got, s1, s2, s3):
-    for q, out in zip(ORDER, (s1, s2, s3)):
+def pair_body(order, part, keep, got, s1, s2, s3):
+    for q, out in zip(order, (s1, s2, s3)):
         out[...] = rows_of(keep, q, got, part).astype(bf16)
 
 
@@ -464,10 +464,10 @@
     chunk = struct((share, rows))
     chunks = struct((SIDE, share, rows))
 
-    def over_heads(keep, give, sections, part=0):
+    def over_heads(keep, give, sections, order, part=0):
         got = routed(give, other_core, sections)
-        sent = call(functools.partial(pair_body, part), [struct(give.shape[1:])] * 3, [keep, got])
-        return [keep, got] + [routed(s, across_z(k), sections) for k, s in zip(ORDER, sent)]
+        sent = call(functools.partial(pair_body, order, part), [struct(give.shape[1:])] * 3, [keep, got])
+        return [keep, got] + [routed(s, across_z(k), sections) for k, s in zip(order, sent)]
 
     *partial, own = call(
         rows_body,
@@ -535,7 +535,7 @@
 
     middle = []
     for i, give in enumerate(gives):
-        sums = over_heads(keep, give, (1,), i)
+        sums = over_heads(keep, give, (1,), MIDDLE_FIRST, i)
         middle += call(functools.partial(total_body, i), [struct((share // 2, rows))], [*sums, own])
 
     arrived = [routed(m, hop(0), (1,)) for m in middle]
@@ -563,7 +563,7 @@
         scratch=wide,
         flops=2 * rows * width * outer,
     )
-    sums = over_heads(keep, give, (0,))
+    sums = over_heads(keep, give, (0,), IN_TURN)
     (result,) = call(result_body, [struct((1, rows, share))], [*sums, *arrived, settled], at)
     return result
 

time: 304 us -> 306 us (level)
  waiting for transfers between devices: 64.6 us -> 68 us
    ppermute x50, waiting for transfers between devices: 55.9 us -> 59.3 us  [routed(): return lax.ppermute(value, AXES, pairs)]
  transfers between devices with their start and end apart: 51 -> 51, of which waited for: 12 -> 13; matrix products, arithmetic and copies ran while one was open for 2% -> 2% of each run, Pallas kernels for 1% -> 1%
where the time goes in v7:
time: 306 us; the launch traced here: 304 us
  starting transfers between devices  107 us (35%)
  blocking collectives  85.3 us (28%)
  waiting for transfers between devices  68 us (22%)
  Pallas kernels  24.6 us (8%)
  local copies, waits for them, and re-layouts  16.2 us (5%)
    ppermute x50, starting transfers between devices, routed(): return lax.ppermute(value, AXES, pairs)  92.6 us
    all_to_all x3, blocking collectives, exchange(): return lax.all_to_all(states, 'ctx', 0, 0)  85.3 us
    ppermute x50, waiting for transfers between devices, routed(): return lax.ppermute(value, AXES, pairs)  59.3 us
    pallas_call x17, Pallas kernels, call(): pl.pallas_call(kernel, in_specs=[pl.BlockSpec(memory_space=pltpu.SMEM)] *...  24.6 us
    all_to_all x1, starting transfers between devices, exchange(): return lax.all_to_all(states, 'ctx', 0, 0)  14.7 us
    unnamed x80, local copies, waits for them, and re-layouts  11.5 us
    all_to_all x1, waiting for transfers between devices, exchange(): return lax.all_to_all(states, 'ctx', 0, 0)  8.74 us
  transfers between devices with their start and end apart: 51, of which 13 were waited for; matrix products, arithmetic and copies ran while one was open for 2% of the time, Pallas kernels for 1%

profile of v7, /device:TPU:32, one launch (start us, length us, event | category | flops | bytes accessed | tf_op | source)
XLA Modules:
  0.0 304.5 jit_solution(2120186770962438750)
XLA Ops:
  0.0 2.8 collective-permute-start.5
  3.7 2.6 constant_dynamic-slice_fusion
  14.3 3.7 %collective-permute-start.7 = (bf16[512,256]{1,0:T(8,128)(2,1)S(1)}, bf16[512,256]{1,0:T(8,128)(2,1)S(1)}, u32[]{:S(2)}, u32[]{:S(2)}) collective-permute-start(bf16[512,256]{1,0:T(8,128)(2,1)S(1)} %slice.41), channel_id=1, source_target_pairs={{0,96},{1,97},{2,98},{3,99},{4,100},{5,101},{6,102},{7,103},{8,104... | collective-permute-start | bytes 786440 | tf_op jit(solution)/shard_map/ppermute | solution.py:33
  26.5 3.1 %collective-permute-start.13 = (bf16[256,1280]{1,0:T(8,128)(2,1)S(1)}, bf16[256,1280]{1,0:T(8,128)(2,1)S(1)}, u32[]{:S(2)}, u32[]{:S(2)}) collective-permute-start(bf16[256,1280]{1,0:T(8,128)(2,1)S(1)} %pad_maximum_fusion.refs_4_.refs_3_), channel_id=1, source_target_pairs={{0,24},{1,25},{2,26},{3,27},{4,28},{5,29},{6,30},{7,31},{8,0},{9,1... | collective-permute-start | bytes 1966088 | tf_op jit(solution)/shard_map/ppermute | solution.py:33
  33.4 9.1 %collective-permute-done.13.refs_8_.refs_7_ = bf16[256,1280]{1,0:T(8,128)(2,1)S(1)} collective-permute-done((bf16[256,1280]{1,0:T(8,128)(2,1)S(1)}, bf16[256,1280]{1,0:T(8,128)(2,1)S(1)}, u32[]{:S(2)}, u32[]{:S(2)}) %collective-permute-start.13) | collective-permute-done | bytes 655392 | tf_op jit(solution)/shard_map/ppermute | solution.py:33
  42.5 3.8 %collective-permute-start.14 = (bf16[128,1280]{1,0:T(8,128)(2,1)S(1)}, bf16[128,1280]{1,0:T(8,128)(2,1)S(1)}, u32[]{:S(2)}, u32[]{:S(2)}) collective-permute-start(bf16[128,1280]{1,0:T(8,128)(2,1)S(1)} %slice.43), channel_id=1, source_target_pairs={{0,24},{1,25},{2,26},{3,27},{4,28},{5,29},{6,30},{7,31},{8,0},{9,1... | collective-permute-start | bytes 983048 | tf_op jit(solution)/shard_map/ppermute | solution.py:33
  46.7 4.5 %collective-permute-done.14.refs_7_.refs_6_ = bf16[128,1280]{1,0:T(8,128)(2,1)S(1)} collective-permute-done((bf16[128,1280]{1,0:T(8,128)(2,1)S(1)}, bf16[128,1280]{1,0:T(8,128)(2,1)S(1)}, u32[]{:S(2)}, u32[]{:S(2)}) %collective-permute-start.14) | collective-permute-done | bytes 327712 | tf_op jit(solution)/shard_map/ppermute | solution.py:33
  51.2 3.7 %collective-permute-done.12.refs_6_.refs_5_ = bf16[128,1280]{1,0:T(8,128)(2,1)S(1)} collective-permute-done((bf16[128,1280]{1,0:T(8,128)(2,1)S(1)}, bf16[128,1280]{1,0:T(8,128)(2,1)S(1)}, u32[]{:S(2)}, u32[]{:S(2)}) %collective-permute-start.12) | collective-permute-done | bytes 327712 | tf_op jit(solution)/shard_map/ppermute | solution.py:33
  56.0 4.1 %collective-permute-start.18 = (bf16[4,256,1280]{2,1,0:T(8,128)(2,1)S(1)}, bf16[4,256,1280]{2,1,0:T(8,128)(2,1)S(1)}, u32[]{:S(2)}, u32[]{:S(2)}) collective-permute-start(bf16[4,256,1280]{2,1,0:T(8,128)(2,1)S(1)} %bitcast.26), channel_id=1, source_target_pairs={{0,96},{1,97},{2,98},{3,99},{4,100},{5,101},{6,102},{7,103},{8,104... | collective-permute-start | bytes 7864328 | tf_op jit(solution)/shard_map/ppermute | solution.py:33
  65.5 3.9 %collective-permute-start.15 = (bf16[4,1024,256]{2,1,0:T(8,128)(2,1)S(1)}, bf16[4,1024,256]{2,1,0:T(8,128)(2,1)S(1)}, u32[]{:S(2)}, u32[]{:S(2)}) collective-permute-start(bf16[4,1024,256]{2,1,0:T(8,128)(2,1)S(1)} %bitcast.30), channel_id=1, source_target_pairs={{0,8},{1,9},{2,10},{3,11},{4,12},{5,13},{6,14},{7,15},{8,16},{9,17... | collective-permute-start | bytes 6291464 | tf_op jit(solution)/shard_map/ppermute | solution.py:33
  69.4 51.3 %all_to_all.20.refs_0_ = bf16[16,80,128]{2,1,0:T(8,128)(2,1)S(1)} all-to-all(bf16[16,80,128]{2,1,0:T(8,128)(2,1)S(1)} %get-tuple-element.125), channel_id=1, replica_groups=mesh['section'=2,'ctx'=16,'heads'=8] {'ctx'}, dimensions={0} | all-to-all | bytes 655360 | tf_op jit(solution)/shard_map/all_to_all | solution.py:442
  125.2 3.7 %collective-permute-start.21 = (bf16[2,256,1280]{2,1,0:T(8,128)(2,1)S(1)}, bf16[2,256,1280]{2,1,0:T(8,128)(2,1)S(1)}, u32[]{:S(2)}, u32[]{:S(2)}) collective-permute-start(bf16[2,256,1280]{2,1,0:T(8,128)(2,1)S(1)} %slice.36), channel_id=1, source_target_pairs={{0,32},{1,33},{2,34},{3,35},{4,36},{5,37},{6,38},{7,39},{8,40},{9,... | collective-permute-start | bytes 3932168 | tf_op jit(solution)/shard_map/ppermute | solution.py:33
  129.0 5.2 %collective-permute-start.20 = (bf16[2,1024,256]{2,1,0:T(8,128)(2,1)S(1)}, bf16[2,1024,256]{2,1,0:T(8,128)(2,1)S(1)}, u32[]{:S(2)}, u32[]{:S(2)}) collective-permute-start(bf16[2,1024,256]{2,1,0:T(8,128)(2,1)S(1)} %slice.35), channel_id=1, source_target_pairs={{0,24},{1,25},{2,26},{3,27},{4,28},{5,29},{6,30},{7,31},{8,0},{9,1... | collective-permute-start | bytes 3145736 | tf_op jit(solution)/shard_map/ppermute | solution.py:33
  136.2 21.9 %all_to_all.21 = bf16[16,64,128]{2,1,0:T(8,128)(2,1)S(1)} all-to-all(bf16[16,64,128]{2,1,0:T(8,128)(2,1)S(1)} %shard_map.94), channel_id=1, replica_groups=mesh['section'=2,'ctx'=16,'heads'=8] {'ctx'}, dimensions={0} | all-to-all | bytes 524288 | tf_op jit(solution)/shard_map/all_to_all | solution.py:442
  158.2 3.1 %shard_map.95.refs_1_ = bf16[1280,256]{1,0:T(8,128)(2,1)S(1)} custom-call(bf16[1024,256]{1,0:T(8,128)(2,1)S(1)} %get-tuple-element.120.refs_0_, f32[16,256]{1,0:T(8,128)S(1)} %get-tuple-element.117.refs_4_.refs_1_.refs_16_, bf16[128,1024]{1,0:T(8,128)(2,1)S(1)} %get-tuple-element.121.refs_2_, bf16[1024,128]{1,0:T(8,128)(2,1)S(1)} %bitcast.34, ...), custom_call_target="tpu_custom_call" | custom-call | flops 268435456 | bytes 7127040 | tf_op jit(solution)/shard_map/pallas_call | solution.py:139
  173.9 11.8 %collective-permute-done.31.refs_1_.refs_6_ = bf16[256,256]{1,0:T(8,128)(2,1)S(1)} collective-permute-done((bf16[256,256]{1,0:T(8,128)(2,1)S(1)}, bf16[256,256]{1,0:T(8,128)(2,1)S(1)}, u32[]{:S(2)}, u32[]{:S(2)}) %collective-permute-start.31) | collective-permute-done | bytes 131104 | tf_op jit(solution)/shard_map/ppermute | solution.py:33
  185.8 5.5 %collective-permute-start.34 = (bf16[256,256]{1,0:T(8,128)(2,1)S(1)}, bf16[256,256]{1,0:T(8,128)(2,1)S(1)}, u32[]{:S(2)}, u32[]{:S(2)}) collective-permute-start(bf16[256,256]{1,0:T(8,128)(2,1)S(1)} %collective-permute-done.31.refs_1_.refs_6_), channel_id=1, source_target_pairs={{0,6},{1,7},{2,4},{3,5},{4,2},{5,3},{6,0},{7,1},{8,14},{9,15},{10,... | collective-permute-start | bytes 393224 | tf_op jit(solution)/shard_map/ppermute | solution.py:33
  193.2 3.4 %collective-permute-start.32 = (bf16[256,256]{1,0:T(8,128)(2,1)S(1)}, bf16[256,256]{1,0:T(8,128)(2,1)S(1)}, u32[]{:S(2)}, u32[]{:S(2)}) collective-permute-start(bf16[256,256]{1,0:T(8,128)(2,1)S(1)} %collective-permute-done.31.refs_1_.refs_6_), channel_id=1, source_target_pairs={{0,2},{1,3},{2,0},{3,1},{4,6},{5,7},{6,4},{7,5},{8,10},{9,11},{10,... | collective-permute-start | bytes 393224 | tf_op jit(solution)/shard_map/ppermute | solution.py:33
  196.6 3.9 %collective-permute-start.42 = (bf16[256,256]{1,0:T(8,128)(2,1)S(1)}, bf16[256,256]{1,0:T(8,128)(2,1)S(1)}, u32[]{:S(2)}, u32[]{:S(2)}) collective-permute-start(bf16[256,256]{1,0:T(8,128)(2,1)S(1)} %collective-permute-done.39.refs_5_.refs_7_), channel_id=1, source_target_pairs={{0,6},{1,7},{2,4},{3,5},{4,2},{5,3},{6,0},{7,1},{8,14},{9,15},{10,... | collective-permute-start | bytes 393224 | tf_op jit(solution)/shard_map/ppermute | solution.py:33
  200.5 2.8 collective-permute-start.41
  214.1 4.6 %shard_map.102 = (bf16[1024,256]{1,0:T(8,128)(2,1)S(1)}, bf16[16,80,128]{2,1,0:T(8,128)(2,1)}) custom-call(s32[5]{0:T(128)S(1)} %copy-done.33, bf16[256,256]{1,0:T(8,128)(2,1)S(1)} %collective-permute-done.31.refs_1_.refs_6_, bf16[256,256]{1,0:T(8,128)(2,1)S(1)} %collective-permute-done.32.refs_2_, bf16[256,256]{1,0:T(8,128)(2,1)S(1)} %collective-permute-done.33.refs_3_, ...), custom_call_target="tpu_custom_call" | custom-call | flops 2147483648 | bytes 11485184 | tf_op jit(solution)/shard_map/pallas_call | solution.py:139
  219.6 14.7 %all-to-all-start.2 = ((bf16[16,80,128]{2,1,0:T(8,128)(2,1)}), bf16[16,80,128]{2,1,0:T(8,128)(2,1)S(1)}, u32[]{:S(2)}, u32[]{:S(2)}) async-start(bf16[16,80,128]{2,1,0:T(8,128)(2,1)} %get-tuple-element.163), calls=%async_computation.2 | async-start | bytes 655360 | tf_op jit(solution)/shard_map/all_to_all | solution.py:442
  235.0 8.7 %all-to-all-done.2.refs_0_ = bf16[16,80,128]{2,1,0:T(8,128)(2,1)S(1)} async-done(((bf16[16,80,128]{2,1,0:T(8,128)(2,1)}), bf16[16,80,128]{2,1,0:T(8,128)(2,1)S(1)}, u32[]{:S(2)}, u32[]{:S(2)}) %all-to-all-start.2) | async-done | bytes 327712 | tf_op jit(solution)/shard_map/all_to_all | solution.py:442
  243.8 12.2 %all_to_all.22 = bf16[16,64,128]{2,1,0:T(8,128)(2,1)} all-to-all(bf16[16,64,128]{2,1,0:T(8,128)(2,1)S(1)} %shard_map.103), channel_id=1, replica_groups=mesh['section'=2,'ctx'=16,'heads'=8] {'ctx'}, dimensions={0} | all-to-all | bytes 524288 | tf_op jit(solution)/shard_map/all_to_all | solution.py:442
  256.0 5.4 %shard_map.104.refs_1_ = bf16[1280,256]{1,0:T(8,128)(2,1)} custom-call(bf16[1024,256]{1,0:T(8,128)(2,1)} %copy-done.21, f32[16,256]{1,0:T(8,128)} %copy-done.28, bf16[128,1024]{1,0:T(8,128)(2,1)} %copy-done.19, bf16[1024,128]{1,0:T(8,128)(2,1)} %bitcast.48, bf16[128,256]{1,0:T(8,128)(2,1)} %copy-done.26, bf16[1024,256]{1,0:T(8,128)(2,1)} %copy-done.9, ...), custom_call_target="tpu_custom_call" | custom-call | flops 268435456 | bytes 7127040 | tf_op jit(solution)/shard_map/pallas_call | solution.py:139
  263.8 3.5 %shard_map.105 = (bf16[4,512,256]{2,1,0:T(8,128)(2,1)S(1)}, bf16[4,512,256]{2,1,0:T(8,128)(2,1)S(1)}) custom-call(s32[5]{0:T(128)S(1)} %copy-done.34, bf16[1280,256]{1,0:T(8,128)(2,1)S(1)} %copy-done.8, bf16[4,256,1280]{2,1,0:T(8,128)(2,1)S(1)} %bitcast.28, bf16[4,256,1280]{2,1,0:T(8,128)(2,1)S(1)} %copy-done.5, bf16[2,256,1280]{2,1,0:T(8,128)(2,1)S(1)} %copy-done.14, ...), custom_call_target="tpu_custom_call" | custom-call | flops 2684354560 | bytes 13238272 | tf_op jit(solution)/shard_map/pallas_call | solution.py:139
  269.3 2.6 collective-permute-done.46.refs_1_.refs_2_
  272.1 4.2 %collective-permute-start.47 = (bf16[512,256]{1,0:T(8,128)(2,1)S(1)}, bf16[512,256]{1,0:T(8,128)(2,1)S(1)}, u32[]{:S(2)}, u32[]{:S(2)}) collective-permute-start(bf16[512,256]{1,0:T(8,128)(2,1)S(1)} %get-tuple-element.169), channel_id=1, source_target_pairs={{0,2},{1,3},{2,0},{3,1},{4,6},{5,7},{6,4},{7,5},{8,10},{9,11},{10,... | collective-permute-start | bytes 786440 | tf_op jit(solution)/shard_map/ppermute | solution.py:33
  278.3 3.4 %collective-permute-start.49 = (bf16[512,256]{1,0:T(8,128)(2,1)S(1)}, bf16[512,256]{1,0:T(8,128)(2,1)S(1)}, u32[]{:S(2)}, u32[]{:S(2)}) collective-permute-start(bf16[512,256]{1,0:T(8,128)(2,1)S(1)} %get-tuple-element.171), channel_id=1, source_target_pairs={{0,6},{1,7},{2,4},{3,5},{4,2},{5,3},{6,0},{7,1},{8,14},{9,15},{10,... | collective-permute-start | bytes 786440 | tf_op jit(solution)/shard_map/ppermute | solution.py:33
  281.6 3.0 collective-permute-done.47.refs_3_
  284.6 11.5 %collective-permute-done.48.refs_4_ = bf16[512,256]{1,0:T(8,128)(2,1)S(1)} collective-permute-done((bf16[512,256]{1,0:T(8,128)(2,1)S(1)}, bf16[512,256]{1,0:T(8,128)(2,1)S(1)}, u32[]{:S(2)}, u32[]{:S(2)}) %collective-permute-start.48) | collective-permute-done | bytes 262176 | tf_op jit(solution)/shard_map/ppermute | solution.py:33
  296.2 6.7 %collective-permute-done.49.refs_5_ = bf16[512,256]{1,0:T(8,128)(2,1)S(1)} collective-permute-done((bf16[512,256]{1,0:T(8,128)(2,1)S(1)}, bf16[512,256]{1,0:T(8,128)(2,1)S(1)}, u32[]{:S(2)}, u32[]{:S(2)}) %collective-permute-start.49) | collective-permute-done | bytes 262176 | tf_op jit(solution)/shard_map/ppermute | solution.py:33
  (190 shorter events, 68.9 us)
Async XLA Ops:
  0.0 14.3 %collective-permute-start.5 = (bf16[1024,256]{1,0:T(8,128)(2,1)}, bf16[1024,256]{1,0:T(8,128)(2,1)S(1)}, u32[]{:S(2)}, u32[]{:S(2)}) collective-permute-start(bf16[1024,256]{1,0:T(8,128)(2,1)} %bitcast.43), channel_id=1, source_target_pairs={{0,96},{1,97},{2,98},{3,99},{4,100},{5,101},{6,102},{7,103},{8,104... | collective-permute-start | bytes 1572872 | tf_op jit(solution)/shard_map/ppermute | solution.py:33
  2.8 15.2 %collective-permute-start.4 = (bf16[1024,256]{1,0:T(8,128)(2,1)}, bf16[1024,256]{1,0:T(8,128)(2,1)S(1)}, u32[]{:S(2)}, u32[]{:S(2)}) collective-permute-start(bf16[1024,256]{1,0:T(8,128)(2,1)} %bitcast.44), channel_id=1, source_target_pairs={{0,32},{1,33},{2,34},{3,35},{4,36},{5,37},{6,38},{7,39},{8,40},{9,... | collective-permute-start | bytes 1572872 | tf_op jit(solution)/shard_map/ppermute | solution.py:33
  7.6 22.1 %collective-permute-start = (bf16[256,1024]{1,0:T(8,128)(2,1)}, bf16[256,1024]{1,0:T(8,128)(2,1)}, u32[]{:S(2)}, u32[]{:S(2)}) collective-permute-start(bf16[256,1024]{1,0:T(8,128)(2,1)} %get-tuple-element.89), channel_id=1, source_target_pairs={{128,160},{129,161},{130,162},{131,163},{132,164},{133,165},{134,1... | collective-permute-start | bytes 1572872 | tf_op jit(solution)/shard_map/ppermute | solution.py:33
  9.1 20.6 %collective-permute-start.3 = (bf16[256,1024]{1,0:T(8,128)(2,1)}, bf16[256,1024]{1,0:T(8,128)(2,1)}, u32[]{:S(2)}, u32[]{:S(2)}) collective-permute-start(bf16[256,1024]{1,0:T(8,128)(2,1)} %get-tuple-element.91), channel_id=1, source_target_pairs={{128,224},{129,225},{130,226},{131,227},{132,228},{133,229},{134,2... | collective-permute-start | bytes 1572872 | tf_op jit(solution)/shard_map/ppermute | solution.py:33
  11.3 18.4 %collective-permute-start.2 = (bf16[128,1024]{1,0:T(8,128)(2,1)}, bf16[128,1024]{1,0:T(8,128)(2,1)S(1)}, u32[]{:S(2)}, u32[]{:S(2)}) collective-permute-start(bf16[128,1024]{1,0:T(8,128)(2,1)} %collective-permute-done.1.refs_3_), channel_id=1, source_target_pairs={{128,129},{129,128},{130,131},{131,130},{132,133},{133,132},{134,1... | collective-permute-start | bytes 786440 | tf_op jit(solution)/shard_map/ppermute | solution.py:33
  14.3 12.2 %collective-permute-start.7 = (bf16[512,256]{1,0:T(8,128)(2,1)S(1)}, bf16[512,256]{1,0:T(8,128)(2,1)S(1)}, u32[]{:S(2)}, u32[]{:S(2)}) collective-permute-start(bf16[512,256]{1,0:T(8,128)(2,1)S(1)} %slice.41), channel_id=1, source_target_pairs={{0,96},{1,97},{2,98},{3,99},{4,100},{5,101},{6,102},{7,103},{8,104... | collective-permute-start | bytes 786440 | tf_op jit(solution)/shard_map/ppermute | solution.py:33
  18.0 8.6 %collective-permute-start.6 = (bf16[512,256]{1,0:T(8,128)(2,1)S(1)}, bf16[512,256]{1,0:T(8,128)(2,1)S(1)}, u32[]{:S(2)}, u32[]{:S(2)}) collective-permute-start(bf16[512,256]{1,0:T(8,128)(2,1)S(1)} %slice.40), channel_id=1, source_target_pairs={{0,32},{1,33},{2,34},{3,35},{4,36},{5,37},{6,38},{7,39},{8,40},{9,... | collective-permute-start | bytes 786440 | tf_op jit(solution)/shard_map/ppermute | solution.py:33
  26.5 15.9 %collective-permute-start.13 = (bf16[256,1280]{1,0:T(8,128)(2,1)S(1)}, bf16[256,1280]{1,0:T(8,128)(2,1)S(1)}, u32[]{:S(2)}, u32[]{:S(2)}) collective-permute-start(bf16[256,1280]{1,0:T(8,128)(2,1)S(1)} %pad_maximum_fusion.refs_4_.refs_3_), channel_id=1, source_target_pairs={{0,24},{1,25},{2,26},{3,27},{4,28},{5,29},{6,30},{7,31},{8,0},{9,1... | collective-permute-start | bytes 1966088 | tf_op jit(solution)/shard_map/ppermute | solution.py:33
  29.6 16.6 %collective-permute-start.11 = (bf16[256,1280]{1,0:T(8,128)(2,1)S(1)}, bf16[256,1280]{1,0:T(8,128)(2,1)S(1)}, u32[]{:S(2)}, u32[]{:S(2)}) collective-permute-start(bf16[256,1280]{1,0:T(8,128)(2,1)S(1)} %pad_maximum_fusion.refs_4_.refs_3_), channel_id=1, source_target_pairs={{0,8},{1,9},{2,10},{3,11},{4,12},{5,13},{6,14},{7,15},{8,16},{9,17... | collective-permute-start | bytes 1966088 | tf_op jit(solution)/shard_map/ppermute | solution.py:33
  31.1 23.8 %collective-permute-start.8 = (bf16[1024,256]{1,0:T(8,128)(2,1)S(1)}, bf16[1024,256]{1,0:T(8,128)(2,1)S(1)}, u32[]{:S(2)}, u32[]{:S(2)}) collective-permute-start(bf16[1024,256]{1,0:T(8,128)(2,1)S(1)} %get-tuple-element.104), channel_id=1, source_target_pairs={{128,224},{129,225},{130,226},{131,227},{132,228},{133,229},{134,2... | collective-permute-start | bytes 1572872 | tf_op jit(solution)/shard_map/ppermute | solution.py:33
  31.8 23.1 %collective-permute-start.9 = (bf16[1024,256]{1,0:T(8,128)(2,1)S(1)}, bf16[1024,256]{1,0:T(8,128)(2,1)S(1)}, u32[]{:S(2)}, u32[]{:S(2)}) collective-permute-start(bf16[1024,256]{1,0:T(8,128)(2,1)S(1)} %get-tuple-element.105), channel_id=1, source_target_pairs={{128,192},{129,193},{130,194},{131,195},{132,196},{133,197},{134,1... | collective-permute-start | bytes 1572872 | tf_op jit(solution)/shard_map/ppermute | solution.py:33
  32.5 22.4 %collective-permute-start.10 = (bf16[1024,256]{1,0:T(8,128)(2,1)S(1)}, bf16[1024,256]{1,0:T(8,128)(2,1)S(1)}, u32[]{:S(2)}, u32[]{:S(2)}) collective-permute-start(bf16[1024,256]{1,0:T(8,128)(2,1)S(1)} %get-tuple-element.106), channel_id=1, source_target_pairs={{128,160},{129,161},{130,162},{131,163},{132,164},{133,165},{134,1... | collective-permute-start | bytes 1572872 | tf_op jit(solution)/shard_map/ppermute | solution.py:33
  42.5 8.7 %collective-permute-start.14 = (bf16[128,1280]{1,0:T(8,128)(2,1)S(1)}, bf16[128,1280]{1,0:T(8,128)(2,1)S(1)}, u32[]{:S(2)}, u32[]{:S(2)}) collective-permute-start(bf16[128,1280]{1,0:T(8,128)(2,1)S(1)} %slice.43), channel_id=1, source_target_pairs={{0,24},{1,25},{2,26},{3,27},{4,28},{5,29},{6,30},{7,31},{8,0},{9,1... | collective-permute-start | bytes 983048 | tf_op jit(solution)/shard_map/ppermute | solution.py:33
  46.3 8.6 %collective-permute-start.12 = (bf16[128,1280]{1,0:T(8,128)(2,1)S(1)}, bf16[128,1280]{1,0:T(8,128)(2,1)S(1)}, u32[]{:S(2)}, u32[]{:S(2)}) collective-permute-start(bf16[128,1280]{1,0:T(8,128)(2,1)S(1)} %slice.42), channel_id=1, source_target_pairs={{0,8},{1,9},{2,10},{3,11},{4,12},{5,13},{6,14},{7,15},{8,16},{9,17... | collective-permute-start | bytes 983048 | tf_op jit(solution)/shard_map/ppermute | solution.py:33
  56.0 64.7 %collective-permute-start.18 = (bf16[4,256,1280]{2,1,0:T(8,128)(2,1)S(1)}, bf16[4,256,1280]{2,1,0:T(8,128)(2,1)S(1)}, u32[]{:S(2)}, u32[]{:S(2)}) collective-permute-start(bf16[4,256,1280]{2,1,0:T(8,128)(2,1)S(1)} %bitcast.26), channel_id=1, source_target_pairs={{0,96},{1,97},{2,98},{3,99},{4,100},{5,101},{6,102},{7,103},{8,104... | collective-permute-start | bytes 7864328 | tf_op jit(solution)/shard_map/ppermute | solution.py:33
  60.2 60.5 %collective-permute-start.17 = (bf16[4,256,1280]{2,1,0:T(8,128)(2,1)S(1)}, bf16[4,256,1280]{2,1,0:T(8,128)(2,1)S(1)}, u32[]{:S(2)}, u32[]{:S(2)}) collective-permute-start(bf16[4,256,1280]{2,1,0:T(8,128)(2,1)S(1)} %bitcast.27), channel_id=1, source_target_pairs={{0,32},{1,33},{2,34},{3,35},{4,36},{5,37},{6,38},{7,39},{8,40},{9,... | collective-permute-start | bytes 7864328 | tf_op jit(solution)/shard_map/ppermute | solution.py:33
  63.6 57.1 %collective-permute-start.16 = (bf16[4,1024,256]{2,1,0:T(8,128)(2,1)S(1)}, bf16[4,1024,256]{2,1,0:T(8,128)(2,1)S(1)}, u32[]{:S(2)}, u32[]{:S(2)}) collective-permute-start(bf16[4,1024,256]{2,1,0:T(8,128)(2,1)S(1)} %bitcast.29), channel_id=1, source_target_pairs={{0,24},{1,25},{2,26},{3,27},{4,28},{5,29},{6,30},{7,31},{8,0},{9,1... | collective-permute-start | bytes 6291464 | tf_op jit(solution)/shard_map/ppermute | solution.py:33
  65.5 55.2 %collective-permute-start.15 = (bf16[4,1024,256]{2,1,0:T(8,128)(2,1)S(1)}, bf16[4,1024,256]{2,1,0:T(8,128)(2,1)S(1)}, u32[]{:S(2)}, u32[]{:S(2)}) collective-permute-start(bf16[4,1024,256]{2,1,0:T(8,128)(2,1)S(1)} %bitcast.30), channel_id=1, source_target_pairs={{0,8},{1,9},{2,10},{3,11},{4,12},{5,13},{6,14},{7,15},{8,16},{9,17... | collective-permute-start | bytes 6291464 | tf_op jit(solution)/shard_map/ppermute | solution.py:33
  123.0 35.1 %collective-permute-start.22 = (bf16[2,256,1280]{2,1,0:T(8,128)(2,1)S(1)}, bf16[2,256,1280]{2,1,0:T(8,128)(2,1)S(1)}, u32[]{:S(2)}, u32[]{:S(2)}) collective-permute-start(bf16[2,256,1280]{2,1,0:T(8,128)(2,1)S(1)} %slice.37), channel_id=1, source_target_pairs={{0,96},{1,97},{2,98},{3,99},{4,100},{5,101},{6,102},{7,103},{8,104... | collective-permute-start | bytes 3932168 | tf_op jit(solution)/shard_map/ppermute | solution.py:33
  125.2 33.0 %collective-permute-start.21 = (bf16[2,256,1280]{2,1,0:T(8,128)(2,1)S(1)}, bf16[2,256,1280]{2,1,0:T(8,128)(2,1)S(1)}, u32[]{:S(2)}, u32[]{:S(2)}) collective-permute-start(bf16[2,256,1280]{2,1,0:T(8,128)(2,1)S(1)} %slice.36), channel_id=1, source_target_pairs={{0,32},{1,33},{2,34},{3,35},{4,36},{5,37},{6,38},{7,39},{8,40},{9,... | collective-permute-start | bytes 3932168 | tf_op jit(solution)/shard_map/ppermute | solution.py:33
  129.0 29.1 %collective-permute-start.20 = (bf16[2,1024,256]{2,1,0:T(8,128)(2,1)S(1)}, bf16[2,1024,256]{2,1,0:T(8,128)(2,1)S(1)}, u32[]{:S(2)}, u32[]{:S(2)}) collective-permute-start(bf16[2,1024,256]{2,1,0:T(8,128)(2,1)S(1)} %slice.35), channel_id=1, source_target_pairs={{0,24},{1,25},{2,26},{3,27},{4,28},{5,29},{6,30},{7,31},{8,0},{9,1... | collective-permute-start | bytes 3145736 | tf_op jit(solution)/shard_map/ppermute | solution.py:33
  134.3 23.8 %collective-permute-start.19 = (bf16[2,1024,256]{2,1,0:T(8,128)(2,1)S(1)}, bf16[2,1024,256]{2,1,0:T(8,128)(2,1)S(1)}, u32[]{:S(2)}, u32[]{:S(2)}) collective-permute-start(bf16[2,1024,256]{2,1,0:T(8,128)(2,1)S(1)} %slice.34), channel_id=1, source_target_pairs={{0,8},{1,9},{2,10},{3,11},{4,12},{5,13},{6,14},{7,15},{8,16},{9,17... | collective-permute-start | bytes 3145736 | tf_op jit(solution)/shard_map/ppermute | solution.py:33
  171.2 14.6 %collective-permute-start.31 = (bf16[256,256]{1,0:T(8,128)(2,1)S(1)}, bf16[256,256]{1,0:T(8,128)(2,1)S(1)}, u32[]{:S(2)}, u32[]{:S(2)}) collective-permute-start(bf16[256,256]{1,0:T(8,128)(2,1)S(1)} %shard_map.99), channel_id=1, source_target_pairs={{128,0},{129,1},{130,32},{131,33},{132,64},{133,65},{134,96},{135,... | collective-permute-start | bytes 393224 | tf_op jit(solution)/shard_map/ppermute | solution.py:33
  172.6 23.9 %collective-permute-start.39 = (bf16[256,256]{1,0:T(8,128)(2,1)S(1)}, bf16[256,256]{1,0:T(8,128)(2,1)S(1)}, u32[]{:S(2)}, u32[]{:S(2)}) collective-permute-start(bf16[256,256]{1,0:T(8,128)(2,1)S(1)} %shard_map.101), channel_id=1, source_target_pairs={{128,0},{129,1},{130,32},{131,33},{132,64},{133,65},{134,96},{135,... | collective-permute-start | bytes 393224 | tf_op jit(solution)/shard_map/ppermute | solution.py:33
  185.8 17.6 %collective-permute-start.34 = (bf16[256,256]{1,0:T(8,128)(2,1)S(1)}, bf16[256,256]{1,0:T(8,128)(2,1)S(1)}, u32[]{:S(2)}, u32[]{:S(2)}) collective-permute-start(bf16[256,256]{1,0:T(8,128)(2,1)S(1)} %collective-permute-done.31.refs_1_.refs_6_), channel_id=1, source_target_pairs={{0,6},{1,7},{2,4},{3,5},{4,2},{5,3},{6,0},{7,1},{8,14},{9,15},{10,... | collective-permute-start | bytes 393224 | tf_op jit(solution)/shard_map/ppermute | solution.py:33
  191.3 14.6 %collective-permute-start.33 = (bf16[256,256]{1,0:T(8,128)(2,1)S(1)}, bf16[256,256]{1,0:T(8,128)(2,1)S(1)}, u32[]{:S(2)}, u32[]{:S(2)}) collective-permute-start(bf16[256,256]{1,0:T(8,128)(2,1)S(1)} %collective-permute-done.31.refs_1_.refs_6_), channel_id=1, source_target_pairs={{0,4},{1,5},{2,6},{3,7},{4,0},{5,1},{6,2},{7,3},{8,12},{9,13},{10,... | collective-permute-start | bytes 393224 | tf_op jit(solution)/shard_map/ppermute | solution.py:33
  193.2 12.7 %collective-permute-start.32 = (bf16[256,256]{1,0:T(8,128)(2,1)S(1)}, bf16[256,256]{1,0:T(8,128)(2,1)S(1)}, u32[]{:S(2)}, u32[]{:S(2)}) collective-permute-start(bf16[256,256]{1,0:T(8,128)(2,1)S(1)} %collective-permute-done.31.refs_1_.refs_6_), channel_id=1, source_target_pairs={{0,2},{1,3},{2,0},{3,1},{4,6},{5,7},{6,4},{7,5},{8,10},{9,11},{10,... | collective-permute-start | bytes 393224 | tf_op jit(solution)/shard_map/ppermute | solution.py:33
  196.6 11.3 %collective-permute-start.42 = (bf16[256,256]{1,0:T(8,128)(2,1)S(1)}, bf16[256,256]{1,0:T(8,128)(2,1)S(1)}, u32[]{:S(2)}, u32[]{:S(2)}) collective-permute-start(bf16[256,256]{1,0:T(8,128)(2,1)S(1)} %collective-permute-done.39.refs_5_.refs_7_), channel_id=1, source_target_pairs={{0,6},{1,7},{2,4},{3,5},{4,2},{5,3},{6,0},{7,1},{8,14},{9,15},{10,... | collective-permute-start | bytes 393224 | tf_op jit(solution)/shard_map/ppermute | solution.py:33
  219.6 24.1 %all-to-all-start.2 = ((bf16[16,80,128]{2,1,0:T(8,128)(2,1)}), bf16[16,80,128]{2,1,0:T(8,128)(2,1)S(1)}, u32[]{:S(2)}, u32[]{:S(2)}) async-start(bf16[16,80,128]{2,1,0:T(8,128)(2,1)} %get-tuple-element.163), calls=%async_computation.2 | async-start | bytes 655360 | tf_op jit(solution)/shard_map/all_to_all | solution.py:442
  272.1 12.5 %collective-permute-start.47 = (bf16[512,256]{1,0:T(8,128)(2,1)S(1)}, bf16[512,256]{1,0:T(8,128)(2,1)S(1)}, u32[]{:S(2)}, u32[]{:S(2)}) collective-permute-start(bf16[512,256]{1,0:T(8,128)(2,1)S(1)} %get-tuple-element.169), channel_id=1, source_target_pairs={{0,2},{1,3},{2,0},{3,1},{4,6},{5,7},{6,4},{7,5},{8,10},{9,11},{10,... | collective-permute-start | bytes 786440 | tf_op jit(solution)/shard_map/ppermute | solution.py:33
  276.3 19.9 %collective-permute-start.48 = (bf16[512,256]{1,0:T(8,128)(2,1)S(1)}, bf16[512,256]{1,0:T(8,128)(2,1)S(1)}, u32[]{:S(2)}, u32[]{:S(2)}) collective-permute-start(bf16[512,256]{1,0:T(8,128)(2,1)S(1)} %get-tuple-element.170), channel_id=1, source_target_pairs={{0,4},{1,5},{2,6},{3,7},{4,0},{5,1},{6,2},{7,3},{8,12},{9,13},{10,... | collective-permute-start | bytes 786440 | tf_op jit(solution)/shard_map/ppermute | solution.py:33
  278.3 24.7 %collective-permute-start.49 = (bf16[512,256]{1,0:T(8,128)(2,1)S(1)}, bf16[512,256]{1,0:T(8,128)(2,1)S(1)}, u32[]{:S(2)}, u32[]{:S(2)}) collective-permute-start(bf16[512,256]{1,0:T(8,128)(2,1)S(1)} %get-tuple-element.171), channel_id=1, source_target_pairs={{0,6},{1,7},{2,4},{3,5},{4,2},{5,3},{6,0},{7,1},{8,14},{9,15},{10,... | collective-permute-start | bytes 786440 | tf_op jit(solution)/shard_map/ppermute | solution.py:33
  (55 other events, 1648.4 us)

commit v8 on v6

--- a/solution.py
+++ b/solution.py
@@ -345,14 +345,21 @@
     to_halves(u, z ^ x ^ behind(x, 2), core, keep, (give_a, give_b))
 
 
-def whole_body(at, g, w0, w1, wl, wh, w3, keep, give, u):
+def whole_body(kept, at, g, w0, w1, wl, wh, w3, out):
     x, y, z, core = at[0], at[1], at[2], at[3]
+    side = core if kept else 1 - core
     fine = w0.shape[1]
     for k in range(SIDE):
-        for j in range(SIDE):
-            w = (w0, w1, wl if j < CORES else wh, w3)[k][j % CORES if k == 2 else j]
-            u[k, span(behind(y, j), fine), :] = dot(w, g[...], 1, 0).astype(bf16)
-        to_halves(u.at[k], z ^ behind(x, k), core, keep, (give,))
+        q = z ^ behind(x, k)
+        for i in range(CORES):
+            j = behind(y, side * CORES + i)
+            rows = slice(i * fine, (i + 1) * fine)
+            if k == 2:
+                within = lax.rem(j, CORES)
+                w = jnp.where(j < CORES, wl[within], wh[within])
+            else:
+                w = (w0, w1, None, w3)[k][j]
+            out[q, rows, :] = dot(w, g[...], 1, 0).astype(bf16)
 
 
 def rows_of(keep, q, got, part):
@@ -555,14 +562,16 @@
     )
     held, settled = tie((exchange(states), settled))
     grads = within(grad_ssd, exchange(scanned(held)), MOST)
-    keep, give = call(
-        whole_body,
-        [chunks, chunks],
-        [grads, back_set, width_sides[0], *width_far, width_sides[1]],
-        at,
-        scratch=wide,
-        flops=2 * rows * width * outer,
-    )
+    give, keep = [
+        call(
+            functools.partial(whole_body, kept),
+            [chunks],
+            [grads, back_set, width_sides[0], *width_far, width_sides[1]],
+            at,
+            flops=rows * width * outer,
+        )[0]
+        for kept in (False, True)
+    ]
     sums = over_heads(keep, give, (0,))
     (result,) = call(result_body, [struct((1, rows, share))], [*sums, *arrived, settled], at)
     return result

time: 304 us -> 303 us (level)
    unnamed x80 -> x76, local copies, waits for them, and re-layouts: 11.5 us -> 10.4 us
    pallas_call x17 -> x18, Pallas kernels: 24.6 us -> 24.5 us  [call(): pl.pallas_call(kernel, in_specs=[pl.BlockSpec(memory_space=pltpu.SMEM)] *...]
  transfers between devices with their start and end apart: 51 -> 51, of which waited for: 12 -> 14; matrix products, arithmetic and copies ran while one was open for 2% -> 2% of each run, Pallas kernels for 1% -> 2%
where the time goes in v8:
time: 303 us; the launch traced here: 301 us
  starting transfers between devices  108 us (36%)
  blocking collectives  84.6 us (28%)
  waiting for transfers between devices  64.9 us (21%)
  Pallas kernels  24.5 us (8%)
  local copies, waits for them, and re-layouts  15.9 us (5%)
    ppermute x50, starting transfers between devices, routed(): return lax.ppermute(value, AXES, pairs)  93.4 us
    all_to_all x3, blocking collectives, exchange(): return lax.all_to_all(states, 'ctx', 0, 0)  84.6 us
    ppermute x50, waiting for transfers between devices, routed(): return lax.ppermute(value, AXES, pairs)  56.9 us
    pallas_call x18, Pallas kernels, call(): pl.pallas_call(kernel, in_specs=[pl.BlockSpec(memory_space=pltpu.SMEM)] *...  24.5 us
    all_to_all x1, starting transfers between devices, exchange(): return lax.all_to_all(states, 'ctx', 0, 0)  14.8 us
    unnamed x76, local copies, waits for them, and re-layouts  10.4 us
    all_to_all x1, waiting for transfers between devices, exchange(): return lax.all_to_all(states, 'ctx', 0, 0)  8.03 us
  transfers between devices with their start and end apart: 51, of which 14 were waited for; matrix products, arithmetic and copies ran while one was open for 2% of the time, Pallas kernels for 2%

profile of v8, /device:TPU:32, one launch (start us, length us, event | category | flops | bytes accessed | tf_op | source)
XLA Modules:
  0.0 300.6 jit_solution(7059656041707286490)
XLA Ops:
  0.0 2.8 collective-permute-start.5
  4.4 2.5 constant_dynamic-slice_fusion
  14.3 3.7 %collective-permute-start.7 = (bf16[512,256]{1,0:T(8,128)(2,1)S(1)}, bf16[512,256]{1,0:T(8,128)(2,1)S(1)}, u32[]{:S(2)}, u32[]{:S(2)}) collective-permute-start(bf16[512,256]{1,0:T(8,128)(2,1)S(1)} %slice.41), channel_id=1, source_target_pairs={{0,96},{1,97},{2,98},{3,99},{4,100},{5,101},{6,102},{7,103},{8,104... | collective-permute-start | bytes 786440 | tf_op jit(solution)/shard_map/ppermute | solution.py:33
  22.6 3.5 %collective-permute-done.6.refs_7_ = bf16[512,256]{1,0:T(8,128)(2,1)S(1)} collective-permute-done((bf16[512,256]{1,0:T(8,128)(2,1)S(1)}, bf16[512,256]{1,0:T(8,128)(2,1)S(1)}, u32[]{:S(2)}, u32[]{:S(2)}) %collective-permute-start.6) | collective-permute-done | bytes 262176 | tf_op jit(solution)/shard_map/ppermute | solution.py:33
  26.2 3.0 %collective-permute-start.13 = (bf16[256,1280]{1,0:T(8,128)(2,1)S(1)}, bf16[256,1280]{1,0:T(8,128)(2,1)S(1)}, u32[]{:S(2)}, u32[]{:S(2)}) collective-permute-start(bf16[256,1280]{1,0:T(8,128)(2,1)S(1)} %pad_maximum_fusion.refs_4_.refs_3_), channel_id=1, source_target_pairs={{0,24},{1,25},{2,26},{3,27},{4,28},{5,29},{6,30},{7,31},{8,0},{9,1... | collective-permute-start | bytes 1966088 | tf_op jit(solution)/shard_map/ppermute | solution.py:33
  32.9 8.2 %collective-permute-done.13.refs_8_.refs_7_ = bf16[256,1280]{1,0:T(8,128)(2,1)S(1)} collective-permute-done((bf16[256,1280]{1,0:T(8,128)(2,1)S(1)}, bf16[256,1280]{1,0:T(8,128)(2,1)S(1)}, u32[]{:S(2)}, u32[]{:S(2)}) %collective-permute-start.13) | collective-permute-done | bytes 655392 | tf_op jit(solution)/shard_map/ppermute | solution.py:33
  41.1 3.8 %collective-permute-start.14 = (bf16[128,1280]{1,0:T(8,128)(2,1)S(1)}, bf16[128,1280]{1,0:T(8,128)(2,1)S(1)}, u32[]{:S(2)}, u32[]{:S(2)}) collective-permute-start(bf16[128,1280]{1,0:T(8,128)(2,1)S(1)} %slice.43), channel_id=1, source_target_pairs={{0,24},{1,25},{2,26},{3,27},{4,28},{5,29},{6,30},{7,31},{8,0},{9,1... | collective-permute-start | bytes 983048 | tf_op jit(solution)/shard_map/ppermute | solution.py:33
  45.3 4.2 %collective-permute-done.14.refs_7_.refs_6_ = bf16[128,1280]{1,0:T(8,128)(2,1)S(1)} collective-permute-done((bf16[128,1280]{1,0:T(8,128)(2,1)S(1)}, bf16[128,1280]{1,0:T(8,128)(2,1)S(1)}, u32[]{:S(2)}, u32[]{:S(2)}) %collective-permute-start.14) | collective-permute-done | bytes 327712 | tf_op jit(solution)/shard_map/ppermute | solution.py:33
  49.5 4.0 %collective-permute-done.12.refs_6_.refs_5_ = bf16[128,1280]{1,0:T(8,128)(2,1)S(1)} collective-permute-done((bf16[128,1280]{1,0:T(8,128)(2,1)S(1)}, bf16[128,1280]{1,0:T(8,128)(2,1)S(1)}, u32[]{:S(2)}, u32[]{:S(2)}) %collective-permute-start.12) | collective-permute-done | bytes 327712 | tf_op jit(solution)/shard_map/ppermute | solution.py:33
  57.0 3.5 %collective-permute-start.17 = (bf16[4,256,1280]{2,1,0:T(8,128)(2,1)S(1)}, bf16[4,256,1280]{2,1,0:T(8,128)(2,1)S(1)}, u32[]{:S(2)}, u32[]{:S(2)}) collective-permute-start(bf16[4,256,1280]{2,1,0:T(8,128)(2,1)S(1)} %bitcast.27), channel_id=1, source_target_pairs={{0,32},{1,33},{2,34},{3,35},{4,36},{5,37},{6,38},{7,39},{8,40},{9,... | collective-permute-start | bytes 7864328 | tf_op jit(solution)/shard_map/ppermute | solution.py:33
  62.4 3.9 %collective-permute-start.15 = (bf16[4,1024,256]{2,1,0:T(8,128)(2,1)S(1)}, bf16[4,1024,256]{2,1,0:T(8,128)(2,1)S(1)}, u32[]{:S(2)}, u32[]{:S(2)}) collective-permute-start(bf16[4,1024,256]{2,1,0:T(8,128)(2,1)S(1)} %bitcast.31), channel_id=1, source_target_pairs={{0,8},{1,9},{2,10},{3,11},{4,12},{5,13},{6,14},{7,15},{8,16},{9,17... | collective-permute-start | bytes 6291464 | tf_op jit(solution)/shard_map/ppermute | solution.py:33
  66.3 50.8 %all_to_all.20.refs_0_ = bf16[16,80,128]{2,1,0:T(8,128)(2,1)S(1)} all-to-all(bf16[16,80,128]{2,1,0:T(8,128)(2,1)S(1)} %get-tuple-element.123), channel_id=1, replica_groups=mesh['section'=2,'ctx'=16,'heads'=8] {'ctx'}, dimensions={0} | all-to-all | bytes 655360 | tf_op jit(solution)/shard_map/all_to_all | solution.py:449
  120.8 3.7 %collective-permute-start.21 = (bf16[2,256,1280]{2,1,0:T(8,128)(2,1)S(1)}, bf16[2,256,1280]{2,1,0:T(8,128)(2,1)S(1)}, u32[]{:S(2)}, u32[]{:S(2)}) collective-permute-start(bf16[2,256,1280]{2,1,0:T(8,128)(2,1)S(1)} %slice.36), channel_id=1, source_target_pairs={{0,32},{1,33},{2,34},{3,35},{4,36},{5,37},{6,38},{7,39},{8,40},{9,... | collective-permute-start | bytes 3932168 | tf_op jit(solution)/shard_map/ppermute | solution.py:33
  124.7 5.2 %collective-permute-start.20 = (bf16[2,1024,256]{2,1,0:T(8,128)(2,1)S(1)}, bf16[2,1024,256]{2,1,0:T(8,128)(2,1)S(1)}, u32[]{:S(2)}, u32[]{:S(2)}) collective-permute-start(bf16[2,1024,256]{2,1,0:T(8,128)(2,1)S(1)} %slice.35), channel_id=1, source_target_pairs={{0,24},{1,25},{2,26},{3,27},{4,28},{5,29},{6,30},{7,31},{8,0},{9,1... | collective-permute-start | bytes 3145736 | tf_op jit(solution)/shard_map/ppermute | solution.py:33
  131.9 21.8 %all_to_all.21 = bf16[16,64,128]{2,1,0:T(8,128)(2,1)S(1)} all-to-all(bf16[16,64,128]{2,1,0:T(8,128)(2,1)S(1)} %shard_map.94), channel_id=1, replica_groups=mesh['section'=2,'ctx'=16,'heads'=8] {'ctx'}, dimensions={0} | all-to-all | bytes 524288 | tf_op jit(solution)/shard_map/all_to_all | solution.py:449
  155.9 3.1 %shard_map.95.refs_1_ = bf16[1280,256]{1,0:T(8,128)(2,1)S(1)} custom-call(bf16[1024,256]{1,0:T(8,128)(2,1)S(1)} %get-tuple-element.118.refs_0_, f32[16,256]{1,0:T(8,128)S(1)} %get-tuple-element.115.refs_4_.refs_1_.refs_16_, bf16[128,1024]{1,0:T(8,128)(2,1)S(1)} %get-tuple-element.119.refs_2_, bf16[1024,128]{1,0:T(8,128)(2,1)S(1)} %bitcast.35, ...), custom_call_target="tpu_custom_call" | custom-call | flops 268435456 | bytes 7127040 | tf_op jit(solution)/shard_map/pallas_call | solution.py:139
  171.6 12.7 %collective-permute-done.31.refs_1_.refs_6_ = bf16[256,256]{1,0:T(8,128)(2,1)S(1)} collective-permute-done((bf16[256,256]{1,0:T(8,128)(2,1)S(1)}, bf16[256,256]{1,0:T(8,128)(2,1)S(1)}, u32[]{:S(2)}, u32[]{:S(2)}) %collective-permute-start.31) | collective-permute-done | bytes 131104 | tf_op jit(solution)/shard_map/ppermute | solution.py:33
  184.3 5.9 %collective-permute-start.34 = (bf16[256,256]{1,0:T(8,128)(2,1)S(1)}, bf16[256,256]{1,0:T(8,128)(2,1)S(1)}, u32[]{:S(2)}, u32[]{:S(2)}) collective-permute-start(bf16[256,256]{1,0:T(8,128)(2,1)S(1)} %collective-permute-done.31.refs_1_.refs_6_), channel_id=1, source_target_pairs={{0,6},{1,7},{2,4},{3,5},{4,2},{5,3},{6,0},{7,1},{8,14},{9,15},{10,... | collective-permute-start | bytes 393224 | tf_op jit(solution)/shard_map/ppermute | solution.py:33
  192.1 3.4 %collective-permute-start.32 = (bf16[256,256]{1,0:T(8,128)(2,1)S(1)}, bf16[256,256]{1,0:T(8,128)(2,1)S(1)}, u32[]{:S(2)}, u32[]{:S(2)}) collective-permute-start(bf16[256,256]{1,0:T(8,128)(2,1)S(1)} %collective-permute-done.31.refs_1_.refs_6_), channel_id=1, source_target_pairs={{0,2},{1,3},{2,0},{3,1},{4,6},{5,7},{6,4},{7,5},{8,10},{9,11},{10,... | collective-permute-start | bytes 393224 | tf_op jit(solution)/shard_map/ppermute | solution.py:33
  195.5 3.9 %collective-permute-start.42 = (bf16[256,256]{1,0:T(8,128)(2,1)S(1)}, bf16[256,256]{1,0:T(8,128)(2,1)S(1)}, u32[]{:S(2)}, u32[]{:S(2)}) collective-permute-start(bf16[256,256]{1,0:T(8,128)(2,1)S(1)} %collective-permute-done.39.refs_5_.refs_7_), channel_id=1, source_target_pairs={{0,6},{1,7},{2,4},{3,5},{4,2},{5,3},{6,0},{7,1},{8,14},{9,15},{10,... | collective-permute-start | bytes 393224 | tf_op jit(solution)/shard_map/ppermute | solution.py:33
  199.5 2.8 collective-permute-start.41
  202.3 2.5 collective-permute-start.40
  213.0 4.1 %shard_map.102 = (bf16[1024,256]{1,0:T(8,128)(2,1)S(1)}, bf16[16,80,128]{2,1,0:T(8,128)(2,1)S(1)}) custom-call(s32[5]{0:T(128)S(1)} %copy-done.29, bf16[256,256]{1,0:T(8,128)(2,1)S(1)} %collective-permute-done.31.refs_1_.refs_6_, bf16[256,256]{1,0:T(8,128)(2,1)S(1)} %collective-permute-done.32.refs_2_, bf16[256,256]{1,0:T(8,128)(2,1)S(1)} %collective-permute-done.33.refs_3_, ...), custom_call_target="tpu_custom_call" | custom-call | flops 2147483648 | bytes 11485184 | tf_op jit(solution)/shard_map/pallas_call | solution.py:139
  218.6 14.8 %all-to-all-start.2 = ((bf16[16,80,128]{2,1,0:T(8,128)(2,1)}), bf16[16,80,128]{2,1,0:T(8,128)(2,1)S(1)}, u32[]{:S(2)}, u32[]{:S(2)}) async-start(bf16[16,80,128]{2,1,0:T(8,128)(2,1)} %copy-done.20), calls=%async_computation.2 | async-start | bytes 655360 | tf_op jit(solution)/shard_map/all_to_all | solution.py:449
  234.9 8.0 %all-to-all-done.2.refs_0_ = bf16[16,80,128]{2,1,0:T(8,128)(2,1)S(1)} async-done(((bf16[16,80,128]{2,1,0:T(8,128)(2,1)}), bf16[16,80,128]{2,1,0:T(8,128)(2,1)S(1)}, u32[]{:S(2)}, u32[]{:S(2)}) %all-to-all-start.2) | async-done | bytes 327712 | tf_op jit(solution)/shard_map/all_to_all | solution.py:449
  243.0 12.0 %all_to_all.22 = bf16[16,64,128]{2,1,0:T(8,128)(2,1)} all-to-all(bf16[16,64,128]{2,1,0:T(8,128)(2,1)S(1)} %shard_map.103), channel_id=1, replica_groups=mesh['section'=2,'ctx'=16,'heads'=8] {'ctx'}, dimensions={0} | all-to-all | bytes 524288 | tf_op jit(solution)/shard_map/all_to_all | solution.py:449
  255.1 5.3 %shard_map.104.refs_1_ = bf16[1280,256]{1,0:T(8,128)(2,1)} custom-call(bf16[1024,256]{1,0:T(8,128)(2,1)} %copy-done.15, f32[16,256]{1,0:T(8,128)} %copy-done.23, bf16[128,1024]{1,0:T(8,128)(2,1)} %copy-done.14, bf16[1024,128]{1,0:T(8,128)(2,1)} %bitcast.49, bf16[128,256]{1,0:T(8,128)(2,1)} %copy-done.21, bf16[1024,256]{1,0:T(8,128)(2,1)} %copy-done.12, ...), custom_call_target="tpu_custom_call" | custom-call | flops 268435456 | bytes 7127040 | tf_op jit(solution)/shard_map/pallas_call | solution.py:139
  271.0 4.1 %collective-permute-start.47 = (bf16[512,256]{1,0:T(8,128)(2,1)S(1)}, bf16[512,256]{1,0:T(8,128)(2,1)S(1)}, u32[]{:S(2)}, u32[]{:S(2)}) collective-permute-start(bf16[512,256]{1,0:T(8,128)(2,1)S(1)} %get-tuple-element.165), channel_id=1, source_target_pairs={{0,4},{1,5},{2,6},{3,7},{4,0},{5,1},{6,2},{7,3},{8,12},{9,13},{10,... | collective-permute-start | bytes 786440 | tf_op jit(solution)/shard_map/ppermute | solution.py:33
  275.1 3.5 %collective-permute-start.48 = (bf16[512,256]{1,0:T(8,128)(2,1)S(1)}, bf16[512,256]{1,0:T(8,128)(2,1)S(1)}, u32[]{:S(2)}, u32[]{:S(2)}) collective-permute-start(bf16[512,256]{1,0:T(8,128)(2,1)S(1)} %get-tuple-element.166), channel_id=1, source_target_pairs={{0,6},{1,7},{2,4},{3,5},{4,2},{5,3},{6,0},{7,1},{8,14},{9,15},{10,... | collective-permute-start | bytes 786440 | tf_op jit(solution)/shard_map/ppermute | solution.py:33
  278.6 2.5 collective-permute-start.49
  281.1 11.0 %collective-permute-done.47.refs_3_ = bf16[512,256]{1,0:T(8,128)(2,1)S(1)} collective-permute-done((bf16[512,256]{1,0:T(8,128)(2,1)S(1)}, bf16[512,256]{1,0:T(8,128)(2,1)S(1)}, u32[]{:S(2)}, u32[]{:S(2)}) %collective-permute-start.47) | collective-permute-done | bytes 262176 | tf_op jit(solution)/shard_map/ppermute | solution.py:33
  292.1 6.9 %collective-permute-done.48.refs_4_ = bf16[512,256]{1,0:T(8,128)(2,1)S(1)} collective-permute-done((bf16[512,256]{1,0:T(8,128)(2,1)S(1)}, bf16[512,256]{1,0:T(8,128)(2,1)S(1)}, u32[]{:S(2)}, u32[]{:S(2)}) %collective-permute-start.48) | collective-permute-done | bytes 262176 | tf_op jit(solution)/shard_map/ppermute | solution.py:33
  (187 shorter events, 68.3 us)
Async XLA Ops:
  0.0 14.3 %collective-permute-start.5 = (bf16[1024,256]{1,0:T(8,128)(2,1)}, bf16[1024,256]{1,0:T(8,128)(2,1)S(1)}, u32[]{:S(2)}, u32[]{:S(2)}) collective-permute-start(bf16[1024,256]{1,0:T(8,128)(2,1)} %bitcast.44), channel_id=1, source_target_pairs={{0,96},{1,97},{2,98},{3,99},{4,100},{5,101},{6,102},{7,103},{8,104... | collective-permute-start | bytes 1572872 | tf_op jit(solution)/shard_map/ppermute | solution.py:33
  2.8 15.2 %collective-permute-start.4 = (bf16[1024,256]{1,0:T(8,128)(2,1)}, bf16[1024,256]{1,0:T(8,128)(2,1)S(1)}, u32[]{:S(2)}, u32[]{:S(2)}) collective-permute-start(bf16[1024,256]{1,0:T(8,128)(2,1)} %bitcast.45), channel_id=1, source_target_pairs={{0,32},{1,33},{2,34},{3,35},{4,36},{5,37},{6,38},{7,39},{8,40},{9,... | collective-permute-start | bytes 1572872 | tf_op jit(solution)/shard_map/ppermute | solution.py:33
  8.4 20.9 %collective-permute-start = (bf16[256,1024]{1,0:T(8,128)(2,1)}, bf16[256,1024]{1,0:T(8,128)(2,1)}, u32[]{:S(2)}, u32[]{:S(2)}) collective-permute-start(bf16[256,1024]{1,0:T(8,128)(2,1)} %get-tuple-element.87), channel_id=1, source_target_pairs={{128,160},{129,161},{130,162},{131,163},{132,164},{133,165},{134,1... | collective-permute-start | bytes 1572872 | tf_op jit(solution)/shard_map/ppermute | solution.py:33
  9.8 19.4 %collective-permute-start.3 = (bf16[256,1024]{1,0:T(8,128)(2,1)}, bf16[256,1024]{1,0:T(8,128)(2,1)}, u32[]{:S(2)}, u32[]{:S(2)}) collective-permute-start(bf16[256,1024]{1,0:T(8,128)(2,1)} %get-tuple-element.89), channel_id=1, source_target_pairs={{128,224},{129,225},{130,226},{131,227},{132,228},{133,229},{134,2... | collective-permute-start | bytes 1572872 | tf_op jit(solution)/shard_map/ppermute | solution.py:33
  12.1 17.2 %collective-permute-start.2 = (bf16[128,1024]{1,0:T(8,128)(2,1)}, bf16[128,1024]{1,0:T(8,128)(2,1)S(1)}, u32[]{:S(2)}, u32[]{:S(2)}) collective-permute-start(bf16[128,1024]{1,0:T(8,128)(2,1)} %collective-permute-done.1.refs_3_), channel_id=1, source_target_pairs={{128,129},{129,128},{130,131},{131,130},{132,133},{133,132},{134,1... | collective-permute-start | bytes 786440 | tf_op jit(solution)/shard_map/ppermute | solution.py:33
  14.3 8.4 %collective-permute-start.7 = (bf16[512,256]{1,0:T(8,128)(2,1)S(1)}, bf16[512,256]{1,0:T(8,128)(2,1)S(1)}, u32[]{:S(2)}, u32[]{:S(2)}) collective-permute-start(bf16[512,256]{1,0:T(8,128)(2,1)S(1)} %slice.41), channel_id=1, source_target_pairs={{0,96},{1,97},{2,98},{3,99},{4,100},{5,101},{6,102},{7,103},{8,104... | collective-permute-start | bytes 786440 | tf_op jit(solution)/shard_map/ppermute | solution.py:33
  26.2 14.9 %collective-permute-start.13 = (bf16[256,1280]{1,0:T(8,128)(2,1)S(1)}, bf16[256,1280]{1,0:T(8,128)(2,1)S(1)}, u32[]{:S(2)}, u32[]{:S(2)}) collective-permute-start(bf16[256,1280]{1,0:T(8,128)(2,1)S(1)} %pad_maximum_fusion.refs_4_.refs_3_), channel_id=1, source_target_pairs={{0,24},{1,25},{2,26},{3,27},{4,28},{5,29},{6,30},{7,31},{8,0},{9,1... | collective-permute-start | bytes 1966088 | tf_op jit(solution)/shard_map/ppermute | solution.py:33
  29.2 15.7 %collective-permute-start.11 = (bf16[256,1280]{1,0:T(8,128)(2,1)S(1)}, bf16[256,1280]{1,0:T(8,128)(2,1)S(1)}, u32[]{:S(2)}, u32[]{:S(2)}) collective-permute-start(bf16[256,1280]{1,0:T(8,128)(2,1)S(1)} %pad_maximum_fusion.refs_4_.refs_3_), channel_id=1, source_target_pairs={{0,8},{1,9},{2,10},{3,11},{4,12},{5,13},{6,14},{7,15},{8,16},{9,17... | collective-permute-start | bytes 1966088 | tf_op jit(solution)/shard_map/ppermute | solution.py:33
  30.6 22.9 %collective-permute-start.8 = (bf16[1024,256]{1,0:T(8,128)(2,1)S(1)}, bf16[1024,256]{1,0:T(8,128)(2,1)S(1)}, u32[]{:S(2)}, u32[]{:S(2)}) collective-permute-start(bf16[1024,256]{1,0:T(8,128)(2,1)S(1)} %get-tuple-element.102), channel_id=1, source_target_pairs={{128,224},{129,225},{130,226},{131,227},{132,228},{133,229},{134,2... | collective-permute-start | bytes 1572872 | tf_op jit(solution)/shard_map/ppermute | solution.py:33
  31.3 22.2 %collective-permute-start.9 = (bf16[1024,256]{1,0:T(8,128)(2,1)S(1)}, bf16[1024,256]{1,0:T(8,128)(2,1)S(1)}, u32[]{:S(2)}, u32[]{:S(2)}) collective-permute-start(bf16[1024,256]{1,0:T(8,128)(2,1)S(1)} %get-tuple-element.103), channel_id=1, source_target_pairs={{128,192},{129,193},{130,194},{131,195},{132,196},{133,197},{134,1... | collective-permute-start | bytes 1572872 | tf_op jit(solution)/shard_map/ppermute | solution.py:33
  32.0 21.5 %collective-permute-start.10 = (bf16[1024,256]{1,0:T(8,128)(2,1)S(1)}, bf16[1024,256]{1,0:T(8,128)(2,1)S(1)}, u32[]{:S(2)}, u32[]{:S(2)}) collective-permute-start(bf16[1024,256]{1,0:T(8,128)(2,1)S(1)} %get-tuple-element.104), channel_id=1, source_target_pairs={{128,160},{129,161},{130,162},{131,163},{132,164},{133,165},{134,1... | collective-permute-start | bytes 1572872 | tf_op jit(solution)/shard_map/ppermute | solution.py:33
  41.1 8.4 %collective-permute-start.14 = (bf16[128,1280]{1,0:T(8,128)(2,1)S(1)}, bf16[128,1280]{1,0:T(8,128)(2,1)S(1)}, u32[]{:S(2)}, u32[]{:S(2)}) collective-permute-start(bf16[128,1280]{1,0:T(8,128)(2,1)S(1)} %slice.43), channel_id=1, source_target_pairs={{0,24},{1,25},{2,26},{3,27},{4,28},{5,29},{6,30},{7,31},{8,0},{9,1... | collective-permute-start | bytes 983048 | tf_op jit(solution)/shard_map/ppermute | solution.py:33
  44.9 8.5 %collective-permute-start.12 = (bf16[128,1280]{1,0:T(8,128)(2,1)S(1)}, bf16[128,1280]{1,0:T(8,128)(2,1)S(1)}, u32[]{:S(2)}, u32[]{:S(2)}) collective-permute-start(bf16[128,1280]{1,0:T(8,128)(2,1)S(1)} %slice.42), channel_id=1, source_target_pairs={{0,8},{1,9},{2,10},{3,11},{4,12},{5,13},{6,14},{7,15},{8,16},{9,17... | collective-permute-start | bytes 983048 | tf_op jit(solution)/shard_map/ppermute | solution.py:33
  54.6 62.5 %collective-permute-start.18 = (bf16[4,256,1280]{2,1,0:T(8,128)(2,1)S(1)}, bf16[4,256,1280]{2,1,0:T(8,128)(2,1)S(1)}, u32[]{:S(2)}, u32[]{:S(2)}) collective-permute-start(bf16[4,256,1280]{2,1,0:T(8,128)(2,1)S(1)} %bitcast.26), channel_id=1, source_target_pairs={{0,96},{1,97},{2,98},{3,99},{4,100},{5,101},{6,102},{7,103},{8,104... | collective-permute-start | bytes 7864328 | tf_op jit(solution)/shard_map/ppermute | solution.py:33
  57.0 60.1 %collective-permute-start.17 = (bf16[4,256,1280]{2,1,0:T(8,128)(2,1)S(1)}, bf16[4,256,1280]{2,1,0:T(8,128)(2,1)S(1)}, u32[]{:S(2)}, u32[]{:S(2)}) collective-permute-start(bf16[4,256,1280]{2,1,0:T(8,128)(2,1)S(1)} %bitcast.27), channel_id=1, source_target_pairs={{0,32},{1,33},{2,34},{3,35},{4,36},{5,37},{6,38},{7,39},{8,40},{9,... | collective-permute-start | bytes 7864328 | tf_op jit(solution)/shard_map/ppermute | solution.py:33
  60.5 56.7 %collective-permute-start.16 = (bf16[4,1024,256]{2,1,0:T(8,128)(2,1)S(1)}, bf16[4,1024,256]{2,1,0:T(8,128)(2,1)S(1)}, u32[]{:S(2)}, u32[]{:S(2)}) collective-permute-start(bf16[4,1024,256]{2,1,0:T(8,128)(2,1)S(1)} %bitcast.30), channel_id=1, source_target_pairs={{0,24},{1,25},{2,26},{3,27},{4,28},{5,29},{6,30},{7,31},{8,0},{9,1... | collective-permute-start | bytes 6291464 | tf_op jit(solution)/shard_map/ppermute | solution.py:33
  62.4 54.7 %collective-permute-start.15 = (bf16[4,1024,256]{2,1,0:T(8,128)(2,1)S(1)}, bf16[4,1024,256]{2,1,0:T(8,128)(2,1)S(1)}, u32[]{:S(2)}, u32[]{:S(2)}) collective-permute-start(bf16[4,1024,256]{2,1,0:T(8,128)(2,1)S(1)} %bitcast.31), channel_id=1, source_target_pairs={{0,8},{1,9},{2,10},{3,11},{4,12},{5,13},{6,14},{7,15},{8,16},{9,17... | collective-permute-start | bytes 6291464 | tf_op jit(solution)/shard_map/ppermute | solution.py:33
  118.7 34.9 %collective-permute-start.22 = (bf16[2,256,1280]{2,1,0:T(8,128)(2,1)S(1)}, bf16[2,256,1280]{2,1,0:T(8,128)(2,1)S(1)}, u32[]{:S(2)}, u32[]{:S(2)}) collective-permute-start(bf16[2,256,1280]{2,1,0:T(8,128)(2,1)S(1)} %slice.37), channel_id=1, source_target_pairs={{0,96},{1,97},{2,98},{3,99},{4,100},{5,101},{6,102},{7,103},{8,104... | collective-permute-start | bytes 3932168 | tf_op jit(solution)/shard_map/ppermute | solution.py:33
  120.8 34.0 %collective-permute-start.21 = (bf16[2,256,1280]{2,1,0:T(8,128)(2,1)S(1)}, bf16[2,256,1280]{2,1,0:T(8,128)(2,1)S(1)}, u32[]{:S(2)}, u32[]{:S(2)}) collective-permute-start(bf16[2,256,1280]{2,1,0:T(8,128)(2,1)S(1)} %slice.36), channel_id=1, source_target_pairs={{0,32},{1,33},{2,34},{3,35},{4,36},{5,37},{6,38},{7,39},{8,40},{9,... | collective-permute-start | bytes 3932168 | tf_op jit(solution)/shard_map/ppermute | solution.py:33
  124.7 28.9 %collective-permute-start.20 = (bf16[2,1024,256]{2,1,0:T(8,128)(2,1)S(1)}, bf16[2,1024,256]{2,1,0:T(8,128)(2,1)S(1)}, u32[]{:S(2)}, u32[]{:S(2)}) collective-permute-start(bf16[2,1024,256]{2,1,0:T(8,128)(2,1)S(1)} %slice.35), channel_id=1, source_target_pairs={{0,24},{1,25},{2,26},{3,27},{4,28},{5,29},{6,30},{7,31},{8,0},{9,1... | collective-permute-start | bytes 3145736 | tf_op jit(solution)/shard_map/ppermute | solution.py:33
  129.9 23.7 %collective-permute-start.19 = (bf16[2,1024,256]{2,1,0:T(8,128)(2,1)S(1)}, bf16[2,1024,256]{2,1,0:T(8,128)(2,1)S(1)}, u32[]{:S(2)}, u32[]{:S(2)}) collective-permute-start(bf16[2,1024,256]{2,1,0:T(8,128)(2,1)S(1)} %slice.34), channel_id=1, source_target_pairs={{0,8},{1,9},{2,10},{3,11},{4,12},{5,13},{6,14},{7,15},{8,16},{9,17... | collective-permute-start | bytes 3145736 | tf_op jit(solution)/shard_map/ppermute | solution.py:33
  168.8 15.4 %collective-permute-start.31 = (bf16[256,256]{1,0:T(8,128)(2,1)S(1)}, bf16[256,256]{1,0:T(8,128)(2,1)S(1)}, u32[]{:S(2)}, u32[]{:S(2)}) collective-permute-start(bf16[256,256]{1,0:T(8,128)(2,1)S(1)} %shard_map.99), channel_id=1, source_target_pairs={{128,0},{129,1},{130,32},{131,33},{132,64},{133,65},{134,96},{135,... | collective-permute-start | bytes 393224 | tf_op jit(solution)/shard_map/ppermute | solution.py:33
  170.3 25.2 %collective-permute-start.39 = (bf16[256,256]{1,0:T(8,128)(2,1)S(1)}, bf16[256,256]{1,0:T(8,128)(2,1)S(1)}, u32[]{:S(2)}, u32[]{:S(2)}) collective-permute-start(bf16[256,256]{1,0:T(8,128)(2,1)S(1)} %shard_map.101), channel_id=1, source_target_pairs={{128,0},{129,1},{130,32},{131,33},{132,64},{133,65},{134,96},{135,... | collective-permute-start | bytes 393224 | tf_op jit(solution)/shard_map/ppermute | solution.py:33
  184.3 18.0 %collective-permute-start.34 = (bf16[256,256]{1,0:T(8,128)(2,1)S(1)}, bf16[256,256]{1,0:T(8,128)(2,1)S(1)}, u32[]{:S(2)}, u32[]{:S(2)}) collective-permute-start(bf16[256,256]{1,0:T(8,128)(2,1)S(1)} %collective-permute-done.31.refs_1_.refs_6_), channel_id=1, source_target_pairs={{0,6},{1,7},{2,4},{3,5},{4,2},{5,3},{6,0},{7,1},{8,14},{9,15},{10,... | collective-permute-start | bytes 393224 | tf_op jit(solution)/shard_map/ppermute | solution.py:33
  190.2 14.6 %collective-permute-start.33 = (bf16[256,256]{1,0:T(8,128)(2,1)S(1)}, bf16[256,256]{1,0:T(8,128)(2,1)S(1)}, u32[]{:S(2)}, u32[]{:S(2)}) collective-permute-start(bf16[256,256]{1,0:T(8,128)(2,1)S(1)} %collective-permute-done.31.refs_1_.refs_6_), channel_id=1, source_target_pairs={{0,4},{1,5},{2,6},{3,7},{4,0},{5,1},{6,2},{7,3},{8,12},{9,13},{10,... | collective-permute-start | bytes 393224 | tf_op jit(solution)/shard_map/ppermute | solution.py:33
  192.1 12.7 %collective-permute-start.32 = (bf16[256,256]{1,0:T(8,128)(2,1)S(1)}, bf16[256,256]{1,0:T(8,128)(2,1)S(1)}, u32[]{:S(2)}, u32[]{:S(2)}) collective-permute-start(bf16[256,256]{1,0:T(8,128)(2,1)S(1)} %collective-permute-done.31.refs_1_.refs_6_), channel_id=1, source_target_pairs={{0,2},{1,3},{2,0},{3,1},{4,6},{5,7},{6,4},{7,5},{8,10},{9,11},{10,... | collective-permute-start | bytes 393224 | tf_op jit(solution)/shard_map/ppermute | solution.py:33
  195.5 11.3 %collective-permute-start.42 = (bf16[256,256]{1,0:T(8,128)(2,1)S(1)}, bf16[256,256]{1,0:T(8,128)(2,1)S(1)}, u32[]{:S(2)}, u32[]{:S(2)}) collective-permute-start(bf16[256,256]{1,0:T(8,128)(2,1)S(1)} %collective-permute-done.39.refs_5_.refs_7_), channel_id=1, source_target_pairs={{0,6},{1,7},{2,4},{3,5},{4,2},{5,3},{6,0},{7,1},{8,14},{9,15},{10,... | collective-permute-start | bytes 393224 | tf_op jit(solution)/shard_map/ppermute | solution.py:33
  199.5 8.4 %collective-permute-start.41 = (bf16[256,256]{1,0:T(8,128)(2,1)S(1)}, bf16[256,256]{1,0:T(8,128)(2,1)S(1)}, u32[]{:S(2)}, u32[]{:S(2)}) collective-permute-start(bf16[256,256]{1,0:T(8,128)(2,1)S(1)} %collective-permute-done.39.refs_5_.refs_7_), channel_id=1, source_target_pairs={{0,4},{1,5},{2,6},{3,7},{4,0},{5,1},{6,2},{7,3},{8,12},{9,13},{10,... | collective-permute-start | bytes 393224 | tf_op jit(solution)/shard_map/ppermute | solution.py:33
  218.6 24.3 %all-to-all-start.2 = ((bf16[16,80,128]{2,1,0:T(8,128)(2,1)}), bf16[16,80,128]{2,1,0:T(8,128)(2,1)S(1)}, u32[]{:S(2)}, u32[]{:S(2)}) async-start(bf16[16,80,128]{2,1,0:T(8,128)(2,1)} %copy-done.20), calls=%async_computation.2 | async-start | bytes 655360 | tf_op jit(solution)/shard_map/all_to_all | solution.py:449
  271.0 21.1 %collective-permute-start.47 = (bf16[512,256]{1,0:T(8,128)(2,1)S(1)}, bf16[512,256]{1,0:T(8,128)(2,1)S(1)}, u32[]{:S(2)}, u32[]{:S(2)}) collective-permute-start(bf16[512,256]{1,0:T(8,128)(2,1)S(1)} %get-tuple-element.165), channel_id=1, source_target_pairs={{0,4},{1,5},{2,6},{3,7},{4,0},{5,1},{6,2},{7,3},{8,12},{9,13},{10,... | collective-permute-start | bytes 786440 | tf_op jit(solution)/shard_map/ppermute | solution.py:33
  275.1 23.9 %collective-permute-start.48 = (bf16[512,256]{1,0:T(8,128)(2,1)S(1)}, bf16[512,256]{1,0:T(8,128)(2,1)S(1)}, u32[]{:S(2)}, u32[]{:S(2)}) collective-permute-start(bf16[512,256]{1,0:T(8,128)(2,1)S(1)} %get-tuple-element.166), channel_id=1, source_target_pairs={{0,6},{1,7},{2,4},{3,5},{4,2},{5,3},{6,0},{7,1},{8,14},{9,15},{10,... | collective-permute-start | bytes 786440 | tf_op jit(solution)/shard_map/ppermute | solution.py:33
  278.6 20.4 %collective-permute-start.49 = (bf16[512,256]{1,0:T(8,128)(2,1)S(1)}, bf16[512,256]{1,0:T(8,128)(2,1)S(1)}, u32[]{:S(2)}, u32[]{:S(2)}) collective-permute-start(bf16[512,256]{1,0:T(8,128)(2,1)S(1)} %get-tuple-element.167), channel_id=1, source_target_pairs={{0,2},{1,3},{2,0},{3,1},{4,6},{5,7},{6,4},{7,5},{8,10},{9,11},{10,... | collective-permute-start | bytes 786440 | tf_op jit(solution)/shard_map/ppermute | solution.py:33
  (53 other events, 1697.1 us)
